TPU v7x, 32 devices: a whole 2x2x4 slice. The times are simulated.
32 devices in a mesh: groups: 2 (over y), mesh: 4 (over z), feat: 4 (over x, core).
Axes of the slice: x: 2, y: 2, z: 4, core: 2. Of those that a mesh axis runs over, the one named last changes fastest.
Arguments:
- nodes: bfloat16 [8192, 512], P(('groups', 'mesh')), parts along dimension 0, may hold values from -6 to 6
- fine_edges: bfloat16 [49152, 512], P(('groups', 'mesh', 'feat')), parts along dimension 0, may hold values from -6 to 6
- fine_send: int32 [49152], P(('groups', 'mesh', 'feat')), parts along dimension 0, may hold values from 0 to 1279, as said below
- fine_recv: int32 [49152], P(('groups', 'mesh', 'feat')), parts along dimension 0, may hold values from 0 to 1024, as said below
- halo_send: int32 [2048], P(('groups', 'mesh')), parts along dimension 0, may hold values from 0 to 1023, as said below
- coarse_edges: bfloat16 [3072, 512], P(('groups', 'mesh', 'feat')), parts along dimension 0, may hold values from -6 to 6
- coarse_send: int32 [3072], P(('groups', 'mesh', 'feat')), parts along dimension 0, may hold values from 0 to 511
- coarse_recv: int32 [3072], P(('groups', 'mesh', 'feat')), parts along dimension 0, may hold values from 0 to 511
- edge_w1: bfloat16 [2, 512, 1536], P(None, 'feat'), may hold values from -0.15625 to 0.15625
- edge_b1: bfloat16 [2, 512], P(None, 'feat'), may hold values from -3 to 3
- edge_w2: bfloat16 [2, 512, 512], P(None, 'feat'), may hold values from -0.25 to 0.25
- edge_gain: bfloat16 [2, 512], replicated, may hold values from 0.25 to 1.75
- node_w1: bfloat16 [2, 512, 1024], P(None, 'feat'), may hold values from -0.1875 to 0.1875
- node_b1: bfloat16 [2, 512], P(None, 'feat'), may hold values from -3 to 3
- node_w2: bfloat16 [2, 512, 512], P(None, 'feat'), may hold values from -0.25 to 0.25
- node_gain: bfloat16 [2, 512], replicated, may hold values from 0.25 to 1.75
Outputs:
- nodes_out: bfloat16 [8192, 512], P(('groups', 'mesh')), parts along dimension 0
There are 2 independent parts, one for each index of `groups`. A program takes and returns all parts, laid end to end along the dimension named above; an argument that names none is the same for every part. Nothing has to cross between parts.
Inputs may be any that keep to these rules, and one draw needn't show every extreme that they name: `fine_send`: values index the extended table of the slot's partition: its 1024 nodes, then 128 rows from the previous and 128 from the next partition. `fine_recv`: the value 1024 marks an unused slot; each partition has from half to all of its 6144 slots in use, and some partition all. `halo_send`: each partition's 2 * 128 entries are distinct rows of that partition: first those for the previous partition, then those for the next.
All inputs are finite; a program needn't handle non-finite values.
Results may differ from a plain program's by a relative error of at most 0.0085.
Values may be sent and summed in bfloat16 or wider, within the bound.
No kernel may reach another device: no remote copies, remote signals or barrier semaphores. Data moves between devices by JAX's collectives and lax.ppermute only.
A program may use at most 64 MiB of HBM per device.

v0:
```python
import jax
import jax.numpy as jnp
from jax import lax
from jax.sharding import PartitionSpec as P

STEPS = 2


def with_halo(cells, sides, width):
    for axis, dim in sides:
        count = lax.axis_size(axis)
        head = lax.slice_in_dim(cells, 0, width, axis=dim)
        tail = lax.slice_in_dim(cells, cells.shape[dim] - width, cells.shape[dim], axis=dim)
        cells = jnp.concatenate(
            [
                lax.ppermute(tail, axis, [(i, (i + 1) % count) for i in range(count)]),
                cells,
                lax.ppermute(head, axis, [((i + 1) % count, i) for i in range(count)]),
            ],
            axis=dim,
        )
    return cells


def layer_norm(values, gain):
    row_mean = jnp.mean(values, axis=-1, keepdims=True)
    centred = values - row_mean
    row_var = jnp.mean(centred * centred, axis=-1, keepdims=True)
    return centred * lax.rsqrt(row_var + 1e-05) * gain.astype(jnp.float32)


def hidden_adder(inputs, pieces):
    w_in, hidden_bias, w_out = pieces
    pre_act = lax.dot_general(
        inputs, w_in, (((1,), (1,)), ((), ())), preferred_element_type=jnp.float32
    )
    activated = jax.nn.silu(pre_act + hidden_bias.astype(jnp.float32)).astype(jnp.bfloat16)
    return jnp.dot(activated, w_out, preferred_element_type=jnp.float32)


def local(
    nodes,
    fine_edges,
    fine_send,
    fine_recv,
    halo_send,
    coarse_edges,
    coarse_send,
    coarse_recv,
    edge_w1,
    edge_b1,
    edge_w2,
    edge_gain,
    node_w1,
    node_b1,
    node_w2,
    node_gain,
):
    node_count = nodes.shape[0]
    width = nodes.shape[1]
    halo_rows = halo_send.shape[0] // 2
    mesh_index = lax.axis_index("mesh")
    per_part = node_count // 8
    fine_count = fine_edges.shape[0]
    recv_safe = jnp.minimum(fine_recv, node_count - 1)
    row_start = 0
    for layer_index in range(STEPS):
        coarse_nodes = lax.all_gather(
            nodes.reshape(per_part, 8, width)[:, 0], "mesh", axis=0, tiled=True
        )
        coarse_count = coarse_nodes.shape[0]
        outgoing = jnp.take(nodes, halo_send, axis=0)
        bordered = with_halo(outgoing, (("mesh", 0),), halo_rows)
        node_table = jnp.concatenate(
            [nodes, bordered[:halo_rows], bordered[3 * halo_rows :]], axis=0
        )
        fine_in = jnp.concatenate(
            [
                fine_edges,
                jnp.take(node_table, fine_send, axis=0),
                jnp.take(nodes, recv_safe, axis=0),
            ],
            axis=1,
        )
        coarse_in = jnp.concatenate(
            [
                coarse_edges,
                jnp.take(coarse_nodes, coarse_send, axis=0),
                jnp.take(coarse_nodes, coarse_recv, axis=0),
            ],
            axis=1,
        )
        inputs = jnp.concatenate([fine_in, coarse_in], axis=0)
        edge_out = hidden_adder(
            inputs,
            (
                lax.all_gather(edge_w1[layer_index], "feat", axis=0, tiled=True),
                lax.all_gather(edge_b1[layer_index], "feat", axis=0, tiled=True),
                lax.all_gather(edge_w2[layer_index], "feat", axis=0, tiled=True),
            ),
        )
        all_edges = jnp.concatenate([fine_edges, coarse_edges], axis=0)
        all_edges = (
            all_edges.astype(jnp.float32) + layer_norm(edge_out, edge_gain[layer_index])
        ).astype(jnp.bfloat16)
        fine_edges = all_edges[:fine_count]
        coarse_edges = all_edges[fine_count:]
        fine_part = jax.ops.segment_sum(fine_edges.astype(jnp.float32), fine_recv, node_count)
        fine_agg = lax.psum(fine_part, "feat")
        coarse_part = jax.ops.segment_sum(
            coarse_edges.astype(jnp.float32), coarse_recv, coarse_count
        )
        coarse_all = lax.psum(coarse_part, ("mesh", "feat"))
        coarse_mine = lax.dynamic_slice_in_dim(
            coarse_all, mesh_index * per_part + row_start // 8, node_count // 8, 0
        )
        summed = (
            fine_agg.reshape(node_count // 8, 8, width)
            .at[:, 0]
            .add(coarse_mine)
            .reshape(node_count, width)
        )
        node_rows = nodes
        node_in = jnp.concatenate([node_rows, summed.astype(jnp.bfloat16)], axis=1)
        node_out = hidden_adder(
            node_in,
            (
                lax.all_gather(node_w1[layer_index], "feat", axis=0, tiled=True),
                lax.all_gather(node_b1[layer_index], "feat", axis=0, tiled=True),
                lax.all_gather(node_w2[layer_index], "feat", axis=0, tiled=True),
            ),
        )
        new_rows = (
            node_rows.astype(jnp.float32) + layer_norm(node_out, node_gain[layer_index])
        ).astype(jnp.bfloat16)
        nodes = new_rows
    return nodes


def solution(mesh):
    placed = (
        P(("groups", "mesh"), None),
        P(("groups", "mesh", "feat"), None),
        P(("groups", "mesh", "feat")),
        P(("groups", "mesh", "feat")),
        P(("groups", "mesh")),
        P(("groups", "mesh", "feat"), None),
        P(("groups", "mesh", "feat")),
        P(("groups", "mesh", "feat")),
        P(None, "feat", None),
        P(None, "feat"),
        P(None, "feat", None),
        P(),
        P(None, "feat", None),
        P(None, "feat"),
        P(None, "feat", None),
        P(),
    )
    return jax.shard_map(
        local, mesh=mesh, in_specs=placed, out_specs=P(("groups", "mesh"), None), check_vma=False
    )
```

profile of v0, /device:TPU:0, one launch (start us, length us, event | category | flops | bytes accessed | tf_op | source)
XLA Modules:
  0.0 505.5 jit_solution(14268354066467535951)
XLA Ops:
  12.0 3.0 collective-permute-start
  18.5 15.7 %all-gather = bf16[512,1,512]{2,0,1:T(8,128)(2,1)S(1)} all-gather(bf16[128,1,512]{2,0,1:T(8,128)(2,1)S(1)} %copy.22), channel_id=2, replica_groups=mesh['groups'=2,'mesh'=4,'feat'=4] {'mesh'}, dimensions={0}, use_global_device_ids=true | all-gather | bytes 655360 | tf_op jit(solution)/shard_map/all_gather | solution.py:68
  35.8 4.8 gather_fusion.2
  44.1 7.1 %all-gather.3 = bf16[1,512,512]{2,1,0:T(8,128)(2,1)S(1)} all-gather(bf16[1,128,512]{2,1,0:T(8,128)(2,1)S(1)} %get-tuple-element.40), channel_id=5, replica_groups=mesh['groups'=2,'mesh'=4,'feat'=4] {'feat'}, dimensions={1}, use_global_device_ids=true | all-gather | bytes 655360 | tf_op jit(solution)/shard_map/all_gather | solution.py:99
  51.2 5.6 %all-gather.2 = bf16[1,512]{1,0:T(2,128)(2,1)S(1)} all-gather(bf16[1,128]{1,0:T(2,128)(2,1)S(1)} %get-tuple-element.52), channel_id=4, replica_groups=mesh['groups'=2,'mesh'=4,'feat'=4] {'feat'}, dimensions={1}, use_global_device_ids=true | all-gather | bytes 1280 | tf_op jit(solution)/shard_map/all_gather | solution.py:98
  57.8 5.4 %gather_fusion.1 = bf16[1536,512]{1,0:T(8,128)(2,1)} fusion(bf16[1280,512]{1,0:T(8,128)(2,1)S(1)} %pad_maximum_fusion, s32[2048]{0:T(1024)S(1)} %pad_clamp_fusion.1), kind=kCustom, calls=%fused_computation.1.clone | custom fusion | bytes 3151872 | tf_op jit(solution)/shard_map/jit(_take)/gather | solution.py:80
  63.2 3.0 broadcast_select_fusion.3
  66.2 18.3 %fusion.106 = (f32[1632]{0:T(1024)S(1)}, f32[1632,512]{1,0:T(8,128)}) fusion(bf16[1,512,512]{2,1,0:T(8,128)(2,1)S(1)} %all-gather.3, bf16[96,512]{1,0:T(8,128)(2,1)S(1)} %broadcast_select_fusion.7, bf16[96,512]{1,0:T(8,128)(2,1)S(1)} %copy-done.11, bf16[96,512]{1,0:T(8,128)(2,1)} %param.33, bf16[1536,512]{1,0:T(8,128)(2,1)} %broadcast_select_fusion.1, ...), kind=kOutput, calls=%fused_computation.151 | convolution fusion | flops 3458480640 | bytes 10461568 | tf_op jit(solution)/shard_map/dot_general | solution.py:38
  92.6 11.2 %scatter_custom_fusion = f32[1024,512]{1,0:T(8,128)} fusion(s32[1536]{0:T(1024)S(1)} %copy-done.13, f32[]{:T(128)} %constant.114.clone.1, bf16[1632,512]{1,0:T(8,128)(2,1)S(1)} %add_convert_fusion.1), kind=kCustom, calls=%fused_computation.46 | custom fusion | flops 1572864 | bytes 3670020 | tf_op jit(solution)/shard_map/scatter-add | solution.py:108
  106.4 8.1 %all-gather.6 = bf16[1,512,512]{2,1,0:T(8,128)(2,1)} all-gather(bf16[1,128,512]{2,1,0:T(8,128)(2,1)S(1)} %get-tuple-element.38), channel_id=8, replica_groups=mesh['groups'=2,'mesh'=4,'feat'=4] {'feat'}, dimensions={1}, use_global_device_ids=true | all-gather | bytes 655360 | tf_op jit(solution)/shard_map/all_gather | solution.py:130
  115.0 5.0 all-gather.5
  120.6 7.8 %all-gather.10 = bf16[1,512,512]{2,1,0:T(8,128)(2,1)} all-gather(bf16[1,128,512]{2,1,0:T(8,128)(2,1)S(1)} %get-tuple-element.39), channel_id=12, replica_groups=mesh['groups'=2,'mesh'=4,'feat'=4] {'feat'}, dimensions={1}, use_global_device_ids=true | all-gather | bytes 655360 | tf_op jit(solution)/shard_map/all_gather | solution.py:99
  128.5 5.0 all-gather.9
  135.3 49.6 %all-reduce.7.cloned.1.call-done = f32[512,512]{1,0:T(8,128)} async-done(((f32[512,512]{1,0:T(8,128)}), f32[512,512]{1,0:T(8,128)}) %all-reduce.7.cloned.1.call-update) | async-done | bytes 1048592 | tf_op jit(solution)/shard_map/psum | solution.py:113
  185.9 52.1 %all-reduce.5.cloned.1.call-done = f32[128,8,512]{2,1,0:T(8,128)} async-done(((f32[128,8,512]{2,1,0:T(8,128)}), f32[128,8,512]{2,1,0:T(8,128)}) %all-reduce.5.cloned.1.call-update) | async-done | bytes 2097168 | tf_op jit(solution)/shard_map/psum | solution.py:109
  239.9 6.3 %scatter-add.40 = f32[128,8,512]{2,1,0:T(8,128)} dynamic-update-slice(f32[128,8,512]{2,1,0:T(8,128)} %all-reduce.5.cloned.1.call-done, f32[128,1,512]{2,1,0:T(1,128)S(1)} %slice_add_fusion.1, s32[]{:T(128)} %constant.122.clone.1, s32[]{:T(128)} %constant.122.clone.1, s32[]{:T(128)} %constant.122.clone.1) | dynamic-update-slice | bytes 524292 | tf_op jit(solution)/shard_map/scatter-add | solution.py:120
  249.1 7.2 %all-gather.21.cloned.1.call-done = bf16[1,512,1024]{2,1,0:T(8,128)(2,1)} async-done(((bf16[1,128,1024]{2,1,0:T(8,128)(2,1)}), bf16[1,512,1024]{2,1,0:T(8,128)(2,1)}) %all-gather.21.cloned.1.call-update) | async-done | bytes 1048592 | tf_op jit(solution)/shard_map/all_gather | solution.py:128
  256.3 3.7 fusion.111
  263.6 16.0 %all-gather.7 = bf16[512,1,512]{2,0,1:T(8,128)(2,1)S(1)} all-gather(bf16[128,1,512]{2,0,1:T(8,128)(2,1)S(1)} %copy.23), channel_id=9, replica_groups=mesh['groups'=2,'mesh'=4,'feat'=4] {'mesh'}, dimensions={0}, use_global_device_ids=true | all-gather | bytes 655360 | tf_op jit(solution)/shard_map/all_gather | solution.py:68
  280.9 5.4 %gather_fusion.7 = bf16[1536,512]{1,0:T(8,128)(2,1)} fusion(bf16[1024,512]{1,0:T(8,128)(2,1)S(1)} %add_convert_fusion.3, s32[2048]{0:T(1024)S(1)} %pad_clamp_fusion), kind=kCustom, calls=%fused_computation.6.clone | custom fusion | bytes 3151872 | tf_op jit(solution)/shard_map/jit(_take)/gather | solution.py:81
  296.8 5.4 %gather_fusion.6 = bf16[1536,512]{1,0:T(8,128)(2,1)} fusion(bf16[1280,512]{1,0:T(8,128)(2,1)S(1)} %pad_maximum_fusion.1, s32[2048]{0:T(1024)S(1)} %pad_clamp_fusion.1), kind=kCustom, calls=%fused_computation.5.clone | custom fusion | bytes 3151872 | tf_op jit(solution)/shard_map/jit(_take)/gather | solution.py:80
  302.3 3.0 broadcast_select_fusion.2
  305.3 8.6 %fusion.116 = (f32[1632]{0:T(1024)S(1)}, f32[1632,512]{1,0:T(8,128)}) fusion(bf16[1,512,512]{2,1,0:T(8,128)(2,1)S(1)} %copy-done.8, bf16[96,512]{1,0:T(8,128)(2,1)S(1)} %broadcast_select_fusion.6, bf16[96,512]{1,0:T(8,128)(2,1)S(1)} %broadcast_select_fusion.8, bf16[96,512]{1,0:T(8,128)(2,1)S(1)} %slice-done, bf16[1536,512]{1,0:T(8,128)(2,1)} %broadcast_select_fusion, ...), kind=kOutput, calls=%fused_computation.153 | convolution fusion | flops 3458480640 | bytes 10461568 | tf_op jit(solution)/shard_map/dot_general | solution.py:38
  316.6 3.5 add_convert_fusion
  322.7 11.7 %scatter_custom_fusion.2 = f32[1024,512]{1,0:T(8,128)} fusion(s32[1536]{0:T(1024)} %param.31, bf16[1632,512]{1,0:T(8,128)(2,1)} %add_convert_fusion, f32[]{:T(128)} %constant.114.clone.1), kind=kCustom, calls=%fused_computation.44 | custom fusion | flops 1572864 | bytes 3670528 | tf_op jit(solution)/shard_map/scatter-add | solution.py:108
  335.2 5.0 all-gather.12
  340.2 7.5 %all-gather.13 = bf16[1,512,512]{2,1,0:T(8,128)(2,1)S(1)} all-gather(bf16[1,128,512]{2,1,0:T(8,128)(2,1)S(1)} %get-tuple-element.37), channel_id=15, replica_groups=mesh['groups'=2,'mesh'=4,'feat'=4] {'feat'}, dimensions={1}, use_global_device_ids=true | all-gather | bytes 655360 | tf_op jit(solution)/shard_map/all_gather | solution.py:130
  347.7 67.9 %all-reduce.11.cloned.1.call-done = f32[512,512]{1,0:T(8,128)} async-done(((f32[512,512]{1,0:T(8,128)}), f32[512,512]{1,0:T(8,128)}) %all-reduce.11.cloned.1.call-update) | async-done | bytes 1048592 | tf_op jit(solution)/shard_map/psum | solution.py:113
  416.6 52.2 %all-reduce.9.cloned.1.call-done = f32[128,8,512]{2,1,0:T(8,128)} async-done(((f32[128,8,512]{2,1,0:T(8,128)}), f32[128,8,512]{2,1,0:T(8,128)}) %all-reduce.9.cloned.1.call-update) | async-done | bytes 2097168 | tf_op jit(solution)/shard_map/psum | solution.py:109
  470.7 6.3 %scatter-add.43 = f32[128,8,512]{2,1,0:T(8,128)} dynamic-update-slice(f32[128,8,512]{2,1,0:T(8,128)} %all-reduce.9.cloned.1.call-done, f32[128,1,512]{2,1,0:T(1,128)S(1)} %slice_add_fusion, s32[]{:T(128)} %constant.122.clone.1, s32[]{:T(128)} %constant.122.clone.1, s32[]{:T(128)} %constant.122.clone.1) | dynamic-update-slice | bytes 524292 | tf_op jit(solution)/shard_map/scatter-add | solution.py:120
  478.9 8.2 %all-gather.25.cloned.1.call-done = bf16[1,512,1024]{2,1,0:T(8,128)(2,1)} async-done(((bf16[1,128,1024]{2,1,0:T(8,128)(2,1)}), bf16[1,512,1024]{2,1,0:T(8,128)(2,1)}) %all-gather.25.cloned.1.call-update) | async-done | bytes 1048592 | tf_op jit(solution)/shard_map/all_gather | solution.py:128
  487.1 4.7 fusion.121
  (175 shorter events, 66.8 us)
Async XLA Ops:
  6.5 10.6 %copy-start.7 = (bf16[2,128,1536]{2,1,0:T(8,128)(2,1)S(1)}, bf16[2,128,1536]{2,1,0:T(8,128)(2,1)}, u32[]{:S(2)}) copy-start(bf16[2,128,1536]{2,1,0:T(8,128)(2,1)} %param.36) | copy-start | bytes 2359300
  6.5 59.7 %all-gather.19.cloned.1.call-start = ((), (), s32[]{:S(2)}) async-start(), calls=%async_computation.4 | async-start | bytes 1966080 | tf_op jit(solution)/shard_map/all_gather | solution.py:97
  8.0 10.0 %copy-start.29 = (pred[256]{0:T(512)(128)(4,1)}, pred[256]{0:T(512)(128)(4,1)S(1)}, u32[]{:S(2)}) copy-start(pred[256]{0:T(512)(128)(4,1)S(1)} %compare_and_fusion.4) | copy-start | bytes 772
  11.1 7.0 %copy-start.12 = (s32[1536]{0:T(1024)S(1)}, s32[1536]{0:T(1024)}, u32[]{:S(2)}) copy-start(s32[1536]{0:T(1024)} %param.30) | copy-start | bytes 18436
  11.2 7.0 %copy-start.36 = (s32[96]{0:T(128)S(1)}, s32[96]{0:T(128)}, u32[]{:S(2)}) copy-start(s32[96]{0:T(128)} %param.34) | copy-start | bytes 1156
  11.2 7.0 %copy-start.37 = (s32[96]{0:T(128)S(1)}, s32[96]{0:T(128)}, u32[]{:S(2)}) copy-start(s32[96]{0:T(128)} %param.35) | copy-start | bytes 1156
  11.2 7.0 %copy-start.13 = (s32[1536]{0:T(1024)S(1)}, s32[1536]{0:T(1024)}, u32[]{:S(2)}) copy-start(s32[1536]{0:T(1024)} %param.31) | copy-start | bytes 18436
  11.2 7.1 %copy-start = (bf16[1024,512]{1,0:T(8,128)(2,1)S(1)}, bf16[1024,512]{1,0:T(8,128)(2,1)}, u32[]{:S(2)}) copy-start(bf16[1024,512]{1,0:T(8,128)(2,1)} %param.28) | copy-start | bytes 3145732
  12.0 44.8 %collective-permute-start = (bf16[128,512]{1,0:T(8,128)(2,1)}, bf16[128,512]{1,0:T(8,128)(2,1)S(1)}, u32[]{:S(2)}, u32[]{:S(2)}) collective-permute-start(bf16[128,512]{1,0:T(8,128)(2,1)} %get-tuple-element.43), channel_id=1, source_target_pairs={{0,4},{4,8},{8,12},{12,0},{1,5},{5,9},{9,13},{13,1},{2,6},{6,10},{... | collective-permute-start | bytes 393224 | tf_op jit(solution)/shard_map/ppermute | solution.py:16
  15.1 41.7 %collective-permute-start.1 = (bf16[128,512]{1,0:T(8,128)(2,1)}, bf16[128,512]{1,0:T(8,128)(2,1)}, u32[]{:S(2)}, u32[]{:S(2)}) collective-permute-start(bf16[128,512]{1,0:T(8,128)(2,1)} %get-tuple-element.44), channel_id=1, source_target_pairs={{4,0},{8,4},{12,8},{0,12},{5,1},{9,5},{13,9},{1,13},{6,2},{10,6},{... | collective-permute-start | bytes 393224 | tf_op jit(solution)/shard_map/ppermute | solution.py:18
  18.1 166.9 %all-reduce.7.cloned.1.call-start = ((), (), s32[]{:S(2)}) async-start(), calls=%async_computation.1 | async-start | bytes 2097152 | tf_op jit(solution)/shard_map/psum | solution.py:113
  18.2 45.1 %copy-start.14 = (pred[1536]{0:T(1024)(128)(4,1)}, pred[1536]{0:T(1024)(128)(4,1)S(1)}, u32[]{:S(2)}) copy-start(pred[1536]{0:T(1024)(128)(4,1)S(1)} %compare_and_fusion.1) | copy-start | bytes 4612
  18.2 23.0 %copy-start.27 = (pred[96]{0:T(512)(128)(4,1)}, pred[96]{0:T(512)(128)(4,1)S(1)}, u32[]{:S(2)}) copy-start(pred[96]{0:T(512)(128)(4,1)S(1)} %get-tuple-element.63) | copy-start | bytes 292
  18.2 23.7 %copy-start.25 = (pred[96]{0:T(512)(128)(4,1)}, pred[96]{0:T(512)(128)(4,1)S(1)}, u32[]{:S(2)}) copy-start(pred[96]{0:T(512)(128)(4,1)S(1)} %get-tuple-element.64) | copy-start | bytes 292
  18.3 24.4 %copy-start.16 = (pred[1536]{0:T(1024)(128)(4,1)}, pred[1536]{0:T(1024)(128)(4,1)S(1)}, u32[]{:S(2)}) copy-start(pred[1536]{0:T(1024)(128)(4,1)S(1)} %compare_and_fusion) | copy-start | bytes 4612
  18.3 17.4 %copy-start.23 = (s32[1024]{0:T(1024)}, s32[1024]{0:T(1024)S(1)}, u32[]{:S(2)}) copy-start(s32[1024]{0:T(1024)S(1)} %pad_clamp_fusion.2) | copy-start | bytes 12292
  35.8 6.8 %copy-start.10 = (bf16[2,128,512]{2,1,0:T(8,128)(2,1)S(1)}, bf16[2,128,512]{2,1,0:T(8,128)(2,1)}, u32[]{:S(2)}) copy-start(bf16[2,128,512]{2,1,0:T(8,128)(2,1)} %param.38) | copy-start | bytes 786436
  90.1 45.3 %copy-start.1 = (bf16[1632,512]{1,0:T(8,128)(2,1)}, bf16[1632,512]{1,0:T(8,128)(2,1)S(1)}, u32[]{:S(2)}) copy-start(bf16[1632,512]{1,0:T(8,128)(2,1)S(1)} %add_convert_fusion.1) | copy-start | bytes 5013508
  92.4 11.5 %copy-start.9 = (bf16[2,128,1024]{2,1,0:T(8,128)(2,1)S(1)}, bf16[2,128,1024]{2,1,0:T(8,128)(2,1)}, u32[]{:S(2)}) copy-start(bf16[2,128,1024]{2,1,0:T(8,128)(2,1)} %param.40) | copy-start | bytes 1572868
  92.4 145.6 %all-reduce.5.cloned.1.call-start = ((), (), s32[]{:S(2)}) async-start(), calls=%async_computation | async-start | bytes 4194304 | tf_op jit(solution)/shard_map/psum | solution.py:109
  103.8 10.7 %copy-start.33 = (bf16[2,128]{1,0:T(2,128)(2,1)S(1)}, bf16[2,128]{1,0:T(2,128)(2,1)}, u32[]{:S(2)}) copy-start(bf16[2,128]{1,0:T(2,128)(2,1)} %param.41) | copy-start | bytes 1540
  103.8 16.3 %copy-start.22 = (bf16[2,512]{1,0:T(2,128)(2,1)S(1)}, bf16[2,512]{1,0:T(2,128)(2,1)}, u32[]{:S(2)}) copy-start(bf16[2,512]{1,0:T(2,128)(2,1)} %param.43) | copy-start | bytes 6148
  103.8 24.7 %copy-start.35 = (bf16[1,128]{1,0:T(2,128)(2,1)S(1)}, bf16[1,128]{1,0:T(2,128)(2,1)}, u32[]{:S(2)}) copy-start(bf16[1,128]{1,0:T(2,128)(2,1)} %get-tuple-element.51) | copy-start | bytes 772
  103.8 152.5 %all-gather.21.cloned.1.call-start = ((), (), s32[]{:S(2)}) async-start(), calls=%async_computation.5 | async-start | bytes 1310720 | tf_op jit(solution)/shard_map/all_gather | solution.py:128
  104.7 200.6 %all-gather.23.cloned.1.call-start = ((), (), s32[]{:S(2)}) async-start(), calls=%async_computation.6 | async-start | bytes 1966080 | tf_op jit(solution)/shard_map/all_gather | solution.py:97
  105.3 310.3 %all-reduce.11.cloned.1.call-start = ((), (), s32[]{:S(2)}) async-start(), calls=%async_computation.3 | async-start | bytes 2097152 | tf_op jit(solution)/shard_map/psum | solution.py:113
  280.9 7.4 %copy-start.30 = (pred[256]{0:T(512)(128)(4,1)S(1)}, pred[256]{0:T(512)(128)(4,1)}, u32[]{:S(2)}) copy-start(pred[256]{0:T(512)(128)(4,1)} %copy-done.29) | copy-start | bytes 772
  288.3 7.1 %copy-start.26 = (pred[96]{0:T(512)(128)(4,1)S(1)}, pred[96]{0:T(512)(128)(4,1)}, u32[]{:S(2)}) copy-start(pred[96]{0:T(512)(128)(4,1)} %copy-done.25) | copy-start | bytes 292
  288.4 7.6 %collective-permute-start.2 = (bf16[128,512]{1,0:T(8,128)(2,1)S(1)}, bf16[128,512]{1,0:T(8,128)(2,1)S(1)}, u32[]{:S(2)}, u32[]{:S(2)}) collective-permute-start(bf16[128,512]{1,0:T(8,128)(2,1)S(1)} %get-tuple-element.41), channel_id=1, source_target_pairs={{0,4},{4,8},{8,12},{12,0},{1,5},{5,9},{9,13},{13,1},{2,6},{6,10},{... | collective-permute-start | bytes 393224 | tf_op jit(solution)/shard_map/ppermute | solution.py:16
  290.2 6.5 %collective-permute-start.3 = (bf16[128,512]{1,0:T(8,128)(2,1)S(1)}, bf16[128,512]{1,0:T(8,128)(2,1)S(1)}, u32[]{:S(2)}, u32[]{:S(2)}) collective-permute-start(bf16[128,512]{1,0:T(8,128)(2,1)S(1)} %get-tuple-element.42), channel_id=1, source_target_pairs={{4,0},{8,4},{12,8},{0,12},{5,1},{9,5},{13,9},{1,13},{6,2},{10,6},{... | collective-permute-start | bytes 393224 | tf_op jit(solution)/shard_map/ppermute | solution.py:18
  322.6 146.1 %all-reduce.9.cloned.1.call-start = ((), (), s32[]{:S(2)}) async-start(), calls=%async_computation.2 | async-start | bytes 4194304 | tf_op jit(solution)/shard_map/psum | solution.py:109
  334.4 152.7 %all-gather.25.cloned.1.call-start = ((), (), s32[]{:S(2)}) async-start(), calls=%async_computation.7 | async-start | bytes 1310720 | tf_op jit(solution)/shard_map/all_gather | solution.py:128
  (19 other events, 60.3 us)
Sparse Core Ops, SparseCore 0:
  18.2 19.3 all-gather.18
  92.5 92.3 all-reduce.6
  187.3 50.6 all-reduce.4
  239.4 16.7 all-gather.20
  257.8 19.6 all-gather.22
  322.7 92.8 all-reduce.10
  418.1 50.6 all-reduce.8
  470.3 16.7 all-gather.24
where the time goes:
time: 510 us; the launch traced here: 505 us
  waiting for transfers between devices  240 us (47%)
  blocking collectives  82.8 us (16%)
  other arithmetic  69.4 us (14%)
  local copies, waits for them, and re-layouts  54.3 us (11%)
  matrix products  35.3 us (7%)
  between operations  14.4 us (3%)
  starting transfers between devices  9.58 us (2%)
    psum x2, waiting for transfers between devices, local(): coarse_all = lax.psum(coarse_part, ('mesh', 'feat'))  117 us
    psum x2, waiting for transfers between devices, local(): fine_agg = lax.psum(fine_part, 'feat')  104 us
    dot_general x4, matrix products, hidden_adder(): return jnp.dot(activated, w_out, preferred_element_type=jnp.float32)  35.3 us
    all_gather x2, blocking collectives, local(): lax.all_gather(nodes.reshape(per_part, 8, width)[:, 0], 'mesh', axis=0, t...  31.7 us
    scatter-add x2, other arithmetic, local(): jax.ops.segment_sum(fine_edges.astype(jnp.float32), fine_recv, node_count)  22.9 us
    all_gather x2, blocking collectives, local(): lax.all_gather(node_w2[layer_index], 'feat', axis=0, tiled=True)  15.5 us
    all_gather x2, waiting for transfers between devices, local(): lax.all_gather(node_w1[layer_index], 'feat', axis=0, tiled=True)  15.4 us
    all_gather x2, blocking collectives, local(): lax.all_gather(edge_w2[layer_index], 'feat', axis=0, tiled=True)  15 us
  transfers between devices with their start and end apart: 12, of which 8 were waited for; matrix products, arithmetic and copies ran while one was open for 19% of the time, Pallas kernels for 0%

commit v1 on v0

v1 whole, which is shorter than its diff:
```python
import functools

import jax
import jax.numpy as jnp
from jax import lax
from jax.experimental import pallas as pl
from jax.experimental.pallas import tpu as pltpu
from jax.sharding import PartitionSpec as P

STEPS = 2
STRIDE = 8
LANES = 128
DIGIT = 64
VMEM_BYTES = 32 * 1024 * 1024


def dot(a, b):
    return jnp.dot(a, b, preferred_element_type=jnp.float32)


def dot_t(a, b):
    return lax.dot_general(a, b, (((1,), (1,)), ((), ())), preferred_element_type=jnp.float32)


def pick_rows(index, count):
    spots = lax.broadcasted_iota(jnp.int32, (index.shape[0], count), 1)
    return (spots == index).astype(jnp.bfloat16)


def silu(x):
    return x * (0.5 * jnp.tanh(0.5 * x) + 0.5)


def layer_norm(values, gain):
    centred = values - jnp.mean(values, axis=-1, keepdims=True)
    row_var = jnp.mean(centred * centred, axis=-1, keepdims=True)
    return centred * lax.rsqrt(row_var + 1e-05) * gain


def mlp(x, groups, biases, gain, k):
    width = gain.shape[-1]
    total = None
    for packs, bias in zip(groups, biases):
        w_in = jnp.concatenate([p[:, :k] for p in packs], axis=0)
        w_out = jnp.concatenate([p[:, k : k + width] for p in packs], axis=0)
        act = silu(dot_t(x, w_in) + bias).astype(jnp.bfloat16)
        part = dot(act, w_out)
        total = part if total is None else total + part
    return layer_norm(total, gain)


def call(kernel, out_shape, args, scratch=(), flops=0, nbytes=0, name=None):
    vmem = pl.BlockSpec(memory_space=pltpu.VMEM)
    out_specs = jax.tree.map(lambda _: vmem, out_shape)
    return pl.pallas_call(
        kernel,
        out_shape=out_shape,
        in_specs=[vmem] * len(args),
        out_specs=out_specs,
        scratch_shapes=list(scratch),
        compiler_params=pltpu.CompilerParams(vmem_limit_bytes=VMEM_BYTES),
        cost_estimate=pl.CostEstimate(flops=flops, bytes_accessed=nbytes, transcendentals=0),
        name=name,
    )(*args)


def bf16(*shape):
    return jax.ShapeDtypeStruct(shape, jnp.bfloat16)


def core_index():
    return lax.rem(lax.axis_index("feat"), 2)


def pack_kernel(nodes, halo, to_prev, to_next, coarse_half, coarse):
    core = core_index()
    count, hr, cp = nodes.shape[0], halo.shape[0] // 2, coarse.shape[0]
    hh, ch = hr // 2, cp // 2
    prev = halo[pl.ds(pl.multiple_of(core * hh, hh), hh), :]
    nxt = halo[pl.ds(pl.multiple_of(hr + core * hh, hh), hh), :]
    table = nodes[...]
    rows = dot(pick_rows(jnp.concatenate([prev, nxt], axis=0), count), table).astype(jnp.bfloat16)
    every = STRIDE * lax.broadcasted_iota(jnp.int32, (cp, 1), 0)
    coarse[...] = dot(pick_rows(every, count), table).astype(jnp.bfloat16)
    mine = coarse[pl.ds(pl.multiple_of(core * ch, ch), ch), :]
    to_prev[pl.ds(0, hh), :] = rows[:hh]
    to_prev[pl.ds(hh, ch), :] = mine
    to_next[pl.ds(0, hh), :] = rows[hh:]
    to_next[pl.ds(hh, ch), :] = mine
    coarse_half[...] = mine


def gather_kernel(tile, nodes, send, recv, sent, received):
    count = nodes.shape[0]

    def body(t, carry):
        rows = pl.ds(pl.multiple_of(t * tile, tile), tile)
        table = nodes[...]
        sent[rows, :] = dot(pick_rows(send[rows, :], count), table).astype(jnp.bfloat16)
        safe = jnp.minimum(recv[rows, :], count - 1)
        received[rows, :] = dot(pick_rows(safe, count), table).astype(jnp.bfloat16)
        return carry

    lax.fori_loop(0, send.shape[0] // tile, body, 0)


def edge_kernel(tile, ctile, sizes, first, *refs):
    count, hr, cp, parts, cores = sizes
    it = iter(refs)
    fine, sent, received, send, recv_row, coarse_own, coarse_edges, coarse_index, gain_ref = (
        next(it) for _ in range(9)
    )
    arrived = [(next(it), next(it)) for _ in range(parts - 1)]
    groups = [[next(it) for _ in range(2)] for _ in range(cores // 2)]
    bias_in = None if first else next(it)
    new_fine, new_coarse, agg_own, agg_other = (next(it) for _ in range(4))
    bias_out = next(it) if first else None
    halo_tab, coarse_tab, latents = (next(it) for _ in range(3))

    core, me = core_index(), lax.axis_index("mesh")
    width = gain_ref.shape[-1]
    k = 3 * width
    hh, ch, nh = hr // 2, cp // 2, count // 2
    fine_count, coarse_count = fine.shape[0], coarse_edges.shape[0]

    coarse_tab[pl.ds(pl.multiple_of(me * cp, cp), cp), :] = coarse_own[...]
    for i, pair in enumerate(arrived):
        owner = lax.rem(me + parts - 1 - i, parts)
        side = {0: 0, parts - 2: hr}.get(i)
        for who, ref in zip((core, 1 - core), pair):
            skip = 0
            if side is not None:
                halo_tab[pl.ds(pl.multiple_of(side + who * hh, hh), hh), :] = ref[pl.ds(0, hh), :]
                skip = hh
            spot = pl.multiple_of(owner * cp + who * ch, ch)
            coarse_tab[pl.ds(spot, ch), :] = ref[pl.ds(skip, ch), :]

    layer = 0 if first else 1
    lane = lax.broadcasted_iota(jnp.int32, (8, LANES), 1)
    row = lax.broadcasted_iota(jnp.int32, (8, LANES), 0)
    if first:
        unit = (lane == row).astype(jnp.bfloat16)
        for g, packs in enumerate(groups):
            for j, p in enumerate(packs):
                hidden = p.shape[0]
                spot = (2 * g + j) * hidden
                bias_out[:, spot : spot + hidden] = dot_t(unit, p[:, k + width :])
        bias_ref = bias_out
    else:
        bias_ref = bias_in
    per = bias_ref.shape[1] // len(groups)
    biases = [bias_ref[layer : layer + 1, g * per : (g + 1) * per] for g in range(len(groups))]
    gain = gain_ref[layer : layer + 1, :].astype(jnp.float32)

    def update(x, old):
        return (old.astype(jnp.float32) + mlp(x, groups, biases, gain, k)).astype(jnp.bfloat16)

    def fine_body(t, carry):
        rows = pl.ds(pl.multiple_of(t * tile, tile), tile)
        border = dot(pick_rows(send[rows, :] - count, 2 * hr), halo_tab[...])
        senders = (sent[rows, :].astype(jnp.float32) + border).astype(jnp.bfloat16)
        old = fine[rows, :]
        new = update(jnp.concatenate([old, senders, received[rows, :]], axis=1), old)
        latents[rows, :] = new
        new_fine[rows, :] = new
        return carry

    lax.fori_loop(0, fine_count // tile, fine_body, 0)

    def digits(at):
        c = coarse_index[at, :].astype(jnp.float32)
        return [(DIGIT * c[:, 2 * j : 2 * j + 1] + c[:, 2 * j + 1 : 2 * j + 2]).astype(jnp.int32) for j in range(2)]

    def coarse_body(t, carry):
        rows = pl.ds(pl.multiple_of(t * ctile, ctile), ctile)
        old = coarse_edges[rows, :]
        ends = [
            dot(pick_rows(d, coarse_tab.shape[0]), coarse_tab[...]).astype(jnp.bfloat16)
            for d in digits(rows)
        ]
        new = update(jnp.concatenate([old] + ends, axis=1), old)
        latents[pl.ds(pl.multiple_of(fine_count + t * ctile, ctile), ctile), :] = new
        new_coarse[rows, :] = new
        return carry

    lax.fori_loop(0, coarse_count // ctile, coarse_body, 0)

    weights = jnp.where(lane == 2, float(DIGIT), jnp.where(lane == 3, 1.0, 0.0)).astype(jnp.bfloat16)
    near = dot_t(weights, coarse_index[...])[:1, :].astype(jnp.int32) - me * cp
    target = jnp.where((near >= 0) & (near < cp), near * STRIDE, -1)
    targets = jnp.concatenate([recv_row[...], target], axis=1)
    block = min(256, nh)

    def aggregate(base, spot):
        spots = lax.broadcasted_iota(jnp.int32, (block, targets.shape[1]), 0) + (base + spot)
        return dot((spots == targets).astype(jnp.bfloat16), latents[...])

    for spot in range(0, nh, block):
        agg_other[pl.ds(spot, block), :] = aggregate((1 - core) * nh, spot).astype(jnp.bfloat16)
    for spot in range(0, nh, block):
        agg_own[pl.ds(spot, block), :] = aggregate(core * nh, spot)


def node_kernel(tile, layer, cores, n_sums, *refs):
    it = iter(refs)
    nodes, bias_ref, gain_ref = (next(it) for _ in range(3))
    sums = [next(it) for _ in range(n_sums)]
    groups = [[next(it) for _ in range(2)] for _ in range(cores // 2)]
    out = next(it)
    width = gain_ref.shape[-1]
    nh = out.shape[0]
    per = bias_ref.shape[1] // len(groups)
    line = STEPS + layer
    biases = [bias_ref[line : line + 1, g * per : (g + 1) * per] for g in range(len(groups))]
    gain = gain_ref[layer : layer + 1, :].astype(jnp.float32)
    core = core_index()
    for t in range(nh // tile):
        rows = pl.ds(t * tile, tile)
        old = nodes[pl.ds(pl.multiple_of(core * nh + t * tile, tile), tile), :]
        agg = sums[0][rows, :].astype(jnp.float32)
        for more in sums[1:]:
            agg = agg + more[rows, :].astype(jnp.float32)
        x = jnp.concatenate([old, agg.astype(jnp.bfloat16)], axis=1)
        y = mlp(x, groups, biases, gain, 2 * width)
        out[rows, :] = (old.astype(jnp.float32) + y).astype(jnp.bfloat16)


def divisor(count, most, unit=16):
    best = unit
    for size in range(unit, min(most, count) + 1, unit):
        if count % size == 0:
            best = size
    return best


def local(
    nodes,
    fine_edges,
    fine_send,
    fine_recv,
    halo_send,
    coarse_edges,
    coarse_send,
    coarse_recv,
    edge_w1,
    edge_b1,
    edge_w2,
    edge_gain,
    node_w1,
    node_b1,
    node_w2,
    node_gain,
):
    count, width = nodes.shape
    hr = halo_send.shape[0] // 2
    cp = count // STRIDE
    nh = count // 2
    fine_count = fine_edges.shape[0]
    parts = lax.axis_size("mesh")
    cores = lax.axis_size("feat")
    core = core_index()

    def swap(x):
        return lax.ppermute(x, "feat", [(i, i ^ 1) for i in range(cores)])

    def across(x):
        return lax.ppermute(x, "feat", [(i, i ^ 2) for i in range(cores)])

    def shift(x, by):
        return lax.ppermute(x, "mesh", [(i, (i + by) % parts) for i in range(parts)])

    def spread(pack):
        if cores != 4:
            every = lax.all_gather(pack, "feat", axis=0)
            return [every[i] for i in range(cores)]
        far = across(pack)
        return [pack, swap(pack), far, swap(far)]

    bias = jnp.concatenate([edge_b1, node_b1], axis=0).T
    bias = jnp.pad(bias, ((0, 0), (0, LANES - bias.shape[1])))
    edge_packs = [
        spread(jnp.concatenate([edge_w1[s], edge_w2[s]] + ([bias] if s == 0 else []), axis=1))
        for s in range(STEPS)
    ]
    node_packs = [
        spread(jnp.concatenate([node_w1[s], node_w2[s]], axis=1)) for s in range(STEPS)
    ]

    digits = [coarse_send // DIGIT, coarse_send % DIGIT, coarse_recv // DIGIT, coarse_recv % DIGIT]
    digits = jnp.stack(digits, axis=1).astype(jnp.bfloat16)
    digits = jnp.pad(digits, ((0, 0), (0, LANES - digits.shape[1])))
    coarse_pack = jnp.concatenate([coarse_edges, digits], axis=1)
    coarse_all = jnp.concatenate(
        [coarse_pack] + [shift(coarse_pack, by) for by in range(1, parts)], axis=0
    )
    coarse_state = coarse_all[:, :width]
    coarse_index = coarse_all[:, width:]
    coarse_count = coarse_all.shape[0]

    send_col = fine_send.reshape(fine_count, 1)
    recv_col = fine_recv.reshape(fine_count, 1)
    recv_row = fine_recv.reshape(1, fine_count)
    halo_col = halo_send.reshape(2 * hr, 1)
    tile = divisor(fine_count, 256)
    ctile = divisor(coarse_count, 256)
    hidden = edge_w1.shape[1] * cores
    sizes = (count, hr, cp, parts, cores)
    bias_rows = None

    for s in range(STEPS):
        half = hr // 2 + cp // 2
        to_prev, to_next, coarse_half, coarse_own = call(
            pack_kernel,
            (bf16(half, width), bf16(half, width), bf16(cp // 2, width), bf16(cp, width)),
            [nodes, halo_col],
            flops=2 * (hr + cp) * count * width,
            name="halo_rows",
        )
        arrived = []
        for by in range(1, parts):
            moved = shift({1: to_next, parts - 1: to_prev}.get(by, coarse_half), by)
            arrived += [moved, swap(moved)]
        sent, received = call(
            functools.partial(gather_kernel, tile),
            (bf16(fine_count, width), bf16(fine_count, width)),
            [nodes, send_col, recv_col],
            flops=4 * fine_count * count * width,
            name="gather_rows",
        )
        first = s == 0
        outs = [
            bf16(fine_count, width),
            bf16(coarse_count, width),
            jax.ShapeDtypeStruct((nh, width), jnp.float32),
            bf16(nh, width),
        ]
        if first:
            outs.append(jax.ShapeDtypeStruct((8, hidden), jnp.float32))
        rows = fine_count + coarse_count
        result = call(
            functools.partial(edge_kernel, tile, ctile, sizes, first),
            tuple(outs),
            [fine_edges, sent, received, send_col, recv_row, coarse_own, coarse_state, coarse_index, edge_gain]
            + arrived
            + edge_packs[s]
            + ([] if first else [bias_rows]),
            scratch=[
                pltpu.VMEM((2 * hr, width), jnp.bfloat16),
                pltpu.VMEM((parts * cp, width), jnp.bfloat16),
                pltpu.VMEM((rows, width), jnp.bfloat16),
            ],
            flops=2 * rows * width * (4 * hidden + count),
            name="edge_update",
        )
        fine_edges, coarse_state, agg_own, agg_other = result[:4]
        if first:
            bias_rows = result[4]
        partial = agg_own + swap(agg_other).astype(jnp.float32)
        if cores == 4:
            partial = partial.astype(jnp.bfloat16)
            sums = [partial, across(partial)]
        else:
            every = lax.all_gather(partial.astype(jnp.bfloat16), "feat", axis=0)
            every = every.reshape(cores // 2, 2, nh, width).astype(jnp.float32)
            sums = [lax.dynamic_index_in_dim(every.sum(axis=0), core, 0, keepdims=False)]
        new_half = call(
            functools.partial(node_kernel, divisor(nh, 256), s, cores, len(sums)),
            bf16(nh, width),
            [nodes, bias_rows, node_gain] + sums + node_packs[s],
            flops=2 * nh * width * 3 * hidden,
            name="node_update",
        )
        other_half = swap(new_half)
        nodes = jnp.where(
            core == 0,
            jnp.concatenate([new_half, other_half], axis=0),
            jnp.concatenate([other_half, new_half], axis=0),
        )
    return nodes


def solution(mesh):
    placed = (
        P(("groups", "mesh"), None),
        P(("groups", "mesh", "feat"), None),
        P(("groups", "mesh", "feat")),
        P(("groups", "mesh", "feat")),
        P(("groups", "mesh")),
        P(("groups", "mesh", "feat"), None),
        P(("groups", "mesh", "feat")),
        P(("groups", "mesh", "feat")),
        P(None, "feat", None),
        P(None, "feat"),
        P(None, "feat", None),
        P(),
        P(None, "feat", None),
        P(None, "feat"),
        P(None, "feat", None),
        P(),
    )
    return jax.shard_map(
        local, mesh=mesh, in_specs=placed, out_specs=P(("groups", "mesh"), None), check_vma=False
    )
```

time: 510 us -> 147 us (0.29)
  waiting for transfers between devices: 240 us -> 66.1 us
  blocking collectives: 82.8 us -> 0 us
  other arithmetic: 69.4 us -> 5.79 us
  local copies, waits for them, and re-layouts: 54.3 us -> 4.57 us
  Pallas kernels: 0 us -> 41.7 us
  matrix products: 35.3 us -> 0 us
  starting transfers between devices: 9.58 us -> 28 us
  between operations: 14.4 us -> 0.47 us
    psum x4 -> x0, waiting for transfers between devices: 222 us -> none  [the longest x2 117 us: local(): coarse_all = lax.psum(coarse_part, ('mesh', 'feat'))]
    all_gather x10 -> x0, blocking collectives: 82.8 us -> none  [the longest x2 31.7 us: local(): lax.all_gather(nodes.reshape(per_part, 8, width)[:, 0], 'mesh', axis=0, t...]
    ppermute x4 -> x33, waiting for transfers between devices: 1.22 us -> 66.1 us  [the longest x6 51.8 us: across(): return lax.ppermute(x, 'feat', [(i, i ^ 2) for i in range(cores)])]
    pallas_call x0 -> x8, Pallas kernels: none -> 41.7 us  [call(): pl.pallas_call(kernel, out_shape=out_shape, in_specs=[vmem] * len(args),...]
    dot_general x4 -> x0, matrix products: 35.3 us -> none  [hidden_adder(): return jnp.dot(activated, w_out, preferred_element_type=jnp.float32)]
    gather x10 -> x0, local copies, waits for them, and re-layouts: 28.5 us -> none  [the longest x2 10.9 us: local(): jnp.take(node_table, fine_send, axis=0)]
    scatter-add x4 -> x0, other arithmetic: 27.6 us -> none  [the longest x2 22.9 us: local(): jax.ops.segment_sum(fine_edges.astype(jnp.float32), fine_recv, node_count)]
    ppermute x4 -> x33, starting transfers between devices: 9.12 us -> 28 us  [the longest x9 15.3 us: shift(): lax.ppermute(x, 'mesh', [(i, (i + by) % parts) for i in range(parts)])]
  transfers between devices with their start and end apart: 12 -> 33, of which waited for: 8 -> 10; matrix products, arithmetic and copies ran while one was open for 19% -> 4% of each run, Pallas kernels for 0% -> 8%
where the time goes in v1:
time: 147 us
  waiting for transfers between devices  66.1 us (45%)
  Pallas kernels  41.7 us (28%)
  starting transfers between devices  28 us (19%)
  other arithmetic  5.79 us (4%)
  local copies, waits for them, and re-layouts  4.57 us (3%)
    ppermute x6, waiting for transfers between devices, across(): return lax.ppermute(x, 'feat', [(i, i ^ 2) for i in range(cores)])  51.8 us
    pallas_call x8, Pallas kernels, call(): pl.pallas_call(kernel, out_shape=out_shape, in_specs=[vmem] * len(args),...  41.7 us
    ppermute x9, starting transfers between devices, shift(): lax.ppermute(x, 'mesh', [(i, (i + by) % parts) for i in range(parts)])  15.3 us
    ppermute x9, waiting for transfers between devices, shift(): lax.ppermute(x, 'mesh', [(i, (i + by) % parts) for i in range(parts)])  10.7 us
    ppermute x6, starting transfers between devices, across(): return lax.ppermute(x, 'feat', [(i, i ^ 2) for i in range(cores)])  9.72 us
    ppermute x18, waiting for transfers between devices, swap(): return lax.ppermute(x, 'feat', [(i, i ^ 1) for i in range(cores)])  3.66 us
    ppermute x18, starting transfers between devices, swap(): return lax.ppermute(x, 'feat', [(i, i ^ 1) for i in range(cores)])  2.96 us
  transfers between devices with their start and end apart: 33, of which 10 were waited for; matrix products, arithmetic and copies ran while one was open for 4% of the time, Pallas kernels for 8%

profile of v1, /device:TPU:0, one launch (start us, length us, event | category | flops | bytes accessed | tf_op | source)
XLA Modules:
  0.0 146.5 jit_solution(17916983864154513857)
XLA Ops:
  0.0 2.0 %slice_bitcast_fusion = (bf16[128,1536]{1,0:T(8,128)(2,1)}, bf16[128,1536]{1,0:T(8,128)(2,1)S(1)}) fusion(bf16[2,128,1536]{2,1,0:T(8,128)(2,1)} %param.24), kind=kLoop, calls=%fused_computation.11 | loop fusion | bytes 1572864 | tf_op jit(solution)/shard_map/squeeze | solution.py:282
  2.9 0.8 fusion.1.refs_15_
  3.7 3.0 %collective-permute-start.10 = (bf16[128,2176]{1,0:T(8,128)(2,1)}, bf16[128,2176]{1,0:T(8,128)(2,1)}, u32[]{:S(2)}, u32[]{:S(2)}) collective-permute-start(bf16[128,2176]{1,0:T(8,128)(2,1)} %fusion.1.refs_15_), channel_id=1, source_target_pairs={{0,2},{1,3},{2,0},{3,1},{4,6},{5,7},{6,4},{7,5},{8,10},{9,11},{10,... | collective-permute-start | bytes 1671176 | tf_op jit(solution)/shard_map/ppermute | solution.py:267
  6.9 1.6 %collective-permute-start = (bf16[96,640]{1,0:T(8,128)(2,1)S(1)}, bf16[96,640]{1,0:T(8,128)(2,1)}, u32[]{:S(2)}, u32[]{:S(2)}) collective-permute-start(bf16[96,640]{1,0:T(8,128)(2,1)S(1)} %pad_maximum_fusion.4), channel_id=1, source_target_pairs={{0,4},{4,8},{8,12},{12,0},{1,5},{5,9},{9,13},{13,1},{2,6},{6,10},{... | collective-permute-start | bytes 368648 | tf_op jit(solution)/shard_map/ppermute | solution.py:270
  8.5 2.6 %collective-permute-start.1 = (bf16[96,640]{1,0:T(8,128)(2,1)S(1)}, bf16[96,640]{1,0:T(8,128)(2,1)}, u32[]{:S(2)}, u32[]{:S(2)}) collective-permute-start(bf16[96,640]{1,0:T(8,128)(2,1)S(1)} %pad_maximum_fusion.4), channel_id=1, source_target_pairs={{0,8},{4,12},{8,0},{12,4},{1,9},{5,13},{9,1},{13,5},{2,10},{6,14},... | collective-permute-start | bytes 368648 | tf_op jit(solution)/shard_map/ppermute | solution.py:270
  12.2 7.4 %collective-permute-done.10.refs_17_ = bf16[128,2176]{1,0:T(8,128)(2,1)} collective-permute-done((bf16[128,2176]{1,0:T(8,128)(2,1)}, bf16[128,2176]{1,0:T(8,128)(2,1)}, u32[]{:S(2)}, u32[]{:S(2)}) %collective-permute-start.10) | collective-permute-done | bytes 557088 | tf_op jit(solution)/shard_map/ppermute | solution.py:267
  20.2 1.5 %collective-permute-done.5.refs_11_ = bf16[64,512]{1,0:T(8,128)(2,1)S(1)} collective-permute-done((bf16[64,512]{1,0:T(8,128)(2,1)S(1)}, bf16[64,512]{1,0:T(8,128)(2,1)S(1)}, u32[]{:S(2)}, u32[]{:S(2)}) %collective-permute-start.5) | collective-permute-done | bytes 65568 | tf_op jit(solution)/shard_map/ppermute | solution.py:270
  21.7 2.4 %collective-permute-start.2 = (bf16[96,640]{1,0:T(8,128)(2,1)S(1)}, bf16[96,640]{1,0:T(8,128)(2,1)S(1)}, u32[]{:S(2)}, u32[]{:S(2)}) collective-permute-start(bf16[96,640]{1,0:T(8,128)(2,1)S(1)} %pad_maximum_fusion.4), channel_id=1, source_target_pairs={{0,12},{4,0},{8,4},{12,8},{1,13},{5,1},{9,5},{13,9},{2,14},{6,2},{... | collective-permute-start | bytes 368648 | tf_op jit(solution)/shard_map/ppermute | solution.py:270
  24.1 3.8 %collective-permute-start.7 = (bf16[128,512]{1,0:T(8,128)(2,1)S(1)}, bf16[128,512]{1,0:T(8,128)(2,1)S(1)}, u32[]{:S(2)}, u32[]{:S(2)}) collective-permute-start(bf16[128,512]{1,0:T(8,128)(2,1)S(1)} %get-tuple-element.29), channel_id=1, source_target_pairs={{0,12},{4,0},{8,4},{12,8},{1,13},{5,1},{9,5},{13,9},{2,14},{6,2},{... | collective-permute-start | bytes 393224 | tf_op jit(solution)/shard_map/ppermute | solution.py:270
  27.9 4.8 %gather_rows.2 = (bf16[1536,512]{1,0:T(8,128)(2,1)S(1)}, bf16[1536,512]{1,0:T(8,128)(2,1)S(1)}) custom-call(bf16[1024,512]{1,0:T(8,128)(2,1)S(1)} %copy-done, s32[1536,1]{1,0:T(8,128)S(1)} %reshape.16.send.refs_3_, s32[1536,1]{1,0:T(8,128)S(1)} %reshape.17.recv), custom_call_target="tpu_custom_call" | custom-call | flops 3221225472 | tf_op jit(solution)/shard_map/gather_rows/pallas_call | solution.py:55
  33.5 1.0 pad_maximum_fusion.1
  35.4 13.6 %edge_update.2 = (bf16[1536,512]{1,0:T(8,128)(2,1)S(1)}, bf16[384,512]{1,0:T(8,128)(2,1)S(1)}, f32[512,512]{1,0:T(8,128)S(1)}, bf16[512,512]{1,0:T(8,128)(2,1)S(1)}, f32[8,512]{1,0:T(8,128)S(1)}) custom-call(bf16[1536,512]{1,0:T(8,128)(2,1)S(1)} %copy-done.2, bf16[1536,512]{1,0:T(8,128)(2,1)S(1)} %get-tuple-element.24.refs_1_, ...), custom_call_target="tpu_custom_call" | custom-call | flops 6039797760 | tf_op jit(solution)/shard_map/edge_update/pallas_call | solution.py:55
  49.5 0.8 slice_bitcast_fusion.2
  50.4 1.5 %collective-permute-start.15 = (bf16[128,1536]{1,0:T(8,128)(2,1)S(1)}, bf16[128,1536]{1,0:T(8,128)(2,1)S(1)}, u32[]{:S(2)}, u32[]{:S(2)}) collective-permute-start(bf16[128,1536]{1,0:T(8,128)(2,1)S(1)} %pad_maximum_fusion.2.refs_5_), channel_id=1, source_target_pairs={{0,2},{1,3},{2,0},{3,1},{4,6},{5,7},{6,4},{7,5},{8,10},{9,11},{10,... | collective-permute-start | bytes 1179656 | tf_op jit(solution)/shard_map/ppermute | solution.py:267
  52.8 9.5 %collective-permute-done.15.refs_7_ = bf16[128,1536]{1,0:T(8,128)(2,1)S(1)} collective-permute-done((bf16[128,1536]{1,0:T(8,128)(2,1)S(1)}, bf16[128,1536]{1,0:T(8,128)(2,1)S(1)}, u32[]{:S(2)}, u32[]{:S(2)}) %collective-permute-start.15) | collective-permute-done | bytes 393248 | tf_op jit(solution)/shard_map/ppermute | solution.py:267
  62.4 0.9 pad_maximum_fusion.refs_15_
  63.2 1.5 %collective-permute-start.25 = (bf16[128,2048]{1,0:T(8,128)(2,1)}, bf16[128,2048]{1,0:T(8,128)(2,1)}, u32[]{:S(2)}, u32[]{:S(2)}) collective-permute-start(bf16[128,2048]{1,0:T(8,128)(2,1)} %pad_maximum_fusion.refs_15_), channel_id=1, source_target_pairs={{0,2},{1,3},{2,0},{3,1},{4,6},{5,7},{6,4},{7,5},{8,10},{9,11},{10,... | collective-permute-start | bytes 1572872 | tf_op jit(solution)/shard_map/ppermute | solution.py:267
  64.7 8.9 %collective-permute-done.13.refs_4_ = bf16[512,512]{1,0:T(8,128)(2,1)S(1)} collective-permute-done((bf16[512,512]{1,0:T(8,128)(2,1)S(1)}, bf16[512,512]{1,0:T(8,128)(2,1)S(1)}, u32[]{:S(2)}, u32[]{:S(2)}) %collective-permute-start.13) | collective-permute-done | bytes 524320 | tf_op jit(solution)/shard_map/ppermute | solution.py:267
  73.6 1.5 %node_update.2 = bf16[512,512]{1,0:T(8,128)(2,1)S(1)} custom-call(bf16[1024,512]{1,0:T(8,128)(2,1)S(1)} %copy-done, f32[8,512]{1,0:T(8,128)S(1)} %get-tuple-element.30.refs_1_.refs_19_, bf16[2,512]{1,0:T(2,128)(2,1)S(1)} %copy-done.1, bf16[512,512]{1,0:T(8,128)(2,1)S(1)} %add_convert_fusion.1.refs_3_, bf16[512,512]{1,0:T(8,128)(2,1)S(1)} %collective-permute-done.13.refs_4_, ...), custom_call_target="tpu_custom_call" | custom-call | flops 805306368 | tf_op jit(solution)/shard_map/node_update/pallas_call | solution.py:55
  75.7 8.6 %collective-permute-done.25.refs_17_ = bf16[128,2048]{1,0:T(8,128)(2,1)} collective-permute-done((bf16[128,2048]{1,0:T(8,128)(2,1)}, bf16[128,2048]{1,0:T(8,128)(2,1)}, u32[]{:S(2)}, u32[]{:S(2)}) %collective-permute-start.25) | collective-permute-done | bytes 524320 | tf_op jit(solution)/shard_map/ppermute | solution.py:267
  85.4 3.9 %collective-permute-start.22 = (bf16[128,512]{1,0:T(8,128)(2,1)S(1)}, bf16[128,512]{1,0:T(8,128)(2,1)S(1)}, u32[]{:S(2)}, u32[]{:S(2)}) collective-permute-start(bf16[128,512]{1,0:T(8,128)(2,1)S(1)} %get-tuple-element.40), channel_id=1, source_target_pairs={{0,12},{4,0},{8,4},{12,8},{1,13},{5,1},{9,5},{13,9},{2,14},{6,2},{... | collective-permute-start | bytes 393224 | tf_op jit(solution)/shard_map/ppermute | solution.py:270
  89.7 9.2 %collective-permute-done.20.refs_11_ = bf16[64,512]{1,0:T(8,128)(2,1)S(1)} collective-permute-done((bf16[64,512]{1,0:T(8,128)(2,1)S(1)}, bf16[64,512]{1,0:T(8,128)(2,1)S(1)}, u32[]{:S(2)}, u32[]{:S(2)}) %collective-permute-start.20) | collective-permute-done | bytes 65568 | tf_op jit(solution)/shard_map/ppermute | solution.py:270
  99.5 5.0 %gather_rows.3 = (bf16[1536,512]{1,0:T(8,128)(2,1)S(1)}, bf16[1536,512]{1,0:T(8,128)(2,1)S(1)}) custom-call(bf16[1024,512]{1,0:T(8,128)(2,1)S(1)} %maximum_select_fusion.nodes.refs_0_, s32[1536,1]{1,0:T(8,128)S(1)} %reshape.16.send.refs_3_, s32[1536,1]{1,0:T(8,128)S(1)} %reshape.17.recv), custom_call_target="tpu_custom_call" | custom-call | flops 3221225472 | tf_op jit(solution)/shard_map/gather_rows/pallas_call | solution.py:55
  104.5 14.3 %edge_update.3 = (bf16[1536,512]{1,0:T(8,128)(2,1)}, bf16[384,512]{1,0:T(8,128)(2,1)}, f32[512,512]{1,0:T(8,128)S(1)}, bf16[512,512]{1,0:T(8,128)(2,1)S(1)}) custom-call(bf16[1536,512]{1,0:T(8,128)(2,1)S(1)} %copy-done.5, bf16[1536,512]{1,0:T(8,128)(2,1)S(1)} %get-tuple-element.34.refs_1_, bf16[1536,512]{1,0:T(8,128)(2,1)S(1)} %get-tuple-element.35.refs_2_, ...), custom_call_target="tpu_custom_call" | custom-call | flops 6039797760 | tf_op jit(solution)/shard_map/edge_update/pallas_call | solution.py:55
  119.3 1.6 %collective-permute-start.30 = (bf16[128,1536]{1,0:T(8,128)(2,1)S(1)}, bf16[128,1536]{1,0:T(8,128)(2,1)S(1)}, u32[]{:S(2)}, u32[]{:S(2)}) collective-permute-start(bf16[128,1536]{1,0:T(8,128)(2,1)S(1)} %pad_maximum_fusion.3.refs_5_), channel_id=1, source_target_pairs={{0,2},{1,3},{2,0},{3,1},{4,6},{5,7},{6,4},{7,5},{8,10},{9,11},{10,... | collective-permute-start | bytes 1179656 | tf_op jit(solution)/shard_map/ppermute | solution.py:267
  121.0 1.5 %collective-permute-start.28 = (bf16[512,512]{1,0:T(8,128)(2,1)S(1)}, bf16[512,512]{1,0:T(8,128)(2,1)S(1)}, u32[]{:S(2)}, u32[]{:S(2)}) collective-permute-start(bf16[512,512]{1,0:T(8,128)(2,1)S(1)} %add_convert_fusion.refs_3_), channel_id=1, source_target_pairs={{0,2},{1,3},{2,0},{3,1},{4,6},{5,7},{6,4},{7,5},{8,10},{9,11},{10,... | collective-permute-start | bytes 1572872 | tf_op jit(solution)/shard_map/ppermute | solution.py:267
  122.6 8.7 %collective-permute-done.30.refs_7_ = bf16[128,1536]{1,0:T(8,128)(2,1)S(1)} collective-permute-done((bf16[128,1536]{1,0:T(8,128)(2,1)S(1)}, bf16[128,1536]{1,0:T(8,128)(2,1)S(1)}, u32[]{:S(2)}, u32[]{:S(2)}) %collective-permute-start.30) | collective-permute-done | bytes 393248 | tf_op jit(solution)/shard_map/ppermute | solution.py:267
  131.3 1.7 %collective-permute-done.31.refs_8_ = bf16[128,1536]{1,0:T(8,128)(2,1)S(1)} collective-permute-done((bf16[128,1536]{1,0:T(8,128)(2,1)S(1)}, bf16[128,1536]{1,0:T(8,128)(2,1)S(1)}, u32[]{:S(2)}, u32[]{:S(2)}) %collective-permute-start.31) | collective-permute-done | bytes 393248 | tf_op jit(solution)/shard_map/ppermute | solution.py:264
  133.0 8.6 %collective-permute-done.28.refs_4_ = bf16[512,512]{1,0:T(8,128)(2,1)S(1)} collective-permute-done((bf16[512,512]{1,0:T(8,128)(2,1)S(1)}, bf16[512,512]{1,0:T(8,128)(2,1)S(1)}, u32[]{:S(2)}, u32[]{:S(2)}) %collective-permute-start.28) | collective-permute-done | bytes 524320 | tf_op jit(solution)/shard_map/ppermute | solution.py:267
  141.7 1.5 %node_update.3 = bf16[512,512]{1,0:T(8,128)(2,1)S(1)} custom-call(bf16[1024,512]{1,0:T(8,128)(2,1)S(1)} %maximum_select_fusion.nodes.refs_0_, f32[8,512]{1,0:T(8,128)S(1)} %get-tuple-element.30.refs_1_.refs_19_, bf16[2,512]{1,0:T(2,128)(2,1)S(1)} %copy-done.1, bf16[512,512]{1,0:T(8,128)(2,1)S(1)} %add_convert_fusion.refs_3_, ...), custom_call_target="tpu_custom_call" | custom-call | flops 805306368 | tf_op jit(solution)/shard_map/node_update/pallas_call | solution.py:55
  143.2 1.9 %collective-permute-done.32 = bf16[512,512]{1,0:T(8,128)(2,1)S(1)} collective-permute-done((bf16[512,512]{1,0:T(8,128)(2,1)S(1)}, bf16[512,512]{1,0:T(8,128)(2,1)S(1)}, u32[]{:S(2)}, u32[]{:S(2)}) %collective-permute-start.32) | collective-permute-done | bytes 524320 | tf_op jit(solution)/shard_map/ppermute | solution.py:264
  145.1 1.4 maximum_select_fusion.1
  (112 shorter events, 9.1 us)
Async XLA Ops:
  3.7 15.9 %collective-permute-start.10 = (bf16[128,2176]{1,0:T(8,128)(2,1)}, bf16[128,2176]{1,0:T(8,128)(2,1)}, u32[]{:S(2)}, u32[]{:S(2)}) collective-permute-start(bf16[128,2176]{1,0:T(8,128)(2,1)} %fusion.1.refs_15_), channel_id=1, source_target_pairs={{0,2},{1,3},{2,0},{3,1},{4,6},{5,7},{6,4},{7,5},{8,10},{9,11},{10,... | collective-permute-start | bytes 1671176 | tf_op jit(solution)/shard_map/ppermute | solution.py:267
  6.9 17.2 %collective-permute-start = (bf16[96,640]{1,0:T(8,128)(2,1)S(1)}, bf16[96,640]{1,0:T(8,128)(2,1)}, u32[]{:S(2)}, u32[]{:S(2)}) collective-permute-start(bf16[96,640]{1,0:T(8,128)(2,1)S(1)} %pad_maximum_fusion.4), channel_id=1, source_target_pairs={{0,4},{4,8},{8,12},{12,0},{1,5},{5,9},{9,13},{13,1},{2,6},{6,10},{... | collective-permute-start | bytes 368648 | tf_op jit(solution)/shard_map/ppermute | solution.py:270
  8.5 15.6 %collective-permute-start.1 = (bf16[96,640]{1,0:T(8,128)(2,1)S(1)}, bf16[96,640]{1,0:T(8,128)(2,1)}, u32[]{:S(2)}, u32[]{:S(2)}) collective-permute-start(bf16[96,640]{1,0:T(8,128)(2,1)S(1)} %pad_maximum_fusion.4), channel_id=1, source_target_pairs={{0,8},{4,12},{8,0},{12,4},{1,9},{5,13},{9,1},{13,5},{2,10},{6,14},... | collective-permute-start | bytes 368648 | tf_op jit(solution)/shard_map/ppermute | solution.py:270
  11.8 9.9 %collective-permute-start.5 = (bf16[64,512]{1,0:T(8,128)(2,1)S(1)}, bf16[64,512]{1,0:T(8,128)(2,1)S(1)}, u32[]{:S(2)}, u32[]{:S(2)}) collective-permute-start(bf16[64,512]{1,0:T(8,128)(2,1)S(1)} %get-tuple-element.28), channel_id=1, source_target_pairs={{0,8},{4,12},{8,0},{12,4},{1,9},{5,13},{9,1},{13,5},{2,10},{6,14},... | collective-permute-start | bytes 196616 | tf_op jit(solution)/shard_map/ppermute | solution.py:270
  12.2 23.1 %collective-permute-start.9 = (bf16[128,2176]{1,0:T(8,128)(2,1)}, bf16[128,2176]{1,0:T(8,128)(2,1)S(1)}, u32[]{:S(2)}, u32[]{:S(2)}) collective-permute-start(bf16[128,2176]{1,0:T(8,128)(2,1)} %fusion.1.refs_15_), channel_id=1, source_target_pairs={{0,1},{1,0},{2,3},{3,2},{4,5},{5,4},{6,7},{7,6},{8,9},{9,8},{10,11... | collective-permute-start | bytes 1671176 | tf_op jit(solution)/shard_map/ppermute | solution.py:264
  19.6 15.7 %collective-permute-start.11 = (bf16[128,2176]{1,0:T(8,128)(2,1)}, bf16[128,2176]{1,0:T(8,128)(2,1)S(1)}, u32[]{:S(2)}, u32[]{:S(2)}) collective-permute-start(bf16[128,2176]{1,0:T(8,128)(2,1)} %collective-permute-done.10.refs_17_), channel_id=1, source_target_pairs={{0,1},{1,0},{2,3},{3,2},{4,5},{5,4},{6,7},{7,6},{8,9},{9,8},{10,11... | collective-permute-start | bytes 1671176 | tf_op jit(solution)/shard_map/ppermute | solution.py:264
  21.7 11.1 %collective-permute-start.2 = (bf16[96,640]{1,0:T(8,128)(2,1)S(1)}, bf16[96,640]{1,0:T(8,128)(2,1)S(1)}, u32[]{:S(2)}, u32[]{:S(2)}) collective-permute-start(bf16[96,640]{1,0:T(8,128)(2,1)S(1)} %pad_maximum_fusion.4), channel_id=1, source_target_pairs={{0,12},{4,0},{8,4},{12,8},{1,13},{5,1},{9,5},{13,9},{2,14},{6,2},{... | collective-permute-start | bytes 368648 | tf_op jit(solution)/shard_map/ppermute | solution.py:270
  24.1 8.8 %collective-permute-start.3 = (bf16[128,512]{1,0:T(8,128)(2,1)S(1)}, bf16[128,512]{1,0:T(8,128)(2,1)S(1)}, u32[]{:S(2)}, u32[]{:S(2)}) collective-permute-start(bf16[128,512]{1,0:T(8,128)(2,1)S(1)} %get-tuple-element.27), channel_id=1, source_target_pairs={{0,4},{4,8},{8,12},{12,0},{1,5},{5,9},{9,13},{13,1},{2,6},{6,10},{... | collective-permute-start | bytes 393224 | tf_op jit(solution)/shard_map/ppermute | solution.py:270
  24.1 9.3 %collective-permute-start.7 = (bf16[128,512]{1,0:T(8,128)(2,1)S(1)}, bf16[128,512]{1,0:T(8,128)(2,1)S(1)}, u32[]{:S(2)}, u32[]{:S(2)}) collective-permute-start(bf16[128,512]{1,0:T(8,128)(2,1)S(1)} %get-tuple-element.29), channel_id=1, source_target_pairs={{0,12},{4,0},{8,4},{12,8},{1,13},{5,1},{9,5},{13,9},{2,14},{6,2},{... | collective-permute-start | bytes 393224 | tf_op jit(solution)/shard_map/ppermute | solution.py:270
  32.8 2.5 %collective-permute-start.6 = (bf16[64,512]{1,0:T(8,128)(2,1)S(1)}, bf16[64,512]{1,0:T(8,128)(2,1)S(1)}, u32[]{:S(2)}, u32[]{:S(2)}) collective-permute-start(bf16[64,512]{1,0:T(8,128)(2,1)S(1)} %collective-permute-done.5.refs_11_), channel_id=1, source_target_pairs={{0,1},{1,0},{2,3},{3,2},{4,5},{5,4},{6,7},{7,6},{8,9},{9,8},{10,11... | collective-permute-start | bytes 196616 | tf_op jit(solution)/shard_map/ppermute | solution.py:264
  32.9 2.4 %collective-permute-start.4 = (bf16[128,512]{1,0:T(8,128)(2,1)S(1)}, bf16[128,512]{1,0:T(8,128)(2,1)S(1)}, u32[]{:S(2)}, u32[]{:S(2)}) collective-permute-start(bf16[128,512]{1,0:T(8,128)(2,1)S(1)} %collective-permute-done.3.refs_9_), channel_id=1, source_target_pairs={{0,1},{1,0},{2,3},{3,2},{4,5},{5,4},{6,7},{7,6},{8,9},{9,8},{10,11... | collective-permute-start | bytes 393224 | tf_op jit(solution)/shard_map/ppermute | solution.py:264
  33.4 1.9 %collective-permute-start.8 = (bf16[128,512]{1,0:T(8,128)(2,1)S(1)}, bf16[128,512]{1,0:T(8,128)(2,1)S(1)}, u32[]{:S(2)}, u32[]{:S(2)}) collective-permute-start(bf16[128,512]{1,0:T(8,128)(2,1)S(1)} %collective-permute-done.7.refs_13_), channel_id=1, source_target_pairs={{0,1},{1,0},{2,3},{3,2},{4,5},{5,4},{6,7},{7,6},{8,9},{9,8},{10,11... | collective-permute-start | bytes 393224 | tf_op jit(solution)/shard_map/ppermute | solution.py:264
  49.0 2.9 %collective-permute-start.12 = (bf16[512,512]{1,0:T(8,128)(2,1)S(1)}, bf16[512,512]{1,0:T(8,128)(2,1)S(1)}, u32[]{:S(2)}, u32[]{:S(2)}) collective-permute-start(bf16[512,512]{1,0:T(8,128)(2,1)S(1)} %get-tuple-element.32), channel_id=1, source_target_pairs={{0,1},{1,0},{2,3},{3,2},{4,5},{5,4},{6,7},{7,6},{8,9},{9,8},{10,11... | collective-permute-start | bytes 1572872 | tf_op jit(solution)/shard_map/ppermute | solution.py:264
  50.4 12.0 %collective-permute-start.15 = (bf16[128,1536]{1,0:T(8,128)(2,1)S(1)}, bf16[128,1536]{1,0:T(8,128)(2,1)S(1)}, u32[]{:S(2)}, u32[]{:S(2)}) collective-permute-start(bf16[128,1536]{1,0:T(8,128)(2,1)S(1)} %pad_maximum_fusion.2.refs_5_), channel_id=1, source_target_pairs={{0,2},{1,3},{2,0},{3,1},{4,6},{5,7},{6,4},{7,5},{8,10},{9,11},{10,... | collective-permute-start | bytes 1179656 | tf_op jit(solution)/shard_map/ppermute | solution.py:267
  52.1 21.5 %collective-permute-start.13 = (bf16[512,512]{1,0:T(8,128)(2,1)S(1)}, bf16[512,512]{1,0:T(8,128)(2,1)S(1)}, u32[]{:S(2)}, u32[]{:S(2)}) collective-permute-start(bf16[512,512]{1,0:T(8,128)(2,1)S(1)} %add_convert_fusion.1.refs_3_), channel_id=1, source_target_pairs={{0,2},{1,3},{2,0},{3,1},{4,6},{5,7},{6,4},{7,5},{8,10},{9,11},{10,... | collective-permute-start | bytes 1572872 | tf_op jit(solution)/shard_map/ppermute | solution.py:267
  52.8 12.0 %collective-permute-start.14 = (bf16[128,1536]{1,0:T(8,128)(2,1)S(1)}, bf16[128,1536]{1,0:T(8,128)(2,1)S(1)}, u32[]{:S(2)}, u32[]{:S(2)}) collective-permute-start(bf16[128,1536]{1,0:T(8,128)(2,1)S(1)} %pad_maximum_fusion.2.refs_5_), channel_id=1, source_target_pairs={{0,1},{1,0},{2,3},{3,2},{4,5},{5,4},{6,7},{7,6},{8,9},{9,8},{10,11... | collective-permute-start | bytes 1179656 | tf_op jit(solution)/shard_map/ppermute | solution.py:264
  62.4 2.4 %collective-permute-start.16 = (bf16[128,1536]{1,0:T(8,128)(2,1)S(1)}, bf16[128,1536]{1,0:T(8,128)(2,1)S(1)}, u32[]{:S(2)}, u32[]{:S(2)}) collective-permute-start(bf16[128,1536]{1,0:T(8,128)(2,1)S(1)} %collective-permute-done.15.refs_7_), channel_id=1, source_target_pairs={{0,1},{1,0},{2,3},{3,2},{4,5},{5,4},{6,7},{7,6},{8,9},{9,8},{10,11... | collective-permute-start | bytes 1179656 | tf_op jit(solution)/shard_map/ppermute | solution.py:264
  63.2 21.0 %collective-permute-start.25 = (bf16[128,2048]{1,0:T(8,128)(2,1)}, bf16[128,2048]{1,0:T(8,128)(2,1)}, u32[]{:S(2)}, u32[]{:S(2)}) collective-permute-start(bf16[128,2048]{1,0:T(8,128)(2,1)} %pad_maximum_fusion.refs_15_), channel_id=1, source_target_pairs={{0,2},{1,3},{2,0},{3,1},{4,6},{5,7},{6,4},{7,5},{8,10},{9,11},{10,... | collective-permute-start | bytes 1572872 | tf_op jit(solution)/shard_map/ppermute | solution.py:267
  75.1 9.2 %collective-permute-start.17 = (bf16[512,512]{1,0:T(8,128)(2,1)S(1)}, bf16[512,512]{1,0:T(8,128)(2,1)S(1)}, u32[]{:S(2)}, u32[]{:S(2)}) collective-permute-start(bf16[512,512]{1,0:T(8,128)(2,1)S(1)} %node_update.2), channel_id=1, source_target_pairs={{0,1},{1,0},{2,3},{3,2},{4,5},{5,4},{6,7},{7,6},{8,9},{9,8},{10,11... | collective-permute-start | bytes 1572872 | tf_op jit(solution)/shard_map/ppermute | solution.py:264
  75.2 29.2 %collective-permute-start.24 = (bf16[128,2048]{1,0:T(8,128)(2,1)}, bf16[128,2048]{1,0:T(8,128)(2,1)S(1)}, u32[]{:S(2)}, u32[]{:S(2)}) collective-permute-start(bf16[128,2048]{1,0:T(8,128)(2,1)} %pad_maximum_fusion.refs_15_), channel_id=1, source_target_pairs={{0,1},{1,0},{2,3},{3,2},{4,5},{5,4},{6,7},{7,6},{8,9},{9,8},{10,11... | collective-permute-start | bytes 1572872 | tf_op jit(solution)/shard_map/ppermute | solution.py:264
  84.2 20.2 %collective-permute-start.26 = (bf16[128,2048]{1,0:T(8,128)(2,1)}, bf16[128,2048]{1,0:T(8,128)(2,1)S(1)}, u32[]{:S(2)}, u32[]{:S(2)}) collective-permute-start(bf16[128,2048]{1,0:T(8,128)(2,1)} %collective-permute-done.25.refs_17_), channel_id=1, source_target_pairs={{0,1},{1,0},{2,3},{3,2},{4,5},{5,4},{6,7},{7,6},{8,9},{9,8},{10,11... | collective-permute-start | bytes 1572872 | tf_op jit(solution)/shard_map/ppermute | solution.py:264
  85.3 13.7 %collective-permute-start.18 = (bf16[128,512]{1,0:T(8,128)(2,1)S(1)}, bf16[128,512]{1,0:T(8,128)(2,1)S(1)}, u32[]{:S(2)}, u32[]{:S(2)}) collective-permute-start(bf16[128,512]{1,0:T(8,128)(2,1)S(1)} %get-tuple-element.38), channel_id=1, source_target_pairs={{0,4},{4,8},{8,12},{12,0},{1,5},{5,9},{9,13},{13,1},{2,6},{6,10},{... | collective-permute-start | bytes 393224 | tf_op jit(solution)/shard_map/ppermute | solution.py:270
  85.4 13.9 %collective-permute-start.22 = (bf16[128,512]{1,0:T(8,128)(2,1)S(1)}, bf16[128,512]{1,0:T(8,128)(2,1)S(1)}, u32[]{:S(2)}, u32[]{:S(2)}) collective-permute-start(bf16[128,512]{1,0:T(8,128)(2,1)S(1)} %get-tuple-element.40), channel_id=1, source_target_pairs={{0,12},{4,0},{8,4},{12,8},{1,13},{5,1},{9,5},{13,9},{2,14},{6,2},{... | collective-permute-start | bytes 393224 | tf_op jit(solution)/shard_map/ppermute | solution.py:270
  89.3 9.5 %collective-permute-start.20 = (bf16[64,512]{1,0:T(8,128)(2,1)S(1)}, bf16[64,512]{1,0:T(8,128)(2,1)S(1)}, u32[]{:S(2)}, u32[]{:S(2)}) collective-permute-start(bf16[64,512]{1,0:T(8,128)(2,1)S(1)} %get-tuple-element.39), channel_id=1, source_target_pairs={{0,8},{4,12},{8,0},{12,4},{1,9},{5,13},{9,1},{13,5},{2,10},{6,14},... | collective-permute-start | bytes 196616 | tf_op jit(solution)/shard_map/ppermute | solution.py:270
  98.9 5.6 %collective-permute-start.21 = (bf16[64,512]{1,0:T(8,128)(2,1)S(1)}, bf16[64,512]{1,0:T(8,128)(2,1)S(1)}, u32[]{:S(2)}, u32[]{:S(2)}) collective-permute-start(bf16[64,512]{1,0:T(8,128)(2,1)S(1)} %collective-permute-done.20.refs_11_), channel_id=1, source_target_pairs={{0,1},{1,0},{2,3},{3,2},{4,5},{5,4},{6,7},{7,6},{8,9},{9,8},{10,11... | collective-permute-start | bytes 196616 | tf_op jit(solution)/shard_map/ppermute | solution.py:264
  98.9 5.5 %collective-permute-start.19 = (bf16[128,512]{1,0:T(8,128)(2,1)S(1)}, bf16[128,512]{1,0:T(8,128)(2,1)S(1)}, u32[]{:S(2)}, u32[]{:S(2)}) collective-permute-start(bf16[128,512]{1,0:T(8,128)(2,1)S(1)} %collective-permute-done.18.refs_9_), channel_id=1, source_target_pairs={{0,1},{1,0},{2,3},{3,2},{4,5},{5,4},{6,7},{7,6},{8,9},{9,8},{10,11... | collective-permute-start | bytes 393224 | tf_op jit(solution)/shard_map/ppermute | solution.py:264
  99.4 5.1 %collective-permute-start.23 = (bf16[128,512]{1,0:T(8,128)(2,1)S(1)}, bf16[128,512]{1,0:T(8,128)(2,1)S(1)}, u32[]{:S(2)}, u32[]{:S(2)}) collective-permute-start(bf16[128,512]{1,0:T(8,128)(2,1)S(1)} %collective-permute-done.22.refs_13_), channel_id=1, source_target_pairs={{0,1},{1,0},{2,3},{3,2},{4,5},{5,4},{6,7},{7,6},{8,9},{9,8},{10,11... | collective-permute-start | bytes 393224 | tf_op jit(solution)/shard_map/ppermute | solution.py:264
  118.8 2.0 %collective-permute-start.27 = (bf16[512,512]{1,0:T(8,128)(2,1)S(1)}, bf16[512,512]{1,0:T(8,128)(2,1)S(1)}, u32[]{:S(2)}, u32[]{:S(2)}) collective-permute-start(bf16[512,512]{1,0:T(8,128)(2,1)S(1)} %get-tuple-element.42), channel_id=1, source_target_pairs={{0,1},{1,0},{2,3},{3,2},{4,5},{5,4},{6,7},{7,6},{8,9},{9,8},{10,11... | collective-permute-start | bytes 1572872 | tf_op jit(solution)/shard_map/ppermute | solution.py:264
  119.3 12.0 %collective-permute-start.30 = (bf16[128,1536]{1,0:T(8,128)(2,1)S(1)}, bf16[128,1536]{1,0:T(8,128)(2,1)S(1)}, u32[]{:S(2)}, u32[]{:S(2)}) collective-permute-start(bf16[128,1536]{1,0:T(8,128)(2,1)S(1)} %pad_maximum_fusion.3.refs_5_), channel_id=1, source_target_pairs={{0,2},{1,3},{2,0},{3,1},{4,6},{5,7},{6,4},{7,5},{8,10},{9,11},{10,... | collective-permute-start | bytes 1179656 | tf_op jit(solution)/shard_map/ppermute | solution.py:267
  121.0 20.7 %collective-permute-start.28 = (bf16[512,512]{1,0:T(8,128)(2,1)S(1)}, bf16[512,512]{1,0:T(8,128)(2,1)S(1)}, u32[]{:S(2)}, u32[]{:S(2)}) collective-permute-start(bf16[512,512]{1,0:T(8,128)(2,1)S(1)} %add_convert_fusion.refs_3_), channel_id=1, source_target_pairs={{0,2},{1,3},{2,0},{3,1},{4,6},{5,7},{6,4},{7,5},{8,10},{9,11},{10,... | collective-permute-start | bytes 1572872 | tf_op jit(solution)/shard_map/ppermute | solution.py:267
  122.5 8.8 %collective-permute-start.29 = (bf16[128,1536]{1,0:T(8,128)(2,1)S(1)}, bf16[128,1536]{1,0:T(8,128)(2,1)S(1)}, u32[]{:S(2)}, u32[]{:S(2)}) collective-permute-start(bf16[128,1536]{1,0:T(8,128)(2,1)S(1)} %pad_maximum_fusion.3.refs_5_), channel_id=1, source_target_pairs={{0,1},{1,0},{2,3},{3,2},{4,5},{5,4},{6,7},{7,6},{8,9},{9,8},{10,11... | collective-permute-start | bytes 1179656 | tf_op jit(solution)/shard_map/ppermute | solution.py:264
  143.1 2.0 %collective-permute-start.32 = (bf16[512,512]{1,0:T(8,128)(2,1)S(1)}, bf16[512,512]{1,0:T(8,128)(2,1)S(1)}, u32[]{:S(2)}, u32[]{:S(2)}) collective-permute-start(bf16[512,512]{1,0:T(8,128)(2,1)S(1)} %node_update.3), channel_id=1, source_target_pairs={{0,1},{1,0},{2,3},{3,2},{4,5},{5,4},{6,7},{7,6},{8,9},{9,8},{10,11... | collective-permute-start | bytes 1572872 | tf_op jit(solution)/shard_map/ppermute | solution.py:264
  (23 other events, 216.9 us)

commit v2 on v1

v2 whole, which is shorter than its diff:
```python
import functools

import jax
import jax.numpy as jnp
from jax import lax
from jax.experimental import pallas as pl
from jax.experimental.pallas import tpu as pltpu
from jax.sharding import PartitionSpec as P

STEPS = 2
STRIDE = 8
LANES = 128
PART = 768
DIGIT = 64
VMEM_BYTES = 20 * 1024 * 1024


def dot(a, b):
    return jnp.dot(a, b, preferred_element_type=jnp.float32)


def dot_t(a, b):
    return lax.dot_general(a, b, (((1,), (1,)), ((), ())), preferred_element_type=jnp.float32)


def pick_rows(index, count):
    spots = lax.broadcasted_iota(jnp.int32, (index.shape[0], count), 1)
    return (spots == index).astype(jnp.bfloat16)


def silu(x):
    return x * (0.5 * jnp.tanh(0.5 * x) + 0.5)


def layer_norm(values, gain):
    centred = values - jnp.mean(values, axis=-1, keepdims=True)
    row_var = jnp.mean(centred * centred, axis=-1, keepdims=True)
    return centred * lax.rsqrt(row_var + 1e-05) * gain


def along_lanes(pieces):
    return jnp.concatenate([pack[:, at:to] for pack, at, to in pieces], axis=1)


def mlp(x, groups, biases, gain):
    total = None
    for shards, bias in zip(groups, biases):
        w_in = jnp.concatenate([along_lanes(pieces) for pieces, _ in shards])
        w_out = jnp.concatenate([along_lanes(pieces) for _, pieces in shards])
        act = silu(dot_t(x, w_in) + bias).astype(jnp.bfloat16)
        part = dot(act, w_out)
        total = part if total is None else total + part
    return layer_norm(total, gain)


def take_groups(it, spots, cores):
    n_packs = 1 + max(pack for pieces in spots for pack, _, _ in pieces)
    groups = []
    for _ in range(cores // 2):
        shards = []
        for _ in range(2):
            refs = [next(it) for _ in range(n_packs)]
            shards.append([[(refs[pack], at, to) for pack, at, to in pieces] for pieces in spots])
        groups.append(shards)
    return groups


def loop(steps, body):
    lax.fori_loop(0, steps, body, 0, unroll=2 if steps % 2 == 0 else 1)


def call(kernel, out_shape, args, scratch=(), flops=0, nbytes=0, memory=None, limit=VMEM_BYTES, name=None):
    in_specs = [pl.BlockSpec(memory_space=m) for m in memory or [pltpu.VMEM] * len(args)]
    out_specs = jax.tree.map(lambda _: pl.BlockSpec(memory_space=pltpu.VMEM), out_shape)
    return pl.pallas_call(
        kernel,
        out_shape=out_shape,
        in_specs=in_specs,
        out_specs=out_specs,
        scratch_shapes=list(scratch),
        compiler_params=pltpu.CompilerParams(vmem_limit_bytes=limit),
        cost_estimate=pl.CostEstimate(flops=flops, bytes_accessed=nbytes, transcendentals=0),
        name=name,
    )(*args)


def bf16(*shape):
    return jax.ShapeDtypeStruct(shape, jnp.bfloat16)


def core_index():
    return lax.rem(lax.axis_index("feat"), 2)


def join_halves(out, own, other):
    core, nh = core_index(), own.shape[0]
    out[pl.ds(pl.multiple_of(core * nh, nh), nh), :] = own[...]
    out[pl.ds(pl.multiple_of((1 - core) * nh, nh), nh), :] = other[...]


def join_kernel(own, other, out):
    join_halves(out, own, other)


def add_kernel(own, arrived, out):
    out[...] = (own[...] + arrived[...].astype(jnp.float32)).astype(out.dtype)


def halo_kernel(first, *refs):
    if first:
        nodes, halo, to_prev, to_next, to_far, coarse = refs
    else:
        own, other, halo, to_prev, to_next, to_far, coarse, nodes = refs
        join_halves(nodes, own, other)
    core = core_index()
    count = nodes.shape[0]
    hr, cp = halo.shape[0] // 2, coarse.shape[0]
    hh, ch = hr // 2, cp // 2
    prev = halo[pl.ds(pl.multiple_of(core * hh, hh), hh), :]
    nxt = halo[pl.ds(pl.multiple_of(hr + core * hh, hh), hh), :]
    table = nodes[...]
    rows = dot(pick_rows(jnp.concatenate([prev, nxt], axis=0), count), table).astype(jnp.bfloat16)
    every = STRIDE * lax.broadcasted_iota(jnp.int32, (cp, 1), 0)
    coarse[...] = dot(pick_rows(every, count), table).astype(jnp.bfloat16)
    mine = coarse[pl.ds(pl.multiple_of(core * ch, ch), ch), :]
    to_prev[pl.ds(0, hh), :] = rows[:hh]
    to_prev[pl.ds(hh, ch), :] = mine
    to_next[pl.ds(0, hh), :] = rows[hh:]
    to_next[pl.ds(hh, ch), :] = mine
    to_far[...] = mine


def gather_kernel(tile, nodes, send, recv, sent, received):
    count = nodes.shape[0]

    def body(t, carry):
        rows = pl.ds(pl.multiple_of(t * tile, tile), tile)
        table = nodes[...]
        sent[rows, :] = dot(pick_rows(send[rows, :], count), table).astype(jnp.bfloat16)
        safe = jnp.minimum(recv[rows, :], count - 1)
        received[rows, :] = dot(pick_rows(safe, count), table).astype(jnp.bfloat16)
        return carry

    loop(send.shape[0] // tile, body)


def bias_rows_of(bias_ref, line, n_groups):
    per = bias_ref.shape[1] // n_groups
    return [bias_ref[line : line + 1, g * per : (g + 1) * per] for g in range(n_groups)]


def weight_kernel(plans, n_in, *refs):
    source, outs, sems = refs[:n_in], refs[n_in:-1], refs[-1]
    copies = []
    for plan, out in zip(plans, outs):
        at = 0
        for which, layer, first, last in plan:
            part = source[which].at[layer, :, first:last]
            spot = out.at[:, at : at + last - first]
            copies.append(pltpu.make_async_copy(part, spot, sems.at[len(copies)]))
            at += last - first
    for copy in copies:
        copy.start()
    for copy in copies:
        copy.wait()


def first_kernel(edge_w1, edge_w2, edge_b1, node_b1, out, sems):
    k, width, hidden = edge_w1.shape[2], edge_w2.shape[2], edge_b1.shape[1]
    copies = [
        pltpu.make_async_copy(edge_w1.at[0], out.at[:, 0:k], sems.at[0]),
        pltpu.make_async_copy(edge_w2.at[0], out.at[:, k : k + width], sems.at[1]),
    ]
    for copy in copies:
        copy.start()
    rows = [edge_b1[...].astype(jnp.float32), node_b1[...].astype(jnp.float32)]
    rows.append(jnp.zeros((16 - 2 * STEPS, hidden), jnp.float32))
    out[0:16, k + width : k + width + hidden] = jnp.concatenate(rows).astype(jnp.bfloat16)
    for copy in copies:
        copy.wait()


def coarse_pack_kernel(edges, send, recv, pack):
    width = edges.shape[1]
    pack[:, :width] = edges[...]
    lane = lax.broadcasted_iota(jnp.int32, (edges.shape[0], LANES), 1)
    digits = jnp.zeros(lane.shape, jnp.int32)
    for j, ref in enumerate((send, recv)):
        index = ref[...]
        high = lax.shift_right_logical(index, DIGIT.bit_length() - 1)
        low = index & (DIGIT - 1)
        digits = jnp.where(lane == 2 * j, high, jnp.where(lane == 2 * j + 1, low, digits))
    pack[:, width:] = digits.astype(jnp.float32).astype(jnp.bfloat16)


def fine_kernel(tile, sizes, spots, layer, *refs):
    count, hr, cp, parts, cores = sizes
    it = iter(refs)
    fine, sent, received, send, gain_ref = (next(it) for _ in range(5))
    prev, nxt = ((next(it), next(it)) for _ in range(2))
    groups = take_groups(it, spots, cores)
    bias_in = None if layer == 0 else next(it)
    new_fine = next(it)
    bias_out = next(it) if layer == 0 else None
    halo_tab = next(it)

    core = core_index()
    width = gain_ref.shape[-1]
    hh = hr // 2
    for side, pair in ((0, prev), (hr, nxt)):
        for who, ref in zip((core, 1 - core), pair):
            halo_tab[pl.ds(pl.multiple_of(side + who * hh, hh), hh), :] = ref[pl.ds(0, hh), :]

    if layer == 0:
        spot = 0
        for shards in groups:
            for _, [(pack, _, at)] in shards:
                hidden = pack.shape[0]
                rows = pack[0:16, at : at + hidden].astype(jnp.float32)
                bias_out[:, spot : spot + hidden] = rows[:8]
                spot += hidden
    biases = bias_rows_of(bias_out if layer == 0 else bias_in, layer, len(groups))
    gain = gain_ref[layer : layer + 1, :].astype(jnp.float32)

    def body(t, carry):
        rows = pl.ds(pl.multiple_of(t * tile, tile), tile)
        border = dot(pick_rows(send[rows, :] - count, 2 * hr), halo_tab[...])
        senders = (sent[rows, :].astype(jnp.float32) + border).astype(jnp.bfloat16)
        old = fine[rows, :]
        x = jnp.concatenate([old, senders, received[rows, :]], axis=1)
        y = mlp(x, groups, biases, gain)
        new_fine[rows, :] = (old.astype(jnp.float32) + y).astype(jnp.bfloat16)
        return carry

    loop(fine.shape[0] // tile, body)


def coarse_target(state, width, me, cp):
    lane = lax.broadcasted_iota(jnp.int32, (8, LANES), 1)
    weights = jnp.where(lane == 2, float(DIGIT), jnp.where(lane == 3, 1.0, 0.0)).astype(jnp.bfloat16)
    near = dot_t(weights, state[:, width : width + LANES])[:1, :].astype(jnp.int32) - me * cp
    return jnp.where((near >= 0) & (near < cp), near * STRIDE, -1)


def row_sums(base, out, new_fine, recv_row, state, target):
    width = out.shape[1]
    block = min(256, out.shape[0])
    for spot in range(0, out.shape[0], block):
        total = None
        for places, latents in ((recv_row[...], new_fine[...]), (target, state[:, :width])):
            rows = lax.broadcasted_iota(jnp.int32, (block, places.shape[1]), 0) + (base + spot)
            part = dot((rows == places).astype(jnp.bfloat16), latents)
            total = part if total is None else total + part
        out[pl.ds(spot, block), :] = total.astype(out.dtype)


def coarse_kernel(tile, sizes, spots, layer, *refs):
    count, hr, cp, parts, cores = sizes
    it = iter(refs)
    new_fine, recv_row, coarse_own, gain_ref, bias_ref = (next(it) for _ in range(5))
    states = [next(it) for _ in range(parts if layer == 0 else 1)]
    arrived = [(next(it), next(it)) for _ in range(parts - 1)]
    groups = take_groups(it, spots, cores)
    state, agg_other, coarse_tab = (next(it) for _ in range(3))

    core, me = core_index(), lax.axis_index("mesh")
    width = gain_ref.shape[-1]
    hh, ch, nh = hr // 2, cp // 2, count // 2

    coarse_tab[pl.ds(pl.multiple_of(me * cp, cp), cp), :] = coarse_own[...]
    for i, pair in enumerate(arrived):
        owner = lax.rem(me + parts - 1 - i, parts)
        skip = hh if i in (0, parts - 2) else 0
        for who, ref in zip((core, 1 - core), pair):
            spot = pl.multiple_of(owner * cp + who * ch, ch)
            coarse_tab[pl.ds(spot, ch), :] = ref[pl.ds(skip, ch), 0:width]
    at = 0
    for one in states:
        state[pl.ds(at, one.shape[0]), :] = one[...]
        at += one.shape[0]

    biases = bias_rows_of(bias_ref, layer, len(groups))
    gain = gain_ref[layer : layer + 1, :].astype(jnp.float32)

    def body(t, carry):
        rows = pl.ds(pl.multiple_of(t * tile, tile), tile)
        old = state[rows, :width]
        digits = state[rows, width : width + LANES].astype(jnp.float32)
        ends = []
        for j in range(2):
            index = DIGIT * digits[:, 2 * j : 2 * j + 1] + digits[:, 2 * j + 1 : 2 * j + 2]
            picked = pick_rows(index.astype(jnp.int32), coarse_tab.shape[0])
            ends.append(dot(picked, coarse_tab[...]).astype(jnp.bfloat16))
        y = mlp(jnp.concatenate([old] + ends, axis=1), groups, biases, gain)
        state[rows, :width] = (old.astype(jnp.float32) + y).astype(jnp.bfloat16)
        return carry

    loop(state.shape[0] // tile, body)
    target = coarse_target(state, width, me, cp)
    row_sums((1 - core) * nh, agg_other, new_fine, recv_row, state, target)


def own_kernel(cp, new_fine, recv_row, state, agg_own):
    core, me = core_index(), lax.axis_index("mesh")
    nh, width = agg_own.shape
    target = coarse_target(state, width, me, cp)
    row_sums(core * nh, agg_own, new_fine, recv_row, state, target)


def node_kernel(tile, layer, cores, spots, n_sums, *refs):
    it = iter(refs)
    nodes, bias_ref, gain_ref = (next(it) for _ in range(3))
    sums = [next(it) for _ in range(n_sums)]
    groups = take_groups(it, spots, cores)
    out = next(it)
    nh = out.shape[0]
    biases = bias_rows_of(bias_ref, STEPS + layer, len(groups))
    gain = gain_ref[layer : layer + 1, :].astype(jnp.float32)
    core = core_index()
    for t in range(nh // tile):
        rows = pl.ds(t * tile, tile)
        old = nodes[pl.ds(pl.multiple_of(core * nh + t * tile, tile), tile), :]
        agg = sums[0][rows, :].astype(jnp.float32)
        for more in sums[1:]:
            agg = agg + more[rows, :].astype(jnp.float32)
        x = jnp.concatenate([old, agg.astype(jnp.bfloat16)], axis=1)
        y = mlp(x, groups, biases, gain)
        out[rows, :] = (old.astype(jnp.float32) + y).astype(jnp.bfloat16)


def divisor(count, most, unit=16):
    best = unit
    for size in range(unit, min(most, count) + 1, unit):
        if count % size == 0:
            best = size
    return best


def local(
    nodes,
    fine_edges,
    fine_send,
    fine_recv,
    halo_send,
    coarse_edges,
    coarse_send,
    coarse_recv,
    edge_w1,
    edge_b1,
    edge_w2,
    edge_gain,
    node_w1,
    node_b1,
    node_w2,
    node_gain,
):
    count, width = nodes.shape
    hr = halo_send.shape[0] // 2
    cp = count // STRIDE
    nh = count // 2
    fine_count = fine_edges.shape[0]
    parts = lax.axis_size("mesh")
    cores = lax.axis_size("feat")
    core = core_index()

    def swap(x):
        return lax.ppermute(x, "feat", [(i, i ^ 1) for i in range(cores)])

    def across(x):
        return lax.ppermute(x, "feat", [(i, i ^ 2) for i in range(cores)])

    def shift(x, by):
        return lax.ppermute(x, "mesh", [(i, (i + by) % parts) for i in range(parts)])

    def both(x):
        return [x, swap(x)]

    def after(x, *earlier):
        return lax.optimization_barrier((x, earlier))[0]

    two = cores == 4

    def spread(pack, *earlier):
        if two:
            return across(after(pack, *earlier) if earlier else pack)
        return lax.all_gather(pack, "feat", axis=0)

    def shards(pack, far):
        if two:
            return both(pack) + both(far)
        return [far[i] for i in range(cores)]

    k, kn = edge_w1.shape[2], node_w1.shape[2]
    w_hidden = edge_w1.shape[1]
    first_pack = call(
        first_kernel,
        bf16(w_hidden, k + width + LANES),
        [edge_w1, edge_w2, edge_b1, node_b1],
        scratch=[pltpu.SemaphoreType.DMA((2,))],
        memory=[pl.ANY, pl.ANY, pltpu.VMEM, pltpu.VMEM],
        limit=3 * VMEM_BYTES,
        name="first_weights",
    )
    stream = ((2, 0, kn), (3, 0, width), (1, 1, width), (0, 1, k), (2, 1, kn), (3, 1, width))
    starts = [0]
    for _, _, lanes in stream:
        starts.append(starts[-1] + lanes)
    cuts = [0, starts[2], starts[3], starts[4] + PART, starts[-1]]

    def pieces(which):
        first, last = starts[which], starts[which + 1]
        found = []
        for pack, (lo, hi) in enumerate(zip(cuts, cuts[1:])):
            if max(lo, first) < min(hi, last):
                found.append((pack, max(lo, first) - lo, min(hi, last) - lo))
        return found

    plans = [[] for _ in cuts[1:]]
    for which, (source, layer, _) in enumerate(stream):
        done = 0
        for pack, at, to in pieces(which):
            plans[pack].append((source, layer, done, done + to - at))
            done += to - at
    packs = call(
        functools.partial(weight_kernel, plans, 4),
        tuple(bf16(w_hidden, hi - lo) for lo, hi in zip(cuts, cuts[1:])),
        [edge_w1, edge_w2, node_w1, node_w2],
        scratch=[pltpu.SemaphoreType.DMA((sum(len(p) for p in plans),))],
        memory=[pl.ANY] * 4,
        limit=3 * VMEM_BYTES,
        name="later_weights",
    )

    def choose(shards_of, w_in, w_out):
        used = sorted({pack for which in (w_in, w_out) for pack, _, _ in pieces(which)})
        spots = [[(used.index(p), at, to) for p, at, to in pieces(w)] for w in (w_in, w_out)]
        return [x for shard in zip(*(shards_of[p] for p in used)) for x in shard], spots

    own_coarse = coarse_edges.shape[0]
    coarse_pack = call(
        coarse_pack_kernel,
        bf16(own_coarse, width + LANES),
        [coarse_edges, coarse_send.reshape(own_coarse, 1), coarse_recv.reshape(own_coarse, 1)],
        name="coarse_pack",
    )
    coarse_count = own_coarse * parts

    send_col = fine_send.reshape(fine_count, 1)
    recv_col = fine_recv.reshape(fine_count, 1)
    recv_row = fine_recv.reshape(1, fine_count)
    halo_col = halo_send.reshape(2 * hr, 1)
    tile = divisor(fine_count, 768)
    ctile = divisor(coarse_count, 384)
    hidden = w_hidden * cores
    sizes = (count, hr, cp, parts, cores)
    bias_rows = None

    def node_rows_out(*given):
        half = hr // 2 + cp // 2
        first = len(given) == 1
        outs = [bf16(half, width), bf16(half, width), bf16(cp // 2, width), bf16(cp, width)]
        return call(
            functools.partial(halo_kernel, first),
            tuple(outs if first else outs + [bf16(count, width)]),
            [*given, halo_col],
            name="halo_rows",
        )

    def exchange(to_prev, to_next, coarse_half):
        return [
            shift({1: to_next, parts - 1: to_prev}.get(by, coarse_half), by)
            for by in range(1, parts)
        ]

    def gather(nodes):
        return call(
            functools.partial(gather_kernel, tile),
            (bf16(fine_count, width), bf16(fine_count, width)),
            [nodes, send_col, recv_col],
            flops=4 * fine_count * count * width,
            name="gather_rows",
        )

    def fine_update(s, fine, sent, received, halo, weights, spots):
        outs = [bf16(fine_count, width)]
        if s == 0:
            outs.append(jax.ShapeDtypeStruct((8, hidden), jnp.float32))
        return call(
            functools.partial(fine_kernel, tile, sizes, spots, s),
            tuple(outs),
            [fine, sent, received, send_col, edge_gain] + halo + weights + ([bias_rows] if s else []),
            scratch=[pltpu.VMEM((2 * hr, width), jnp.bfloat16)],
            flops=8 * fine_count * width * hidden,
            name="fine_edges",
        )

    def coarse_update(s, new_fine, coarse_own, states, arrived, weights, spots):
        return call(
            functools.partial(coarse_kernel, ctile, sizes, spots, s),
            (bf16(coarse_count, width + LANES), bf16(nh, width)),
            [new_fine, recv_row, coarse_own, edge_gain, bias_rows] + states + arrived + weights,
            scratch=[pltpu.VMEM((parts * cp, width), jnp.bfloat16)],
            name="coarse_edges_and_sums",
        )

    def own_sums(new_fine, state):
        return call(
            functools.partial(own_kernel, cp),
            jax.ShapeDtypeStruct((nh, width), jnp.float32),
            [new_fine, recv_row, state],
            name="own_sums",
        )

    def node_update(s, nodes, sums, weights, spots):
        return both(
            call(
                functools.partial(node_kernel, divisor(nh, 256), s, cores, spots, len(sums)),
                bf16(nh, width),
                [nodes, bias_rows, node_gain] + sums + weights,
                name="node_update",
            )
        )

    def core_sum(agg_own, agg_other):
        return call(add_kernel, bf16(nh, width), [agg_own, swap(agg_other)], name="core_sum")

    def chip_sums(partial):
        if two:
            return [partial, across(partial)]
        every = lax.all_gather(partial, "feat", axis=0)
        every = every.reshape(cores // 2, 2, nh, width).astype(jnp.float32)
        return [lax.dynamic_index_in_dim(every.sum(axis=0), core, 0, keepdims=False)]

    def halo_of(moved, swapped):
        return [moved[0], swapped[0], moved[-1], swapped[-1]]

    def pairs(moved, swapped):
        return [x for pair in zip(moved, swapped) for x in pair]

    far_first = spread(first_pack)
    to_prev, to_next, to_far, coarse_own = node_rows_out(nodes)
    moved = exchange(to_prev, to_next, to_far)
    send_col, recv_col, recv_row, coarse_pack, *packs = after(
        (send_col, recv_col, recv_row, coarse_pack, *packs), to_prev
    )
    sent, received = gather(nodes)
    coarse_pack = after(coarse_pack, sent)
    states = [coarse_pack] + [shift(coarse_pack, by) for by in range(1, parts)]
    *moved, far_first = after((*moved, far_first), sent)
    swapped = [swap(m) for m in moved]
    weights, spots = shards(first_pack, far_first), (((0, 0, k),), ((0, k, k + width),))
    far = spread(packs[0], far_first)
    fine_edges, bias_rows = fine_update(
        0, fine_edges, sent, received, halo_of(moved, swapped), weights, spots
    )
    states, fine_edges, far = after((states, fine_edges, far))
    packs_of = [shards(packs[0], far)]
    far = spread(packs[1], far)
    state, agg_other = coarse_update(
        0, fine_edges, coarse_own, states, pairs(moved, swapped), weights, spots
    )
    state, agg_other, far = after((state, agg_other, far))
    packs_of.append(shards(packs[1], far))
    agg_own = own_sums(fine_edges, state)
    sums = chip_sums(core_sum(agg_own, agg_other))
    far = spread(packs[2], sums)
    halves = node_update(0, nodes, sums, *choose(packs_of, 0, 1))

    to_prev, to_next, to_far, coarse_own, nodes = node_rows_out(*halves)
    moved = exchange(to_prev, to_next, to_far)
    sent, received = gather(nodes)
    *moved, far = after((*moved, far), sent)
    packs_of.append(shards(packs[2], far))
    swapped = [swap(m) for m in moved]
    far = spread(packs[3], far)
    weights, spots = choose(packs_of, 3, 2)
    (fine_edges,) = fine_update(
        1, fine_edges, sent, received, halo_of(moved, swapped), weights, spots
    )
    fine_edges, far = after((fine_edges, far))
    packs_of.append(shards(packs[3], far))
    state, agg_other = coarse_update(
        1, fine_edges, coarse_own, [state], pairs(moved, swapped), weights, spots
    )
    agg_own = own_sums(fine_edges, state)
    sums = chip_sums(core_sum(agg_own, agg_other))
    halves = node_update(1, nodes, sums, *choose(packs_of, 4, 5))
    return call(join_kernel, bf16(count, width), halves, name="nodes_out")


def solution(mesh):
    placed = (
        P(("groups", "mesh"), None),
        P(("groups", "mesh", "feat"), None),
        P(("groups", "mesh", "feat")),
        P(("groups", "mesh", "feat")),
        P(("groups", "mesh")),
        P(("groups", "mesh", "feat"), None),
        P(("groups", "mesh", "feat")),
        P(("groups", "mesh", "feat")),
        P(None, "feat", None),
        P(None, "feat"),
        P(None, "feat", None),
        P(),
        P(None, "feat", None),
        P(None, "feat"),
        P(None, "feat", None),
        P(),
    )
    return jax.shard_map(
        local, mesh=mesh, in_specs=placed, out_specs=P(("groups", "mesh"), None), check_vma=False
    )
```

time: 147 us -> 111 us (0.76)
  waiting for transfers between devices: 66.1 us -> 46.2 us
  other arithmetic: 5.79 us -> 0 us
  starting transfers between devices: 28 us -> 23.1 us
  local copies, waits for them, and re-layouts: 4.57 us -> 1.68 us
  Pallas kernels: 41.7 us -> 39.2 us
    ppermute x6 -> x7, waiting for transfers between devices: 51.8 us -> 30 us  [across(): return lax.ppermute(x, 'feat', [(i, i ^ 2) for i in range(cores)])]
    ppermute x18 -> x20, waiting for transfers between devices: 3.66 us -> 9.94 us  [swap(): return lax.ppermute(x, 'feat', [(i, i ^ 1) for i in range(cores)])]
    ppermute x9, waiting for transfers between devices: 10.7 us -> 6.32 us  [shift(): lax.ppermute(x, 'mesh', [(i, (i + by) % parts) for i in range(parts)])]
    squeeze x4 -> x0, local copies, waits for them, and re-layouts: 3.52 us -> none  [the longest x1 2.02 us: local(): edge_w1[s]]
    ppermute x9, starting transfers between devices: 15.3 us -> 12.2 us  [shift(): lax.ppermute(x, 'mesh', [(i, (i + by) % parts) for i in range(parts)])]
    concatenate x7 -> x0, other arithmetic: 2.77 us -> none  [the longest x2 1.7 us: local(): jnp.concatenate([edge_w1[s], edge_w2[s]] + ([bias] if s == 0 else []), ax...]
    pallas_call x8 -> x18, Pallas kernels: 41.7 us -> 39.2 us  [call(): pl.pallas_call(kernel, out_shape=out_shape, in_specs=in_specs, out_specs=...]
    ppermute x6 -> x7, starting transfers between devices: 9.72 us -> 7.37 us  [across(): return lax.ppermute(x, 'feat', [(i, i ^ 2) for i in range(cores)])]
  transfers between devices with their start and end apart: 33 -> 36, of which waited for: 10 -> 18; matrix products, arithmetic and copies ran while one was open for 4% -> 1% of each run, Pallas kernels for 8% -> 26%
where the time goes in v2:
time: 111 us
  waiting for transfers between devices  46.2 us (42%)
  Pallas kernels  39.2 us (35%)
  starting transfers between devices  23.1 us (21%)
  local copies, waits for them, and re-layouts  1.68 us (2%)
    pallas_call x18, Pallas kernels, call(): pl.pallas_call(kernel, out_shape=out_shape, in_specs=in_specs, out_specs=...  39.2 us
    ppermute x7, waiting for transfers between devices, across(): return lax.ppermute(x, 'feat', [(i, i ^ 2) for i in range(cores)])  30 us
    ppermute x9, starting transfers between devices, shift(): lax.ppermute(x, 'mesh', [(i, (i + by) % parts) for i in range(parts)])  12.2 us
    ppermute x20, waiting for transfers between devices, swap(): return lax.ppermute(x, 'feat', [(i, i ^ 1) for i in range(cores)])  9.94 us
    ppermute x7, starting transfers between devices, across(): return lax.ppermute(x, 'feat', [(i, i ^ 2) for i in range(cores)])  7.37 us
    ppermute x9, waiting for transfers between devices, shift(): lax.ppermute(x, 'mesh', [(i, (i + by) % parts) for i in range(parts)])  6.32 us
    ppermute x20, starting transfers between devices, swap(): return lax.ppermute(x, 'feat', [(i, i ^ 1) for i in range(cores)])  3.56 us
  transfers between devices with their start and end apart: 36, of which 18 were waited for; matrix products, arithmetic and copies ran while one was open for 1% of the time, Pallas kernels for 26%

profile of v2, /device:TPU:0, one launch (start us, length us, event | category | flops | bytes accessed | tf_op | source)
XLA Modules:
  0.0 110.6 jit_solution(7466287035031317734)
XLA Ops:
  0.0 2.6 %first_weights.1.refs_9_.refs_15_ = bf16[128,2176]{1,0:T(8,128)(2,1)} custom-call(bf16[2,128,1536]{2,1,0:T(8,128)(2,1)} %edge_w1.1, bf16[2,128,512]{2,1,0:T(8,128)(2,1)} %edge_w2.1, bf16[2,128]{1,0:T(2,128)(2,1)} %edge_b1.1, bf16[2,128]{1,0:T(2,128)(2,1)} %node_b1.1), custom_call_target="tpu_custom_call" | custom-call | tf_op jit(solution)/shard_map/first_weights/pallas_call | solution.py:75
  2.7 3.0 %collective-permute-start.3 = (bf16[128,2176]{1,0:T(8,128)(2,1)}, bf16[128,2176]{1,0:T(8,128)(2,1)S(1)}, u32[]{:S(2)}, u32[]{:S(2)}) collective-permute-start(bf16[128,2176]{1,0:T(8,128)(2,1)} %first_weights.1.refs_9_.refs_15_), channel_id=1, source_target_pairs={{0,2},{1,3},{2,0},{3,1},{4,6},{5,7},{6,4},{7,5},{8,10},{9,11},{10,... | collective-permute-start | bytes 1671176 | tf_op jit(solution)/shard_map/ppermute | solution.py:370
  5.8 1.3 %halo_rows.2 = (bf16[128,512]{1,0:T(8,128)(2,1)}, bf16[128,512]{1,0:T(8,128)(2,1)}, bf16[64,512]{1,0:T(8,128)(2,1)}, bf16[128,512]{1,0:T(8,128)(2,1)S(1)}) custom-call(bf16[1024,512]{1,0:T(8,128)(2,1)S(1)} %copy-done, s32[256,1]{1,0:T(8,128)S(1)} %copy.21.refs_1_.refs_2_), custom_call_target="tpu_custom_call" | custom-call | tf_op jit(solution)/shard_map/halo_rows/pallas_call | solution.py:75
  7.8 3.6 %collective-permute-start.2 = (bf16[128,512]{1,0:T(8,128)(2,1)}, bf16[128,512]{1,0:T(8,128)(2,1)}, u32[]{:S(2)}, u32[]{:S(2)}) collective-permute-start(bf16[128,512]{1,0:T(8,128)(2,1)} %get-tuple-element.64), channel_id=1, source_target_pairs={{0,12},{4,0},{8,4},{12,8},{1,13},{5,1},{9,5},{13,9},{2,14},{6,2},{... | collective-permute-start | bytes 393224 | tf_op jit(solution)/shard_map/ppermute | solution.py:373
  11.4 1.0 collective-permute-start.1
  12.6 2.4 %later_weights.1 = (bf16[128,1536]{1,0:T(8,128)(2,1)}, bf16[128,512]{1,0:T(8,128)(2,1)}, bf16[128,2304]{1,0:T(8,128)(2,1)}, bf16[128,768]{1,0:T(8,128)(2,1)}) custom-call(bf16[2,128,1536]{2,1,0:T(8,128)(2,1)} %edge_w1.1, bf16[2,128,512]{2,1,0:T(8,128)(2,1)} %edge_w2.1, bf16[2,128,1024]{2,1,0:T(8,128)(2,1)} %refs_2_.3, bf16[2,128,512]{2,1,0:T(8,128)(2,1)} %refs_3_.3), custom_call_target="tpu_custom_call" | custom-call | tf_op jit(solution)/shard_map/later_weights/pallas_call | solution.py:75
  15.8 3.5 %gather_rows.2 = (bf16[1536,512]{1,0:T(8,128)(2,1)S(1)}, bf16[1536,512]{1,0:T(8,128)(2,1)S(1)}) custom-call(bf16[1024,512]{1,0:T(8,128)(2,1)S(1)} %copy-done, s32[1536,1]{1,0:T(8,128)S(1)} %copy.22.send.refs_3_, s32[1536,1]{1,0:T(8,128)S(1)} %copy.23.recv), custom_call_target="tpu_custom_call" | custom-call | flops 3221225472 | tf_op jit(solution)/shard_map/gather_rows/pallas_call | solution.py:75
  19.3 1.6 %collective-permute-done.1.refs_11_ = bf16[64,512]{1,0:T(8,128)(2,1)S(1)} collective-permute-done((bf16[64,512]{1,0:T(8,128)(2,1)}, bf16[64,512]{1,0:T(8,128)(2,1)S(1)}, u32[]{:S(2)}, u32[]{:S(2)}) %collective-permute-start.1) | collective-permute-done | bytes 65568 | tf_op jit(solution)/shard_map/ppermute | solution.py:373
  22.2 2.2 %collective-permute-start.10 = (bf16[96,640]{1,0:T(8,128)(2,1)S(1)}, bf16[96,640]{1,0:T(8,128)(2,1)S(1)}, u32[]{:S(2)}, u32[]{:S(2)}) collective-permute-start(bf16[96,640]{1,0:T(8,128)(2,1)S(1)} %coarse_pack.1.refs_5_), channel_id=1, source_target_pairs={{0,12},{4,0},{8,4},{12,8},{1,13},{5,1},{9,5},{13,9},{2,14},{6,2},{... | collective-permute-start | bytes 368648 | tf_op jit(solution)/shard_map/ppermute | solution.py:373
  25.9 6.0 %fine_edges.2 = (bf16[1536,512]{1,0:T(8,128)(2,1)S(1)}, f32[8,512]{1,0:T(8,128)S(1)}) custom-call(bf16[1536,512]{1,0:T(8,128)(2,1)S(1)} %copy-done.11, bf16[1536,512]{1,0:T(8,128)(2,1)S(1)} %get-tuple-element.67.refs_1_, bf16[1536,512]{1,0:T(8,128)(2,1)S(1)} %get-tuple-element.68.refs_2_, s32[1536,1]{1,0:T(8,128)S(1)} %copy.22.send.refs_3_, ...), custom_call_target="tpu_custom_call" | custom-call | flops 3221225472 | tf_op jit(solution)/shard_map/fine_edges/pallas_call | solution.py:75
  32.4 4.2 %collective-permute-done.9.refs_7_ = bf16[96,640]{1,0:T(8,128)(2,1)S(1)} collective-permute-done((bf16[96,640]{1,0:T(8,128)(2,1)S(1)}, bf16[96,640]{1,0:T(8,128)(2,1)S(1)}, u32[]{:S(2)}, u32[]{:S(2)}) %collective-permute-start.9) | collective-permute-done | bytes 122912 | tf_op jit(solution)/shard_map/ppermute | solution.py:373
  36.6 1.5 %collective-permute-start.13 = (bf16[128,512]{1,0:T(8,128)(2,1)S(1)}, bf16[128,512]{1,0:T(8,128)(2,1)S(1)}, u32[]{:S(2)}, u32[]{:S(2)}) collective-permute-start(bf16[128,512]{1,0:T(8,128)(2,1)S(1)} %copy-done.5), channel_id=1, source_target_pairs={{0,2},{1,3},{2,0},{3,1},{4,6},{5,7},{6,4},{7,5},{8,10},{9,11},{10,... | collective-permute-start | bytes 393224 | tf_op jit(solution)/shard_map/ppermute | solution.py:370
  38.2 1.3 %collective-permute-done.12.refs_12_ = bf16[64,512]{1,0:T(8,128)(2,1)S(1)} collective-permute-done((bf16[64,512]{1,0:T(8,128)(2,1)S(1)}, bf16[64,512]{1,0:T(8,128)(2,1)S(1)}, u32[]{:S(2)}, u32[]{:S(2)}) %collective-permute-start.12) | collective-permute-done | bytes 65568 | tf_op jit(solution)/shard_map/ppermute | solution.py:367
  39.4 4.4 %coarse_edges_and_sums.2 = (bf16[384,640]{1,0:T(8,128)(2,1)S(1)}, bf16[512,512]{1,0:T(8,128)(2,1)S(1)}) custom-call(bf16[1536,512]{1,0:T(8,128)(2,1)S(1)} %get-tuple-element.80.refs_0_.new_fine, s32[1,1536]{1,0:T(1,128)S(1)} %reshape.20.refs_1_.recv_row, bf16[128,512]{1,0:T(8,128)(2,1)S(1)} %copy-done.7, bf16[2,512]{1,0:T(2,128)(2,1)S(1)} %copy-done.9, ...), custom_call_target="tpu_custom_call" | custom-call | tf_op jit(solution)/shard_map/coarse_edges_and_sums/pallas_call | solution.py:75
  44.0 1.4 %own_sums.2.own = f32[512,512]{1,0:T(8,128)S(1)} custom-call(bf16[1536,512]{1,0:T(8,128)(2,1)S(1)} %get-tuple-element.80.refs_0_.new_fine, s32[1,1536]{1,0:T(1,128)S(1)} %reshape.20.refs_1_.recv_row, bf16[384,640]{1,0:T(8,128)(2,1)S(1)} %get-tuple-element.93.state.refs_5_), custom_call_target="tpu_custom_call" | custom-call | tf_op jit(solution)/shard_map/own_sums/pallas_call | solution.py:75
  47.0 1.2 %collective-permute-done.16.refs_6_ = bf16[128,1536]{1,0:T(8,128)(2,1)S(1)} collective-permute-done((bf16[128,1536]{1,0:T(8,128)(2,1)S(1)}, bf16[128,1536]{1,0:T(8,128)(2,1)S(1)}, u32[]{:S(2)}, u32[]{:S(2)}) %collective-permute-start.16) | collective-permute-done | bytes 393248 | tf_op jit(solution)/shard_map/ppermute | solution.py:367
  48.7 11.2 %collective-permute-done.15.refs_4_ = bf16[512,512]{1,0:T(8,128)(2,1)S(1)} collective-permute-done((bf16[512,512]{1,0:T(8,128)(2,1)S(1)}, bf16[512,512]{1,0:T(8,128)(2,1)S(1)}, u32[]{:S(2)}, u32[]{:S(2)}) %collective-permute-start.15) | collective-permute-done | bytes 524320 | tf_op jit(solution)/shard_map/ppermute | solution.py:370
  59.9 1.4 %node_update.2.refs_0_ = bf16[512,512]{1,0:T(8,128)(2,1)S(1)} custom-call(bf16[1024,512]{1,0:T(8,128)(2,1)S(1)} %copy-done, f32[8,512]{1,0:T(8,128)S(1)} %get-tuple-element.74.refs_4_.refs_1_.refs_17_, bf16[2,512]{1,0:T(2,128)(2,1)S(1)} %copy-done.10, bf16[512,512]{1,0:T(8,128)(2,1)S(1)} %core_sum.2.refs_3_, ...), custom_call_target="tpu_custom_call" | custom-call | tf_op jit(solution)/shard_map/node_update/pallas_call | solution.py:75
  62.2 1.1 %collective-permute-done.18.refs_1_ = bf16[512,512]{1,0:T(8,128)(2,1)S(1)} collective-permute-done((bf16[512,512]{1,0:T(8,128)(2,1)S(1)}, bf16[512,512]{1,0:T(8,128)(2,1)S(1)}, u32[]{:S(2)}, u32[]{:S(2)}) %collective-permute-start.18) | collective-permute-done | bytes 524320 | tf_op jit(solution)/shard_map/ppermute | solution.py:367
  64.0 3.8 %collective-permute-start.21 = (bf16[128,512]{1,0:T(8,128)(2,1)S(1)}, bf16[128,512]{1,0:T(8,128)(2,1)S(1)}, u32[]{:S(2)}, u32[]{:S(2)}) collective-permute-start(bf16[128,512]{1,0:T(8,128)(2,1)S(1)} %get-tuple-element.100), channel_id=1, source_target_pairs={{0,12},{4,0},{8,4},{12,8},{1,13},{5,1},{9,5},{13,9},{2,14},{6,2},{... | collective-permute-start | bytes 393224 | tf_op jit(solution)/shard_map/ppermute | solution.py:373
  67.8 3.5 %gather_rows.3 = (bf16[1536,512]{1,0:T(8,128)(2,1)S(1)}, bf16[1536,512]{1,0:T(8,128)(2,1)S(1)}) custom-call(bf16[1024,512]{1,0:T(8,128)(2,1)S(1)} %get-tuple-element.95.nodes.refs_0_, s32[1536,1]{1,0:T(8,128)S(1)} %copy.22.send.refs_3_, s32[1536,1]{1,0:T(8,128)S(1)} %copy.23.recv), custom_call_target="tpu_custom_call" | custom-call | flops 3221225472 | tf_op jit(solution)/shard_map/gather_rows/pallas_call | solution.py:75
  71.3 5.9 %collective-permute-done.22.refs_14_.refs_17_.refs_9_ = bf16[128,2304]{1,0:T(8,128)(2,1)S(1)} collective-permute-done((bf16[128,2304]{1,0:T(8,128)(2,1)S(1)}, bf16[128,2304]{1,0:T(8,128)(2,1)S(1)}, u32[]{:S(2)}, u32[]{:S(2)}) %collective-permute-start.22) | collective-permute-done | bytes 589856 | tf_op jit(solution)/shard_map/ppermute | solution.py:370
  78.3 1.2 %collective-permute-done.25.refs_11_.refs_14_ = bf16[128,512]{1,0:T(8,128)(2,1)S(1)} collective-permute-done((bf16[128,512]{1,0:T(8,128)(2,1)S(1)}, bf16[128,512]{1,0:T(8,128)(2,1)S(1)}, u32[]{:S(2)}, u32[]{:S(2)}) %collective-permute-start.25) | collective-permute-done | bytes 131104 | tf_op jit(solution)/shard_map/ppermute | solution.py:367
  80.8 4.8 %fine_edges.3.refs_0_.new_fine = bf16[1536,512]{1,0:T(8,128)(2,1)S(1)} custom-call(bf16[1536,512]{1,0:T(8,128)(2,1)S(1)} %get-tuple-element.80.refs_0_.new_fine, bf16[1536,512]{1,0:T(8,128)(2,1)S(1)} %get-tuple-element.96.refs_1_, bf16[1536,512]{1,0:T(8,128)(2,1)S(1)} %get-tuple-element.97.refs_2_, s32[1536,1]{1,0:T(8,128)S(1)} %copy.22.send.refs_3_, ...), custom_call_target="tpu_custom_call" | custom-call | flops 3221225472 | tf_op jit(solution)/shard_map/fine_edges/pallas_call | solution.py:75
  85.7 1.1 %collective-permute-done.29.refs_10_ = bf16[128,768]{1,0:T(8,128)(2,1)S(1)} collective-permute-done((bf16[128,768]{1,0:T(8,128)(2,1)S(1)}, bf16[128,768]{1,0:T(8,128)(2,1)S(1)}, u32[]{:S(2)}, u32[]{:S(2)}) %collective-permute-start.29) | collective-permute-done | bytes 196640 | tf_op jit(solution)/shard_map/ppermute | solution.py:370
  86.8 3.2 %coarse_edges_and_sums.3 = (bf16[384,640]{1,0:T(8,128)(2,1)S(1)}, bf16[512,512]{1,0:T(8,128)(2,1)S(1)}) custom-call(bf16[1536,512]{1,0:T(8,128)(2,1)S(1)} %fine_edges.3.refs_0_.new_fine, s32[1,1536]{1,0:T(1,128)S(1)} %reshape.20.refs_1_.recv_row, bf16[128,512]{1,0:T(8,128)(2,1)S(1)} %get-tuple-element.110.refs_2_, bf16[2,512]{1,0:T(2,128)(2,1)S(1)} %copy-done.9, ...), custom_call_target="tpu_custom_call" | custom-call | tf_op jit(solution)/shard_map/coarse_edges_and_sums/pallas_call | solution.py:75
  90.0 1.4 %own_sums.3.own = f32[512,512]{1,0:T(8,128)S(1)} custom-call(bf16[1536,512]{1,0:T(8,128)(2,1)S(1)} %fine_edges.3.refs_0_.new_fine, s32[1,1536]{1,0:T(1,128)S(1)} %reshape.20.refs_1_.recv_row, bf16[384,640]{1,0:T(8,128)(2,1)S(1)} %get-tuple-element.112.state), custom_call_target="tpu_custom_call" | custom-call | tf_op jit(solution)/shard_map/own_sums/pallas_call | solution.py:75
  93.2 0.9 collective-permute-done.33.refs_8_
  94.4 11.7 %collective-permute-done.32.refs_4_ = bf16[512,512]{1,0:T(8,128)(2,1)S(1)} collective-permute-done((bf16[512,512]{1,0:T(8,128)(2,1)S(1)}, bf16[512,512]{1,0:T(8,128)(2,1)S(1)}, u32[]{:S(2)}, u32[]{:S(2)}) %collective-permute-start.32) | collective-permute-done | bytes 524320 | tf_op jit(solution)/shard_map/ppermute | solution.py:370
  106.1 1.5 %node_update.3.own = bf16[512,512]{1,0:T(8,128)(2,1)S(1)} custom-call(bf16[1024,512]{1,0:T(8,128)(2,1)S(1)} %get-tuple-element.95.nodes.refs_0_, f32[8,512]{1,0:T(8,128)S(1)} %get-tuple-element.74.refs_4_.refs_1_.refs_17_, bf16[2,512]{1,0:T(2,128)(2,1)S(1)} %copy-done.10, bf16[512,512]{1,0:T(8,128)(2,1)S(1)} %core_sum.3.refs_3_, ...), custom_call_target="tpu_custom_call" | custom-call | tf_op jit(solution)/shard_map/node_update/pallas_call | solution.py:75
  107.7 1.9 %collective-permute-done.35.other = bf16[512,512]{1,0:T(8,128)(2,1)S(1)} collective-permute-done((bf16[512,512]{1,0:T(8,128)(2,1)S(1)}, bf16[512,512]{1,0:T(8,128)(2,1)S(1)}, u32[]{:S(2)}, u32[]{:S(2)}) %collective-permute-start.35) | collective-permute-done | bytes 524320 | tf_op jit(solution)/shard_map/ppermute | solution.py:367
  109.6 1.1 nodes_out.1
  (100 shorter events, 13.4 us)
Async XLA Ops:
  2.7 18.3 %collective-permute-start.3 = (bf16[128,2176]{1,0:T(8,128)(2,1)}, bf16[128,2176]{1,0:T(8,128)(2,1)S(1)}, u32[]{:S(2)}, u32[]{:S(2)}) collective-permute-start(bf16[128,2176]{1,0:T(8,128)(2,1)} %first_weights.1.refs_9_.refs_15_), channel_id=1, source_target_pairs={{0,2},{1,3},{2,0},{3,1},{4,6},{5,7},{6,4},{7,5},{8,10},{9,11},{10,... | collective-permute-start | bytes 1671176 | tf_op jit(solution)/shard_map/ppermute | solution.py:370
  5.7 16.5 %collective-permute-start.6 = (bf16[128,2176]{1,0:T(8,128)(2,1)}, bf16[128,2176]{1,0:T(8,128)(2,1)}, u32[]{:S(2)}, u32[]{:S(2)}) collective-permute-start(bf16[128,2176]{1,0:T(8,128)(2,1)} %first_weights.1.refs_9_.refs_15_), channel_id=1, source_target_pairs={{0,1},{1,0},{2,3},{3,2},{4,5},{5,4},{6,7},{7,6},{8,9},{9,8},{10,11... | collective-permute-start | bytes 1671176 | tf_op jit(solution)/shard_map/ppermute | solution.py:367
  7.8 13.2 %collective-permute-start.2 = (bf16[128,512]{1,0:T(8,128)(2,1)}, bf16[128,512]{1,0:T(8,128)(2,1)}, u32[]{:S(2)}, u32[]{:S(2)}) collective-permute-start(bf16[128,512]{1,0:T(8,128)(2,1)} %get-tuple-element.64), channel_id=1, source_target_pairs={{0,12},{4,0},{8,4},{12,8},{1,13},{5,1},{9,5},{13,9},{2,14},{6,2},{... | collective-permute-start | bytes 393224 | tf_op jit(solution)/shard_map/ppermute | solution.py:373
  11.4 9.6 %collective-permute-start = (bf16[128,512]{1,0:T(8,128)(2,1)}, bf16[128,512]{1,0:T(8,128)(2,1)}, u32[]{:S(2)}, u32[]{:S(2)}) collective-permute-start(bf16[128,512]{1,0:T(8,128)(2,1)} %get-tuple-element.69), channel_id=1, source_target_pairs={{0,4},{4,8},{8,12},{12,0},{1,5},{5,9},{9,13},{13,1},{2,6},{6,10},{... | collective-permute-start | bytes 393224 | tf_op jit(solution)/shard_map/ppermute | solution.py:373
  11.4 9.6 %collective-permute-start.1 = (bf16[64,512]{1,0:T(8,128)(2,1)}, bf16[64,512]{1,0:T(8,128)(2,1)S(1)}, u32[]{:S(2)}, u32[]{:S(2)}) collective-permute-start(bf16[64,512]{1,0:T(8,128)(2,1)} %get-tuple-element.70), channel_id=1, source_target_pairs={{0,8},{4,12},{8,0},{12,4},{1,9},{5,13},{9,1},{13,5},{2,10},{6,14},... | collective-permute-start | bytes 196616 | tf_op jit(solution)/shard_map/ppermute | solution.py:373
  21.0 4.9 %collective-permute-start.7 = (bf16[128,2176]{1,0:T(8,128)(2,1)S(1)}, bf16[128,2176]{1,0:T(8,128)(2,1)S(1)}, u32[]{:S(2)}, u32[]{:S(2)}) collective-permute-start(bf16[128,2176]{1,0:T(8,128)(2,1)S(1)} %collective-permute-done.3.refs_11_.refs_17_), channel_id=1, source_target_pairs={{0,1},{1,0},{2,3},{3,2},{4,5},{5,4},{6,7},{7,6},{8,9},{9,8},{10,11... | collective-permute-start | bytes 1671176 | tf_op jit(solution)/shard_map/ppermute | solution.py:367
  21.0 3.3 %collective-permute-start.4 = (bf16[128,512]{1,0:T(8,128)(2,1)}, bf16[128,512]{1,0:T(8,128)(2,1)S(1)}, u32[]{:S(2)}, u32[]{:S(2)}) collective-permute-start(bf16[128,512]{1,0:T(8,128)(2,1)} %collective-permute-done.refs_5_.refs_9_), channel_id=1, source_target_pairs={{0,1},{1,0},{2,3},{3,2},{4,5},{5,4},{6,7},{7,6},{8,9},{9,8},{10,11... | collective-permute-start | bytes 393224 | tf_op jit(solution)/shard_map/ppermute | solution.py:367
  21.5 3.6 %collective-permute-start.5 = (bf16[128,512]{1,0:T(8,128)(2,1)}, bf16[128,512]{1,0:T(8,128)(2,1)S(1)}, u32[]{:S(2)}, u32[]{:S(2)}) collective-permute-start(bf16[128,512]{1,0:T(8,128)(2,1)} %collective-permute-done.2.refs_7_.refs_13_), channel_id=1, source_target_pairs={{0,1},{1,0},{2,3},{3,2},{4,5},{5,4},{6,7},{7,6},{8,9},{9,8},{10,11... | collective-permute-start | bytes 393224 | tf_op jit(solution)/shard_map/ppermute | solution.py:367
  21.6 15.0 %collective-permute-start.11 = (bf16[128,1536]{1,0:T(8,128)(2,1)S(1)}, bf16[128,1536]{1,0:T(8,128)(2,1)S(1)}, u32[]{:S(2)}, u32[]{:S(2)}) collective-permute-start(bf16[128,1536]{1,0:T(8,128)(2,1)S(1)} %copy-done.3), channel_id=1, source_target_pairs={{0,2},{1,3},{2,0},{3,1},{4,6},{5,7},{6,4},{7,5},{8,10},{9,11},{10,... | collective-permute-start | bytes 1179656 | tf_op jit(solution)/shard_map/ppermute | solution.py:370
  22.2 9.8 %collective-permute-start.10 = (bf16[96,640]{1,0:T(8,128)(2,1)S(1)}, bf16[96,640]{1,0:T(8,128)(2,1)S(1)}, u32[]{:S(2)}, u32[]{:S(2)}) collective-permute-start(bf16[96,640]{1,0:T(8,128)(2,1)S(1)} %coarse_pack.1.refs_5_), channel_id=1, source_target_pairs={{0,12},{4,0},{8,4},{12,8},{1,13},{5,1},{9,5},{13,9},{2,14},{6,2},{... | collective-permute-start | bytes 368648 | tf_op jit(solution)/shard_map/ppermute | solution.py:373
  24.4 8.0 %collective-permute-start.8 = (bf16[96,640]{1,0:T(8,128)(2,1)S(1)}, bf16[96,640]{1,0:T(8,128)(2,1)S(1)}, u32[]{:S(2)}, u32[]{:S(2)}) collective-permute-start(bf16[96,640]{1,0:T(8,128)(2,1)S(1)} %coarse_pack.1.refs_5_), channel_id=1, source_target_pairs={{0,4},{4,8},{8,12},{12,0},{1,5},{5,9},{9,13},{13,1},{2,6},{6,10},{... | collective-permute-start | bytes 368648 | tf_op jit(solution)/shard_map/ppermute | solution.py:373
  25.1 11.5 %collective-permute-start.9 = (bf16[96,640]{1,0:T(8,128)(2,1)S(1)}, bf16[96,640]{1,0:T(8,128)(2,1)S(1)}, u32[]{:S(2)}, u32[]{:S(2)}) collective-permute-start(bf16[96,640]{1,0:T(8,128)(2,1)S(1)} %coarse_pack.1.refs_5_), channel_id=1, source_target_pairs={{0,8},{4,12},{8,0},{12,4},{1,9},{5,13},{9,1},{13,5},{2,10},{6,14},... | collective-permute-start | bytes 368648 | tf_op jit(solution)/shard_map/ppermute | solution.py:373
  36.6 7.1 %collective-permute-start.13 = (bf16[128,512]{1,0:T(8,128)(2,1)S(1)}, bf16[128,512]{1,0:T(8,128)(2,1)S(1)}, u32[]{:S(2)}, u32[]{:S(2)}) collective-permute-start(bf16[128,512]{1,0:T(8,128)(2,1)S(1)} %copy-done.5), channel_id=1, source_target_pairs={{0,2},{1,3},{2,0},{3,1},{4,6},{5,7},{6,4},{7,5},{8,10},{9,11},{10,... | collective-permute-start | bytes 393224 | tf_op jit(solution)/shard_map/ppermute | solution.py:370
  43.8 2.0 %collective-permute-start.14 = (bf16[512,512]{1,0:T(8,128)(2,1)S(1)}, bf16[512,512]{1,0:T(8,128)(2,1)S(1)}, u32[]{:S(2)}, u32[]{:S(2)}) collective-permute-start(bf16[512,512]{1,0:T(8,128)(2,1)S(1)} %get-tuple-element.94), channel_id=1, source_target_pairs={{0,1},{1,0},{2,3},{3,2},{4,5},{5,4},{6,7},{7,6},{8,9},{9,8},{10,11... | collective-permute-start | bytes 1572872 | tf_op jit(solution)/shard_map/ppermute | solution.py:367
  45.9 14.1 %collective-permute-start.15 = (bf16[512,512]{1,0:T(8,128)(2,1)S(1)}, bf16[512,512]{1,0:T(8,128)(2,1)S(1)}, u32[]{:S(2)}, u32[]{:S(2)}) collective-permute-start(bf16[512,512]{1,0:T(8,128)(2,1)S(1)} %core_sum.2.refs_3_), channel_id=1, source_target_pairs={{0,2},{1,3},{2,0},{3,1},{4,6},{5,7},{6,4},{7,5},{8,10},{9,11},{10,... | collective-permute-start | bytes 1572872 | tf_op jit(solution)/shard_map/ppermute | solution.py:370
  46.5 1.7 %collective-permute-start.16 = (bf16[128,1536]{1,0:T(8,128)(2,1)S(1)}, bf16[128,1536]{1,0:T(8,128)(2,1)S(1)}, u32[]{:S(2)}, u32[]{:S(2)}) collective-permute-start(bf16[128,1536]{1,0:T(8,128)(2,1)S(1)} %copy-done.3), channel_id=1, source_target_pairs={{0,1},{1,0},{2,3},{3,2},{4,5},{5,4},{6,7},{7,6},{8,9},{9,8},{10,11... | collective-permute-start | bytes 1179656 | tf_op jit(solution)/shard_map/ppermute | solution.py:367
  46.5 2.3 %collective-permute-start.17 = (bf16[128,1536]{1,0:T(8,128)(2,1)S(1)}, bf16[128,1536]{1,0:T(8,128)(2,1)S(1)}, u32[]{:S(2)}, u32[]{:S(2)}) collective-permute-start(bf16[128,1536]{1,0:T(8,128)(2,1)S(1)} %collective-permute-done.11.refs_7_), channel_id=1, source_target_pairs={{0,1},{1,0},{2,3},{3,2},{4,5},{5,4},{6,7},{7,6},{8,9},{9,8},{10,11... | collective-permute-start | bytes 1179656 | tf_op jit(solution)/shard_map/ppermute | solution.py:367
  61.4 2.0 %collective-permute-start.18 = (bf16[512,512]{1,0:T(8,128)(2,1)S(1)}, bf16[512,512]{1,0:T(8,128)(2,1)S(1)}, u32[]{:S(2)}, u32[]{:S(2)}) collective-permute-start(bf16[512,512]{1,0:T(8,128)(2,1)S(1)} %node_update.2.refs_0_), channel_id=1, source_target_pairs={{0,1},{1,0},{2,3},{3,2},{4,5},{5,4},{6,7},{7,6},{8,9},{9,8},{10,11... | collective-permute-start | bytes 1572872 | tf_op jit(solution)/shard_map/ppermute | solution.py:367
  61.5 15.7 %collective-permute-start.22 = (bf16[128,2304]{1,0:T(8,128)(2,1)S(1)}, bf16[128,2304]{1,0:T(8,128)(2,1)S(1)}, u32[]{:S(2)}, u32[]{:S(2)}) collective-permute-start(bf16[128,2304]{1,0:T(8,128)(2,1)S(1)} %copy-done.1), channel_id=1, source_target_pairs={{0,2},{1,3},{2,0},{3,1},{4,6},{5,7},{6,4},{7,5},{8,10},{9,11},{10,... | collective-permute-start | bytes 1769480 | tf_op jit(solution)/shard_map/ppermute | solution.py:370
  62.1 17.6 %collective-permute-start.26 = (bf16[128,2304]{1,0:T(8,128)(2,1)S(1)}, bf16[128,2304]{1,0:T(8,128)(2,1)S(1)}, u32[]{:S(2)}, u32[]{:S(2)}) collective-permute-start(bf16[128,2304]{1,0:T(8,128)(2,1)S(1)} %copy-done.1), channel_id=1, source_target_pairs={{0,1},{1,0},{2,3},{3,2},{4,5},{5,4},{6,7},{7,6},{8,9},{9,8},{10,11... | collective-permute-start | bytes 1769480 | tf_op jit(solution)/shard_map/ppermute | solution.py:367
  63.9 13.3 %collective-permute-start.19 = (bf16[128,512]{1,0:T(8,128)(2,1)S(1)}, bf16[128,512]{1,0:T(8,128)(2,1)S(1)}, u32[]{:S(2)}, u32[]{:S(2)}) collective-permute-start(bf16[128,512]{1,0:T(8,128)(2,1)S(1)} %get-tuple-element.98), channel_id=1, source_target_pairs={{0,4},{4,8},{8,12},{12,0},{1,5},{5,9},{9,13},{13,1},{2,6},{6,10},{... | collective-permute-start | bytes 393224 | tf_op jit(solution)/shard_map/ppermute | solution.py:373
  64.0 13.2 %collective-permute-start.21 = (bf16[128,512]{1,0:T(8,128)(2,1)S(1)}, bf16[128,512]{1,0:T(8,128)(2,1)S(1)}, u32[]{:S(2)}, u32[]{:S(2)}) collective-permute-start(bf16[128,512]{1,0:T(8,128)(2,1)S(1)} %get-tuple-element.100), channel_id=1, source_target_pairs={{0,12},{4,0},{8,4},{12,8},{1,13},{5,1},{9,5},{13,9},{2,14},{6,2},{... | collective-permute-start | bytes 393224 | tf_op jit(solution)/shard_map/ppermute | solution.py:373
  67.8 9.4 %collective-permute-start.20 = (bf16[64,512]{1,0:T(8,128)(2,1)S(1)}, bf16[64,512]{1,0:T(8,128)(2,1)S(1)}, u32[]{:S(2)}, u32[]{:S(2)}) collective-permute-start(bf16[64,512]{1,0:T(8,128)(2,1)S(1)} %get-tuple-element.99), channel_id=1, source_target_pairs={{0,8},{4,12},{8,0},{12,4},{1,9},{5,13},{9,1},{13,5},{2,10},{6,14},... | collective-permute-start | bytes 196616 | tf_op jit(solution)/shard_map/ppermute | solution.py:373
  77.2 3.6 %collective-permute-start.28 = (bf16[128,2304]{1,0:T(8,128)(2,1)S(1)}, bf16[128,2304]{1,0:T(8,128)(2,1)S(1)}, u32[]{:S(2)}, u32[]{:S(2)}) collective-permute-start(bf16[128,2304]{1,0:T(8,128)(2,1)S(1)} %collective-permute-done.22.refs_14_.refs_17_.refs_9_), channel_id=1, source_target_pairs={{0,1},{1,0},{2,3},{3,2},{4,5},{5,4},{6,7},{7,6},{8,9},{9,8},{10,11... | collective-permute-start | bytes 1769480 | tf_op jit(solution)/shard_map/ppermute | solution.py:367
  77.3 2.2 %collective-permute-start.25 = (bf16[128,512]{1,0:T(8,128)(2,1)S(1)}, bf16[128,512]{1,0:T(8,128)(2,1)S(1)}, u32[]{:S(2)}, u32[]{:S(2)}) collective-permute-start(bf16[128,512]{1,0:T(8,128)(2,1)S(1)} %copy-done.5), channel_id=1, source_target_pairs={{0,1},{1,0},{2,3},{3,2},{4,5},{5,4},{6,7},{7,6},{8,9},{9,8},{10,11... | collective-permute-start | bytes 393224 | tf_op jit(solution)/shard_map/ppermute | solution.py:367
  77.8 2.4 %collective-permute-start.27 = (bf16[128,512]{1,0:T(8,128)(2,1)S(1)}, bf16[128,512]{1,0:T(8,128)(2,1)S(1)}, u32[]{:S(2)}, u32[]{:S(2)}) collective-permute-start(bf16[128,512]{1,0:T(8,128)(2,1)S(1)} %collective-permute-done.13.refs_13_.refs_16_), channel_id=1, source_target_pairs={{0,1},{1,0},{2,3},{3,2},{4,5},{5,4},{6,7},{7,6},{8,9},{9,8},{10,11... | collective-permute-start | bytes 393224 | tf_op jit(solution)/shard_map/ppermute | solution.py:367
  77.9 2.4 %collective-permute-start.23 = (bf16[128,512]{1,0:T(8,128)(2,1)S(1)}, bf16[128,512]{1,0:T(8,128)(2,1)S(1)}, u32[]{:S(2)}, u32[]{:S(2)}) collective-permute-start(bf16[128,512]{1,0:T(8,128)(2,1)S(1)} %collective-permute-done.19.refs_5_.refs_6_), channel_id=1, source_target_pairs={{0,1},{1,0},{2,3},{3,2},{4,5},{5,4},{6,7},{7,6},{8,9},{9,8},{10,11... | collective-permute-start | bytes 393224 | tf_op jit(solution)/shard_map/ppermute | solution.py:367
  79.6 7.2 %collective-permute-start.29 = (bf16[128,768]{1,0:T(8,128)(2,1)S(1)}, bf16[128,768]{1,0:T(8,128)(2,1)S(1)}, u32[]{:S(2)}, u32[]{:S(2)}) collective-permute-start(bf16[128,768]{1,0:T(8,128)(2,1)S(1)} %copy-done.4), channel_id=1, source_target_pairs={{0,2},{1,3},{2,0},{3,1},{4,6},{5,7},{6,4},{7,5},{8,10},{9,11},{10,... | collective-permute-start | bytes 589832 | tf_op jit(solution)/shard_map/ppermute | solution.py:370
  80.2 6.6 %collective-permute-start.30 = (bf16[64,512]{1,0:T(8,128)(2,1)S(1)}, bf16[64,512]{1,0:T(8,128)(2,1)S(1)}, u32[]{:S(2)}, u32[]{:S(2)}) collective-permute-start(bf16[64,512]{1,0:T(8,128)(2,1)S(1)} %collective-permute-done.20.refs_8_), channel_id=1, source_target_pairs={{0,1},{1,0},{2,3},{3,2},{4,5},{5,4},{6,7},{7,6},{8,9},{9,8},{10,11... | collective-permute-start | bytes 196616 | tf_op jit(solution)/shard_map/ppermute | solution.py:367
  90.0 2.0 %collective-permute-start.31 = (bf16[512,512]{1,0:T(8,128)(2,1)S(1)}, bf16[512,512]{1,0:T(8,128)(2,1)S(1)}, u32[]{:S(2)}, u32[]{:S(2)}) collective-permute-start(bf16[512,512]{1,0:T(8,128)(2,1)S(1)} %get-tuple-element.113), channel_id=1, source_target_pairs={{0,1},{1,0},{2,3},{3,2},{4,5},{5,4},{6,7},{7,6},{8,9},{9,8},{10,11... | collective-permute-start | bytes 1572872 | tf_op jit(solution)/shard_map/ppermute | solution.py:367
  92.1 14.0 %collective-permute-start.32 = (bf16[512,512]{1,0:T(8,128)(2,1)S(1)}, bf16[512,512]{1,0:T(8,128)(2,1)S(1)}, u32[]{:S(2)}, u32[]{:S(2)}) collective-permute-start(bf16[512,512]{1,0:T(8,128)(2,1)S(1)} %core_sum.3.refs_3_), channel_id=1, source_target_pairs={{0,2},{1,3},{2,0},{3,1},{4,6},{5,7},{6,4},{7,5},{8,10},{9,11},{10,... | collective-permute-start | bytes 1572872 | tf_op jit(solution)/shard_map/ppermute | solution.py:370
  107.6 2.0 %collective-permute-start.35 = (bf16[512,512]{1,0:T(8,128)(2,1)S(1)}, bf16[512,512]{1,0:T(8,128)(2,1)S(1)}, u32[]{:S(2)}, u32[]{:S(2)}) collective-permute-start(bf16[512,512]{1,0:T(8,128)(2,1)S(1)} %node_update.3.own), channel_id=1, source_target_pairs={{0,1},{1,0},{2,3},{3,2},{4,5},{5,4},{6,7},{7,6},{8,9},{9,8},{10,11... | collective-permute-start | bytes 1572872 | tf_op jit(solution)/shard_map/ppermute | solution.py:367
  (21 other events, 179.3 us)

commit v3 on v2

--- a/solution.py
+++ b/solution.py
@@ -10,7 +10,8 @@
 STEPS = 2
 STRIDE = 8
 LANES = 128
-PART = 768
+PART = 256
+COARSE_FLOPS = (0, 0)
 DIGIT = 64
 VMEM_BYTES = 20 * 1024 * 1024
 
@@ -98,61 +99,80 @@
     out[pl.ds(pl.multiple_of((1 - core) * nh, nh), nh), :] = other[...]
 
 
-def join_kernel(own, other, out):
-    join_halves(out, own, other)
-
-
-def add_kernel(own, arrived, out):
-    out[...] = (own[...] + arrived[...].astype(jnp.float32)).astype(out.dtype)
+def join_kernel(*refs):
+    out = refs[-1]
+    core, at = core_index(), 0
+    for own, other in zip(refs[:-1:2], refs[1:-1:2]):
+        rows = own.shape[0]
+        for who, ref in ((core, own), (1 - core, other)):
+            spot = pl.multiple_of(who * (out.shape[0] // 2) + at, rows)
+            out[pl.ds(spot, rows), :] = ref[...]
+        at += rows
+
+
+def add_kernel(own, arrived, *outs):
+    at = 0
+    for out in outs:
+        rows = pl.ds(at, out.shape[0])
+        out[...] = (own[rows, :] + arrived[rows, :].astype(jnp.float32)).astype(out.dtype)
+        at += out.shape[0]
+
+
+def index_digits(ref, lanes):
+    index = ref[...]
+    high = lax.shift_right_logical(index, DIGIT.bit_length() - 1)
+    rows = jnp.concatenate([high, index & (DIGIT - 1)]).astype(jnp.float32)
+    if lanes == index.shape[1]:
+        return rows
+    return jnp.concatenate([rows, jnp.zeros((2, lanes - index.shape[1]), jnp.float32)], axis=1)
+
+
+def to_column(ref):
+    count = ref.shape[1]
+    rows = jnp.concatenate([index_digits(ref, count), jnp.zeros((6, count), jnp.float32)])
+    unit = lax.broadcasted_iota(jnp.int32, (count, count), 0)
+    unit = unit == lax.broadcasted_iota(jnp.int32, (count, count), 1)
+    digits = dot_t(unit.astype(jnp.bfloat16), rows.astype(jnp.bfloat16))
+    return (DIGIT * digits[:, 0:1] + digits[:, 1:2]).astype(jnp.int32)
 
 
 def halo_kernel(first, *refs):
     if first:
-        nodes, halo, to_prev, to_next, to_far, coarse = refs
+        nodes, halo, edges, send, recv, *outs, coarse, block = refs
+        count, width = edges.shape
+        block[0:count, :] = edges[...]
+        digits = [index_digits(ref, width) for ref in (send, recv)]
+        digits.append(jnp.zeros((16 - 4, width), jnp.float32))
+        block[count : count + 16, :] = jnp.concatenate(digits).astype(jnp.bfloat16)
     else:
-        own, other, halo, to_prev, to_next, to_far, coarse, nodes = refs
+        own, other, halo, *outs, coarse, nodes = refs
         join_halves(nodes, own, other)
+    to_prev, to_next, to_far = outs
     core = core_index()
     count = nodes.shape[0]
-    hr, cp = halo.shape[0] // 2, coarse.shape[0]
+    hr, cp = halo.shape[1] // 2, coarse.shape[0]
     hh, ch = hr // 2, cp // 2
-    prev = halo[pl.ds(pl.multiple_of(core * hh, hh), hh), :]
-    nxt = halo[pl.ds(pl.multiple_of(hr + core * hh, hh), hh), :]
+    index = to_column(halo)
+    mine = [jnp.where(core == 0, x[:hh], x[hh:]) for x in (index[:hr], index[hr:])]
     table = nodes[...]
-    rows = dot(pick_rows(jnp.concatenate([prev, nxt], axis=0), count), table).astype(jnp.bfloat16)
+    rows = dot(pick_rows(jnp.concatenate(mine), count), table).astype(jnp.bfloat16)
     every = STRIDE * lax.broadcasted_iota(jnp.int32, (cp, 1), 0)
     coarse[...] = dot(pick_rows(every, count), table).astype(jnp.bfloat16)
     mine = coarse[pl.ds(pl.multiple_of(core * ch, ch), ch), :]
     to_prev[pl.ds(0, hh), :] = rows[:hh]
-    to_prev[pl.ds(hh, ch), :] = mine
     to_next[pl.ds(0, hh), :] = rows[hh:]
-    to_next[pl.ds(hh, ch), :] = mine
-    to_far[...] = mine
-
-
-def gather_kernel(tile, nodes, send, recv, sent, received):
-    count = nodes.shape[0]
-
-    def body(t, carry):
-        rows = pl.ds(pl.multiple_of(t * tile, tile), tile)
-        table = nodes[...]
-        sent[rows, :] = dot(pick_rows(send[rows, :], count), table).astype(jnp.bfloat16)
-        safe = jnp.minimum(recv[rows, :], count - 1)
-        received[rows, :] = dot(pick_rows(safe, count), table).astype(jnp.bfloat16)
-        return carry
-
-    loop(send.shape[0] // tile, body)
-
-
-def bias_rows_of(bias_ref, line, n_groups):
-    per = bias_ref.shape[1] // n_groups
-    return [bias_ref[line : line + 1, g * per : (g + 1) * per] for g in range(n_groups)]
-
-
-def weight_kernel(plans, n_in, *refs):
-    source, outs, sems = refs[:n_in], refs[n_in:-1], refs[-1]
+    for out, skip in ((to_prev, hh), (to_next, hh), (to_far, 0)):
+        out[pl.ds(skip, ch), :] = mine
+        if first:
+            out[pl.ds(skip + ch, block.shape[0]), :] = block[...]
+
+
+def prepare_kernel(plans, cut, *refs):
+    source, (edge_b1, node_b1, nodes, halo, edges, send, recv) = refs[:4], refs[4:11]
+    packs, rest = refs[11 : 11 + len(plans)], refs[11 + len(plans) :]
+    *rest, sems = rest
     copies = []
-    for plan, out in zip(plans, outs):
+    for plan, out in zip(plans, packs):
         at = 0
         for which, layer, first, last in plan:
             part = source[which].at[layer, :, first:last]
@@ -161,47 +181,50 @@
             at += last - first
     for copy in copies:
         copy.start()
+    hidden = edge_b1.shape[1]
+    rows = [edge_b1[...].astype(jnp.float32), node_b1[...].astype(jnp.float32)]
+    rows.append(jnp.zeros((16 - 2 * STEPS, hidden), jnp.float32))
+    at = packs[0].shape[1] - LANES
+    packs[0][0:16, at : at + hidden] = jnp.concatenate(rows).astype(jnp.bfloat16)
+    if cut:
+        part, *rest = rest
+    halo_kernel(True, nodes, halo, edges, send, recv, *rest)
     for copy in copies:
         copy.wait()
-
-
-def first_kernel(edge_w1, edge_w2, edge_b1, node_b1, out, sems):
-    k, width, hidden = edge_w1.shape[2], edge_w2.shape[2], edge_b1.shape[1]
-    copies = [
-        pltpu.make_async_copy(edge_w1.at[0], out.at[:, 0:k], sems.at[0]),
-        pltpu.make_async_copy(edge_w2.at[0], out.at[:, k : k + width], sems.at[1]),
-    ]
-    for copy in copies:
-        copy.start()
-    rows = [edge_b1[...].astype(jnp.float32), node_b1[...].astype(jnp.float32)]
-    rows.append(jnp.zeros((16 - 2 * STEPS, hidden), jnp.float32))
-    out[0:16, k + width : k + width + hidden] = jnp.concatenate(rows).astype(jnp.bfloat16)
-    for copy in copies:
-        copy.wait()
-
-
-def coarse_pack_kernel(edges, send, recv, pack):
-    width = edges.shape[1]
-    pack[:, :width] = edges[...]
-    lane = lax.broadcasted_iota(jnp.int32, (edges.shape[0], LANES), 1)
-    digits = jnp.zeros(lane.shape, jnp.int32)
-    for j, ref in enumerate((send, recv)):
-        index = ref[...]
-        high = lax.shift_right_logical(index, DIGIT.bit_length() - 1)
-        low = index & (DIGIT - 1)
-        digits = jnp.where(lane == 2 * j, high, jnp.where(lane == 2 * j + 1, low, digits))
-    pack[:, width:] = digits.astype(jnp.float32).astype(jnp.bfloat16)
+    if cut:
+        last = packs[-1]
+        group = lax.axis_index("groups")
+        part[...] = jnp.where(group == 0, last[:, :cut], last[:, cut:])
+
+
+def gather_kernel(tile, nodes, send, recv, sent, received):
+    count = nodes.shape[0]
+
+    def body(t, carry):
+        rows = pl.ds(pl.multiple_of(t * tile, tile), tile)
+        table = nodes[...]
+        sent[rows, :] = dot(pick_rows(send[rows, :], count), table).astype(jnp.bfloat16)
+        safe = jnp.minimum(recv[rows, :], count - 1)
+        received[rows, :] = dot(pick_rows(safe, count), table).astype(jnp.bfloat16)
+        return carry
+
+    loop(send.shape[0] // tile, body)
+
+
+def bias_rows_of(bias_ref, line, n_groups):
+    per = bias_ref.shape[1] // n_groups
+    return [bias_ref[line : line + 1, g * per : (g + 1) * per] for g in range(n_groups)]
 
 
 def fine_kernel(tile, sizes, spots, layer, *refs):
     count, hr, cp, parts, cores = sizes
     it = iter(refs)
-    fine, sent, received, send, gain_ref = (next(it) for _ in range(5))
+    fine, sent, received, send, recv_row, gain_ref = (next(it) for _ in range(6))
     prev, nxt = ((next(it), next(it)) for _ in range(2))
     groups = take_groups(it, spots, cores)
     bias_in = None if layer == 0 else next(it)
     new_fine = next(it)
-    bias_out = next(it) if layer == 0 else None
+    bias_out, aggs = (next(it), [next(it), next(it)]) if layer == 0 else (None, None)
     halo_tab = next(it)
 
     core = core_index()
@@ -233,6 +256,10 @@
         return carry
 
     loop(fine.shape[0] // tile, body)
+    if layer == 0:
+        for out, half in zip(aggs, (1 - core, core)):
+            place = place_in_half((count // 2, recv_row[...] - half * (count // 2)))
+            sum_rows(out, 0, [place], [new_fine[...]])
 
 
 def coarse_target(state, width, me, cp):
@@ -254,14 +281,31 @@
         out[pl.ds(spot, block), :] = total.astype(out.dtype)
 
 
+def place_in_half(row):
+    count, row = row
+    group, rest = lax.shift_right_logical(row, 3), row & (STRIDE - 1)
+    fine_rows = count - count // STRIDE
+    place = jnp.where(rest == 0, fine_rows + group, (STRIDE - 1) * group + rest - 1)
+    return jnp.where((row >= 0) & (row < count), place, -1)
+
+
+def sum_rows(out, first, places, latents):
+    total = None
+    for place, latent in zip(places, latents):
+        rows = lax.broadcasted_iota(jnp.int32, (out.shape[0], place.shape[1]), 0) + first
+        part = dot((rows == place).astype(jnp.bfloat16), latent)
+        total = part if total is None else total + part
+    out[...] = total.astype(out.dtype)
+
+
 def coarse_kernel(tile, sizes, spots, layer, *refs):
     count, hr, cp, parts, cores = sizes
     it = iter(refs)
     new_fine, recv_row, coarse_own, gain_ref, bias_ref = (next(it) for _ in range(5))
-    states = [next(it) for _ in range(parts if layer == 0 else 1)]
+    given = next(it)
     arrived = [(next(it), next(it)) for _ in range(parts - 1)]
     groups = take_groups(it, spots, cores)
-    state, agg_other, coarse_tab = (next(it) for _ in range(3))
+    state, *aggs, coarse_tab = it
 
     core, me = core_index(), lax.axis_index("mesh")
     width = gain_ref.shape[-1]
@@ -274,10 +318,21 @@
         for who, ref in zip((core, 1 - core), pair):
             spot = pl.multiple_of(owner * cp + who * ch, ch)
             coarse_tab[pl.ds(spot, ch), :] = ref[pl.ds(skip, ch), 0:width]
-    at = 0
-    for one in states:
-        state[pl.ds(at, one.shape[0]), :] = one[...]
-        at += one.shape[0]
+    if layer == 0:
+        per = given.shape[0] - 16
+        lane = lax.broadcasted_iota(jnp.int32, (per, width), 1)
+        unit = (lane == lax.broadcasted_iota(jnp.int32, (per, width), 0)).astype(jnp.bfloat16)
+        blocks = [(given, 0)]
+        for i, (ref, _) in enumerate(arrived):
+            blocks.append((ref, ch + (hh if i in (0, parts - 2) else 0)))
+        for i, (ref, skip) in enumerate(blocks):
+            rows = pl.ds(i * per, per)
+            state[rows, :width] = ref[pl.ds(skip, per), :]
+            digits = ref[pl.ds(skip + per, 16), :].astype(jnp.float32)
+            digits = jnp.concatenate([digits, jnp.zeros((LANES - 16, width), jnp.float32)])
+            state[rows, width:] = dot_t(unit, digits.astype(jnp.bfloat16)).astype(jnp.bfloat16)
+    else:
+        state[...] = given[...]
 
     biases = bias_rows_of(bias_ref, layer, len(groups))
     gain = gain_ref[layer : layer + 1, :].astype(jnp.float32)
@@ -297,7 +352,13 @@
 
     loop(state.shape[0] // tile, body)
     target = coarse_target(state, width, me, cp)
-    row_sums((1 - core) * nh, agg_other, new_fine, recv_row, state, target)
+    if layer > 0:
+        row_sums((1 - core) * nh, aggs[0], new_fine, recv_row, state, target)
+        return
+    latents = [new_fine[...], state[:, :width]]
+    for out, half in zip(aggs, (1 - core, core)):
+        places = [place_in_half((nh, at - half * nh)) for at in (recv_row[...], target)]
+        sum_rows(out, nh - ch, places, latents)
 
 
 def own_kernel(cp, new_fine, recv_row, state, agg_own):
@@ -307,23 +368,42 @@
     row_sums(core * nh, agg_own, new_fine, recv_row, state, target)
 
 
-def node_kernel(tile, layer, cores, spots, n_sums, *refs):
+def node_kernel(tile, layer, cores, spots, n_sums, cut, start, *refs):
     it = iter(refs)
     nodes, bias_ref, gain_ref = (next(it) for _ in range(3))
-    sums = [next(it) for _ in range(n_sums)]
-    groups = take_groups(it, spots, cores)
-    out = next(it)
+    sums = [[next(it) for _ in range(n)] for n in n_sums]
+    if cut:
+        groups = take_groups(it, spots, 2)
+        parts = [(next(it), next(it)) for _ in range(2)]
+    else:
+        groups = take_groups(it, spots, cores)
+    out, agg_ref, *far = it
+    if cut:
+        group = lax.axis_index("groups")
+        for ref, (mine, other) in zip(far, parts):
+            ref[:, pl.ds(pl.multiple_of(group * cut, LANES), cut)] = mine[...]
+            ref[:, pl.ds(pl.multiple_of((1 - group) * cut, LANES), cut)] = other[...]
+        groups.append([[[(ref, at, to) for _, at, to in pieces] for pieces in spots] for ref in far])
     nh = out.shape[0]
+    agg = []
+    for terms in sums:
+        total = terms[0][...].astype(jnp.float32)
+        for more in terms[1:]:
+            total = total + more[...].astype(jnp.float32)
+        agg.append(total.astype(jnp.bfloat16))
+    if len(agg) > 1:
+        row = lax.broadcasted_iota(jnp.int32, (nh, 1), 0)
+        order = pick_rows(place_in_half((nh, row)), nh)
+        agg = [dot(order, jnp.concatenate(agg)).astype(jnp.bfloat16)]
+    agg_ref[...] = agg[0]
     biases = bias_rows_of(bias_ref, STEPS + layer, len(groups))
     gain = gain_ref[layer : layer + 1, :].astype(jnp.float32)
     core = core_index()
+    half = nodes.shape[0] // 2
     for t in range(nh // tile):
         rows = pl.ds(t * tile, tile)
-        old = nodes[pl.ds(pl.multiple_of(core * nh + t * tile, tile), tile), :]
-        agg = sums[0][rows, :].astype(jnp.float32)
-        for more in sums[1:]:
-            agg = agg + more[rows, :].astype(jnp.float32)
-        x = jnp.concatenate([old, agg.astype(jnp.bfloat16)], axis=1)
+        old = nodes[pl.ds(pl.multiple_of(core * half + start + t * tile, tile), tile), :]
+        x = jnp.concatenate([old, agg_ref[rows, :]], axis=1)
         y = mlp(x, groups, biases, gain)
         out[rows, :] = (old.astype(jnp.float32) + y).astype(jnp.bfloat16)
 
@@ -392,20 +472,11 @@
 
     k, kn = edge_w1.shape[2], node_w1.shape[2]
     w_hidden = edge_w1.shape[1]
-    first_pack = call(
-        first_kernel,
-        bf16(w_hidden, k + width + LANES),
-        [edge_w1, edge_w2, edge_b1, node_b1],
-        scratch=[pltpu.SemaphoreType.DMA((2,))],
-        memory=[pl.ANY, pl.ANY, pltpu.VMEM, pltpu.VMEM],
-        limit=3 * VMEM_BYTES,
-        name="first_weights",
-    )
     stream = ((2, 0, kn), (3, 0, width), (1, 1, width), (0, 1, k), (2, 1, kn), (3, 1, width))
     starts = [0]
     for _, _, lanes in stream:
         starts.append(starts[-1] + lanes)
-    cuts = [0, starts[2], starts[3], starts[4] + PART, starts[-1]]
+    cuts = [0, starts[2] + PART, starts[4], starts[-1]]
 
     def pieces(which):
         first, last = starts[which], starts[which + 1]
@@ -421,48 +492,50 @@
         for pack, at, to in pieces(which):
             plans[pack].append((source, layer, done, done + to - at))
             done += to - at
-    packs = call(
-        functools.partial(weight_kernel, plans, 4),
-        tuple(bf16(w_hidden, hi - lo) for lo, hi in zip(cuts, cuts[1:])),
-        [edge_w1, edge_w2, node_w1, node_w2],
+    halo_row = halo_send.reshape(1, 2 * hr)
+    own_coarse = coarse_edges.shape[0]
+    coarse_count = own_coarse * parts
+    plans = [[(0, 0, 0, k), (1, 0, 0, width)], *plans]
+    lanes = [k + width + LANES] + [hi - lo for lo, hi in zip(cuts, cuts[1:])]
+    cut = lanes[-1] // 2 if two and lax.axis_size("groups") == 2 else 0
+    block = own_coarse + 16
+    near, far = hr // 2 + cp // 2 + block, cp // 2 + block
+    shapes = [(w_hidden, n) for n in lanes] + ([(w_hidden, cut)] if cut else [])
+    shapes += [(near, width), (near, width), (far, width), (cp, width), (block, width)]
+    first_pack, *packs = call(
+        functools.partial(prepare_kernel, plans, cut),
+        tuple(bf16(*shape) for shape in shapes),
+        [edge_w1, edge_w2, node_w1, node_w2, edge_b1, node_b1, nodes, halo_row, coarse_edges]
+        + [x.reshape(1, own_coarse) for x in (coarse_send, coarse_recv)],
         scratch=[pltpu.SemaphoreType.DMA((sum(len(p) for p in plans),))],
-        memory=[pl.ANY] * 4,
+        memory=[pl.ANY] * 4 + [pltpu.VMEM] * 7,
         limit=3 * VMEM_BYTES,
-        name="later_weights",
+        name="weights_and_halo_rows",
     )
+    to_prev, to_next, to_far, coarse_own, block = packs[-5:]
+    cut_part = packs[-6] if cut else None
+    packs = packs[: len(plans) - 1]
 
     def choose(shards_of, w_in, w_out):
         used = sorted({pack for which in (w_in, w_out) for pack, _, _ in pieces(which)})
         spots = [[(used.index(p), at, to) for p, at, to in pieces(w)] for w in (w_in, w_out)]
         return [x for shard in zip(*(shards_of[p] for p in used)) for x in shard], spots
 
-    own_coarse = coarse_edges.shape[0]
-    coarse_pack = call(
-        coarse_pack_kernel,
-        bf16(own_coarse, width + LANES),
-        [coarse_edges, coarse_send.reshape(own_coarse, 1), coarse_recv.reshape(own_coarse, 1)],
-        name="coarse_pack",
-    )
-    coarse_count = own_coarse * parts
-
     send_col = fine_send.reshape(fine_count, 1)
     recv_col = fine_recv.reshape(fine_count, 1)
     recv_row = fine_recv.reshape(1, fine_count)
-    halo_col = halo_send.reshape(2 * hr, 1)
     tile = divisor(fine_count, 768)
     ctile = divisor(coarse_count, 384)
     hidden = w_hidden * cores
     sizes = (count, hr, cp, parts, cores)
     bias_rows = None
 
-    def node_rows_out(*given):
-        half = hr // 2 + cp // 2
-        first = len(given) == 1
-        outs = [bf16(half, width), bf16(half, width), bf16(cp // 2, width), bf16(cp, width)]
+    def node_rows_out(own, other):
+        near, far = hr // 2 + cp // 2, cp // 2
         return call(
-            functools.partial(halo_kernel, first),
-            tuple(outs if first else outs + [bf16(count, width)]),
-            [*given, halo_col],
+            functools.partial(halo_kernel, False),
+            (bf16(near, width), bf16(near, width), bf16(far, width), bf16(cp, width), bf16(count, width)),
+            [own, other, halo_row],
             name="halo_rows",
         )
 
@@ -484,22 +557,26 @@
     def fine_update(s, fine, sent, received, halo, weights, spots):
         outs = [bf16(fine_count, width)]
         if s == 0:
+            fine_rows = nh - cp // 2
             outs.append(jax.ShapeDtypeStruct((8, hidden), jnp.float32))
+            outs += [bf16(fine_rows, width), jax.ShapeDtypeStruct((fine_rows, width), jnp.float32)]
         return call(
             functools.partial(fine_kernel, tile, sizes, spots, s),
             tuple(outs),
-            [fine, sent, received, send_col, edge_gain] + halo + weights + ([bias_rows] if s else []),
+            [fine, sent, received, send_col, recv_row, edge_gain] + halo + weights + ([bias_rows] if s else []),
             scratch=[pltpu.VMEM((2 * hr, width), jnp.bfloat16)],
             flops=8 * fine_count * width * hidden,
             name="fine_edges",
         )
 
-    def coarse_update(s, new_fine, coarse_own, states, arrived, weights, spots):
+    def coarse_update(s, new_fine, coarse_own, state, arrived, weights, spots):
+        aggs = [bf16(nh, width)] if s else [bf16(cp // 2, width), jax.ShapeDtypeStruct((cp // 2, width), jnp.float32)]
         return call(
             functools.partial(coarse_kernel, ctile, sizes, spots, s),
-            (bf16(coarse_count, width + LANES), bf16(nh, width)),
-            [new_fine, recv_row, coarse_own, edge_gain, bias_rows] + states + arrived + weights,
+            (bf16(coarse_count, width + LANES), *aggs),
+            [new_fine, recv_row, coarse_own, edge_gain, bias_rows, state] + arrived + weights,
             scratch=[pltpu.VMEM((parts * cp, width), jnp.bfloat16)],
+            flops=COARSE_FLOPS[s],
             name="coarse_edges_and_sums",
         )
 
@@ -511,24 +588,31 @@
             name="own_sums",
         )
 
-    def node_update(s, nodes, sums, weights, spots):
+    def node_update(s, nodes, sums, weights, spots, cut=0, start=0):
+        far = [pltpu.VMEM((w_hidden, 2 * cut), jnp.bfloat16)] * 2 if cut else []
+        rows = sum(part[0].shape[0] for part in sums)
         return both(
             call(
-                functools.partial(node_kernel, divisor(nh, 256), s, cores, spots, len(sums)),
-                bf16(nh, width),
-                [nodes, bias_rows, node_gain] + sums + weights,
+                functools.partial(node_kernel, rows, s, cores, spots, [len(part) for part in sums], cut, start),
+                bf16(rows, width),
+                [nodes, bias_rows, node_gain] + [x for part in sums for x in part] + weights,
+                scratch=[pltpu.VMEM((rows, width), jnp.bfloat16), *far],
                 name="node_update",
             )
         )
 
-    def core_sum(agg_own, agg_other):
-        return call(add_kernel, bf16(nh, width), [agg_own, swap(agg_other)], name="core_sum")
+    def core_sum(agg_own, agg_other, cuts=1):
+        rows = agg_own.shape[0] // cuts
+        parts = call(
+            add_kernel, (bf16(rows, width),) * cuts, [agg_own, swap(agg_other)], name="core_sum"
+        )
+        return parts if cuts > 1 else parts[0]
 
     def chip_sums(partial):
         if two:
             return [partial, across(partial)]
         every = lax.all_gather(partial, "feat", axis=0)
-        every = every.reshape(cores // 2, 2, nh, width).astype(jnp.float32)
+        every = every.reshape(cores // 2, 2, *partial.shape).astype(jnp.float32)
         return [lax.dynamic_index_in_dim(every.sum(axis=0), core, 0, keepdims=False)]
 
     def halo_of(moved, swapped):
@@ -538,53 +622,62 @@
         return [x for pair in zip(moved, swapped) for x in pair]
 
     far_first = spread(first_pack)
-    to_prev, to_next, to_far, coarse_own = node_rows_out(nodes)
     moved = exchange(to_prev, to_next, to_far)
-    send_col, recv_col, recv_row, coarse_pack, *packs = after(
-        (send_col, recv_col, recv_row, coarse_pack, *packs), to_prev
+    send_col, recv_col, recv_row, *packs = after(
+        (send_col, recv_col, recv_row, *packs), to_prev
     )
     sent, received = gather(nodes)
-    coarse_pack = after(coarse_pack, sent)
-    states = [coarse_pack] + [shift(coarse_pack, by) for by in range(1, parts)]
-    *moved, far_first = after((*moved, far_first), sent)
-    swapped = [swap(m) for m in moved]
+    moved[0], moved[-1], far_first = after((moved[0], moved[-1], far_first), sent)
+    swapped = {i: swap(moved[i]) for i in (0, -1)}
     weights, spots = shards(first_pack, far_first), (((0, 0, k),), ((0, k, k + width),))
     far = spread(packs[0], far_first)
-    fine_edges, bias_rows = fine_update(
+    fine_edges, bias_rows, other, own = fine_update(
         0, fine_edges, sent, received, halo_of(moved, swapped), weights, spots
     )
-    states, fine_edges, far = after((states, fine_edges, far))
+    other, far, *moved[1:-1] = after((other, far, *moved[1:-1]))
+    swapped = [swapped[0], *(swap(m) for m in moved[1:-1]), swapped[-1]]
+    partial = core_sum(own, other)
+    fine_edges, far = after((fine_edges, far), partial)
     packs_of = [shards(packs[0], far)]
-    far = spread(packs[1], far)
-    state, agg_other = coarse_update(
-        0, fine_edges, coarse_own, states, pairs(moved, swapped), weights, spots
+    fine_part = chip_sums(partial)
+    state, other, own = coarse_update(
+        0, fine_edges, coarse_own, block, pairs(moved, swapped), weights, spots
     )
-    state, agg_other, far = after((state, agg_other, far))
-    packs_of.append(shards(packs[1], far))
-    agg_own = own_sums(fine_edges, state)
-    sums = chip_sums(core_sum(agg_own, agg_other))
-    far = spread(packs[2], sums)
+    sums = [fine_part, chip_sums(core_sum(own, other))]
+    far = spread(packs[1], sums)
     halves = node_update(0, nodes, sums, *choose(packs_of, 0, 1))
 
     to_prev, to_next, to_far, coarse_own, nodes = node_rows_out(*halves)
     moved = exchange(to_prev, to_next, to_far)
     sent, received = gather(nodes)
     *moved, far = after((*moved, far), sent)
-    packs_of.append(shards(packs[2], far))
+    packs_of.append(shards(packs[1], far))
     swapped = [swap(m) for m in moved]
-    far = spread(packs[3], far)
+    far = across(after(cut_part, far)) if cut else spread(packs[2], far)
     weights, spots = choose(packs_of, 3, 2)
     (fine_edges,) = fine_update(
         1, fine_edges, sent, received, halo_of(moved, swapped), weights, spots
     )
     fine_edges, far = after((fine_edges, far))
-    packs_of.append(shards(packs[3], far))
     state, agg_other = coarse_update(
-        1, fine_edges, coarse_own, [state], pairs(moved, swapped), weights, spots
+        1, fine_edges, coarse_own, state, pairs(moved, swapped), weights, spots
     )
     agg_own = own_sums(fine_edges, state)
-    sums = chip_sums(core_sum(agg_own, agg_other))
-    halves = node_update(1, nodes, sums, *choose(packs_of, 4, 5))
+    partial = core_sum(agg_own, agg_other, 2)
+    sums = [chip_sums(part) for part in partial]
+    if cut:
+        mine = both(far)
+        others = both(lax.ppermute(after(far, partial), "groups", [(0, 1), (1, 0)]))
+        weights = both(packs[2]) + pairs(mine, others)
+        spots = [[(0, at - starts[4], at - starts[4] + n)] for at, n in zip(starts[4:], (kn, width))]
+    else:
+        packs_of.append(shards(packs[2], far))
+        weights, spots = choose(packs_of, 4, 5)
+    halves = [
+        half
+        for i, part in enumerate(sums)
+        for half in node_update(1, nodes, [part], weights, spots, cut, i * nh // 2)
+    ]
     return call(join_kernel, bf16(count, width), halves, name="nodes_out")
 
 

time: 111 us -> 102 us (0.919)
  waiting for transfers between devices: 46.2 us -> 41.1 us
  Pallas kernels: 39.2 us -> 37.7 us
    ppermute x7 -> x8, waiting for transfers between devices: 30 us -> 16.2 us  [across(): return lax.ppermute(x, 'feat', [(i, i ^ 2) for i in range(cores)])]
    ppermute x9 -> x6, waiting for transfers between devices: 6.32 us -> 13.1 us  [shift(): lax.ppermute(x, 'mesh', [(i, (i + by) % parts) for i in range(parts)])]
    ppermute x9 -> x6, starting transfers between devices: 12.2 us -> 8.22 us  [shift(): lax.ppermute(x, 'mesh', [(i, (i + by) % parts) for i in range(parts)])]
    ppermute x0 -> x1, waiting for transfers between devices: none -> 3.39 us  [local(): others = both(lax.ppermute(after(far, partial), 'groups', [(0, 1), (1, 0)]))]
    ppermute x0 -> x1, starting transfers between devices: none -> 1.58 us  [local(): others = both(lax.ppermute(after(far, partial), 'groups', [(0, 1), (1, 0)]))]
    ppermute x7 -> x8, starting transfers between devices: 7.37 us -> 8.93 us  [across(): return lax.ppermute(x, 'feat', [(i, i ^ 2) for i in range(cores)])]
    pallas_call x18 -> x16, Pallas kernels: 39.2 us -> 37.7 us  [call(): pl.pallas_call(kernel, out_shape=out_shape, in_specs=in_specs, out_specs=...]
    ppermute x20 -> x21, waiting for transfers between devices: 9.94 us -> 8.41 us  [swap(): return lax.ppermute(x, 'feat', [(i, i ^ 1) for i in range(cores)])]
  transfers between devices with their start and end apart: 36 -> 36, of which waited for: 18 -> 20; matrix products, arithmetic and copies ran while one was open for 1% -> 1% of each run, Pallas kernels for 26% -> 27%
where the time goes in v3:
time: 102 us
  waiting for transfers between devices  41.1 us (40%)
  Pallas kernels  37.7 us (37%)
  starting transfers between devices  22.1 us (22%)
    pallas_call x16, Pallas kernels, call(): pl.pallas_call(kernel, out_shape=out_shape, in_specs=in_specs, out_specs=...  37.7 us
    ppermute x8, waiting for transfers between devices, across(): return lax.ppermute(x, 'feat', [(i, i ^ 2) for i in range(cores)])  16.2 us
    ppermute x6, waiting for transfers between devices, shift(): lax.ppermute(x, 'mesh', [(i, (i + by) % parts) for i in range(parts)])  13.1 us
    ppermute x8, starting transfers between devices, across(): return lax.ppermute(x, 'feat', [(i, i ^ 2) for i in range(cores)])  8.93 us
    ppermute x21, waiting for transfers between devices, swap(): return lax.ppermute(x, 'feat', [(i, i ^ 1) for i in range(cores)])  8.41 us
    ppermute x6, starting transfers between devices, shift(): lax.ppermute(x, 'mesh', [(i, (i + by) % parts) for i in range(parts)])  8.22 us
    ppermute x21, starting transfers between devices, swap(): return lax.ppermute(x, 'feat', [(i, i ^ 1) for i in range(cores)])  3.41 us
    ppermute x1, waiting for transfers between devices, local(): others = both(lax.ppermute(after(far, partial), 'groups', [(0, 1), (1, 0)]))  3.39 us
  transfers between devices with their start and end apart: 36, of which 20 were waited for; matrix products, arithmetic and copies ran while one was open for 1% of the time, Pallas kernels for 27%

profile of v3, /device:TPU:0, one launch (start us, length us, event | category | flops | bytes accessed | tf_op | source)
XLA Modules:
  0.0 101.9 jit_solution(16659561825568235795)
XLA Ops:
  0.0 4.5 %weights_and_halo_rows.1 = (bf16[128,2176]{1,0:T(8,128)(2,1)}, bf16[128,1792]{1,0:T(8,128)(2,1)}, bf16[128,1792]{1,0:T(8,128)(2,1)}, bf16[128,1536]{1,0:T(8,128)...) custom-call(bf16[2,128,1536]{2,1,0:T(8,128)(2,1)} %refs_0_.3, ...), custom_call_target="tpu_custom_call" | custom-call | tf_op jit(solution)/shard_map/weights_and_halo_rows/pallas_call | solution.py:76
  4.6 3.0 %collective-permute-start.2 = (bf16[128,2176]{1,0:T(8,128)(2,1)}, bf16[128,2176]{1,0:T(8,128)(2,1)S(1)}, u32[]{:S(2)}, u32[]{:S(2)}) collective-permute-start(bf16[128,2176]{1,0:T(8,128)(2,1)} %get-tuple-element.69.refs_10_.refs_12_), channel_id=1, source_target_pairs={{0,2},{1,3},{2,0},{3,1},{4,6},{5,7},{6,4},{7,5},{8,10},{9,11},{10,... | collective-permute-start | bytes 1671176 | tf_op jit(solution)/shard_map/ppermute | solution.py:450
  7.6 3.6 %collective-permute-start.1 = (bf16[240,512]{1,0:T(8,128)(2,1)}, bf16[240,512]{1,0:T(8,128)(2,1)S(1)}, u32[]{:S(2)}, u32[]{:S(2)}) collective-permute-start(bf16[240,512]{1,0:T(8,128)(2,1)} %get-tuple-element.62), channel_id=1, source_target_pairs={{0,12},{4,0},{8,4},{12,8},{1,13},{5,1},{9,5},{13,9},{2,14},{6,2},{... | collective-permute-start | bytes 737288 | tf_op jit(solution)/shard_map/ppermute | solution.py:453
  11.9 3.5 %gather_rows.2 = (bf16[1536,512]{1,0:T(8,128)(2,1)S(1)}, bf16[1536,512]{1,0:T(8,128)(2,1)S(1)}) custom-call(bf16[1024,512]{1,0:T(8,128)(2,1)S(1)} %copy-done, s32[1536,1]{1,0:T(8,128)S(1)} %copy.17.send.refs_3_, s32[1536,1]{1,0:T(8,128)S(1)} %copy.18.recv), custom_call_target="tpu_custom_call" | custom-call | flops 3221225472 | tf_op jit(solution)/shard_map/gather_rows/pallas_call | solution.py:76
  15.4 2.4 %collective-permute-done.1.refs_8_.refs_10_ = bf16[240,512]{1,0:T(8,128)(2,1)S(1)} collective-permute-done((bf16[240,512]{1,0:T(8,128)(2,1)}, bf16[240,512]{1,0:T(8,128)(2,1)S(1)}, u32[]{:S(2)}, u32[]{:S(2)}) %collective-permute-start.1) | collective-permute-done | bytes 245792 | tf_op jit(solution)/shard_map/ppermute | solution.py:453
  17.8 5.7 %collective-permute-done.refs_6_ = bf16[240,512]{1,0:T(8,128)(2,1)} collective-permute-done((bf16[240,512]{1,0:T(8,128)(2,1)}, bf16[240,512]{1,0:T(8,128)(2,1)}, u32[]{:S(2)}, u32[]{:S(2)}) %collective-permute-start) | collective-permute-done | bytes 245792 | tf_op jit(solution)/shard_map/ppermute | solution.py:453
  26.2 7.2 %fine_edges.2 = (bf16[1536,512]{1,0:T(8,128)(2,1)S(1)}, f32[8,512]{1,0:T(8,128)S(1)}, bf16[448,512]{1,0:T(8,128)(2,1)S(1)}, f32[448,512]{1,0:T(8,128)S(1)}) custom-call(bf16[1536,512]{1,0:T(8,128)(2,1)S(1)} %copy-done.10, bf16[1536,512]{1,0:T(8,128)(2,1)S(1)} %get-tuple-element.65.refs_1_, bf16[1536,512]{1,0:T(8,128)(2,1)S(1)} %get-tuple-element.66.refs_2_, ...), custom_call_target="tpu_custom_call" | custom-call | flops 3221225472 | tf_op jit(solution)/shard_map/fine_edges/pallas_call | solution.py:76
  33.4 2.6 %collective-permute-done.8.refs_8_ = bf16[176,512]{1,0:T(8,128)(2,1)S(1)} collective-permute-done((bf16[176,512]{1,0:T(8,128)(2,1)S(1)}, bf16[176,512]{1,0:T(8,128)(2,1)S(1)}, u32[]{:S(2)}, u32[]{:S(2)}) %collective-permute-start.8) | collective-permute-done | bytes 180256 | tf_op jit(solution)/shard_map/ppermute | solution.py:453
  37.5 1.3 %collective-permute-done.9.arrived = bf16[448,512]{1,0:T(8,128)(2,1)S(1)} collective-permute-done((bf16[448,512]{1,0:T(8,128)(2,1)S(1)}, bf16[448,512]{1,0:T(8,128)(2,1)S(1)}, u32[]{:S(2)}, u32[]{:S(2)}) %collective-permute-start.9) | collective-permute-done | bytes 458784 | tf_op jit(solution)/shard_map/ppermute | solution.py:447
  40.0 1.6 %collective-permute-done.11.refs_9_ = bf16[176,512]{1,0:T(8,128)(2,1)S(1)} collective-permute-done((bf16[176,512]{1,0:T(8,128)(2,1)S(1)}, bf16[176,512]{1,0:T(8,128)(2,1)S(1)}, u32[]{:S(2)}, u32[]{:S(2)}) %collective-permute-start.11) | collective-permute-done | bytes 180256 | tf_op jit(solution)/shard_map/ppermute | solution.py:447
  41.6 4.1 %coarse_edges_and_sums.2 = (bf16[384,640]{1,0:T(8,128)(2,1)S(1)}, bf16[64,512]{1,0:T(8,128)(2,1)S(1)}, f32[64,512]{1,0:T(8,128)S(1)}) custom-call(bf16[1536,512]{1,0:T(8,128)(2,1)S(1)} %get-tuple-element.82.refs_0_, s32[1,1536]{1,0:T(1,128)S(1)} %reshape.20.refs_4_.refs_1_.recv_row, bf16[128,512]{1,0:T(8,128)(2,1)S(1)} %copy-done.5, ...), custom_call_target="tpu_custom_call" | custom-call | tf_op jit(solution)/shard_map/coarse_edges_and_sums/pallas_call | solution.py:76
  45.9 1.1 %collective-permute-done.12.arrived = bf16[64,512]{1,0:T(8,128)(2,1)S(1)} collective-permute-done((bf16[64,512]{1,0:T(8,128)(2,1)S(1)}, bf16[64,512]{1,0:T(8,128)(2,1)S(1)}, u32[]{:S(2)}, u32[]{:S(2)}) %collective-permute-start.12) | collective-permute-done | bytes 65568 | tf_op jit(solution)/shard_map/ppermute | solution.py:447
  47.0 1.5 %collective-permute-start.13 = (bf16[64,512]{1,0:T(8,128)(2,1)S(1)}, bf16[64,512]{1,0:T(8,128)(2,1)S(1)}, u32[]{:S(2)}, u32[]{:S(2)}) collective-permute-start(bf16[64,512]{1,0:T(8,128)(2,1)S(1)} %core_sum.4.refs_5_), channel_id=1, source_target_pairs={{0,2},{1,3},{2,0},{3,1},{4,6},{5,7},{6,4},{7,5},{8,10},{9,11},{10,... | collective-permute-start | bytes 196616 | tf_op jit(solution)/shard_map/ppermute | solution.py:450
  48.6 4.4 %collective-permute-done.13.refs_6_ = bf16[64,512]{1,0:T(8,128)(2,1)S(1)} collective-permute-done((bf16[64,512]{1,0:T(8,128)(2,1)S(1)}, bf16[64,512]{1,0:T(8,128)(2,1)S(1)}, u32[]{:S(2)}, u32[]{:S(2)}) %collective-permute-start.13) | collective-permute-done | bytes 65568 | tf_op jit(solution)/shard_map/ppermute | solution.py:450
  53.0 1.7 %node_update.3.refs_0_ = bf16[512,512]{1,0:T(8,128)(2,1)S(1)} custom-call(bf16[1024,512]{1,0:T(8,128)(2,1)S(1)} %copy-done, f32[8,512]{1,0:T(8,128)S(1)} %get-tuple-element.73.refs_4_.refs_1_.refs_18_, bf16[2,512]{1,0:T(2,128)(2,1)S(1)} %copy-done.7, bf16[448,512]{1,0:T(8,128)(2,1)S(1)} %core_sum.3.refs_3_, ...), custom_call_target="tpu_custom_call" | custom-call | tf_op jit(solution)/shard_map/node_update/pallas_call | solution.py:76
  55.5 1.1 %collective-permute-done.16.refs_1_ = bf16[512,512]{1,0:T(8,128)(2,1)S(1)} collective-permute-done((bf16[512,512]{1,0:T(8,128)(2,1)S(1)}, bf16[512,512]{1,0:T(8,128)(2,1)S(1)}, u32[]{:S(2)}, u32[]{:S(2)}) %collective-permute-start.16) | collective-permute-done | bytes 524320 | tf_op jit(solution)/shard_map/ppermute | solution.py:447
  57.4 1.7 %collective-permute-start.17 = (bf16[128,512]{1,0:T(8,128)(2,1)S(1)}, bf16[128,512]{1,0:T(8,128)(2,1)S(1)}, u32[]{:S(2)}, u32[]{:S(2)}) collective-permute-start(bf16[128,512]{1,0:T(8,128)(2,1)S(1)} %get-tuple-element.92), channel_id=1, source_target_pairs={{0,4},{4,8},{8,12},{12,0},{1,5},{5,9},{9,13},{13,1},{2,6},{6,10},{... | collective-permute-start | bytes 393224 | tf_op jit(solution)/shard_map/ppermute | solution.py:453
  59.0 2.2 %collective-permute-start.19 = (bf16[128,512]{1,0:T(8,128)(2,1)S(1)}, bf16[128,512]{1,0:T(8,128)(2,1)S(1)}, u32[]{:S(2)}, u32[]{:S(2)}) collective-permute-start(bf16[128,512]{1,0:T(8,128)(2,1)S(1)} %get-tuple-element.94), channel_id=1, source_target_pairs={{0,12},{4,0},{8,4},{12,8},{1,13},{5,1},{9,5},{13,9},{2,14},{6,2},{... | collective-permute-start | bytes 393224 | tf_op jit(solution)/shard_map/ppermute | solution.py:453
  61.3 3.5 %gather_rows.3 = (bf16[1536,512]{1,0:T(8,128)(2,1)S(1)}, bf16[1536,512]{1,0:T(8,128)(2,1)S(1)}) custom-call(bf16[1024,512]{1,0:T(8,128)(2,1)S(1)} %get-tuple-element.89.nodes.refs_0_, s32[1536,1]{1,0:T(8,128)S(1)} %copy.17.send.refs_3_, s32[1536,1]{1,0:T(8,128)S(1)} %copy.18.recv), custom_call_target="tpu_custom_call" | custom-call | flops 3221225472 | tf_op jit(solution)/shard_map/gather_rows/pallas_call | solution.py:76
  64.7 2.9 %collective-permute-done.20.refs_15_.refs_17_ = bf16[128,1792]{1,0:T(8,128)(2,1)S(1)} collective-permute-done((bf16[128,1792]{1,0:T(8,128)(2,1)S(1)}, bf16[128,1792]{1,0:T(8,128)(2,1)S(1)}, u32[]{:S(2)}, u32[]{:S(2)}) %collective-permute-start.20) | collective-permute-done | bytes 458784 | tf_op jit(solution)/shard_map/ppermute | solution.py:450
  67.6 2.2 %collective-permute-done.18.refs_8_ = bf16[64,512]{1,0:T(8,128)(2,1)S(1)} collective-permute-done((bf16[64,512]{1,0:T(8,128)(2,1)S(1)}, bf16[64,512]{1,0:T(8,128)(2,1)S(1)}, u32[]{:S(2)}, u32[]{:S(2)}) %collective-permute-start.18) | collective-permute-done | bytes 65568 | tf_op jit(solution)/shard_map/ppermute | solution.py:453
  72.1 4.8 %fine_edges.3.refs_0_.new_fine = bf16[1536,512]{1,0:T(8,128)(2,1)S(1)} custom-call(bf16[1536,512]{1,0:T(8,128)(2,1)S(1)} %get-tuple-element.82.refs_0_, bf16[1536,512]{1,0:T(8,128)(2,1)S(1)} %get-tuple-element.90.refs_1_, bf16[1536,512]{1,0:T(8,128)(2,1)S(1)} %get-tuple-element.91.refs_2_, s32[1536,1]{1,0:T(8,128)S(1)} %copy.17.send.refs_3_, ...), custom_call_target="tpu_custom_call" | custom-call | flops 3221225472 | tf_op jit(solution)/shard_map/fine_edges/pallas_call | solution.py:76
  77.7 3.2 %coarse_edges_and_sums.3 = (bf16[384,640]{1,0:T(8,128)(2,1)S(1)}, bf16[512,512]{1,0:T(8,128)(2,1)S(1)}) custom-call(bf16[1536,512]{1,0:T(8,128)(2,1)S(1)} %fine_edges.3.refs_0_.new_fine, s32[1,1536]{1,0:T(1,128)S(1)} %reshape.20.refs_4_.refs_1_.recv_row, bf16[128,512]{1,0:T(8,128)(2,1)S(1)} %get-tuple-element.103.refs_2_, bf16[2,512]{1,0:T(2,128)(2,1)S(1)} %copy-done.8, ...), custom_call_target="tpu_custom_call" | custom-call | tf_op jit(solution)/shard_map/coarse_edges_and_sums/pallas_call | solution.py:76
  81.5 1.4 %own_sums.1.own = f32[512,512]{1,0:T(8,128)S(1)} custom-call(bf16[1536,512]{1,0:T(8,128)(2,1)S(1)} %fine_edges.3.refs_0_.new_fine, s32[1,1536]{1,0:T(1,128)S(1)} %reshape.20.refs_4_.refs_1_.recv_row, bf16[384,640]{1,0:T(8,128)(2,1)S(1)} %get-tuple-element.106.state), custom_call_target="tpu_custom_call" | custom-call | tf_op jit(solution)/shard_map/own_sums/pallas_call | solution.py:76
  83.0 1.6 %collective-permute-start.30 = (bf16[128,768]{1,0:T(8,128)(2,1)S(1)}, bf16[128,768]{1,0:T(8,128)(2,1)S(1)}, u32[]{:S(2)}, u32[]{:S(2)}) collective-permute-start(bf16[128,768]{1,0:T(8,128)(2,1)S(1)} %collective-permute-done.25.refs_7_), channel_id=1, source_target_pairs={{0,16},{16,0},{1,17},{17,1},{2,18},{18,2},{3,19},{19,3},{4,20},{20... | collective-permute-start | bytes 589832 | tf_op jit(solution)/shard_map/ppermute | solution.py:670
  85.2 1.4 %collective-permute-start.28 = (bf16[256,512]{1,0:T(8,128)(2,1)S(1)}, bf16[256,512]{1,0:T(8,128)(2,1)S(1)}, u32[]{:S(2)}, u32[]{:S(2)}) collective-permute-start(bf16[256,512]{1,0:T(8,128)(2,1)S(1)} %get-tuple-element.108.refs_3_), channel_id=1, source_target_pairs={{0,2},{1,3},{2,0},{3,1},{4,6},{5,7},{6,4},{7,5},{8,10},{9,11},{10,... | collective-permute-start | bytes 786440 | tf_op jit(solution)/shard_map/ppermute | solution.py:450
  86.6 3.4 %collective-permute-done.30.refs_8_ = bf16[128,768]{1,0:T(8,128)(2,1)S(1)} collective-permute-done((bf16[128,768]{1,0:T(8,128)(2,1)S(1)}, bf16[128,768]{1,0:T(8,128)(2,1)S(1)}, u32[]{:S(2)}, u32[]{:S(2)}) %collective-permute-start.30) | collective-permute-done | bytes 196640 | tf_op jit(solution)/shard_map/ppermute | solution.py:670
  90.0 3.8 %collective-permute-done.34.refs_4_ = bf16[256,512]{1,0:T(8,128)(2,1)S(1)} collective-permute-done((bf16[256,512]{1,0:T(8,128)(2,1)S(1)}, bf16[256,512]{1,0:T(8,128)(2,1)S(1)}, u32[]{:S(2)}, u32[]{:S(2)}) %collective-permute-start.34) | collective-permute-done | bytes 262176 | tf_op jit(solution)/shard_map/ppermute | solution.py:450
  94.8 3.5 %collective-permute-done.28.refs_4_ = bf16[256,512]{1,0:T(8,128)(2,1)S(1)} collective-permute-done((bf16[256,512]{1,0:T(8,128)(2,1)S(1)}, bf16[256,512]{1,0:T(8,128)(2,1)S(1)}, u32[]{:S(2)}, u32[]{:S(2)}) %collective-permute-start.28) | collective-permute-done | bytes 262176 | tf_op jit(solution)/shard_map/ppermute | solution.py:450
  98.3 1.0 node_update.4.refs_0_
  99.3 1.5 %collective-permute-done.33.refs_1_ = bf16[256,512]{1,0:T(8,128)(2,1)S(1)} collective-permute-done((bf16[256,512]{1,0:T(8,128)(2,1)S(1)}, bf16[256,512]{1,0:T(8,128)(2,1)S(1)}, u32[]{:S(2)}, u32[]{:S(2)}) %collective-permute-start.33) | collective-permute-done | bytes 262176 | tf_op jit(solution)/shard_map/ppermute | solution.py:447
  100.8 1.1 %nodes_out.1 = bf16[1024,512]{1,0:T(8,128)(2,1)} custom-call(bf16[256,512]{1,0:T(8,128)(2,1)S(1)} %node_update.4.refs_0_, bf16[256,512]{1,0:T(8,128)(2,1)S(1)} %collective-permute-done.33.refs_1_, bf16[256,512]{1,0:T(8,128)(2,1)S(1)} %node_update.5.refs_2_, bf16[256,512]{1,0:T(8,128)(2,1)S(1)} %collective-permute-done.35.refs_3_), custom_call_target="tpu_custom_call" | custom-call | tf_op jit(solution)/shard_map/nodes_out/pallas_call | solution.py:76
  (91 shorter events, 13.2 us)
Async XLA Ops:
  4.6 19.0 %collective-permute-start.2 = (bf16[128,2176]{1,0:T(8,128)(2,1)}, bf16[128,2176]{1,0:T(8,128)(2,1)S(1)}, u32[]{:S(2)}, u32[]{:S(2)}) collective-permute-start(bf16[128,2176]{1,0:T(8,128)(2,1)} %get-tuple-element.69.refs_10_.refs_12_), channel_id=1, source_target_pairs={{0,2},{1,3},{2,0},{3,1},{4,6},{5,7},{6,4},{7,5},{8,10},{9,11},{10,... | collective-permute-start | bytes 1671176 | tf_op jit(solution)/shard_map/ppermute | solution.py:450
  7.6 17.0 %collective-permute-start.5 = (bf16[128,2176]{1,0:T(8,128)(2,1)}, bf16[128,2176]{1,0:T(8,128)(2,1)}, u32[]{:S(2)}, u32[]{:S(2)}) collective-permute-start(bf16[128,2176]{1,0:T(8,128)(2,1)} %get-tuple-element.69.refs_10_.refs_12_), channel_id=1, source_target_pairs={{0,1},{1,0},{2,3},{3,2},{4,5},{5,4},{6,7},{7,6},{8,9},{9,8},{10,11... | collective-permute-start | bytes 1671176 | tf_op jit(solution)/shard_map/ppermute | solution.py:447
  7.6 10.2 %collective-permute-start.1 = (bf16[240,512]{1,0:T(8,128)(2,1)}, bf16[240,512]{1,0:T(8,128)(2,1)S(1)}, u32[]{:S(2)}, u32[]{:S(2)}) collective-permute-start(bf16[240,512]{1,0:T(8,128)(2,1)} %get-tuple-element.62), channel_id=1, source_target_pairs={{0,12},{4,0},{8,4},{12,8},{1,13},{5,1},{9,5},{13,9},{2,14},{6,2},{... | collective-permute-start | bytes 737288 | tf_op jit(solution)/shard_map/ppermute | solution.py:453
  11.2 12.4 %collective-permute-start = (bf16[240,512]{1,0:T(8,128)(2,1)}, bf16[240,512]{1,0:T(8,128)(2,1)}, u32[]{:S(2)}, u32[]{:S(2)}) collective-permute-start(bf16[240,512]{1,0:T(8,128)(2,1)} %get-tuple-element.68), channel_id=1, source_target_pairs={{0,4},{4,8},{8,12},{12,0},{1,5},{5,9},{9,13},{13,1},{2,6},{6,10},{... | collective-permute-start | bytes 737288 | tf_op jit(solution)/shard_map/ppermute | solution.py:453
  23.6 2.7 %collective-permute-start.6 = (bf16[128,2176]{1,0:T(8,128)(2,1)S(1)}, bf16[128,2176]{1,0:T(8,128)(2,1)S(1)}, u32[]{:S(2)}, u32[]{:S(2)}) collective-permute-start(bf16[128,2176]{1,0:T(8,128)(2,1)S(1)} %collective-permute-done.2.refs_12_.refs_14_), channel_id=1, source_target_pairs={{0,1},{1,0},{2,3},{3,2},{4,5},{5,4},{6,7},{7,6},{8,9},{9,8},{10,11... | collective-permute-start | bytes 1671176 | tf_op jit(solution)/shard_map/ppermute | solution.py:447
  23.6 2.5 %collective-permute-start.3 = (bf16[240,512]{1,0:T(8,128)(2,1)}, bf16[240,512]{1,0:T(8,128)(2,1)S(1)}, u32[]{:S(2)}, u32[]{:S(2)}) collective-permute-start(bf16[240,512]{1,0:T(8,128)(2,1)} %collective-permute-done.refs_6_), channel_id=1, source_target_pairs={{0,1},{1,0},{2,3},{3,2},{4,5},{5,4},{6,7},{7,6},{8,9},{9,8},{10,11... | collective-permute-start | bytes 737288 | tf_op jit(solution)/shard_map/ppermute | solution.py:447
  24.1 2.1 %collective-permute-start.4 = (bf16[240,512]{1,0:T(8,128)(2,1)S(1)}, bf16[240,512]{1,0:T(8,128)(2,1)S(1)}, u32[]{:S(2)}, u32[]{:S(2)}) collective-permute-start(bf16[240,512]{1,0:T(8,128)(2,1)S(1)} %collective-permute-done.1.refs_8_.refs_10_), channel_id=1, source_target_pairs={{0,1},{1,0},{2,3},{3,2},{4,5},{5,4},{6,7},{7,6},{8,9},{9,8},{10,11... | collective-permute-start | bytes 737288 | tf_op jit(solution)/shard_map/ppermute | solution.py:447
  24.1 12.9 %collective-permute-start.7 = (bf16[128,1792]{1,0:T(8,128)(2,1)S(1)}, bf16[128,1792]{1,0:T(8,128)(2,1)S(1)}, u32[]{:S(2)}, u32[]{:S(2)}) collective-permute-start(bf16[128,1792]{1,0:T(8,128)(2,1)S(1)} %copy-done.1), channel_id=1, source_target_pairs={{0,2},{1,3},{2,0},{3,1},{4,6},{5,7},{6,4},{7,5},{8,10},{9,11},{10,... | collective-permute-start | bytes 1376264 | tf_op jit(solution)/shard_map/ppermute | solution.py:450
  24.6 11.4 %collective-permute-start.8 = (bf16[176,512]{1,0:T(8,128)(2,1)S(1)}, bf16[176,512]{1,0:T(8,128)(2,1)S(1)}, u32[]{:S(2)}, u32[]{:S(2)}) collective-permute-start(bf16[176,512]{1,0:T(8,128)(2,1)S(1)} %copy-done.14), channel_id=1, source_target_pairs={{0,8},{4,12},{8,0},{12,4},{1,9},{5,13},{9,1},{13,5},{2,10},{6,14},... | collective-permute-start | bytes 540680 | tf_op jit(solution)/shard_map/ppermute | solution.py:453
  37.0 11.6 %collective-permute-start.14 = (bf16[128,1792]{1,0:T(8,128)(2,1)S(1)}, bf16[128,1792]{1,0:T(8,128)(2,1)S(1)}, u32[]{:S(2)}, u32[]{:S(2)}) collective-permute-start(bf16[128,1792]{1,0:T(8,128)(2,1)S(1)} %copy-done.1), channel_id=1, source_target_pairs={{0,1},{1,0},{2,3},{3,2},{4,5},{5,4},{6,7},{7,6},{8,9},{9,8},{10,11... | collective-permute-start | bytes 1376264 | tf_op jit(solution)/shard_map/ppermute | solution.py:447
  38.9 14.0 %collective-permute-start.10 = (bf16[448,512]{1,0:T(8,128)(2,1)S(1)}, bf16[448,512]{1,0:T(8,128)(2,1)S(1)}, u32[]{:S(2)}, u32[]{:S(2)}) collective-permute-start(bf16[448,512]{1,0:T(8,128)(2,1)S(1)} %core_sum.3.refs_3_), channel_id=1, source_target_pairs={{0,2},{1,3},{2,0},{3,1},{4,6},{5,7},{6,4},{7,5},{8,10},{9,11},{10,... | collective-permute-start | bytes 1376264 | tf_op jit(solution)/shard_map/ppermute | solution.py:450
  39.5 13.4 %collective-permute-start.15 = (bf16[128,1792]{1,0:T(8,128)(2,1)S(1)}, bf16[128,1792]{1,0:T(8,128)(2,1)S(1)}, u32[]{:S(2)}, u32[]{:S(2)}) collective-permute-start(bf16[128,1792]{1,0:T(8,128)(2,1)S(1)} %collective-permute-done.7.refs_9_.refs_14_.refs_16_), channel_id=1, source_target_pairs={{0,1},{1,0},{2,3},{3,2},{4,5},{5,4},{6,7},{7,6},{8,9},{9,8},{10,11... | collective-permute-start | bytes 1376264 | tf_op jit(solution)/shard_map/ppermute | solution.py:447
  39.5 2.1 %collective-permute-start.11 = (bf16[176,512]{1,0:T(8,128)(2,1)S(1)}, bf16[176,512]{1,0:T(8,128)(2,1)S(1)}, u32[]{:S(2)}, u32[]{:S(2)}) collective-permute-start(bf16[176,512]{1,0:T(8,128)(2,1)S(1)} %collective-permute-done.8.refs_8_), channel_id=1, source_target_pairs={{0,1},{1,0},{2,3},{3,2},{4,5},{5,4},{6,7},{7,6},{8,9},{9,8},{10,11... | collective-permute-start | bytes 540680 | tf_op jit(solution)/shard_map/ppermute | solution.py:447
  47.0 5.9 %collective-permute-start.13 = (bf16[64,512]{1,0:T(8,128)(2,1)S(1)}, bf16[64,512]{1,0:T(8,128)(2,1)S(1)}, u32[]{:S(2)}, u32[]{:S(2)}) collective-permute-start(bf16[64,512]{1,0:T(8,128)(2,1)S(1)} %core_sum.4.refs_5_), channel_id=1, source_target_pairs={{0,2},{1,3},{2,0},{3,1},{4,6},{5,7},{6,4},{7,5},{8,10},{9,11},{10,... | collective-permute-start | bytes 196616 | tf_op jit(solution)/shard_map/ppermute | solution.py:450
  54.6 2.0 %collective-permute-start.16 = (bf16[512,512]{1,0:T(8,128)(2,1)S(1)}, bf16[512,512]{1,0:T(8,128)(2,1)S(1)}, u32[]{:S(2)}, u32[]{:S(2)}) collective-permute-start(bf16[512,512]{1,0:T(8,128)(2,1)S(1)} %node_update.3.refs_0_), channel_id=1, source_target_pairs={{0,1},{1,0},{2,3},{3,2},{4,5},{5,4},{6,7},{7,6},{8,9},{9,8},{10,11... | collective-permute-start | bytes 1572872 | tf_op jit(solution)/shard_map/ppermute | solution.py:447
  54.7 12.9 %collective-permute-start.20 = (bf16[128,1792]{1,0:T(8,128)(2,1)S(1)}, bf16[128,1792]{1,0:T(8,128)(2,1)S(1)}, u32[]{:S(2)}, u32[]{:S(2)}) collective-permute-start(bf16[128,1792]{1,0:T(8,128)(2,1)S(1)} %copy-done.4), channel_id=1, source_target_pairs={{0,2},{1,3},{2,0},{3,1},{4,6},{5,7},{6,4},{7,5},{8,10},{9,11},{10,... | collective-permute-start | bytes 1376264 | tf_op jit(solution)/shard_map/ppermute | solution.py:450
  55.3 15.7 %collective-permute-start.23 = (bf16[128,1792]{1,0:T(8,128)(2,1)S(1)}, bf16[128,1792]{1,0:T(8,128)(2,1)S(1)}, u32[]{:S(2)}, u32[]{:S(2)}) collective-permute-start(bf16[128,1792]{1,0:T(8,128)(2,1)S(1)} %copy-done.4), channel_id=1, source_target_pairs={{0,1},{1,0},{2,3},{3,2},{4,5},{5,4},{6,7},{7,6},{8,9},{9,8},{10,11... | collective-permute-start | bytes 1376264 | tf_op jit(solution)/shard_map/ppermute | solution.py:447
  57.4 12.5 %collective-permute-start.17 = (bf16[128,512]{1,0:T(8,128)(2,1)S(1)}, bf16[128,512]{1,0:T(8,128)(2,1)S(1)}, u32[]{:S(2)}, u32[]{:S(2)}) collective-permute-start(bf16[128,512]{1,0:T(8,128)(2,1)S(1)} %get-tuple-element.92), channel_id=1, source_target_pairs={{0,4},{4,8},{8,12},{12,0},{1,5},{5,9},{9,13},{13,1},{2,6},{6,10},{... | collective-permute-start | bytes 393224 | tf_op jit(solution)/shard_map/ppermute | solution.py:453
  59.0 10.8 %collective-permute-start.19 = (bf16[128,512]{1,0:T(8,128)(2,1)S(1)}, bf16[128,512]{1,0:T(8,128)(2,1)S(1)}, u32[]{:S(2)}, u32[]{:S(2)}) collective-permute-start(bf16[128,512]{1,0:T(8,128)(2,1)S(1)} %get-tuple-element.94), channel_id=1, source_target_pairs={{0,12},{4,0},{8,4},{12,8},{1,13},{5,1},{9,5},{13,9},{2,14},{6,2},{... | collective-permute-start | bytes 393224 | tf_op jit(solution)/shard_map/ppermute | solution.py:453
  61.2 8.6 %collective-permute-start.18 = (bf16[64,512]{1,0:T(8,128)(2,1)S(1)}, bf16[64,512]{1,0:T(8,128)(2,1)S(1)}, u32[]{:S(2)}, u32[]{:S(2)}) collective-permute-start(bf16[64,512]{1,0:T(8,128)(2,1)S(1)} %get-tuple-element.93), channel_id=1, source_target_pairs={{0,8},{4,12},{8,0},{12,4},{1,9},{5,13},{9,1},{13,5},{2,10},{6,14},... | collective-permute-start | bytes 196616 | tf_op jit(solution)/shard_map/ppermute | solution.py:453
  69.9 2.2 %collective-permute-start.24 = (bf16[128,1792]{1,0:T(8,128)(2,1)S(1)}, bf16[128,1792]{1,0:T(8,128)(2,1)S(1)}, u32[]{:S(2)}, u32[]{:S(2)}) collective-permute-start(bf16[128,1792]{1,0:T(8,128)(2,1)S(1)} %collective-permute-done.20.refs_15_.refs_17_), channel_id=1, source_target_pairs={{0,1},{1,0},{2,3},{3,2},{4,5},{5,4},{6,7},{7,6},{8,9},{9,8},{10,11... | collective-permute-start | bytes 1376264 | tf_op jit(solution)/shard_map/ppermute | solution.py:447
  69.9 2.0 %collective-permute-start.21 = (bf16[128,512]{1,0:T(8,128)(2,1)S(1)}, bf16[128,512]{1,0:T(8,128)(2,1)S(1)}, u32[]{:S(2)}, u32[]{:S(2)}) collective-permute-start(bf16[128,512]{1,0:T(8,128)(2,1)S(1)} %collective-permute-done.17.refs_6_), channel_id=1, source_target_pairs={{0,1},{1,0},{2,3},{3,2},{4,5},{5,4},{6,7},{7,6},{8,9},{9,8},{10,11... | collective-permute-start | bytes 393224 | tf_op jit(solution)/shard_map/ppermute | solution.py:447
  70.5 7.2 %collective-permute-start.25 = (bf16[128,768]{1,0:T(8,128)(2,1)S(1)}, bf16[128,768]{1,0:T(8,128)(2,1)S(1)}, u32[]{:S(2)}, u32[]{:S(2)}) collective-permute-start(bf16[128,768]{1,0:T(8,128)(2,1)S(1)} %copy-done.13), channel_id=1, source_target_pairs={{0,2},{1,3},{2,0},{3,1},{4,6},{5,7},{6,4},{7,5},{8,10},{9,11},{10,... | collective-permute-start | bytes 589832 | tf_op jit(solution)/shard_map/ppermute | solution.py:450
  71.1 6.7 %collective-permute-start.26 = (bf16[64,512]{1,0:T(8,128)(2,1)S(1)}, bf16[64,512]{1,0:T(8,128)(2,1)S(1)}, u32[]{:S(2)}, u32[]{:S(2)}) collective-permute-start(bf16[64,512]{1,0:T(8,128)(2,1)S(1)} %collective-permute-done.18.refs_8_), channel_id=1, source_target_pairs={{0,1},{1,0},{2,3},{3,2},{4,5},{5,4},{6,7},{7,6},{8,9},{9,8},{10,11... | collective-permute-start | bytes 196616 | tf_op jit(solution)/shard_map/ppermute | solution.py:447
  80.9 2.0 %collective-permute-start.27 = (bf16[512,512]{1,0:T(8,128)(2,1)S(1)}, bf16[512,512]{1,0:T(8,128)(2,1)S(1)}, u32[]{:S(2)}, u32[]{:S(2)}) collective-permute-start(bf16[512,512]{1,0:T(8,128)(2,1)S(1)} %get-tuple-element.107), channel_id=1, source_target_pairs={{0,1},{1,0},{2,3},{3,2},{4,5},{5,4},{6,7},{7,6},{8,9},{9,8},{10,11... | collective-permute-start | bytes 1572872 | tf_op jit(solution)/shard_map/ppermute | solution.py:447
  81.0 9.0 %collective-permute-start.29 = (bf16[128,1536]{1,0:T(8,128)(2,1)S(1)}, bf16[128,1536]{1,0:T(8,128)(2,1)S(1)}, u32[]{:S(2)}, u32[]{:S(2)}) collective-permute-start(bf16[128,1536]{1,0:T(8,128)(2,1)S(1)} %copy-done.2), channel_id=1, source_target_pairs={{0,1},{1,0},{2,3},{3,2},{4,5},{5,4},{6,7},{7,6},{8,9},{9,8},{10,11... | collective-permute-start | bytes 1179656 | tf_op jit(solution)/shard_map/ppermute | solution.py:447
  83.0 7.0 %collective-permute-start.30 = (bf16[128,768]{1,0:T(8,128)(2,1)S(1)}, bf16[128,768]{1,0:T(8,128)(2,1)S(1)}, u32[]{:S(2)}, u32[]{:S(2)}) collective-permute-start(bf16[128,768]{1,0:T(8,128)(2,1)S(1)} %collective-permute-done.25.refs_7_), channel_id=1, source_target_pairs={{0,16},{16,0},{1,17},{17,1},{2,18},{18,2},{3,19},{19,3},{4,20},{20... | collective-permute-start | bytes 589832 | tf_op jit(solution)/shard_map/ppermute | solution.py:670
  84.6 9.2 %collective-permute-start.34 = (bf16[256,512]{1,0:T(8,128)(2,1)S(1)}, bf16[256,512]{1,0:T(8,128)(2,1)S(1)}, u32[]{:S(2)}, u32[]{:S(2)}) collective-permute-start(bf16[256,512]{1,0:T(8,128)(2,1)S(1)} %get-tuple-element.111.refs_3_), channel_id=1, source_target_pairs={{0,2},{1,3},{2,0},{3,1},{4,6},{5,7},{6,4},{7,5},{8,10},{9,11},{10,... | collective-permute-start | bytes 786440 | tf_op jit(solution)/shard_map/ppermute | solution.py:450
  85.2 13.1 %collective-permute-start.28 = (bf16[256,512]{1,0:T(8,128)(2,1)S(1)}, bf16[256,512]{1,0:T(8,128)(2,1)S(1)}, u32[]{:S(2)}, u32[]{:S(2)}) collective-permute-start(bf16[256,512]{1,0:T(8,128)(2,1)S(1)} %get-tuple-element.108.refs_3_), channel_id=1, source_target_pairs={{0,2},{1,3},{2,0},{3,1},{4,6},{5,7},{6,4},{7,5},{8,10},{9,11},{10,... | collective-permute-start | bytes 786440 | tf_op jit(solution)/shard_map/ppermute | solution.py:450
  86.6 3.4 %collective-permute-start.31 = (bf16[128,768]{1,0:T(8,128)(2,1)S(1)}, bf16[128,768]{1,0:T(8,128)(2,1)S(1)}, u32[]{:S(2)}, u32[]{:S(2)}) collective-permute-start(bf16[128,768]{1,0:T(8,128)(2,1)S(1)} %collective-permute-done.25.refs_7_), channel_id=1, source_target_pairs={{0,1},{1,0},{2,3},{3,2},{4,5},{5,4},{6,7},{7,6},{8,9},{9,8},{10,11... | collective-permute-start | bytes 589832 | tf_op jit(solution)/shard_map/ppermute | solution.py:447
  90.0 3.8 %collective-permute-start.32 = (bf16[128,768]{1,0:T(8,128)(2,1)S(1)}, bf16[128,768]{1,0:T(8,128)(2,1)S(1)}, u32[]{:S(2)}, u32[]{:S(2)}) collective-permute-start(bf16[128,768]{1,0:T(8,128)(2,1)S(1)} %collective-permute-done.30.refs_8_), channel_id=1, source_target_pairs={{0,1},{1,0},{2,3},{3,2},{4,5},{5,4},{6,7},{7,6},{8,9},{9,8},{10,11... | collective-permute-start | bytes 589832 | tf_op jit(solution)/shard_map/ppermute | solution.py:447
  94.7 4.6 %collective-permute-start.35 = (bf16[256,512]{1,0:T(8,128)(2,1)S(1)}, bf16[256,512]{1,0:T(8,128)(2,1)S(1)}, u32[]{:S(2)}, u32[]{:S(2)}) collective-permute-start(bf16[256,512]{1,0:T(8,128)(2,1)S(1)} %node_update.5.refs_2_), channel_id=1, source_target_pairs={{0,1},{1,0},{2,3},{3,2},{4,5},{5,4},{6,7},{7,6},{8,9},{9,8},{10,11... | collective-permute-start | bytes 786440 | tf_op jit(solution)/shard_map/ppermute | solution.py:447
  (19 other events, 166.2 us)

commit v4 on v3

--- a/solution.py
+++ b/solution.py
@@ -10,8 +10,8 @@
 STEPS = 2
 STRIDE = 8
 LANES = 128
-PART = 256
 COARSE_FLOPS = (0, 0)
+RELAYED = 4
 DIGIT = 64
 VMEM_BYTES = 20 * 1024 * 1024
 
@@ -70,9 +70,9 @@
     lax.fori_loop(0, steps, body, 0, unroll=2 if steps % 2 == 0 else 1)
 
 
-def call(kernel, out_shape, args, scratch=(), flops=0, nbytes=0, memory=None, limit=VMEM_BYTES, name=None):
+def call(kernel, out_shape, args, scratch=(), flops=0, nbytes=0, memory=None, out_memory=pltpu.VMEM, limit=VMEM_BYTES, name=None):
     in_specs = [pl.BlockSpec(memory_space=m) for m in memory or [pltpu.VMEM] * len(args)]
-    out_specs = jax.tree.map(lambda _: pl.BlockSpec(memory_space=pltpu.VMEM), out_shape)
+    out_specs = jax.tree.map(lambda _: pl.BlockSpec(memory_space=out_memory), out_shape)
     return pl.pallas_call(
         kernel,
         out_shape=out_shape,
@@ -99,23 +99,12 @@
     out[pl.ds(pl.multiple_of((1 - core) * nh, nh), nh), :] = other[...]
 
 
-def join_kernel(*refs):
-    out = refs[-1]
-    core, at = core_index(), 0
-    for own, other in zip(refs[:-1:2], refs[1:-1:2]):
-        rows = own.shape[0]
-        for who, ref in ((core, own), (1 - core, other)):
-            spot = pl.multiple_of(who * (out.shape[0] // 2) + at, rows)
-            out[pl.ds(spot, rows), :] = ref[...]
-        at += rows
-
-
-def add_kernel(own, arrived, *outs):
-    at = 0
-    for out in outs:
-        rows = pl.ds(at, out.shape[0])
-        out[...] = (own[rows, :] + arrived[rows, :].astype(jnp.float32)).astype(out.dtype)
-        at += out.shape[0]
+def join_kernel(own, other, out):
+    join_halves(out, own, other)
+
+
+def add_kernel(own, arrived, out):
+    out[...] = (own[...] + arrived[...].astype(jnp.float32)).astype(out.dtype)
 
 
 def index_digits(ref, lanes):
@@ -167,34 +156,50 @@
             out[pl.ds(skip + ch, block.shape[0]), :] = block[...]
 
 
-def prepare_kernel(plans, cut, *refs):
-    source, (edge_b1, node_b1, nodes, halo, edges, send, recv) = refs[:4], refs[4:11]
-    packs, rest = refs[11 : 11 + len(plans)], refs[11 + len(plans) :]
-    *rest, sems = rest
-    copies = []
-    for plan, out in zip(plans, packs):
-        at = 0
+def prepare_kernel(plans, cut, n_small, *refs):
+    n_out = len(plans) + 5 + (1 if cut else 0)
+    source, given, outs = refs[:4], refs[4 : 4 + n_small], refs[4 + n_small :][:n_out]
+    refs = refs[4 + n_small + n_out :]
+    small, made, sems = refs[:n_small], refs[n_small:-1], refs[-1]
+    started = []
+
+    def start(src, dst):
+        copy = pltpu.make_async_copy(src, dst, sems.at[len(started)])
+        copy.start()
+        started.append(copy)
+        return copy
+
+    arriving = [start(src, dst) for src, dst in zip(given, small)]
+    loads = []
+    for plan, pack in zip(plans, made):
+        at, parts = 0, []
         for which, layer, first, last in plan:
-            part = source[which].at[layer, :, first:last]
-            spot = out.at[:, at : at + last - first]
-            copies.append(pltpu.make_async_copy(part, spot, sems.at[len(copies)]))
+            spot = pack.at[:, at : at + last - first]
+            parts.append(start(source[which].at[layer, :, first:last], spot))
             at += last - first
-    for copy in copies:
-        copy.start()
+        loads.append(parts)
+    for copy in arriving:
+        copy.wait()
+    edge_b1, node_b1, nodes, halo, edges, send, recv = small
     hidden = edge_b1.shape[1]
     rows = [edge_b1[...].astype(jnp.float32), node_b1[...].astype(jnp.float32)]
     rows.append(jnp.zeros((16 - 2 * STEPS, hidden), jnp.float32))
-    at = packs[0].shape[1] - LANES
-    packs[0][0:16, at : at + hidden] = jnp.concatenate(rows).astype(jnp.bfloat16)
+    at = made[0].shape[1] - LANES
+    made[0][0:16, at : at + hidden] = jnp.concatenate(rows).astype(jnp.bfloat16)
+    n_packs = len(plans) + (1 if cut else 0)
+    halo_kernel(True, nodes, halo, edges, send, recv, *made[n_packs:])
+    stores = [start(src, dst) for src, dst in zip(made[n_packs:], outs[n_packs:])]
+    for parts, src, dst in zip(loads, made, outs):
+        for copy in parts:
+            copy.wait()
+        stores.append(start(src, dst))
     if cut:
-        part, *rest = rest
-    halo_kernel(True, nodes, halo, edges, send, recv, *rest)
-    for copy in copies:
+        last = made[len(plans) - 1]
+        group = lax.axis_index("groups")
+        made[len(plans)][...] = jnp.where(group == 0, last[:, :cut], last[:, cut:])
+        stores.append(start(made[len(plans)], outs[len(plans)]))
+    for copy in stores:
         copy.wait()
-    if cut:
-        last = packs[-1]
-        group = lax.axis_index("groups")
-        part[...] = jnp.where(group == 0, last[:, :cut], last[:, cut:])
 
 
 def gather_kernel(tile, nodes, send, recv, sent, received):
@@ -224,7 +229,8 @@
     groups = take_groups(it, spots, cores)
     bias_in = None if layer == 0 else next(it)
     new_fine = next(it)
-    bias_out, aggs = (next(it), [next(it), next(it)]) if layer == 0 else (None, None)
+    bias_out = next(it) if layer == 0 else None
+    aggs = [next(it), next(it)]
     halo_tab = next(it)
 
     core = core_index()
@@ -256,10 +262,9 @@
         return carry
 
     loop(fine.shape[0] // tile, body)
-    if layer == 0:
-        for out, half in zip(aggs, (1 - core, core)):
-            place = place_in_half((count // 2, recv_row[...] - half * (count // 2)))
-            sum_rows(out, 0, [place], [new_fine[...]])
+    for out, half in zip(aggs, (1 - core, core)):
+        place = place_in_half((count // 2, recv_row[...] - half * (count // 2)))
+        sum_rows(out, 0, [place], [new_fine[...]])
 
 
 def coarse_target(state, width, me, cp):
@@ -267,18 +272,6 @@
     weights = jnp.where(lane == 2, float(DIGIT), jnp.where(lane == 3, 1.0, 0.0)).astype(jnp.bfloat16)
     near = dot_t(weights, state[:, width : width + LANES])[:1, :].astype(jnp.int32) - me * cp
     return jnp.where((near >= 0) & (near < cp), near * STRIDE, -1)
-
-
-def row_sums(base, out, new_fine, recv_row, state, target):
-    width = out.shape[1]
-    block = min(256, out.shape[0])
-    for spot in range(0, out.shape[0], block):
-        total = None
-        for places, latents in ((recv_row[...], new_fine[...]), (target, state[:, :width])):
-            rows = lax.broadcasted_iota(jnp.int32, (block, places.shape[1]), 0) + (base + spot)
-            part = dot((rows == places).astype(jnp.bfloat16), latents)
-            total = part if total is None else total + part
-        out[pl.ds(spot, block), :] = total.astype(out.dtype)
 
 
 def place_in_half(row):
@@ -314,7 +307,7 @@
     coarse_tab[pl.ds(pl.multiple_of(me * cp, cp), cp), :] = coarse_own[...]
     for i, pair in enumerate(arrived):
         owner = lax.rem(me + parts - 1 - i, parts)
-        skip = hh if i in (0, parts - 2) else 0
+        skip = hh if i in (0, parts - 2) or (parts == RELAYED and layer == 0) else 0
         for who, ref in zip((core, 1 - core), pair):
             spot = pl.multiple_of(owner * cp + who * ch, ch)
             coarse_tab[pl.ds(spot, ch), :] = ref[pl.ds(skip, ch), 0:width]
@@ -324,7 +317,8 @@
         unit = (lane == lax.broadcasted_iota(jnp.int32, (per, width), 0)).astype(jnp.bfloat16)
         blocks = [(given, 0)]
         for i, (ref, _) in enumerate(arrived):
-            blocks.append((ref, ch + (hh if i in (0, parts - 2) else 0)))
+            near = i in (0, parts - 2) or parts == RELAYED
+            blocks.append((ref, ch + (hh if near else 0)))
         for i, (ref, skip) in enumerate(blocks):
             rows = pl.ds(i * per, per)
             state[rows, :width] = ref[pl.ds(skip, per), :]
@@ -352,23 +346,13 @@
 
     loop(state.shape[0] // tile, body)
     target = coarse_target(state, width, me, cp)
-    if layer > 0:
-        row_sums((1 - core) * nh, aggs[0], new_fine, recv_row, state, target)
-        return
     latents = [new_fine[...], state[:, :width]]
     for out, half in zip(aggs, (1 - core, core)):
         places = [place_in_half((nh, at - half * nh)) for at in (recv_row[...], target)]
         sum_rows(out, nh - ch, places, latents)
 
 
-def own_kernel(cp, new_fine, recv_row, state, agg_own):
-    core, me = core_index(), lax.axis_index("mesh")
-    nh, width = agg_own.shape
-    target = coarse_target(state, width, me, cp)
-    row_sums(core * nh, agg_own, new_fine, recv_row, state, target)
-
-
-def node_kernel(tile, layer, cores, spots, n_sums, cut, start, *refs):
+def node_kernel(tile, layer, cores, spots, n_sums, cut, *refs):
     it = iter(refs)
     nodes, bias_ref, gain_ref = (next(it) for _ in range(3))
     sums = [[next(it) for _ in range(n)] for n in n_sums]
@@ -402,7 +386,7 @@
     half = nodes.shape[0] // 2
     for t in range(nh // tile):
         rows = pl.ds(t * tile, tile)
-        old = nodes[pl.ds(pl.multiple_of(core * half + start + t * tile, tile), tile), :]
+        old = nodes[pl.ds(pl.multiple_of(core * half + t * tile, tile), tile), :]
         x = jnp.concatenate([old, agg_ref[rows, :]], axis=1)
         y = mlp(x, groups, biases, gain)
         out[rows, :] = (old.astype(jnp.float32) + y).astype(jnp.bfloat16)
@@ -476,7 +460,7 @@
     starts = [0]
     for _, _, lanes in stream:
         starts.append(starts[-1] + lanes)
-    cuts = [0, starts[2] + PART, starts[4], starts[-1]]
+    cuts = [0, starts[2], starts[4], starts[-1]]
 
     def pieces(which):
         first, last = starts[which], starts[which + 1]
@@ -502,13 +486,18 @@
     near, far = hr // 2 + cp // 2 + block, cp // 2 + block
     shapes = [(w_hidden, n) for n in lanes] + ([(w_hidden, cut)] if cut else [])
     shapes += [(near, width), (near, width), (far, width), (cp, width), (block, width)]
+    small = [edge_b1, node_b1, nodes, halo_row, coarse_edges]
+    small += [x.reshape(1, own_coarse) for x in (coarse_send, coarse_recv)]
+    n_copies = len(small) + sum(len(p) for p in plans) + len(shapes)
     first_pack, *packs = call(
-        functools.partial(prepare_kernel, plans, cut),
+        functools.partial(prepare_kernel, plans, cut, len(small)),
         tuple(bf16(*shape) for shape in shapes),
-        [edge_w1, edge_w2, node_w1, node_w2, edge_b1, node_b1, nodes, halo_row, coarse_edges]
-        + [x.reshape(1, own_coarse) for x in (coarse_send, coarse_recv)],
-        scratch=[pltpu.SemaphoreType.DMA((sum(len(p) for p in plans),))],
-        memory=[pl.ANY] * 4 + [pltpu.VMEM] * 7,
+        [edge_w1, edge_w2, node_w1, node_w2, *small],
+        scratch=[pltpu.VMEM(x.shape, x.dtype) for x in small]
+        + [pltpu.VMEM(shape, jnp.bfloat16) for shape in shapes]
+        + [pltpu.SemaphoreType.DMA((n_copies,))],
+        memory=[pl.ANY] * (4 + len(small)),
+        out_memory=pl.ANY,
         limit=3 * VMEM_BYTES,
         name="weights_and_halo_rows",
     )
@@ -539,11 +528,15 @@
             name="halo_rows",
         )
 
-    def exchange(to_prev, to_next, coarse_half):
+    def exchange(to_prev, to_next, to_far, relayed=False):
         return [
-            shift({1: to_next, parts - 1: to_prev}.get(by, coarse_half), by)
+            shift({1: to_next, parts - 1: to_prev}.get(by, to_far), by)
             for by in range(1, parts)
+            if by in (1, parts - 1) or not relayed
         ]
+
+    def far_rows(moved):
+        return [shift(moved[0], 1)] if parts == RELAYED else moved[1:-1]
 
     def gather(nodes):
         return call(
@@ -557,9 +550,9 @@
     def fine_update(s, fine, sent, received, halo, weights, spots):
         outs = [bf16(fine_count, width)]
         if s == 0:
-            fine_rows = nh - cp // 2
             outs.append(jax.ShapeDtypeStruct((8, hidden), jnp.float32))
-            outs += [bf16(fine_rows, width), jax.ShapeDtypeStruct((fine_rows, width), jnp.float32)]
+        fine_rows = nh - cp // 2
+        outs += [bf16(fine_rows, width), jax.ShapeDtypeStruct((fine_rows, width), jnp.float32)]
         return call(
             functools.partial(fine_kernel, tile, sizes, spots, s),
             tuple(outs),
@@ -570,7 +563,7 @@
         )
 
     def coarse_update(s, new_fine, coarse_own, state, arrived, weights, spots):
-        aggs = [bf16(nh, width)] if s else [bf16(cp // 2, width), jax.ShapeDtypeStruct((cp // 2, width), jnp.float32)]
+        aggs = [bf16(cp // 2, width), jax.ShapeDtypeStruct((cp // 2, width), jnp.float32)]
         return call(
             functools.partial(coarse_kernel, ctile, sizes, spots, s),
             (bf16(coarse_count, width + LANES), *aggs),
@@ -580,20 +573,12 @@
             name="coarse_edges_and_sums",
         )
 
-    def own_sums(new_fine, state):
-        return call(
-            functools.partial(own_kernel, cp),
-            jax.ShapeDtypeStruct((nh, width), jnp.float32),
-            [new_fine, recv_row, state],
-            name="own_sums",
-        )
-
-    def node_update(s, nodes, sums, weights, spots, cut=0, start=0):
+    def node_update(s, nodes, sums, weights, spots, cut=0):
         far = [pltpu.VMEM((w_hidden, 2 * cut), jnp.bfloat16)] * 2 if cut else []
         rows = sum(part[0].shape[0] for part in sums)
         return both(
             call(
-                functools.partial(node_kernel, rows, s, cores, spots, [len(part) for part in sums], cut, start),
+                functools.partial(node_kernel, rows, s, cores, spots, [len(part) for part in sums], cut),
                 bf16(rows, width),
                 [nodes, bias_rows, node_gain] + [x for part in sums for x in part] + weights,
                 scratch=[pltpu.VMEM((rows, width), jnp.bfloat16), *far],
@@ -601,12 +586,8 @@
             )
         )
 
-    def core_sum(agg_own, agg_other, cuts=1):
-        rows = agg_own.shape[0] // cuts
-        parts = call(
-            add_kernel, (bf16(rows, width),) * cuts, [agg_own, swap(agg_other)], name="core_sum"
-        )
-        return parts if cuts > 1 else parts[0]
+    def core_sum(agg_own, agg_other):
+        return call(add_kernel, bf16(*agg_own.shape), [agg_own, swap(agg_other)], name="core_sum")
 
     def chip_sums(partial):
         if two:
@@ -622,20 +603,22 @@
         return [x for pair in zip(moved, swapped) for x in pair]
 
     far_first = spread(first_pack)
-    moved = exchange(to_prev, to_next, to_far)
+    moved = exchange(to_prev, to_next, to_far, parts == RELAYED)
     send_col, recv_col, recv_row, *packs = after(
         (send_col, recv_col, recv_row, *packs), to_prev
     )
     sent, received = gather(nodes)
     moved[0], moved[-1], far_first = after((moved[0], moved[-1], far_first), sent)
+    relayed = far_rows(moved)
     swapped = {i: swap(moved[i]) for i in (0, -1)}
     weights, spots = shards(first_pack, far_first), (((0, 0, k),), ((0, k, k + width),))
     far = spread(packs[0], far_first)
     fine_edges, bias_rows, other, own = fine_update(
         0, fine_edges, sent, received, halo_of(moved, swapped), weights, spots
     )
-    other, far, *moved[1:-1] = after((other, far, *moved[1:-1]))
-    swapped = [swapped[0], *(swap(m) for m in moved[1:-1]), swapped[-1]]
+    other, far, *relayed = after((other, far, *relayed))
+    swapped = [swapped[0], *(swap(m) for m in relayed), swapped[-1]]
+    moved = [moved[0], *relayed, moved[-1]]
     partial = core_sum(own, other)
     fine_edges, far = after((fine_edges, far), partial)
     packs_of = [shards(packs[0], far)]
@@ -655,29 +638,26 @@
     swapped = [swap(m) for m in moved]
     far = across(after(cut_part, far)) if cut else spread(packs[2], far)
     weights, spots = choose(packs_of, 3, 2)
-    (fine_edges,) = fine_update(
+    fine_edges, other, own = fine_update(
         1, fine_edges, sent, received, halo_of(moved, swapped), weights, spots
     )
-    fine_edges, far = after((fine_edges, far))
-    state, agg_other = coarse_update(
+    other, far = after((other, far))
+    partial = core_sum(own, other)
+    fine_part = chip_sums(partial)
+    state, other, own = coarse_update(
         1, fine_edges, coarse_own, state, pairs(moved, swapped), weights, spots
     )
-    agg_own = own_sums(fine_edges, state)
-    partial = core_sum(agg_own, agg_other, 2)
-    sums = [chip_sums(part) for part in partial]
     if cut:
         mine = both(far)
-        others = both(lax.ppermute(after(far, partial), "groups", [(0, 1), (1, 0)]))
-        weights = both(packs[2]) + pairs(mine, others)
+        others = lax.ppermute(far, "groups", [(0, 1), (1, 0)])
+        own, others = after((own, others))
+        weights = both(packs[2]) + pairs(mine, both(others))
         spots = [[(0, at - starts[4], at - starts[4] + n)] for at, n in zip(starts[4:], (kn, width))]
     else:
         packs_of.append(shards(packs[2], far))
         weights, spots = choose(packs_of, 4, 5)
-    halves = [
-        half
-        for i, part in enumerate(sums)
-        for half in node_update(1, nodes, [part], weights, spots, cut, i * nh // 2)
-    ]
+    sums = [fine_part, chip_sums(core_sum(own, other))]
+    halves = node_update(1, nodes, sums, weights, spots, cut)
     return call(join_kernel, bf16(count, width), halves, name="nodes_out")
 
 

time: 102 us -> 97.1 us (0.952)
  waiting for transfers between devices: 41.1 us -> 36.1 us
    ppermute x21, waiting for transfers between devices: 8.41 us -> 13.1 us  [swap(): return lax.ppermute(x, 'feat', [(i, i ^ 1) for i in range(cores)])]
    ppermute x8, waiting for transfers between devices: 16.2 us -> 12.6 us  [across(): return lax.ppermute(x, 'feat', [(i, i ^ 2) for i in range(cores)])]
    ppermute x1, waiting for transfers between devices: 3.39 us -> 0.01 us  [local(): others = lax.ppermute(far, 'groups', [(0, 1), (1, 0)])]
    ppermute x6, waiting for transfers between devices: 13.1 us -> 10.3 us  [shift(): lax.ppermute(x, 'mesh', [(i, (i + by) % parts) for i in range(parts)])]
    pallas_call x16 -> x15, Pallas kernels: 37.7 us -> 36.8 us  [call(): pl.pallas_call(kernel, out_shape=out_shape, in_specs=in_specs, out_specs=...]
  transfers between devices with their start and end apart: 36 -> 36, of which waited for: 20 -> 18; matrix products, arithmetic and copies ran while one was open for 1% -> 1% of each run, Pallas kernels for 27% -> 29%
where the time goes in v4:
time: 97.1 us; the launch traced here: 97 us
  Pallas kernels  36.8 us (38%)
  waiting for transfers between devices  36.1 us (37%)
  starting transfers between devices  23.1 us (24%)
    pallas_call x15, Pallas kernels, call(): pl.pallas_call(kernel, out_shape=out_shape, in_specs=in_specs, out_specs=...  36.8 us
    ppermute x21, waiting for transfers between devices, swap(): return lax.ppermute(x, 'feat', [(i, i ^ 1) for i in range(cores)])  13.1 us
    ppermute x8, waiting for transfers between devices, across(): return lax.ppermute(x, 'feat', [(i, i ^ 2) for i in range(cores)])  12.6 us
    ppermute x6, waiting for transfers between devices, shift(): lax.ppermute(x, 'mesh', [(i, (i + by) % parts) for i in range(parts)])  10.3 us
    ppermute x8, starting transfers between devices, across(): return lax.ppermute(x, 'feat', [(i, i ^ 2) for i in range(cores)])  9.13 us
    ppermute x6, starting transfers between devices, shift(): lax.ppermute(x, 'mesh', [(i, (i + by) % parts) for i in range(parts)])  9.11 us
    ppermute x21, starting transfers between devices, swap(): return lax.ppermute(x, 'feat', [(i, i ^ 1) for i in range(cores)])  3.35 us
  transfers between devices with their start and end apart: 36, of which 18 were waited for; matrix products, arithmetic and copies ran while one was open for 1% of the time, Pallas kernels for 29%

profile of v4, /device:TPU:0, one launch (start us, length us, event | category | flops | bytes accessed | tf_op | source)
XLA Modules:
  0.0 97.0 jit_solution(2758667831804347625)
XLA Ops:
  0.0 3.9 %weights_and_halo_rows.1 = (bf16[128,2176]{1,0:T(8,128)(2,1)}, bf16[128,1536]{1,0:T(8,128)(2,1)}, bf16[128,2048]{1,0:T(8,128)(2,1)}, bf16[128,1536]{1,0:T(8,128)...) custom-call(bf16[2,128,1536]{2,1,0:T(8,128)(2,1)} %refs_0_.3, ...), custom_call_target="tpu_custom_call" | custom-call | tf_op jit(solution)/shard_map/weights_and_halo_rows/pallas_call | solution.py:76
  3.9 3.0 %collective-permute-start.2 = (bf16[128,2176]{1,0:T(8,128)(2,1)}, bf16[128,2176]{1,0:T(8,128)(2,1)S(1)}, u32[]{:S(2)}, u32[]{:S(2)}) collective-permute-start(bf16[128,2176]{1,0:T(8,128)(2,1)} %get-tuple-element.70.refs_10_.refs_12_), channel_id=1, source_target_pairs={{0,2},{1,3},{2,0},{3,1},{4,6},{5,7},{6,4},{7,5},{8,10},{9,11},{10,... | collective-permute-start | bytes 1671176 | tf_op jit(solution)/shard_map/ppermute | solution.py:434
  7.0 3.6 %collective-permute-start.1 = (bf16[240,512]{1,0:T(8,128)(2,1)}, bf16[240,512]{1,0:T(8,128)(2,1)S(1)}, u32[]{:S(2)}, u32[]{:S(2)}) collective-permute-start(bf16[240,512]{1,0:T(8,128)(2,1)} %get-tuple-element.63), channel_id=1, source_target_pairs={{0,12},{4,0},{8,4},{12,8},{1,13},{5,1},{9,5},{13,9},{2,14},{6,2},{... | collective-permute-start | bytes 737288 | tf_op jit(solution)/shard_map/ppermute | solution.py:437
  11.3 3.5 %gather_rows.2 = (bf16[1536,512]{1,0:T(8,128)(2,1)S(1)}, bf16[1536,512]{1,0:T(8,128)(2,1)S(1)}) custom-call(bf16[1024,512]{1,0:T(8,128)(2,1)S(1)} %copy-done, s32[1536,1]{1,0:T(8,128)S(1)} %copy.17.send.refs_3_, s32[1536,1]{1,0:T(8,128)S(1)} %copy.18.recv), custom_call_target="tpu_custom_call" | custom-call | flops 3221225472 | tf_op jit(solution)/shard_map/gather_rows/pallas_call | solution.py:76
  14.8 2.4 %collective-permute-done.1.refs_8_.refs_10_ = bf16[240,512]{1,0:T(8,128)(2,1)S(1)} collective-permute-done((bf16[240,512]{1,0:T(8,128)(2,1)}, bf16[240,512]{1,0:T(8,128)(2,1)S(1)}, u32[]{:S(2)}, u32[]{:S(2)}) %collective-permute-start.1) | collective-permute-done | bytes 245792 | tf_op jit(solution)/shard_map/ppermute | solution.py:437
  17.2 5.7 %collective-permute-done.refs_6_ = bf16[240,512]{1,0:T(8,128)(2,1)} collective-permute-done((bf16[240,512]{1,0:T(8,128)(2,1)}, bf16[240,512]{1,0:T(8,128)(2,1)}, u32[]{:S(2)}, u32[]{:S(2)}) %collective-permute-start) | collective-permute-done | bytes 245792 | tf_op jit(solution)/shard_map/ppermute | solution.py:437
  24.0 1.6 %collective-permute-start.8 = (bf16[240,512]{1,0:T(8,128)(2,1)}, bf16[240,512]{1,0:T(8,128)(2,1)S(1)}, u32[]{:S(2)}, u32[]{:S(2)}) collective-permute-start(bf16[240,512]{1,0:T(8,128)(2,1)} %collective-permute-done.refs_6_), channel_id=1, source_target_pairs={{0,4},{4,8},{8,12},{12,0},{1,5},{5,9},{9,13},{13,1},{2,6},{6,10},{... | collective-permute-start | bytes 737288 | tf_op jit(solution)/shard_map/ppermute | solution.py:437
  25.7 7.2 %fine_edges.2 = (bf16[1536,512]{1,0:T(8,128)(2,1)S(1)}, f32[8,512]{1,0:T(8,128)S(1)}, bf16[448,512]{1,0:T(8,128)(2,1)S(1)}, f32[448,512]{1,0:T(8,128)S(1)}) custom-call(bf16[1536,512]{1,0:T(8,128)(2,1)S(1)} %copy-done.10, bf16[1536,512]{1,0:T(8,128)(2,1)S(1)} %get-tuple-element.66.refs_1_, bf16[1536,512]{1,0:T(8,128)(2,1)S(1)} %get-tuple-element.67.refs_2_, ...), custom_call_target="tpu_custom_call" | custom-call | flops 3221225472 | tf_op jit(solution)/shard_map/fine_edges/pallas_call | solution.py:76
  32.9 1.2 %collective-permute-done.8.refs_8_ = bf16[240,512]{1,0:T(8,128)(2,1)S(1)} collective-permute-done((bf16[240,512]{1,0:T(8,128)(2,1)}, bf16[240,512]{1,0:T(8,128)(2,1)S(1)}, u32[]{:S(2)}, u32[]{:S(2)}) %collective-permute-start.8) | collective-permute-done | bytes 245792 | tf_op jit(solution)/shard_map/ppermute | solution.py:437
  35.0 1.8 %collective-permute-done.9.arrived = bf16[448,512]{1,0:T(8,128)(2,1)S(1)} collective-permute-done((bf16[448,512]{1,0:T(8,128)(2,1)S(1)}, bf16[448,512]{1,0:T(8,128)(2,1)S(1)}, u32[]{:S(2)}, u32[]{:S(2)}) %collective-permute-start.9) | collective-permute-done | bytes 458784 | tf_op jit(solution)/shard_map/ppermute | solution.py:431
  38.1 2.1 %collective-permute-done.11.refs_9_ = bf16[240,512]{1,0:T(8,128)(2,1)S(1)} collective-permute-done((bf16[240,512]{1,0:T(8,128)(2,1)S(1)}, bf16[240,512]{1,0:T(8,128)(2,1)S(1)}, u32[]{:S(2)}, u32[]{:S(2)}) %collective-permute-start.11) | collective-permute-done | bytes 245792 | tf_op jit(solution)/shard_map/ppermute | solution.py:431
  40.2 4.1 %coarse_edges_and_sums.2 = (bf16[384,640]{1,0:T(8,128)(2,1)S(1)}, bf16[64,512]{1,0:T(8,128)(2,1)S(1)}, f32[64,512]{1,0:T(8,128)S(1)}) custom-call(bf16[1536,512]{1,0:T(8,128)(2,1)S(1)} %get-tuple-element.82.refs_0_, s32[1,1536]{1,0:T(1,128)S(1)} %reshape.20.refs_4_.refs_1_, bf16[128,512]{1,0:T(8,128)(2,1)S(1)} %copy-done.5, bf16[2,512]{1,0:T(2,128)(2,1)S(1)} %copy-done.7, ...), custom_call_target="tpu_custom_call" | custom-call | tf_op jit(solution)/shard_map/coarse_edges_and_sums/pallas_call | solution.py:76
  44.5 1.1 %collective-permute-done.12.arrived = bf16[64,512]{1,0:T(8,128)(2,1)S(1)} collective-permute-done((bf16[64,512]{1,0:T(8,128)(2,1)S(1)}, bf16[64,512]{1,0:T(8,128)(2,1)S(1)}, u32[]{:S(2)}, u32[]{:S(2)}) %collective-permute-start.12) | collective-permute-done | bytes 65568 | tf_op jit(solution)/shard_map/ppermute | solution.py:431
  45.6 1.5 %collective-permute-start.13 = (bf16[64,512]{1,0:T(8,128)(2,1)S(1)}, bf16[64,512]{1,0:T(8,128)(2,1)S(1)}, u32[]{:S(2)}, u32[]{:S(2)}) collective-permute-start(bf16[64,512]{1,0:T(8,128)(2,1)S(1)} %core_sum.5.refs_5_), channel_id=1, source_target_pairs={{0,2},{1,3},{2,0},{3,1},{4,6},{5,7},{6,4},{7,5},{8,10},{9,11},{10,... | collective-permute-start | bytes 196616 | tf_op jit(solution)/shard_map/ppermute | solution.py:434
  47.1 3.8 %collective-permute-done.13.refs_6_ = bf16[64,512]{1,0:T(8,128)(2,1)S(1)} collective-permute-done((bf16[64,512]{1,0:T(8,128)(2,1)S(1)}, bf16[64,512]{1,0:T(8,128)(2,1)S(1)}, u32[]{:S(2)}, u32[]{:S(2)}) %collective-permute-start.13) | collective-permute-done | bytes 65568 | tf_op jit(solution)/shard_map/ppermute | solution.py:434
  50.9 1.7 %node_update.2.refs_0_ = bf16[512,512]{1,0:T(8,128)(2,1)S(1)} custom-call(bf16[1024,512]{1,0:T(8,128)(2,1)S(1)} %copy-done, f32[8,512]{1,0:T(8,128)S(1)} %get-tuple-element.74.refs_4_.refs_1_.refs_14_, bf16[2,512]{1,0:T(2,128)(2,1)S(1)} %copy-done.8, bf16[448,512]{1,0:T(8,128)(2,1)S(1)} %core_sum.4.refs_3_, ...), custom_call_target="tpu_custom_call" | custom-call | tf_op jit(solution)/shard_map/node_update/pallas_call | solution.py:76
  53.5 1.1 %collective-permute-done.16.refs_1_ = bf16[512,512]{1,0:T(8,128)(2,1)S(1)} collective-permute-done((bf16[512,512]{1,0:T(8,128)(2,1)S(1)}, bf16[512,512]{1,0:T(8,128)(2,1)S(1)}, u32[]{:S(2)}, u32[]{:S(2)}) %collective-permute-start.16) | collective-permute-done | bytes 524320 | tf_op jit(solution)/shard_map/ppermute | solution.py:431
  55.3 1.7 %collective-permute-start.17 = (bf16[128,512]{1,0:T(8,128)(2,1)S(1)}, bf16[128,512]{1,0:T(8,128)(2,1)S(1)}, u32[]{:S(2)}, u32[]{:S(2)}) collective-permute-start(bf16[128,512]{1,0:T(8,128)(2,1)S(1)} %get-tuple-element.92), channel_id=1, source_target_pairs={{0,4},{4,8},{8,12},{12,0},{1,5},{5,9},{9,13},{13,1},{2,6},{6,10},{... | collective-permute-start | bytes 393224 | tf_op jit(solution)/shard_map/ppermute | solution.py:437
  57.0 2.2 %collective-permute-start.19 = (bf16[128,512]{1,0:T(8,128)(2,1)S(1)}, bf16[128,512]{1,0:T(8,128)(2,1)S(1)}, u32[]{:S(2)}, u32[]{:S(2)}) collective-permute-start(bf16[128,512]{1,0:T(8,128)(2,1)S(1)} %get-tuple-element.94), channel_id=1, source_target_pairs={{0,12},{4,0},{8,4},{12,8},{1,13},{5,1},{9,5},{13,9},{2,14},{6,2},{... | collective-permute-start | bytes 393224 | tf_op jit(solution)/shard_map/ppermute | solution.py:437
  59.2 3.5 %gather_rows.3 = (bf16[1536,512]{1,0:T(8,128)(2,1)S(1)}, bf16[1536,512]{1,0:T(8,128)(2,1)S(1)}) custom-call(bf16[1024,512]{1,0:T(8,128)(2,1)S(1)} %get-tuple-element.89.nodes.refs_0_, s32[1536,1]{1,0:T(8,128)S(1)} %copy.17.send.refs_3_, s32[1536,1]{1,0:T(8,128)S(1)} %copy.18.recv), custom_call_target="tpu_custom_call" | custom-call | flops 3221225472 | tf_op jit(solution)/shard_map/gather_rows/pallas_call | solution.py:76
  62.7 4.3 %collective-permute-done.20.refs_12_.refs_14_ = bf16[128,2048]{1,0:T(8,128)(2,1)S(1)} collective-permute-done((bf16[128,2048]{1,0:T(8,128)(2,1)S(1)}, bf16[128,2048]{1,0:T(8,128)(2,1)S(1)}, u32[]{:S(2)}, u32[]{:S(2)}) %collective-permute-start.20) | collective-permute-done | bytes 524320 | tf_op jit(solution)/shard_map/ppermute | solution.py:434
  70.2 6.0 %fine_edges.3 = (bf16[1536,512]{1,0:T(8,128)(2,1)S(1)}, bf16[448,512]{1,0:T(8,128)(2,1)S(1)}, f32[448,512]{1,0:T(8,128)S(1)}) custom-call(bf16[1536,512]{1,0:T(8,128)(2,1)S(1)} %get-tuple-element.82.refs_0_, bf16[1536,512]{1,0:T(8,128)(2,1)S(1)} %get-tuple-element.90.refs_1_, bf16[1536,512]{1,0:T(8,128)(2,1)S(1)} %get-tuple-element.91.refs_2_, ...), custom_call_target="tpu_custom_call" | custom-call | flops 3221225472 | tf_op jit(solution)/shard_map/fine_edges/pallas_call | solution.py:76
  76.4 1.7 %collective-permute-done.26.arrived = bf16[448,512]{1,0:T(8,128)(2,1)S(1)} collective-permute-done((bf16[448,512]{1,0:T(8,128)(2,1)S(1)}, bf16[448,512]{1,0:T(8,128)(2,1)S(1)}, u32[]{:S(2)}, u32[]{:S(2)}) %collective-permute-start.26) | collective-permute-done | bytes 458784 | tf_op jit(solution)/shard_map/ppermute | solution.py:431
  78.9 1.5 %collective-permute-start.29 = (bf16[128,768]{1,0:T(8,128)(2,1)S(1)}, bf16[128,768]{1,0:T(8,128)(2,1)S(1)}, u32[]{:S(2)}, u32[]{:S(2)}) collective-permute-start(bf16[128,768]{1,0:T(8,128)(2,1)S(1)} %collective-permute-done.25.refs_9_), channel_id=1, source_target_pairs={{0,16},{16,0},{1,17},{17,1},{2,18},{18,2},{3,19},{19,3},{4,20},{20... | collective-permute-start | bytes 589832 | tf_op jit(solution)/shard_map/ppermute | solution.py:652
  80.9 1.3 %collective-permute-done.28.refs_9_ = bf16[64,512]{1,0:T(8,128)(2,1)S(1)} collective-permute-done((bf16[64,512]{1,0:T(8,128)(2,1)S(1)}, bf16[64,512]{1,0:T(8,128)(2,1)S(1)}, u32[]{:S(2)}, u32[]{:S(2)}) %collective-permute-start.28) | collective-permute-done | bytes 65568 | tf_op jit(solution)/shard_map/ppermute | solution.py:431
  82.2 3.3 %coarse_edges_and_sums.3 = (bf16[384,640]{1,0:T(8,128)(2,1)}, bf16[64,512]{1,0:T(8,128)(2,1)S(1)}, f32[64,512]{1,0:T(8,128)S(1)}) custom-call(bf16[1536,512]{1,0:T(8,128)(2,1)S(1)} %get-tuple-element.105.refs_0_, s32[1,1536]{1,0:T(1,128)S(1)} %reshape.20.refs_4_.refs_1_, bf16[128,512]{1,0:T(8,128)(2,1)S(1)} %get-tuple-element.106.refs_2_, ...), custom_call_target="tpu_custom_call" | custom-call | tf_op jit(solution)/shard_map/coarse_edges_and_sums/pallas_call | solution.py:76
  86.0 1.0 %collective-permute-done.30.arrived = bf16[64,512]{1,0:T(8,128)(2,1)S(1)} collective-permute-done((bf16[64,512]{1,0:T(8,128)(2,1)S(1)}, bf16[64,512]{1,0:T(8,128)(2,1)S(1)}, u32[]{:S(2)}, u32[]{:S(2)}) %collective-permute-start.30) | collective-permute-done | bytes 65568 | tf_op jit(solution)/shard_map/ppermute | solution.py:431
  87.1 1.5 %collective-permute-start.31 = (bf16[64,512]{1,0:T(8,128)(2,1)S(1)}, bf16[64,512]{1,0:T(8,128)(2,1)S(1)}, u32[]{:S(2)}, u32[]{:S(2)}) collective-permute-start(bf16[64,512]{1,0:T(8,128)(2,1)S(1)} %core_sum.7.refs_5_), channel_id=1, source_target_pairs={{0,2},{1,3},{2,0},{3,1},{4,6},{5,7},{6,4},{7,5},{8,10},{9,11},{10,... | collective-permute-start | bytes 196616 | tf_op jit(solution)/shard_map/ppermute | solution.py:434
  88.6 3.6 %collective-permute-done.31.refs_6_ = bf16[64,512]{1,0:T(8,128)(2,1)S(1)} collective-permute-done((bf16[64,512]{1,0:T(8,128)(2,1)S(1)}, bf16[64,512]{1,0:T(8,128)(2,1)S(1)}, u32[]{:S(2)}, u32[]{:S(2)}) %collective-permute-start.31) | collective-permute-done | bytes 65568 | tf_op jit(solution)/shard_map/ppermute | solution.py:434
  92.2 1.7 %node_update.3.own = bf16[512,512]{1,0:T(8,128)(2,1)S(1)} custom-call(bf16[1024,512]{1,0:T(8,128)(2,1)S(1)} %get-tuple-element.89.nodes.refs_0_, f32[8,512]{1,0:T(8,128)S(1)} %get-tuple-element.74.refs_4_.refs_1_.refs_14_, bf16[2,512]{1,0:T(2,128)(2,1)S(1)} %copy-done.8, bf16[448,512]{1,0:T(8,128)(2,1)S(1)} %core_sum.6.refs_3_, ...), custom_call_target="tpu_custom_call" | custom-call | tf_op jit(solution)/shard_map/node_update/pallas_call | solution.py:76
  94.0 1.9 %collective-permute-done.35.other = bf16[512,512]{1,0:T(8,128)(2,1)S(1)} collective-permute-done((bf16[512,512]{1,0:T(8,128)(2,1)S(1)}, bf16[512,512]{1,0:T(8,128)(2,1)S(1)}, u32[]{:S(2)}, u32[]{:S(2)}) %collective-permute-start.35) | collective-permute-done | bytes 524320 | tf_op jit(solution)/shard_map/ppermute | solution.py:431
  95.9 1.1 %nodes_out.1 = bf16[1024,512]{1,0:T(8,128)(2,1)} custom-call(bf16[512,512]{1,0:T(8,128)(2,1)S(1)} %node_update.3.own, bf16[512,512]{1,0:T(8,128)(2,1)S(1)} %collective-permute-done.35.other), custom_call_target="tpu_custom_call" | custom-call | tf_op jit(solution)/shard_map/nodes_out/pallas_call | solution.py:76
  (88 shorter events, 11.0 us)
Async XLA Ops:
  3.9 19.0 %collective-permute-start.2 = (bf16[128,2176]{1,0:T(8,128)(2,1)}, bf16[128,2176]{1,0:T(8,128)(2,1)S(1)}, u32[]{:S(2)}, u32[]{:S(2)}) collective-permute-start(bf16[128,2176]{1,0:T(8,128)(2,1)} %get-tuple-element.70.refs_10_.refs_12_), channel_id=1, source_target_pairs={{0,2},{1,3},{2,0},{3,1},{4,6},{5,7},{6,4},{7,5},{8,10},{9,11},{10,... | collective-permute-start | bytes 1671176 | tf_op jit(solution)/shard_map/ppermute | solution.py:434
  7.0 17.0 %collective-permute-start.5 = (bf16[128,2176]{1,0:T(8,128)(2,1)}, bf16[128,2176]{1,0:T(8,128)(2,1)}, u32[]{:S(2)}, u32[]{:S(2)}) collective-permute-start(bf16[128,2176]{1,0:T(8,128)(2,1)} %get-tuple-element.70.refs_10_.refs_12_), channel_id=1, source_target_pairs={{0,1},{1,0},{2,3},{3,2},{4,5},{5,4},{6,7},{7,6},{8,9},{9,8},{10,11... | collective-permute-start | bytes 1671176 | tf_op jit(solution)/shard_map/ppermute | solution.py:431
  7.0 10.2 %collective-permute-start.1 = (bf16[240,512]{1,0:T(8,128)(2,1)}, bf16[240,512]{1,0:T(8,128)(2,1)S(1)}, u32[]{:S(2)}, u32[]{:S(2)}) collective-permute-start(bf16[240,512]{1,0:T(8,128)(2,1)} %get-tuple-element.63), channel_id=1, source_target_pairs={{0,12},{4,0},{8,4},{12,8},{1,13},{5,1},{9,5},{13,9},{2,14},{6,2},{... | collective-permute-start | bytes 737288 | tf_op jit(solution)/shard_map/ppermute | solution.py:437
  10.6 12.4 %collective-permute-start = (bf16[240,512]{1,0:T(8,128)(2,1)}, bf16[240,512]{1,0:T(8,128)(2,1)}, u32[]{:S(2)}, u32[]{:S(2)}) collective-permute-start(bf16[240,512]{1,0:T(8,128)(2,1)} %get-tuple-element.69), channel_id=1, source_target_pairs={{0,4},{4,8},{8,12},{12,0},{1,5},{5,9},{9,13},{13,1},{2,6},{6,10},{... | collective-permute-start | bytes 737288 | tf_op jit(solution)/shard_map/ppermute | solution.py:437
  22.9 2.7 %collective-permute-start.6 = (bf16[128,2176]{1,0:T(8,128)(2,1)S(1)}, bf16[128,2176]{1,0:T(8,128)(2,1)S(1)}, u32[]{:S(2)}, u32[]{:S(2)}) collective-permute-start(bf16[128,2176]{1,0:T(8,128)(2,1)S(1)} %collective-permute-done.2.refs_12_.refs_14_), channel_id=1, source_target_pairs={{0,1},{1,0},{2,3},{3,2},{4,5},{5,4},{6,7},{7,6},{8,9},{9,8},{10,11... | collective-permute-start | bytes 1671176 | tf_op jit(solution)/shard_map/ppermute | solution.py:431
  22.9 2.7 %collective-permute-start.3 = (bf16[240,512]{1,0:T(8,128)(2,1)}, bf16[240,512]{1,0:T(8,128)(2,1)S(1)}, u32[]{:S(2)}, u32[]{:S(2)}) collective-permute-start(bf16[240,512]{1,0:T(8,128)(2,1)} %collective-permute-done.refs_6_), channel_id=1, source_target_pairs={{0,1},{1,0},{2,3},{3,2},{4,5},{5,4},{6,7},{7,6},{8,9},{9,8},{10,11... | collective-permute-start | bytes 737288 | tf_op jit(solution)/shard_map/ppermute | solution.py:431
  23.5 2.2 %collective-permute-start.4 = (bf16[240,512]{1,0:T(8,128)(2,1)S(1)}, bf16[240,512]{1,0:T(8,128)(2,1)S(1)}, u32[]{:S(2)}, u32[]{:S(2)}) collective-permute-start(bf16[240,512]{1,0:T(8,128)(2,1)S(1)} %collective-permute-done.1.refs_8_.refs_10_), channel_id=1, source_target_pairs={{0,1},{1,0},{2,3},{3,2},{4,5},{5,4},{6,7},{7,6},{8,9},{9,8},{10,11... | collective-permute-start | bytes 737288 | tf_op jit(solution)/shard_map/ppermute | solution.py:431
  23.5 11.5 %collective-permute-start.7 = (bf16[128,1536]{1,0:T(8,128)(2,1)S(1)}, bf16[128,1536]{1,0:T(8,128)(2,1)S(1)}, u32[]{:S(2)}, u32[]{:S(2)}) collective-permute-start(bf16[128,1536]{1,0:T(8,128)(2,1)S(1)} %copy-done.4), channel_id=1, source_target_pairs={{0,2},{1,3},{2,0},{3,1},{4,6},{5,7},{6,4},{7,5},{8,10},{9,11},{10,... | collective-permute-start | bytes 1179656 | tf_op jit(solution)/shard_map/ppermute | solution.py:434
  24.0 10.1 %collective-permute-start.8 = (bf16[240,512]{1,0:T(8,128)(2,1)}, bf16[240,512]{1,0:T(8,128)(2,1)S(1)}, u32[]{:S(2)}, u32[]{:S(2)}) collective-permute-start(bf16[240,512]{1,0:T(8,128)(2,1)} %collective-permute-done.refs_6_), channel_id=1, source_target_pairs={{0,4},{4,8},{8,12},{12,0},{1,5},{5,9},{9,13},{13,1},{2,6},{6,10},{... | collective-permute-start | bytes 737288 | tf_op jit(solution)/shard_map/ppermute | solution.py:437
  35.0 1.8 %collective-permute-start.9 = (bf16[448,512]{1,0:T(8,128)(2,1)S(1)}, bf16[448,512]{1,0:T(8,128)(2,1)S(1)}, u32[]{:S(2)}, u32[]{:S(2)}) collective-permute-start(bf16[448,512]{1,0:T(8,128)(2,1)S(1)} %get-tuple-element.79), channel_id=1, source_target_pairs={{0,1},{1,0},{2,3},{3,2},{4,5},{5,4},{6,7},{7,6},{8,9},{9,8},{10,11... | collective-permute-start | bytes 1376264 | tf_op jit(solution)/shard_map/ppermute | solution.py:431
  36.9 14.0 %collective-permute-start.10 = (bf16[448,512]{1,0:T(8,128)(2,1)S(1)}, bf16[448,512]{1,0:T(8,128)(2,1)S(1)}, u32[]{:S(2)}, u32[]{:S(2)}) collective-permute-start(bf16[448,512]{1,0:T(8,128)(2,1)S(1)} %core_sum.4.refs_3_), channel_id=1, source_target_pairs={{0,2},{1,3},{2,0},{3,1},{4,6},{5,7},{6,4},{7,5},{8,10},{9,11},{10,... | collective-permute-start | bytes 1376264 | tf_op jit(solution)/shard_map/ppermute | solution.py:434
  37.6 9.6 %collective-permute-start.14 = (bf16[128,1536]{1,0:T(8,128)(2,1)S(1)}, bf16[128,1536]{1,0:T(8,128)(2,1)S(1)}, u32[]{:S(2)}, u32[]{:S(2)}) collective-permute-start(bf16[128,1536]{1,0:T(8,128)(2,1)S(1)} %copy-done.4), channel_id=1, source_target_pairs={{0,1},{1,0},{2,3},{3,2},{4,5},{5,4},{6,7},{7,6},{8,9},{9,8},{10,11... | collective-permute-start | bytes 1179656 | tf_op jit(solution)/shard_map/ppermute | solution.py:431
  37.6 13.4 %collective-permute-start.15 = (bf16[128,1536]{1,0:T(8,128)(2,1)S(1)}, bf16[128,1536]{1,0:T(8,128)(2,1)S(1)}, u32[]{:S(2)}, u32[]{:S(2)}) collective-permute-start(bf16[128,1536]{1,0:T(8,128)(2,1)S(1)} %collective-permute-done.7.refs_9_), channel_id=1, source_target_pairs={{0,1},{1,0},{2,3},{3,2},{4,5},{5,4},{6,7},{7,6},{8,9},{9,8},{10,11... | collective-permute-start | bytes 1179656 | tf_op jit(solution)/shard_map/ppermute | solution.py:431
  38.1 2.1 %collective-permute-start.11 = (bf16[240,512]{1,0:T(8,128)(2,1)S(1)}, bf16[240,512]{1,0:T(8,128)(2,1)S(1)}, u32[]{:S(2)}, u32[]{:S(2)}) collective-permute-start(bf16[240,512]{1,0:T(8,128)(2,1)S(1)} %collective-permute-done.8.refs_8_), channel_id=1, source_target_pairs={{0,1},{1,0},{2,3},{3,2},{4,5},{5,4},{6,7},{7,6},{8,9},{9,8},{10,11... | collective-permute-start | bytes 737288 | tf_op jit(solution)/shard_map/ppermute | solution.py:431
  45.6 5.3 %collective-permute-start.13 = (bf16[64,512]{1,0:T(8,128)(2,1)S(1)}, bf16[64,512]{1,0:T(8,128)(2,1)S(1)}, u32[]{:S(2)}, u32[]{:S(2)}) collective-permute-start(bf16[64,512]{1,0:T(8,128)(2,1)S(1)} %core_sum.5.refs_5_), channel_id=1, source_target_pairs={{0,2},{1,3},{2,0},{3,1},{4,6},{5,7},{6,4},{7,5},{8,10},{9,11},{10,... | collective-permute-start | bytes 196616 | tf_op jit(solution)/shard_map/ppermute | solution.py:434
  52.6 2.0 %collective-permute-start.16 = (bf16[512,512]{1,0:T(8,128)(2,1)S(1)}, bf16[512,512]{1,0:T(8,128)(2,1)S(1)}, u32[]{:S(2)}, u32[]{:S(2)}) collective-permute-start(bf16[512,512]{1,0:T(8,128)(2,1)S(1)} %node_update.2.refs_0_), channel_id=1, source_target_pairs={{0,1},{1,0},{2,3},{3,2},{4,5},{5,4},{6,7},{7,6},{8,9},{9,8},{10,11... | collective-permute-start | bytes 1572872 | tf_op jit(solution)/shard_map/ppermute | solution.py:431
  52.7 14.3 %collective-permute-start.20 = (bf16[128,2048]{1,0:T(8,128)(2,1)S(1)}, bf16[128,2048]{1,0:T(8,128)(2,1)S(1)}, u32[]{:S(2)}, u32[]{:S(2)}) collective-permute-start(bf16[128,2048]{1,0:T(8,128)(2,1)S(1)} %copy-done.2), channel_id=1, source_target_pairs={{0,2},{1,3},{2,0},{3,1},{4,6},{5,7},{6,4},{7,5},{8,10},{9,11},{10,... | collective-permute-start | bytes 1572872 | tf_op jit(solution)/shard_map/ppermute | solution.py:434
  53.4 15.7 %collective-permute-start.23 = (bf16[128,2048]{1,0:T(8,128)(2,1)S(1)}, bf16[128,2048]{1,0:T(8,128)(2,1)S(1)}, u32[]{:S(2)}, u32[]{:S(2)}) collective-permute-start(bf16[128,2048]{1,0:T(8,128)(2,1)S(1)} %copy-done.2), channel_id=1, source_target_pairs={{0,1},{1,0},{2,3},{3,2},{4,5},{5,4},{6,7},{7,6},{8,9},{9,8},{10,11... | collective-permute-start | bytes 1572872 | tf_op jit(solution)/shard_map/ppermute | solution.py:431
  55.3 12.6 %collective-permute-start.17 = (bf16[128,512]{1,0:T(8,128)(2,1)S(1)}, bf16[128,512]{1,0:T(8,128)(2,1)S(1)}, u32[]{:S(2)}, u32[]{:S(2)}) collective-permute-start(bf16[128,512]{1,0:T(8,128)(2,1)S(1)} %get-tuple-element.92), channel_id=1, source_target_pairs={{0,4},{4,8},{8,12},{12,0},{1,5},{5,9},{9,13},{13,1},{2,6},{6,10},{... | collective-permute-start | bytes 393224 | tf_op jit(solution)/shard_map/ppermute | solution.py:437
  57.0 10.9 %collective-permute-start.19 = (bf16[128,512]{1,0:T(8,128)(2,1)S(1)}, bf16[128,512]{1,0:T(8,128)(2,1)S(1)}, u32[]{:S(2)}, u32[]{:S(2)}) collective-permute-start(bf16[128,512]{1,0:T(8,128)(2,1)S(1)} %get-tuple-element.94), channel_id=1, source_target_pairs={{0,12},{4,0},{8,4},{12,8},{1,13},{5,1},{9,5},{13,9},{2,14},{6,2},{... | collective-permute-start | bytes 393224 | tf_op jit(solution)/shard_map/ppermute | solution.py:437
  59.2 8.7 %collective-permute-start.18 = (bf16[64,512]{1,0:T(8,128)(2,1)S(1)}, bf16[64,512]{1,0:T(8,128)(2,1)S(1)}, u32[]{:S(2)}, u32[]{:S(2)}) collective-permute-start(bf16[64,512]{1,0:T(8,128)(2,1)S(1)} %get-tuple-element.93), channel_id=1, source_target_pairs={{0,8},{4,12},{8,0},{12,4},{1,9},{5,13},{9,1},{13,5},{2,10},{6,14},... | collective-permute-start | bytes 196616 | tf_op jit(solution)/shard_map/ppermute | solution.py:437
  67.9 2.3 %collective-permute-start.24 = (bf16[128,2048]{1,0:T(8,128)(2,1)S(1)}, bf16[128,2048]{1,0:T(8,128)(2,1)S(1)}, u32[]{:S(2)}, u32[]{:S(2)}) collective-permute-start(bf16[128,2048]{1,0:T(8,128)(2,1)S(1)} %collective-permute-done.20.refs_12_.refs_14_), channel_id=1, source_target_pairs={{0,1},{1,0},{2,3},{3,2},{4,5},{5,4},{6,7},{7,6},{8,9},{9,8},{10,11... | collective-permute-start | bytes 1572872 | tf_op jit(solution)/shard_map/ppermute | solution.py:431
  67.9 2.1 %collective-permute-start.21 = (bf16[128,512]{1,0:T(8,128)(2,1)S(1)}, bf16[128,512]{1,0:T(8,128)(2,1)S(1)}, u32[]{:S(2)}, u32[]{:S(2)}) collective-permute-start(bf16[128,512]{1,0:T(8,128)(2,1)S(1)} %collective-permute-done.17.refs_6_), channel_id=1, source_target_pairs={{0,1},{1,0},{2,3},{3,2},{4,5},{5,4},{6,7},{7,6},{8,9},{9,8},{10,11... | collective-permute-start | bytes 393224 | tf_op jit(solution)/shard_map/ppermute | solution.py:431
  68.5 7.7 %collective-permute-start.25 = (bf16[128,768]{1,0:T(8,128)(2,1)S(1)}, bf16[128,768]{1,0:T(8,128)(2,1)S(1)}, u32[]{:S(2)}, u32[]{:S(2)}) collective-permute-start(bf16[128,768]{1,0:T(8,128)(2,1)S(1)} %copy-done.13), channel_id=1, source_target_pairs={{0,2},{1,3},{2,0},{3,1},{4,6},{5,7},{6,4},{7,5},{8,10},{9,11},{10,... | collective-permute-start | bytes 589832 | tf_op jit(solution)/shard_map/ppermute | solution.py:434
  76.2 1.9 %collective-permute-start.26 = (bf16[448,512]{1,0:T(8,128)(2,1)S(1)}, bf16[448,512]{1,0:T(8,128)(2,1)S(1)}, u32[]{:S(2)}, u32[]{:S(2)}) collective-permute-start(bf16[448,512]{1,0:T(8,128)(2,1)S(1)} %get-tuple-element.104), channel_id=1, source_target_pairs={{0,1},{1,0},{2,3},{3,2},{4,5},{5,4},{6,7},{7,6},{8,9},{9,8},{10,11... | collective-permute-start | bytes 1376264 | tf_op jit(solution)/shard_map/ppermute | solution.py:431
  78.2 14.0 %collective-permute-start.27 = (bf16[448,512]{1,0:T(8,128)(2,1)S(1)}, bf16[448,512]{1,0:T(8,128)(2,1)S(1)}, u32[]{:S(2)}, u32[]{:S(2)}) collective-permute-start(bf16[448,512]{1,0:T(8,128)(2,1)S(1)} %core_sum.6.refs_3_), channel_id=1, source_target_pairs={{0,2},{1,3},{2,0},{3,1},{4,6},{5,7},{6,4},{7,5},{8,10},{9,11},{10,... | collective-permute-start | bytes 1376264 | tf_op jit(solution)/shard_map/ppermute | solution.py:434
  78.9 6.7 %collective-permute-start.29 = (bf16[128,768]{1,0:T(8,128)(2,1)S(1)}, bf16[128,768]{1,0:T(8,128)(2,1)S(1)}, u32[]{:S(2)}, u32[]{:S(2)}) collective-permute-start(bf16[128,768]{1,0:T(8,128)(2,1)S(1)} %collective-permute-done.25.refs_9_), channel_id=1, source_target_pairs={{0,16},{16,0},{1,17},{17,1},{2,18},{18,2},{3,19},{19,3},{4,20},{20... | collective-permute-start | bytes 589832 | tf_op jit(solution)/shard_map/ppermute | solution.py:652
  80.4 8.2 %collective-permute-start.32 = (bf16[128,1536]{1,0:T(8,128)(2,1)S(1)}, bf16[128,1536]{1,0:T(8,128)(2,1)S(1)}, u32[]{:S(2)}, u32[]{:S(2)}) collective-permute-start(bf16[128,1536]{1,0:T(8,128)(2,1)S(1)} %copy-done.3), channel_id=1, source_target_pairs={{0,1},{1,0},{2,3},{3,2},{4,5},{5,4},{6,7},{7,6},{8,9},{9,8},{10,11... | collective-permute-start | bytes 1179656 | tf_op jit(solution)/shard_map/ppermute | solution.py:431
  80.9 7.7 %collective-permute-start.33 = (bf16[128,768]{1,0:T(8,128)(2,1)S(1)}, bf16[128,768]{1,0:T(8,128)(2,1)S(1)}, u32[]{:S(2)}, u32[]{:S(2)}) collective-permute-start(bf16[128,768]{1,0:T(8,128)(2,1)S(1)} %collective-permute-done.25.refs_9_), channel_id=1, source_target_pairs={{0,1},{1,0},{2,3},{3,2},{4,5},{5,4},{6,7},{7,6},{8,9},{9,8},{10,11... | collective-permute-start | bytes 589832 | tf_op jit(solution)/shard_map/ppermute | solution.py:431
  85.5 6.7 %collective-permute-start.34 = (bf16[128,768]{1,0:T(8,128)(2,1)S(1)}, bf16[128,768]{1,0:T(8,128)(2,1)S(1)}, u32[]{:S(2)}, u32[]{:S(2)}) collective-permute-start(bf16[128,768]{1,0:T(8,128)(2,1)S(1)} %collective-permute-done.29.refs_10_), channel_id=1, source_target_pairs={{0,1},{1,0},{2,3},{3,2},{4,5},{5,4},{6,7},{7,6},{8,9},{9,8},{10,11... | collective-permute-start | bytes 589832 | tf_op jit(solution)/shard_map/ppermute | solution.py:431
  87.1 5.2 %collective-permute-start.31 = (bf16[64,512]{1,0:T(8,128)(2,1)S(1)}, bf16[64,512]{1,0:T(8,128)(2,1)S(1)}, u32[]{:S(2)}, u32[]{:S(2)}) collective-permute-start(bf16[64,512]{1,0:T(8,128)(2,1)S(1)} %core_sum.7.refs_5_), channel_id=1, source_target_pairs={{0,2},{1,3},{2,0},{3,1},{4,6},{5,7},{6,4},{7,5},{8,10},{9,11},{10,... | collective-permute-start | bytes 196616 | tf_op jit(solution)/shard_map/ppermute | solution.py:434
  93.9 2.0 %collective-permute-start.35 = (bf16[512,512]{1,0:T(8,128)(2,1)S(1)}, bf16[512,512]{1,0:T(8,128)(2,1)S(1)}, u32[]{:S(2)}, u32[]{:S(2)}) collective-permute-start(bf16[512,512]{1,0:T(8,128)(2,1)S(1)} %node_update.3.own), channel_id=1, source_target_pairs={{0,1},{1,0},{2,3},{3,2},{4,5},{5,4},{6,7},{7,6},{8,9},{9,8},{10,11... | collective-permute-start | bytes 1572872 | tf_op jit(solution)/shard_map/ppermute | solution.py:431
  (18 other events, 149.0 us)

commit v5 on v4

--- a/solution.py
+++ b/solution.py
@@ -99,8 +99,15 @@
     out[pl.ds(pl.multiple_of((1 - core) * nh, nh), nh), :] = other[...]
 
 
-def join_kernel(own, other, out):
-    join_halves(out, own, other)
+def join_kernel(own, other, out, sems):
+    core, nh = core_index(), own.shape[0]
+    copies = []
+    for i, (half, ref) in enumerate(((core, own), (1 - core, other))):
+        spot = out.at[pl.ds(pl.multiple_of(half * nh, nh), nh), :]
+        copies.append(pltpu.make_async_copy(ref, spot, sems.at[i]))
+        copies[i].start()
+    for copy in copies:
+        copy.wait()
 
 
 def add_kernel(own, arrived, out):
@@ -127,16 +134,15 @@
 
 def halo_kernel(first, *refs):
     if first:
-        nodes, halo, edges, send, recv, *outs, coarse, block = refs
+        nodes, halo, edges, send, recv, to_prev, to_next, *far, coarse, block = refs
         count, width = edges.shape
         block[0:count, :] = edges[...]
         digits = [index_digits(ref, width) for ref in (send, recv)]
         digits.append(jnp.zeros((16 - 4, width), jnp.float32))
         block[count : count + 16, :] = jnp.concatenate(digits).astype(jnp.bfloat16)
     else:
-        own, other, halo, *outs, coarse, nodes = refs
+        own, other, halo, to_prev, to_next, *far, coarse, nodes = refs
         join_halves(nodes, own, other)
-    to_prev, to_next, to_far = outs
     core = core_index()
     count = nodes.shape[0]
     hr, cp = halo.shape[1] // 2, coarse.shape[0]
@@ -150,14 +156,15 @@
     mine = coarse[pl.ds(pl.multiple_of(core * ch, ch), ch), :]
     to_prev[pl.ds(0, hh), :] = rows[:hh]
     to_next[pl.ds(0, hh), :] = rows[hh:]
-    for out, skip in ((to_prev, hh), (to_next, hh), (to_far, 0)):
+    for out, skip in [(to_prev, hh), (to_next, hh)] + [(ref, 0) for ref in far]:
         out[pl.ds(skip, ch), :] = mine
         if first:
             out[pl.ds(skip + ch, block.shape[0]), :] = block[...]
 
 
-def prepare_kernel(plans, cut, n_small, *refs):
-    n_out = len(plans) + 5 + (1 if cut else 0)
+def prepare_kernel(plans, halves, cut, n_small, *refs):
+    n_out = len(refs) - 4 - n_small - 1
+    n_out = (n_out - n_small) // 2
     source, given, outs = refs[:4], refs[4 : 4 + n_small], refs[4 + n_small :][:n_out]
     refs = refs[4 + n_small + n_out :]
     small, made, sems = refs[:n_small], refs[n_small:-1], refs[-1]
@@ -172,11 +179,11 @@
     arriving = [start(src, dst) for src, dst in zip(given, small)]
     loads = []
     for plan, pack in zip(plans, made):
-        at, parts = 0, []
-        for which, layer, first, last in plan:
-            spot = pack.at[:, at : at + last - first]
-            parts.append(start(source[which].at[layer, :, first:last], spot))
-            at += last - first
+        parts = []
+        for which, layer, at in plan:
+            part = source[which].at[layer]
+            spot = pack.at[:, at : at + part.shape[1]]
+            parts.append(start(part, spot))
         loads.append(parts)
     for copy in arriving:
         copy.wait()
@@ -186,24 +193,30 @@
     rows.append(jnp.zeros((16 - 2 * STEPS, hidden), jnp.float32))
     at = made[0].shape[1] - LANES
     made[0][0:16, at : at + hidden] = jnp.concatenate(rows).astype(jnp.bfloat16)
-    n_packs = len(plans) + (1 if cut else 0)
+    n_packs = len(plans)
     halo_kernel(True, nodes, halo, edges, send, recv, *made[n_packs:])
     stores = [start(src, dst) for src, dst in zip(made[n_packs:], outs[n_packs:])]
-    for parts, src, dst in zip(loads, made, outs):
+    group = lax.axis_index("groups")
+    for i, parts in enumerate(loads):
         for copy in parts:
             copy.wait()
-        stores.append(start(src, dst))
-    if cut:
-        last = made[len(plans) - 1]
-        group = lax.axis_index("groups")
-        made[len(plans)][...] = jnp.where(group == 0, last[:, :cut], last[:, cut:])
-        stores.append(start(made[len(plans)], outs[len(plans)]))
+        if cut and i in halves:
+            whole = made[halves[i]]
+            made[i][:, :cut] = jnp.where(group == 0, whole[:, :cut], whole[:, cut:])
+        stores.append(start(made[i], outs[i]))
     for copy in stores:
         copy.wait()
 
 
-def gather_kernel(tile, nodes, send, recv, sent, received):
+def part_kernel(pack, out):
+    out[...] = pack[:, : out.shape[1]]
+
+
+def gather_kernel(tile, nodes, send, recv, *refs):
+    carried, (sent, received) = refs[: len(refs) - 2], refs[len(refs) - 2 :]
     count = nodes.shape[0]
+    if carried:
+        carried[1][...] = carried[0][...]
 
     def body(t, carry):
         rows = pl.ds(pl.multiple_of(t * tile, tile), tile)
@@ -219,6 +232,14 @@
 def bias_rows_of(bias_ref, line, n_groups):
     per = bias_ref.shape[1] // n_groups
     return [bias_ref[line : line + 1, g * per : (g + 1) * per] for g in range(n_groups)]
+
+
+def half_sums(out, half, nh, new_fine, recv_row):
+    sum_rows(out, 0, [place_in_half((nh, recv_row[...] - half * nh))], [new_fine[...]])
+
+
+def own_sums_kernel(nh, new_fine, recv_row, out):
+    half_sums(out, core_index(), nh, new_fine, recv_row)
 
 
 def fine_kernel(tile, sizes, spots, layer, *refs):
@@ -230,8 +251,7 @@
     bias_in = None if layer == 0 else next(it)
     new_fine = next(it)
     bias_out = next(it) if layer == 0 else None
-    aggs = [next(it), next(it)]
-    halo_tab = next(it)
+    agg_other, halo_tab = it
 
     core = core_index()
     width = gain_ref.shape[-1]
@@ -262,9 +282,7 @@
         return carry
 
     loop(fine.shape[0] // tile, body)
-    for out, half in zip(aggs, (1 - core, core)):
-        place = place_in_half((count // 2, recv_row[...] - half * (count // 2)))
-        sum_rows(out, 0, [place], [new_fine[...]])
+    half_sums(agg_other, 1 - core, count // 2, new_fine, recv_row)
 
 
 def coarse_target(state, width, me, cp):
@@ -307,7 +325,7 @@
     coarse_tab[pl.ds(pl.multiple_of(me * cp, cp), cp), :] = coarse_own[...]
     for i, pair in enumerate(arrived):
         owner = lax.rem(me + parts - 1 - i, parts)
-        skip = hh if i in (0, parts - 2) or (parts == RELAYED and layer == 0) else 0
+        skip = hh if i in (0, parts - 2) or parts == RELAYED else 0
         for who, ref in zip((core, 1 - core), pair):
             spot = pl.multiple_of(owner * cp + who * ch, ch)
             coarse_tab[pl.ds(spot, ch), :] = ref[pl.ds(skip, ch), 0:width]
@@ -365,7 +383,7 @@
     if cut:
         group = lax.axis_index("groups")
         for ref, (mine, other) in zip(far, parts):
-            ref[:, pl.ds(pl.multiple_of(group * cut, LANES), cut)] = mine[...]
+            ref[:, pl.ds(pl.multiple_of(group * cut, LANES), cut)] = mine[:, :cut]
             ref[:, pl.ds(pl.multiple_of((1 - group) * cut, LANES), cut)] = other[...]
         groups.append([[[(ref, at, to) for _, at, to in pieces] for pieces in spots] for ref in far])
     nh = out.shape[0]
@@ -439,15 +457,13 @@
     def both(x):
         return [x, swap(x)]
 
-    def after(x, *earlier):
-        return lax.optimization_barrier((x, earlier))[0]
+    def after(xs):
+        return lax.optimization_barrier(tuple(xs))
 
     two = cores == 4
 
-    def spread(pack, *earlier):
-        if two:
-            return across(after(pack, *earlier) if earlier else pack)
-        return lax.all_gather(pack, "feat", axis=0)
+    def spread(pack):
+        return across(pack) if two else lax.all_gather(pack, "feat", axis=0)
 
     def shards(pack, far):
         if two:
@@ -456,41 +472,31 @@
 
     k, kn = edge_w1.shape[2], node_w1.shape[2]
     w_hidden = edge_w1.shape[1]
-    stream = ((2, 0, kn), (3, 0, width), (1, 1, width), (0, 1, k), (2, 1, kn), (3, 1, width))
-    starts = [0]
-    for _, _, lanes in stream:
-        starts.append(starts[-1] + lanes)
-    cuts = [0, starts[2], starts[4], starts[-1]]
-
-    def pieces(which):
-        first, last = starts[which], starts[which + 1]
-        found = []
-        for pack, (lo, hi) in enumerate(zip(cuts, cuts[1:])):
-            if max(lo, first) < min(hi, last):
-                found.append((pack, max(lo, first) - lo, min(hi, last) - lo))
-        return found
-
-    plans = [[] for _ in cuts[1:]]
-    for which, (source, layer, _) in enumerate(stream):
-        done = 0
-        for pack, at, to in pieces(which):
-            plans[pack].append((source, layer, done, done + to - at))
-            done += to - at
     halo_row = halo_send.reshape(1, 2 * hr)
     own_coarse = coarse_edges.shape[0]
     coarse_count = own_coarse * parts
-    plans = [[(0, 0, 0, k), (1, 0, 0, width)], *plans]
-    lanes = [k + width + LANES] + [hi - lo for lo, hi in zip(cuts, cuts[1:])]
-    cut = lanes[-1] // 2 if two and lax.axis_size("groups") == 2 else 0
+    lanes = kn + width
+    cut = lanes // 2 if two and lax.axis_size("groups") == 2 else 0
+    plans = [
+        [(0, 0, 0), (1, 0, k)],
+        [(2, 0, 0), (3, 0, kn)],
+        [(2, 1, 0), (3, 1, kn)],
+        [(1, 1, cut)],
+        [(0, 1, 0)],
+    ] + ([[]] if cut else [])
+    halves = {3: 1, 5: 2}
     block = own_coarse + 16
     near, far = hr // 2 + cp // 2 + block, cp // 2 + block
-    shapes = [(w_hidden, n) for n in lanes] + ([(w_hidden, cut)] if cut else [])
-    shapes += [(near, width), (near, width), (far, width), (cp, width), (block, width)]
+    widths = [k + width + LANES, lanes, lanes, cut + width, k] + ([cut] if cut else [])
+    shapes = [(w_hidden, n) for n in widths]
+    direct = parts != RELAYED
+    shapes += [(near, width), (near, width)] + [(far, width)] * direct
+    shapes += [(cp, width), (block, width)]
     small = [edge_b1, node_b1, nodes, halo_row, coarse_edges]
     small += [x.reshape(1, own_coarse) for x in (coarse_send, coarse_recv)]
     n_copies = len(small) + sum(len(p) for p in plans) + len(shapes)
-    first_pack, *packs = call(
-        functools.partial(prepare_kernel, plans, cut, len(small)),
+    made = call(
+        functools.partial(prepare_kernel, plans, halves, cut, len(small)),
         tuple(bf16(*shape) for shape in shapes),
         [edge_w1, edge_w2, node_w1, node_w2, *small],
         scratch=[pltpu.VMEM(x.shape, x.dtype) for x in small]
@@ -501,14 +507,9 @@
         limit=3 * VMEM_BYTES,
         name="weights_and_halo_rows",
     )
-    to_prev, to_next, to_far, coarse_own, block = packs[-5:]
-    cut_part = packs[-6] if cut else None
-    packs = packs[: len(plans) - 1]
-
-    def choose(shards_of, w_in, w_out):
-        used = sorted({pack for which in (w_in, w_out) for pack, _, _ in pieces(which)})
-        spots = [[(used.index(p), at, to) for p, at, to in pieces(w)] for w in (w_in, w_out)]
-        return [x for shard in zip(*(shards_of[p] for p in used)) for x in shard], spots
+    first_pack, node0, node1, mixed, edge1, *node1_half = made[: len(widths)]
+    *rows_out, coarse_own, block = made[len(widths) :]
+    node_spots = (((0, 0, kn),), ((0, kn, lanes),))
 
     send_col = fine_send.reshape(fine_count, 1)
     recv_col = fine_recv.reshape(fine_count, 1)
@@ -520,29 +521,26 @@
     bias_rows = None
 
     def node_rows_out(own, other):
-        near, far = hr // 2 + cp // 2, cp // 2
+        near, far = bf16(hr // 2 + cp // 2, width), bf16(cp // 2, width)
         return call(
             functools.partial(halo_kernel, False),
-            (bf16(near, width), bf16(near, width), bf16(far, width), bf16(cp, width), bf16(count, width)),
+            (near, near, *[far] * direct, bf16(cp, width), bf16(count, width)),
             [own, other, halo_row],
             name="halo_rows",
         )
 
-    def exchange(to_prev, to_next, to_far, relayed=False):
-        return [
-            shift({1: to_next, parts - 1: to_prev}.get(by, to_far), by)
-            for by in range(1, parts)
-            if by in (1, parts - 1) or not relayed
-        ]
+    def exchange(to_prev, to_next, *to_far):
+        between = [shift(to_far[0], by) for by in range(2, parts - 1)] if to_far else []
+        return [shift(to_next, 1), *between, shift(to_prev, parts - 1)]
 
     def far_rows(moved):
         return [shift(moved[0], 1)] if parts == RELAYED else moved[1:-1]
 
-    def gather(nodes):
+    def gather(nodes, *carried):
         return call(
             functools.partial(gather_kernel, tile),
-            (bf16(fine_count, width), bf16(fine_count, width)),
-            [nodes, send_col, recv_col],
+            (*(bf16(*x.shape) for x in carried), bf16(fine_count, width), bf16(fine_count, width)),
+            [nodes, send_col, recv_col, *carried],
             flops=4 * fine_count * count * width,
             name="gather_rows",
         )
@@ -552,7 +550,7 @@
         if s == 0:
             outs.append(jax.ShapeDtypeStruct((8, hidden), jnp.float32))
         fine_rows = nh - cp // 2
-        outs += [bf16(fine_rows, width), jax.ShapeDtypeStruct((fine_rows, width), jnp.float32)]
+        outs.append(bf16(fine_rows, width))
         return call(
             functools.partial(fine_kernel, tile, sizes, spots, s),
             tuple(outs),
@@ -560,6 +558,14 @@
             scratch=[pltpu.VMEM((2 * hr, width), jnp.bfloat16)],
             flops=8 * fine_count * width * hidden,
             name="fine_edges",
+        )
+
+    def own_sums(new_fine):
+        return call(
+            functools.partial(own_sums_kernel, nh),
+            jax.ShapeDtypeStruct((nh - cp // 2, width), jnp.float32),
+            [new_fine, recv_row],
+            name="own_sums",
         )
 
     def coarse_update(s, new_fine, coarse_own, state, arrived, weights, spots):
@@ -602,63 +608,81 @@
     def pairs(moved, swapped):
         return [x for pair in zip(moved, swapped) for x in pair]
 
+    def other_group(x):
+        return lax.ppermute(x, "groups", [(0, 1), (1, 0)])
+
     far_first = spread(first_pack)
-    moved = exchange(to_prev, to_next, to_far, parts == RELAYED)
-    send_col, recv_col, recv_row, *packs = after(
-        (send_col, recv_col, recv_row, *packs), to_prev
-    )
-    sent, received = gather(nodes)
-    moved[0], moved[-1], far_first = after((moved[0], moved[-1], far_first), sent)
+    moved = exchange(*rows_out)
+    send_col, recv_col, recv_row = after((send_col, recv_col, recv_row))
+    if two:
+        near, sent, received = gather(nodes, swap(first_pack))
+    else:
+        sent, received = gather(nodes)
+    moved[0], moved[-1], far_first, sent = after((moved[0], moved[-1], far_first, sent))
     relayed = far_rows(moved)
     swapped = {i: swap(moved[i]) for i in (0, -1)}
-    weights, spots = shards(first_pack, far_first), (((0, 0, k),), ((0, k, k + width),))
-    far = spread(packs[0], far_first)
-    fine_edges, bias_rows, other, own = fine_update(
+    weights = [first_pack, near, *both(far_first)] if two else shards(first_pack, far_first)
+    spots = (((0, 0, k),), ((0, k, k + width),))
+    far = spread(mixed)
+    fine_edges, bias_rows, other = fine_update(
         0, fine_edges, sent, received, halo_of(moved, swapped), weights, spots
     )
     other, far, *relayed = after((other, far, *relayed))
     swapped = [swapped[0], *(swap(m) for m in relayed), swapped[-1]]
     moved = [moved[0], *relayed, moved[-1]]
-    partial = core_sum(own, other)
-    fine_edges, far = after((fine_edges, far), partial)
-    packs_of = [shards(packs[0], far)]
+    partial = core_sum(own_sums(fine_edges), other)
+    mixed = shards(mixed, far)
     fine_part = chip_sums(partial)
     state, other, own = coarse_update(
         0, fine_edges, coarse_own, block, pairs(moved, swapped), weights, spots
     )
+    if cut:
+        others = other_group(call(part_kernel, bf16(w_hidden, cut), [far], name="part"))
+        own, others = after((own, others))
+        weights = both(node0) + pairs(mixed[2:], both(others))
+    else:
+        weights = shards(node0, spread(node0))
     sums = [fine_part, chip_sums(core_sum(own, other))]
-    far = spread(packs[1], sums)
-    halves = node_update(0, nodes, sums, *choose(packs_of, 0, 1))
-
-    to_prev, to_next, to_far, coarse_own, nodes = node_rows_out(*halves)
-    moved = exchange(to_prev, to_next, to_far)
+    sums[1][-1], edge1 = after((sums[1][-1], edge1))
+    far = spread(edge1)
+    halves = node_update(0, nodes, sums, weights, node_spots, cut)
+
+    *rows_out, coarse_own, nodes = node_rows_out(*halves)
+    moved = exchange(*rows_out)
     sent, received = gather(nodes)
-    *moved, far = after((*moved, far), sent)
-    packs_of.append(shards(packs[1], far))
-    swapped = [swap(m) for m in moved]
-    far = across(after(cut_part, far)) if cut else spread(packs[2], far)
-    weights, spots = choose(packs_of, 3, 2)
-    fine_edges, other, own = fine_update(
+    *moved, far, sent = after((*moved, far, sent))
+    weights = pairs(shards(edge1, far), mixed)
+    spots = (((0, 0, k),), ((1, cut, cut + width),))
+    relayed = far_rows(moved)
+    swapped = {i: swap(moved[i]) for i in (0, -1)}
+    far = across(node1_half[0]) if cut else spread(node1)
+    fine_edges, other = fine_update(
         1, fine_edges, sent, received, halo_of(moved, swapped), weights, spots
     )
-    other, far = after((other, far))
-    partial = core_sum(own, other)
+    other, far, *relayed = after((other, far, *relayed))
+    swapped = [swapped[0], *(swap(m) for m in relayed), swapped[-1]]
+    moved = [moved[0], *relayed, moved[-1]]
+    partial = core_sum(own_sums(fine_edges), other)
     fine_part = chip_sums(partial)
     state, other, own = coarse_update(
         1, fine_edges, coarse_own, state, pairs(moved, swapped), weights, spots
     )
     if cut:
-        mine = both(far)
-        others = lax.ppermute(far, "groups", [(0, 1), (1, 0)])
+        others = other_group(far)
         own, others = after((own, others))
-        weights = both(packs[2]) + pairs(mine, both(others))
-        spots = [[(0, at - starts[4], at - starts[4] + n)] for at, n in zip(starts[4:], (kn, width))]
+        weights = both(node1) + pairs(both(far), both(others))
     else:
-        packs_of.append(shards(packs[2], far))
-        weights, spots = choose(packs_of, 4, 5)
+        weights = shards(node1, far)
     sums = [fine_part, chip_sums(core_sum(own, other))]
-    halves = node_update(1, nodes, sums, weights, spots, cut)
-    return call(join_kernel, bf16(count, width), halves, name="nodes_out")
+    halves = node_update(1, nodes, sums, weights, node_spots, cut)
+    return call(
+        join_kernel,
+        bf16(count, width),
+        halves,
+        scratch=[pltpu.SemaphoreType.DMA((2,))],
+        out_memory=pl.ANY,
+        name="nodes_out",
+    )
 
 
 def solution(mesh):

time: 97.1 us -> 93.9 us (0.967)
  waiting for transfers between devices: 36.1 us -> 28.5 us
  starting transfers between devices: 23.1 us -> 26.3 us
  Pallas kernels: 36.8 us -> 37.8 us
    ppermute x6, waiting for transfers between devices: 10.3 us -> 6.75 us  [shift(): lax.ppermute(x, 'mesh', [(i, (i + by) % parts) for i in range(parts)])]
    ppermute x21 -> x23, waiting for transfers between devices: 13.1 us -> 9.87 us  [swap(): return lax.ppermute(x, 'feat', [(i, i ^ 1) for i in range(cores)])]
    ppermute x8, waiting for transfers between devices: 12.6 us -> 10.4 us  [across(): return lax.ppermute(x, 'feat', [(i, i ^ 2) for i in range(cores)])]
    ppermute x1 -> x2, starting transfers between devices: 1.5 us -> 3.11 us  [other_group(): return lax.ppermute(x, 'groups', [(0, 1), (1, 0)])]
    ppermute x1 -> x2, waiting for transfers between devices: 0.01 us -> 1.43 us  [other_group(): return lax.ppermute(x, 'groups', [(0, 1), (1, 0)])]
    ppermute x21 -> x23, starting transfers between devices: 3.35 us -> 4.43 us  [swap(): return lax.ppermute(x, 'feat', [(i, i ^ 1) for i in range(cores)])]
    pallas_call x15 -> x18, Pallas kernels: 36.8 us -> 37.8 us  [call(): pl.pallas_call(kernel, out_shape=out_shape, in_specs=in_specs, out_specs=...]
  transfers between devices with their start and end apart: 36 -> 39, of which waited for: 18 -> 20; matrix products, arithmetic and copies ran while one was open for 1% -> 1% of each run, Pallas kernels for 29% -> 31%
where the time goes in v5:
time: 93.9 us; the launch traced here: 93.7 us
  Pallas kernels  37.8 us (40%)
  waiting for transfers between devices  28.5 us (30%)
  starting transfers between devices  26.3 us (28%)
    pallas_call x18, Pallas kernels, call(): pl.pallas_call(kernel, out_shape=out_shape, in_specs=in_specs, out_specs=...  37.8 us
    ppermute x8, waiting for transfers between devices, across(): return lax.ppermute(x, 'feat', [(i, i ^ 2) for i in range(cores)])  10.4 us
    ppermute x6, starting transfers between devices, shift(): lax.ppermute(x, 'mesh', [(i, (i + by) % parts) for i in range(parts)])  9.9 us
    ppermute x23, waiting for transfers between devices, swap(): return lax.ppermute(x, 'feat', [(i, i ^ 1) for i in range(cores)])  9.87 us
    ppermute x8, starting transfers between devices, across(): return lax.ppermute(x, 'feat', [(i, i ^ 2) for i in range(cores)])  8.82 us
    ppermute x6, waiting for transfers between devices, shift(): lax.ppermute(x, 'mesh', [(i, (i + by) % parts) for i in range(parts)])  6.75 us
    ppermute x23, starting transfers between devices, swap(): return lax.ppermute(x, 'feat', [(i, i ^ 1) for i in range(cores)])  4.43 us
    ppermute x2, starting transfers between devices, other_group(): return lax.ppermute(x, 'groups', [(0, 1), (1, 0)])  3.11 us
  transfers between devices with their start and end apart: 39, of which 20 were waited for; matrix products, arithmetic and copies ran while one was open for 1% of the time, Pallas kernels for 31%

profile of v5, /device:TPU:0, one launch (start us, length us, event | category | flops | bytes accessed | tf_op | source)
XLA Modules:
  0.0 93.7 jit_solution(6303111579622387625)
XLA Ops:
  0.0 3.9 %weights_and_halo_rows.1 = (bf16[128,2176]{1,0:T(8,128)(2,1)}, bf16[128,1536]{1,0:T(8,128)(2,1)}, bf16[128,1536]{1,0:T(8,128)(2,1)}, bf16[128,1280]{1,0:T(8,128)...) custom-call(bf16[2,128,1536]{2,1,0:T(8,128)(2,1)} %refs_0_.3, ...), custom_call_target="tpu_custom_call" | custom-call | tf_op jit(solution)/shard_map/weights_and_halo_rows/pallas_call | solution.py:76
  4.5 2.6 %collective-permute-start.2 = (bf16[128,2176]{1,0:T(8,128)(2,1)}, bf16[128,2176]{1,0:T(8,128)(2,1)S(1)}, u32[]{:S(2)}, u32[]{:S(2)}) collective-permute-start(bf16[128,2176]{1,0:T(8,128)(2,1)} %get-tuple-element.59.refs_10_.refs_12_), channel_id=1, source_target_pairs={{0,2},{1,3},{2,0},{3,1},{4,6},{5,7},{6,4},{7,5},{8,10},{9,11},{10,... | collective-permute-start | bytes 1671176 | tf_op jit(solution)/shard_map/ppermute | solution.py:452
  7.0 1.6 %collective-permute-start = (bf16[240,512]{1,0:T(8,128)(2,1)}, bf16[240,512]{1,0:T(8,128)(2,1)S(1)}, u32[]{:S(2)}, u32[]{:S(2)}) collective-permute-start(bf16[240,512]{1,0:T(8,128)(2,1)} %get-tuple-element.57), channel_id=1, source_target_pairs={{0,4},{4,8},{8,12},{12,0},{1,5},{5,9},{9,13},{13,1},{2,6},{6,10},{... | collective-permute-start | bytes 737288 | tf_op jit(solution)/shard_map/ppermute | solution.py:455
  8.6 2.2 %collective-permute-start.1 = (bf16[240,512]{1,0:T(8,128)(2,1)}, bf16[240,512]{1,0:T(8,128)(2,1)}, u32[]{:S(2)}, u32[]{:S(2)}) collective-permute-start(bf16[240,512]{1,0:T(8,128)(2,1)} %get-tuple-element.58), channel_id=1, source_target_pairs={{0,12},{4,0},{8,4},{12,8},{1,13},{5,1},{9,5},{13,9},{2,14},{6,2},{... | collective-permute-start | bytes 737288 | tf_op jit(solution)/shard_map/ppermute | solution.py:455
  11.6 4.7 %gather_rows.2 = (bf16[128,2176]{1,0:T(8,128)(2,1)S(1)}, bf16[1536,512]{1,0:T(8,128)(2,1)S(1)}, bf16[1536,512]{1,0:T(8,128)(2,1)S(1)}) custom-call(bf16[1024,512]{1,0:T(8,128)(2,1)S(1)} %copy-done, s32[1536,1]{1,0:T(8,128)S(1)} %copy.17.send.refs_3_, s32[1536,1]{1,0:T(8,128)S(1)} %copy.18.recv, bf16[128,2176]{1,0:T(8,128)(2,1)} %collective-permute-done.3.refs_0_), custom_call_target="tpu_custom_call" | custom-call | flops 3221225472 | tf_op jit(solution)/shard_map/gather_rows/pallas_call | solution.py:76
  16.3 1.6 %collective-permute-done.refs_6_ = bf16[240,512]{1,0:T(8,128)(2,1)S(1)} collective-permute-done((bf16[240,512]{1,0:T(8,128)(2,1)}, bf16[240,512]{1,0:T(8,128)(2,1)S(1)}, u32[]{:S(2)}, u32[]{:S(2)}) %collective-permute-start) | collective-permute-done | bytes 245792 | tf_op jit(solution)/shard_map/ppermute | solution.py:455
  17.9 4.1 %collective-permute-done.1.refs_8_.refs_10_ = bf16[240,512]{1,0:T(8,128)(2,1)} collective-permute-done((bf16[240,512]{1,0:T(8,128)(2,1)}, bf16[240,512]{1,0:T(8,128)(2,1)}, u32[]{:S(2)}, u32[]{:S(2)}) %collective-permute-start.1) | collective-permute-done | bytes 245792 | tf_op jit(solution)/shard_map/ppermute | solution.py:455
  23.0 1.3 %collective-permute-start.8 = (bf16[240,512]{1,0:T(8,128)(2,1)S(1)}, bf16[240,512]{1,0:T(8,128)(2,1)S(1)}, u32[]{:S(2)}, u32[]{:S(2)}) collective-permute-start(bf16[240,512]{1,0:T(8,128)(2,1)S(1)} %collective-permute-done.refs_6_), channel_id=1, source_target_pairs={{0,4},{4,8},{8,12},{12,0},{1,5},{5,9},{9,13},{13,1},{2,6},{6,10},{... | collective-permute-start | bytes 737288 | tf_op jit(solution)/shard_map/ppermute | solution.py:455
  24.8 6.2 %fine_edges.2 = (bf16[1536,512]{1,0:T(8,128)(2,1)S(1)}, f32[8,512]{1,0:T(8,128)S(1)}, bf16[448,512]{1,0:T(8,128)(2,1)S(1)}) custom-call(bf16[1536,512]{1,0:T(8,128)(2,1)S(1)} %copy-done.11, bf16[1536,512]{1,0:T(8,128)(2,1)S(1)} %get-tuple-element.63.refs_1_, bf16[1536,512]{1,0:T(8,128)(2,1)S(1)} %get-tuple-element.64.refs_2_, ...), custom_call_target="tpu_custom_call" | custom-call | flops 3221225472 | tf_op jit(solution)/shard_map/fine_edges/pallas_call | solution.py:76
  31.1 1.5 %collective-permute-done.7.pack.refs_9_.refs_15_.refs_17_ = bf16[128,1280]{1,0:T(8,128)(2,1)S(1)} collective-permute-done((bf16[128,1280]{1,0:T(8,128)(2,1)S(1)}, bf16[128,1280]{1,0:T(8,128)(2,1)S(1)}, u32[]{:S(2)}, u32[]{:S(2)}) %collective-permute-start.7) | collective-permute-done | bytes 327712 | tf_op jit(solution)/shard_map/ppermute | solution.py:452
  34.8 1.5 %collective-permute-start.10 = (bf16[448,512]{1,0:T(8,128)(2,1)S(1)}, bf16[448,512]{1,0:T(8,128)(2,1)S(1)}, u32[]{:S(2)}, u32[]{:S(2)}) collective-permute-start(bf16[448,512]{1,0:T(8,128)(2,1)S(1)} %core_sum.4.refs_3_), channel_id=1, source_target_pairs={{0,2},{1,3},{2,0},{3,1},{4,6},{5,7},{6,4},{7,5},{8,10},{9,11},{10,... | collective-permute-start | bytes 1376264 | tf_op jit(solution)/shard_map/ppermute | solution.py:452
  36.4 1.6 %collective-permute-start.12 = (bf16[128,768]{1,0:T(8,128)(2,1)S(1)}, bf16[128,768]{1,0:T(8,128)(2,1)S(1)}, u32[]{:S(2)}, u32[]{:S(2)}) collective-permute-start(bf16[128,768]{1,0:T(8,128)(2,1)S(1)} %part.1), channel_id=1, source_target_pairs={{0,16},{16,0},{1,17},{17,1},{2,18},{18,2},{3,19},{19,3},{4,20},{20... | collective-permute-start | bytes 589832 | tf_op jit(solution)/shard_map/ppermute | solution.py:612
  38.5 3.8 %coarse_edges_and_sums.2 = (bf16[384,640]{1,0:T(8,128)(2,1)S(1)}, bf16[64,512]{1,0:T(8,128)(2,1)S(1)}, f32[64,512]{1,0:T(8,128)S(1)}) custom-call(bf16[1536,512]{1,0:T(8,128)(2,1)S(1)} %get-tuple-element.71.new_fine.refs_0_, s32[1,1536]{1,0:T(1,128)S(1)} %reshape.23.refs_4_.recv_row.refs_1_, bf16[128,512]{1,0:T(8,128)(2,1)S(1)} %copy-done.6, ...), custom_call_target="tpu_custom_call" | custom-call | tf_op jit(solution)/shard_map/coarse_edges_and_sums/pallas_call | solution.py:76
  42.3 1.4 %collective-permute-done.12.refs_10_ = bf16[128,768]{1,0:T(8,128)(2,1)S(1)} collective-permute-done((bf16[128,768]{1,0:T(8,128)(2,1)S(1)}, bf16[128,768]{1,0:T(8,128)(2,1)S(1)}, u32[]{:S(2)}, u32[]{:S(2)}) %collective-permute-start.12) | collective-permute-done | bytes 196640 | tf_op jit(solution)/shard_map/ppermute | solution.py:612
  44.2 1.0 %collective-permute-done.13.arrived = bf16[64,512]{1,0:T(8,128)(2,1)S(1)} collective-permute-done((bf16[64,512]{1,0:T(8,128)(2,1)S(1)}, bf16[64,512]{1,0:T(8,128)(2,1)S(1)}, u32[]{:S(2)}, u32[]{:S(2)}) %collective-permute-start.13) | collective-permute-done | bytes 65568 | tf_op jit(solution)/shard_map/ppermute | solution.py:449
  45.9 3.7 %collective-permute-done.14.refs_6_ = bf16[64,512]{1,0:T(8,128)(2,1)S(1)} collective-permute-done((bf16[64,512]{1,0:T(8,128)(2,1)S(1)}, bf16[64,512]{1,0:T(8,128)(2,1)S(1)}, u32[]{:S(2)}, u32[]{:S(2)}) %collective-permute-start.14) | collective-permute-done | bytes 65568 | tf_op jit(solution)/shard_map/ppermute | solution.py:452
  49.7 1.7 %node_update.2.refs_0_ = bf16[512,512]{1,0:T(8,128)(2,1)S(1)} custom-call(bf16[1024,512]{1,0:T(8,128)(2,1)S(1)} %copy-done, f32[8,512]{1,0:T(8,128)S(1)} %get-tuple-element.70.refs_4_.refs_1_.refs_18_, bf16[2,512]{1,0:T(2,128)(2,1)S(1)} %copy-done.9, bf16[448,512]{1,0:T(8,128)(2,1)S(1)} %core_sum.4.refs_3_, ...), custom_call_target="tpu_custom_call" | custom-call | tf_op jit(solution)/shard_map/node_update/pallas_call | solution.py:76
  52.3 1.0 %collective-permute-done.18.refs_1_ = bf16[512,512]{1,0:T(8,128)(2,1)S(1)} collective-permute-done((bf16[512,512]{1,0:T(8,128)(2,1)S(1)}, bf16[512,512]{1,0:T(8,128)(2,1)S(1)}, u32[]{:S(2)}, u32[]{:S(2)}) %collective-permute-start.18) | collective-permute-done | bytes 524320 | tf_op jit(solution)/shard_map/ppermute | solution.py:449
  54.2 3.8 %collective-permute-start.20 = (bf16[128,512]{1,0:T(8,128)(2,1)S(1)}, bf16[128,512]{1,0:T(8,128)(2,1)S(1)}, u32[]{:S(2)}, u32[]{:S(2)}) collective-permute-start(bf16[128,512]{1,0:T(8,128)(2,1)S(1)} %get-tuple-element.88), channel_id=1, source_target_pairs={{0,12},{4,0},{8,4},{12,8},{1,13},{5,1},{9,5},{13,9},{2,14},{6,2},{... | collective-permute-start | bytes 393224 | tf_op jit(solution)/shard_map/ppermute | solution.py:455
  58.0 3.5 %gather_rows.3 = (bf16[1536,512]{1,0:T(8,128)(2,1)S(1)}, bf16[1536,512]{1,0:T(8,128)(2,1)S(1)}) custom-call(bf16[1024,512]{1,0:T(8,128)(2,1)S(1)} %get-tuple-element.86.nodes.refs_0_, s32[1536,1]{1,0:T(8,128)S(1)} %copy.17.send.refs_3_, s32[1536,1]{1,0:T(8,128)S(1)} %copy.18.recv), custom_call_target="tpu_custom_call" | custom-call | flops 3221225472 | tf_op jit(solution)/shard_map/gather_rows/pallas_call | solution.py:76
  61.4 1.5 %collective-permute-done.21.refs_14_.refs_16_ = bf16[128,1536]{1,0:T(8,128)(2,1)S(1)} collective-permute-done((bf16[128,1536]{1,0:T(8,128)(2,1)S(1)}, bf16[128,1536]{1,0:T(8,128)(2,1)S(1)}, u32[]{:S(2)}, u32[]{:S(2)}) %collective-permute-start.21) | collective-permute-done | bytes 393248 | tf_op jit(solution)/shard_map/ppermute | solution.py:452
  64.0 1.2 %collective-permute-done.25.refs_13_.refs_15_ = bf16[128,1280]{1,0:T(8,128)(2,1)S(1)} collective-permute-done((bf16[128,1280]{1,0:T(8,128)(2,1)S(1)}, bf16[128,1280]{1,0:T(8,128)(2,1)S(1)}, u32[]{:S(2)}, u32[]{:S(2)}) %collective-permute-start.25) | collective-permute-done | bytes 327712 | tf_op jit(solution)/shard_map/ppermute | solution.py:449
  66.7 5.3 %fine_edges.3 = (bf16[1536,512]{1,0:T(8,128)(2,1)S(1)}, bf16[448,512]{1,0:T(8,128)(2,1)S(1)}) custom-call(bf16[1536,512]{1,0:T(8,128)(2,1)S(1)} %get-tuple-element.71.new_fine.refs_0_, bf16[1536,512]{1,0:T(8,128)(2,1)S(1)} %get-tuple-element.91.refs_1_, bf16[1536,512]{1,0:T(8,128)(2,1)S(1)} %get-tuple-element.92.refs_2_, s32[1536,1]{1,0:T(8,128)S(1)} %copy.17.send.refs_3_, ...), custom_call_target="tpu_custom_call" | custom-call | flops 3221225472 | tf_op jit(solution)/shard_map/fine_edges/pallas_call | solution.py:76
  74.8 1.4 %collective-permute-start.30 = (bf16[448,512]{1,0:T(8,128)(2,1)S(1)}, bf16[448,512]{1,0:T(8,128)(2,1)S(1)}, u32[]{:S(2)}, u32[]{:S(2)}) collective-permute-start(bf16[448,512]{1,0:T(8,128)(2,1)S(1)} %core_sum.6.refs_3_), channel_id=1, source_target_pairs={{0,2},{1,3},{2,0},{3,1},{4,6},{5,7},{6,4},{7,5},{8,10},{9,11},{10,... | collective-permute-start | bytes 1376264 | tf_op jit(solution)/shard_map/ppermute | solution.py:452
  76.2 1.5 %collective-permute-start.32 = (bf16[128,768]{1,0:T(8,128)(2,1)S(1)}, bf16[128,768]{1,0:T(8,128)(2,1)S(1)}, u32[]{:S(2)}, u32[]{:S(2)}) collective-permute-start(bf16[128,768]{1,0:T(8,128)(2,1)S(1)} %collective-permute-done.27.refs_9_), channel_id=1, source_target_pairs={{0,16},{16,0},{1,17},{17,1},{2,18},{18,2},{3,19},{19,3},{4,20},{20... | collective-permute-start | bytes 589832 | tf_op jit(solution)/shard_map/ppermute | solution.py:612
  78.3 1.4 %collective-permute-done.31.refs_9_ = bf16[128,512]{1,0:T(8,128)(2,1)S(1)} collective-permute-done((bf16[128,512]{1,0:T(8,128)(2,1)S(1)}, bf16[128,512]{1,0:T(8,128)(2,1)S(1)}, u32[]{:S(2)}, u32[]{:S(2)}) %collective-permute-start.31) | collective-permute-done | bytes 131104 | tf_op jit(solution)/shard_map/ppermute | solution.py:449
  79.7 3.3 %coarse_edges_and_sums.3 = (bf16[384,640]{1,0:T(8,128)(2,1)}, bf16[64,512]{1,0:T(8,128)(2,1)S(1)}, f32[64,512]{1,0:T(8,128)S(1)}) custom-call(bf16[1536,512]{1,0:T(8,128)(2,1)S(1)} %get-tuple-element.96.new_fine.refs_0_, s32[1,1536]{1,0:T(1,128)S(1)} %reshape.23.refs_4_.recv_row.refs_1_, bf16[128,512]{1,0:T(8,128)(2,1)S(1)} %get-tuple-element.100.refs_2_, ...), custom_call_target="tpu_custom_call" | custom-call | tf_op jit(solution)/shard_map/coarse_edges_and_sums/pallas_call | solution.py:76
  83.5 1.0 %collective-permute-done.33.arrived = bf16[64,512]{1,0:T(8,128)(2,1)S(1)} collective-permute-done((bf16[64,512]{1,0:T(8,128)(2,1)S(1)}, bf16[64,512]{1,0:T(8,128)(2,1)S(1)}, u32[]{:S(2)}, u32[]{:S(2)}) %collective-permute-start.33) | collective-permute-done | bytes 65568 | tf_op jit(solution)/shard_map/ppermute | solution.py:449
  85.3 3.6 %collective-permute-done.34.refs_6_ = bf16[64,512]{1,0:T(8,128)(2,1)S(1)} collective-permute-done((bf16[64,512]{1,0:T(8,128)(2,1)S(1)}, bf16[64,512]{1,0:T(8,128)(2,1)S(1)}, u32[]{:S(2)}, u32[]{:S(2)}) %collective-permute-start.34) | collective-permute-done | bytes 65568 | tf_op jit(solution)/shard_map/ppermute | solution.py:452
  88.9 1.7 %node_update.3.own = bf16[512,512]{1,0:T(8,128)(2,1)S(1)} custom-call(bf16[1024,512]{1,0:T(8,128)(2,1)S(1)} %get-tuple-element.86.nodes.refs_0_, f32[8,512]{1,0:T(8,128)S(1)} %get-tuple-element.70.refs_4_.refs_1_.refs_18_, bf16[2,512]{1,0:T(2,128)(2,1)S(1)} %copy-done.9, bf16[448,512]{1,0:T(8,128)(2,1)S(1)} %core_sum.6.refs_3_, ...), custom_call_target="tpu_custom_call" | custom-call | tf_op jit(solution)/shard_map/node_update/pallas_call | solution.py:76
  90.6 1.9 %collective-permute-done.38.other = bf16[512,512]{1,0:T(8,128)(2,1)S(1)} collective-permute-done((bf16[512,512]{1,0:T(8,128)(2,1)S(1)}, bf16[512,512]{1,0:T(8,128)(2,1)S(1)}, u32[]{:S(2)}, u32[]{:S(2)}) %collective-permute-start.38) | collective-permute-done | bytes 524320 | tf_op jit(solution)/shard_map/ppermute | solution.py:449
  92.5 1.0 %nodes_out.1 = bf16[1024,512]{1,0:T(8,128)(2,1)} custom-call(bf16[512,512]{1,0:T(8,128)(2,1)S(1)} %node_update.3.own, bf16[512,512]{1,0:T(8,128)(2,1)S(1)} %collective-permute-done.38.other), custom_call_target="tpu_custom_call" | custom-call | tf_op jit(solution)/shard_map/nodes_out/pallas_call | solution.py:76
  (99 shorter events, 15.7 us)
Async XLA Ops:
  3.9 7.6 %collective-permute-start.3 = (bf16[128,2176]{1,0:T(8,128)(2,1)}, bf16[128,2176]{1,0:T(8,128)(2,1)}, u32[]{:S(2)}, u32[]{:S(2)}) collective-permute-start(bf16[128,2176]{1,0:T(8,128)(2,1)} %get-tuple-element.59.refs_10_.refs_12_), channel_id=1, source_target_pairs={{0,1},{1,0},{2,3},{3,2},{4,5},{5,4},{6,7},{7,6},{8,9},{9,8},{10,11... | collective-permute-start | bytes 1671176 | tf_op jit(solution)/shard_map/ppermute | solution.py:449
  4.5 17.5 %collective-permute-start.2 = (bf16[128,2176]{1,0:T(8,128)(2,1)}, bf16[128,2176]{1,0:T(8,128)(2,1)S(1)}, u32[]{:S(2)}, u32[]{:S(2)}) collective-permute-start(bf16[128,2176]{1,0:T(8,128)(2,1)} %get-tuple-element.59.refs_10_.refs_12_), channel_id=1, source_target_pairs={{0,2},{1,3},{2,0},{3,1},{4,6},{5,7},{6,4},{7,5},{8,10},{9,11},{10,... | collective-permute-start | bytes 1671176 | tf_op jit(solution)/shard_map/ppermute | solution.py:452
  7.0 10.8 %collective-permute-start = (bf16[240,512]{1,0:T(8,128)(2,1)}, bf16[240,512]{1,0:T(8,128)(2,1)S(1)}, u32[]{:S(2)}, u32[]{:S(2)}) collective-permute-start(bf16[240,512]{1,0:T(8,128)(2,1)} %get-tuple-element.57), channel_id=1, source_target_pairs={{0,4},{4,8},{8,12},{12,0},{1,5},{5,9},{9,13},{13,1},{2,6},{6,10},{... | collective-permute-start | bytes 737288 | tf_op jit(solution)/shard_map/ppermute | solution.py:455
  8.6 13.3 %collective-permute-start.1 = (bf16[240,512]{1,0:T(8,128)(2,1)}, bf16[240,512]{1,0:T(8,128)(2,1)}, u32[]{:S(2)}, u32[]{:S(2)}) collective-permute-start(bf16[240,512]{1,0:T(8,128)(2,1)} %get-tuple-element.58), channel_id=1, source_target_pairs={{0,12},{4,0},{8,4},{12,8},{1,13},{5,1},{9,5},{13,9},{2,14},{6,2},{... | collective-permute-start | bytes 737288 | tf_op jit(solution)/shard_map/ppermute | solution.py:455
  21.9 2.9 %collective-permute-start.6 = (bf16[128,2176]{1,0:T(8,128)(2,1)S(1)}, bf16[128,2176]{1,0:T(8,128)(2,1)S(1)}, u32[]{:S(2)}, u32[]{:S(2)}) collective-permute-start(bf16[128,2176]{1,0:T(8,128)(2,1)S(1)} %collective-permute-done.2.refs_12_.refs_14_), channel_id=1, source_target_pairs={{0,1},{1,0},{2,3},{3,2},{4,5},{5,4},{6,7},{7,6},{8,9},{9,8},{10,11... | collective-permute-start | bytes 1671176 | tf_op jit(solution)/shard_map/ppermute | solution.py:449
  21.9 2.7 %collective-permute-start.4 = (bf16[240,512]{1,0:T(8,128)(2,1)S(1)}, bf16[240,512]{1,0:T(8,128)(2,1)S(1)}, u32[]{:S(2)}, u32[]{:S(2)}) collective-permute-start(bf16[240,512]{1,0:T(8,128)(2,1)S(1)} %collective-permute-done.refs_6_), channel_id=1, source_target_pairs={{0,1},{1,0},{2,3},{3,2},{4,5},{5,4},{6,7},{7,6},{8,9},{9,8},{10,11... | collective-permute-start | bytes 737288 | tf_op jit(solution)/shard_map/ppermute | solution.py:449
  22.4 2.4 %collective-permute-start.5 = (bf16[240,512]{1,0:T(8,128)(2,1)}, bf16[240,512]{1,0:T(8,128)(2,1)S(1)}, u32[]{:S(2)}, u32[]{:S(2)}) collective-permute-start(bf16[240,512]{1,0:T(8,128)(2,1)} %collective-permute-done.1.refs_8_.refs_10_), channel_id=1, source_target_pairs={{0,1},{1,0},{2,3},{3,2},{4,5},{5,4},{6,7},{7,6},{8,9},{9,8},{10,11... | collective-permute-start | bytes 737288 | tf_op jit(solution)/shard_map/ppermute | solution.py:449
  22.5 10.1 %collective-permute-start.7 = (bf16[128,1280]{1,0:T(8,128)(2,1)S(1)}, bf16[128,1280]{1,0:T(8,128)(2,1)S(1)}, u32[]{:S(2)}, u32[]{:S(2)}) collective-permute-start(bf16[128,1280]{1,0:T(8,128)(2,1)S(1)} %copy-done.5), channel_id=1, source_target_pairs={{0,2},{1,3},{2,0},{3,1},{4,6},{5,7},{6,4},{7,5},{8,10},{9,11},{10,... | collective-permute-start | bytes 983048 | tf_op jit(solution)/shard_map/ppermute | solution.py:452
  23.0 9.9 %collective-permute-start.8 = (bf16[240,512]{1,0:T(8,128)(2,1)S(1)}, bf16[240,512]{1,0:T(8,128)(2,1)S(1)}, u32[]{:S(2)}, u32[]{:S(2)}) collective-permute-start(bf16[240,512]{1,0:T(8,128)(2,1)S(1)} %collective-permute-done.refs_6_), channel_id=1, source_target_pairs={{0,4},{4,8},{8,12},{12,0},{1,5},{5,9},{9,13},{13,1},{2,6},{6,10},{... | collective-permute-start | bytes 737288 | tf_op jit(solution)/shard_map/ppermute | solution.py:455
  34.8 14.9 %collective-permute-start.10 = (bf16[448,512]{1,0:T(8,128)(2,1)S(1)}, bf16[448,512]{1,0:T(8,128)(2,1)S(1)}, u32[]{:S(2)}, u32[]{:S(2)}) collective-permute-start(bf16[448,512]{1,0:T(8,128)(2,1)S(1)} %core_sum.4.refs_3_), channel_id=1, source_target_pairs={{0,2},{1,3},{2,0},{3,1},{4,6},{5,7},{6,4},{7,5},{8,10},{9,11},{10,... | collective-permute-start | bytes 1376264 | tf_op jit(solution)/shard_map/ppermute | solution.py:452
  36.3 2.1 %collective-permute-start.11 = (bf16[240,512]{1,0:T(8,128)(2,1)S(1)}, bf16[240,512]{1,0:T(8,128)(2,1)S(1)}, u32[]{:S(2)}, u32[]{:S(2)}) collective-permute-start(bf16[240,512]{1,0:T(8,128)(2,1)S(1)} %collective-permute-done.8.refs_8_), channel_id=1, source_target_pairs={{0,1},{1,0},{2,3},{3,2},{4,5},{5,4},{6,7},{7,6},{8,9},{9,8},{10,11... | collective-permute-start | bytes 737288 | tf_op jit(solution)/shard_map/ppermute | solution.py:449
  36.4 7.4 %collective-permute-start.12 = (bf16[128,768]{1,0:T(8,128)(2,1)S(1)}, bf16[128,768]{1,0:T(8,128)(2,1)S(1)}, u32[]{:S(2)}, u32[]{:S(2)}) collective-permute-start(bf16[128,768]{1,0:T(8,128)(2,1)S(1)} %part.1), channel_id=1, source_target_pairs={{0,16},{16,0},{1,17},{17,1},{2,18},{18,2},{3,19},{19,3},{4,20},{20... | collective-permute-start | bytes 589832 | tf_op jit(solution)/shard_map/ppermute | solution.py:612
  37.9 11.7 %collective-permute-start.15 = (bf16[128,1536]{1,0:T(8,128)(2,1)S(1)}, bf16[128,1536]{1,0:T(8,128)(2,1)S(1)}, u32[]{:S(2)}, u32[]{:S(2)}) collective-permute-start(bf16[128,1536]{1,0:T(8,128)(2,1)S(1)} %copy-done.4), channel_id=1, source_target_pairs={{0,1},{1,0},{2,3},{3,2},{4,5},{5,4},{6,7},{7,6},{8,9},{9,8},{10,11... | collective-permute-start | bytes 1179656 | tf_op jit(solution)/shard_map/ppermute | solution.py:449
  38.2 11.5 %collective-permute-start.16 = (bf16[128,1280]{1,0:T(8,128)(2,1)S(1)}, bf16[128,1280]{1,0:T(8,128)(2,1)S(1)}, u32[]{:S(2)}, u32[]{:S(2)}) collective-permute-start(bf16[128,1280]{1,0:T(8,128)(2,1)S(1)} %collective-permute-done.7.pack.refs_9_.refs_15_.refs_17_), channel_id=1, source_target_pairs={{0,1},{1,0},{2,3},{3,2},{4,5},{5,4},{6,7},{7,6},{8,9},{9,8},{10,11... | collective-permute-start | bytes 983048 | tf_op jit(solution)/shard_map/ppermute | solution.py:449
  43.7 5.9 %collective-permute-start.17 = (bf16[128,768]{1,0:T(8,128)(2,1)S(1)}, bf16[128,768]{1,0:T(8,128)(2,1)S(1)}, u32[]{:S(2)}, u32[]{:S(2)}) collective-permute-start(bf16[128,768]{1,0:T(8,128)(2,1)S(1)} %collective-permute-done.12.refs_10_), channel_id=1, source_target_pairs={{0,1},{1,0},{2,3},{3,2},{4,5},{5,4},{6,7},{7,6},{8,9},{9,8},{10,11... | collective-permute-start | bytes 589832 | tf_op jit(solution)/shard_map/ppermute | solution.py:449
  45.3 4.3 %collective-permute-start.14 = (bf16[64,512]{1,0:T(8,128)(2,1)S(1)}, bf16[64,512]{1,0:T(8,128)(2,1)S(1)}, u32[]{:S(2)}, u32[]{:S(2)}) collective-permute-start(bf16[64,512]{1,0:T(8,128)(2,1)S(1)} %core_sum.5.refs_5_), channel_id=1, source_target_pairs={{0,2},{1,3},{2,0},{3,1},{4,6},{5,7},{6,4},{7,5},{8,10},{9,11},{10,... | collective-permute-start | bytes 196616 | tf_op jit(solution)/shard_map/ppermute | solution.py:452
  51.4 11.5 %collective-permute-start.21 = (bf16[128,1536]{1,0:T(8,128)(2,1)S(1)}, bf16[128,1536]{1,0:T(8,128)(2,1)S(1)}, u32[]{:S(2)}, u32[]{:S(2)}) collective-permute-start(bf16[128,1536]{1,0:T(8,128)(2,1)S(1)} %copy-done.2), channel_id=1, source_target_pairs={{0,2},{1,3},{2,0},{3,1},{4,6},{5,7},{6,4},{7,5},{8,10},{9,11},{10,... | collective-permute-start | bytes 1179656 | tf_op jit(solution)/shard_map/ppermute | solution.py:452
  52.2 13.7 %collective-permute-start.24 = (bf16[128,1536]{1,0:T(8,128)(2,1)S(1)}, bf16[128,1536]{1,0:T(8,128)(2,1)S(1)}, u32[]{:S(2)}, u32[]{:S(2)}) collective-permute-start(bf16[128,1536]{1,0:T(8,128)(2,1)S(1)} %copy-done.2), channel_id=1, source_target_pairs={{0,1},{1,0},{2,3},{3,2},{4,5},{5,4},{6,7},{7,6},{8,9},{9,8},{10,11... | collective-permute-start | bytes 1179656 | tf_op jit(solution)/shard_map/ppermute | solution.py:449
  54.1 8.9 %collective-permute-start.19 = (bf16[128,512]{1,0:T(8,128)(2,1)S(1)}, bf16[128,512]{1,0:T(8,128)(2,1)S(1)}, u32[]{:S(2)}, u32[]{:S(2)}) collective-permute-start(bf16[128,512]{1,0:T(8,128)(2,1)S(1)} %get-tuple-element.87), channel_id=1, source_target_pairs={{0,4},{4,8},{8,12},{12,0},{1,5},{5,9},{9,13},{13,1},{2,6},{6,10},{... | collective-permute-start | bytes 393224 | tf_op jit(solution)/shard_map/ppermute | solution.py:455
  54.2 8.8 %collective-permute-start.20 = (bf16[128,512]{1,0:T(8,128)(2,1)S(1)}, bf16[128,512]{1,0:T(8,128)(2,1)S(1)}, u32[]{:S(2)}, u32[]{:S(2)}) collective-permute-start(bf16[128,512]{1,0:T(8,128)(2,1)S(1)} %get-tuple-element.88), channel_id=1, source_target_pairs={{0,12},{4,0},{8,4},{12,8},{1,13},{5,1},{9,5},{13,9},{2,14},{6,2},{... | collective-permute-start | bytes 393224 | tf_op jit(solution)/shard_map/ppermute | solution.py:455
  63.0 3.8 %collective-permute-start.26 = (bf16[128,1536]{1,0:T(8,128)(2,1)S(1)}, bf16[128,1536]{1,0:T(8,128)(2,1)S(1)}, u32[]{:S(2)}, u32[]{:S(2)}) collective-permute-start(bf16[128,1536]{1,0:T(8,128)(2,1)S(1)} %collective-permute-done.21.refs_14_.refs_16_), channel_id=1, source_target_pairs={{0,1},{1,0},{2,3},{3,2},{4,5},{5,4},{6,7},{7,6},{8,9},{9,8},{10,11... | collective-permute-start | bytes 1179656 | tf_op jit(solution)/shard_map/ppermute | solution.py:449
  63.0 2.2 %collective-permute-start.25 = (bf16[128,1280]{1,0:T(8,128)(2,1)S(1)}, bf16[128,1280]{1,0:T(8,128)(2,1)S(1)}, u32[]{:S(2)}, u32[]{:S(2)}) collective-permute-start(bf16[128,1280]{1,0:T(8,128)(2,1)S(1)} %copy-done.5), channel_id=1, source_target_pairs={{0,1},{1,0},{2,3},{3,2},{4,5},{5,4},{6,7},{7,6},{8,9},{9,8},{10,11... | collective-permute-start | bytes 983048 | tf_op jit(solution)/shard_map/ppermute | solution.py:449
  63.5 3.3 %collective-permute-start.22 = (bf16[128,512]{1,0:T(8,128)(2,1)S(1)}, bf16[128,512]{1,0:T(8,128)(2,1)S(1)}, u32[]{:S(2)}, u32[]{:S(2)}) collective-permute-start(bf16[128,512]{1,0:T(8,128)(2,1)S(1)} %collective-permute-done.19.refs_6_), channel_id=1, source_target_pairs={{0,1},{1,0},{2,3},{3,2},{4,5},{5,4},{6,7},{7,6},{8,9},{9,8},{10,11... | collective-permute-start | bytes 393224 | tf_op jit(solution)/shard_map/ppermute | solution.py:449
  63.5 3.2 %collective-permute-start.23 = (bf16[128,512]{1,0:T(8,128)(2,1)S(1)}, bf16[128,512]{1,0:T(8,128)(2,1)S(1)}, u32[]{:S(2)}, u32[]{:S(2)}) collective-permute-start(bf16[128,512]{1,0:T(8,128)(2,1)S(1)} %collective-permute-done.20.refs_8_.refs_10_), channel_id=1, source_target_pairs={{0,1},{1,0},{2,3},{3,2},{4,5},{5,4},{6,7},{7,6},{8,9},{9,8},{10,11... | collective-permute-start | bytes 393224 | tf_op jit(solution)/shard_map/ppermute | solution.py:449
  65.2 6.9 %collective-permute-start.27 = (bf16[128,768]{1,0:T(8,128)(2,1)S(1)}, bf16[128,768]{1,0:T(8,128)(2,1)S(1)}, u32[]{:S(2)}, u32[]{:S(2)}) collective-permute-start(bf16[128,768]{1,0:T(8,128)(2,1)S(1)} %copy-done.14), channel_id=1, source_target_pairs={{0,2},{1,3},{2,0},{3,1},{4,6},{5,7},{6,4},{7,5},{8,10},{9,11},{10,... | collective-permute-start | bytes 589832 | tf_op jit(solution)/shard_map/ppermute | solution.py:452
  65.8 7.1 %collective-permute-start.28 = (bf16[128,512]{1,0:T(8,128)(2,1)S(1)}, bf16[128,512]{1,0:T(8,128)(2,1)S(1)}, u32[]{:S(2)}, u32[]{:S(2)}) collective-permute-start(bf16[128,512]{1,0:T(8,128)(2,1)S(1)} %collective-permute-done.19.refs_6_), channel_id=1, source_target_pairs={{0,4},{4,8},{8,12},{12,0},{1,5},{5,9},{9,13},{13,1},{2,6},{6,10},{... | collective-permute-start | bytes 393224 | tf_op jit(solution)/shard_map/ppermute | solution.py:455
  74.8 14.1 %collective-permute-start.30 = (bf16[448,512]{1,0:T(8,128)(2,1)S(1)}, bf16[448,512]{1,0:T(8,128)(2,1)S(1)}, u32[]{:S(2)}, u32[]{:S(2)}) collective-permute-start(bf16[448,512]{1,0:T(8,128)(2,1)S(1)} %core_sum.6.refs_3_), channel_id=1, source_target_pairs={{0,2},{1,3},{2,0},{3,1},{4,6},{5,7},{6,4},{7,5},{8,10},{9,11},{10,... | collective-permute-start | bytes 1376264 | tf_op jit(solution)/shard_map/ppermute | solution.py:452
  76.2 6.8 %collective-permute-start.32 = (bf16[128,768]{1,0:T(8,128)(2,1)S(1)}, bf16[128,768]{1,0:T(8,128)(2,1)S(1)}, u32[]{:S(2)}, u32[]{:S(2)}) collective-permute-start(bf16[128,768]{1,0:T(8,128)(2,1)S(1)} %collective-permute-done.27.refs_9_), channel_id=1, source_target_pairs={{0,16},{16,0},{1,17},{17,1},{2,18},{18,2},{3,19},{19,3},{4,20},{20... | collective-permute-start | bytes 589832 | tf_op jit(solution)/shard_map/ppermute | solution.py:612
  77.7 7.5 %collective-permute-start.35 = (bf16[128,1536]{1,0:T(8,128)(2,1)S(1)}, bf16[128,1536]{1,0:T(8,128)(2,1)S(1)}, u32[]{:S(2)}, u32[]{:S(2)}) collective-permute-start(bf16[128,1536]{1,0:T(8,128)(2,1)S(1)} %copy-done.3), channel_id=1, source_target_pairs={{0,1},{1,0},{2,3},{3,2},{4,5},{5,4},{6,7},{7,6},{8,9},{9,8},{10,11... | collective-permute-start | bytes 1179656 | tf_op jit(solution)/shard_map/ppermute | solution.py:449
  78.3 7.0 %collective-permute-start.36 = (bf16[128,768]{1,0:T(8,128)(2,1)S(1)}, bf16[128,768]{1,0:T(8,128)(2,1)S(1)}, u32[]{:S(2)}, u32[]{:S(2)}) collective-permute-start(bf16[128,768]{1,0:T(8,128)(2,1)S(1)} %collective-permute-done.27.refs_9_), channel_id=1, source_target_pairs={{0,1},{1,0},{2,3},{3,2},{4,5},{5,4},{6,7},{7,6},{8,9},{9,8},{10,11... | collective-permute-start | bytes 589832 | tf_op jit(solution)/shard_map/ppermute | solution.py:449
  83.0 5.9 %collective-permute-start.37 = (bf16[128,768]{1,0:T(8,128)(2,1)S(1)}, bf16[128,768]{1,0:T(8,128)(2,1)S(1)}, u32[]{:S(2)}, u32[]{:S(2)}) collective-permute-start(bf16[128,768]{1,0:T(8,128)(2,1)S(1)} %collective-permute-done.32.refs_10_), channel_id=1, source_target_pairs={{0,1},{1,0},{2,3},{3,2},{4,5},{5,4},{6,7},{7,6},{8,9},{9,8},{10,11... | collective-permute-start | bytes 589832 | tf_op jit(solution)/shard_map/ppermute | solution.py:449
  84.5 4.3 %collective-permute-start.34 = (bf16[64,512]{1,0:T(8,128)(2,1)S(1)}, bf16[64,512]{1,0:T(8,128)(2,1)S(1)}, u32[]{:S(2)}, u32[]{:S(2)}) collective-permute-start(bf16[64,512]{1,0:T(8,128)(2,1)S(1)} %core_sum.7.refs_5_), channel_id=1, source_target_pairs={{0,2},{1,3},{2,0},{3,1},{4,6},{5,7},{6,4},{7,5},{8,10},{9,11},{10,... | collective-permute-start | bytes 196616 | tf_op jit(solution)/shard_map/ppermute | solution.py:452
  (22 other events, 138.8 us)

commit v6 on v5

--- a/solution.py
+++ b/solution.py
@@ -162,54 +162,75 @@
             out[pl.ds(skip + ch, block.shape[0]), :] = block[...]
 
 
-def prepare_kernel(plans, halves, cut, n_small, *refs):
-    n_out = len(refs) - 4 - n_small - 1
-    n_out = (n_out - n_small) // 2
-    source, given, outs = refs[:4], refs[4 : 4 + n_small], refs[4 + n_small :][:n_out]
-    refs = refs[4 + n_small + n_out :]
-    small, made, sems = refs[:n_small], refs[n_small:-1], refs[-1]
-    started = []
-
-    def start(src, dst):
-        copy = pltpu.make_async_copy(src, dst, sems.at[len(started)])
+class Copies:
+    def __init__(self, sems):
+        self.sems, self.started = sems, []
+
+    def start(self, src, dst):
+        copy = pltpu.make_async_copy(src, dst, self.sems.at[len(self.started)])
         copy.start()
-        started.append(copy)
+        self.started.append(copy)
         return copy
 
-    arriving = [start(src, dst) for src, dst in zip(given, small)]
-    loads = []
-    for plan, pack in zip(plans, made):
-        parts = []
-        for which, layer, at in plan:
-            part = source[which].at[layer]
-            spot = pack.at[:, at : at + part.shape[1]]
-            parts.append(start(part, spot))
-        loads.append(parts)
+
+def first_kernel(n_in, n_out, *refs):
+    edge_w1, edge_w2, *given = refs[:n_in]
+    outs = refs[n_in : n_in + n_out]
+    small, made, sems = refs[n_in + n_out :][: len(given)], refs[-1 - n_out : -1], refs[-1]
+    copies = Copies(sems)
+    arriving = [copies.start(src, dst) for src, dst in zip(given, small)]
+    pack, k = made[0], edge_w1.shape[2]
+    loads = [
+        copies.start(edge_w1.at[0], pack.at[:, 0:k]),
+        copies.start(edge_w2.at[0], pack.at[:, k : k + edge_w2.shape[2]]),
+    ]
     for copy in arriving:
         copy.wait()
     edge_b1, node_b1, nodes, halo, edges, send, recv = small
     hidden = edge_b1.shape[1]
     rows = [edge_b1[...].astype(jnp.float32), node_b1[...].astype(jnp.float32)]
     rows.append(jnp.zeros((16 - 2 * STEPS, hidden), jnp.float32))
-    at = made[0].shape[1] - LANES
-    made[0][0:16, at : at + hidden] = jnp.concatenate(rows).astype(jnp.bfloat16)
-    n_packs = len(plans)
-    halo_kernel(True, nodes, halo, edges, send, recv, *made[n_packs:])
-    stores = [start(src, dst) for src, dst in zip(made[n_packs:], outs[n_packs:])]
+    at = pack.shape[1] - LANES
+    pack[0:16, at : at + hidden] = jnp.concatenate(rows).astype(jnp.bfloat16)
+    halo_kernel(True, nodes, halo, edges, send, recv, *made[1:])
+    for copy in loads:
+        copy.wait()
+    for copy in [copies.start(src, dst) for src, dst in zip(made, outs)]:
+        copy.wait()
+
+
+def later_kernel(plans, halves, *refs):
+    source, outs, made, sems = refs[:4], refs[4 : 4 + len(plans)], refs[4 + len(plans) : -1], refs[-1]
+    copies = Copies(sems)
+    loads = []
+    for plan, pack in zip(plans, made):
+        parts = []
+        for which, layer, at in plan:
+            part = source[which].at[layer]
+            parts.append(copies.start(part, pack.at[:, at : at + part.shape[1]]))
+        loads.append(parts)
     group = lax.axis_index("groups")
+    stores = []
     for i, parts in enumerate(loads):
         for copy in parts:
             copy.wait()
-        if cut and i in halves:
-            whole = made[halves[i]]
-            made[i][:, :cut] = jnp.where(group == 0, whole[:, :cut], whole[:, cut:])
-        stores.append(start(made[i], outs[i]))
+        for which, at in halves.get(i, ()):
+            whole = made[which]
+            lanes = whole.shape[1] // 2
+            part = jnp.where(group == 0, whole[:, :lanes], whole[:, lanes:])
+            made[i][:, at : at + lanes] = part
+        stores.append(copies.start(made[i], outs[i]))
     for copy in stores:
         copy.wait()
 
 
-def part_kernel(pack, out):
-    out[...] = pack[:, : out.shape[1]]
+def parts_kernel(pack, first, last):
+    first[...] = pack[:, : first.shape[1]]
+    last[...] = pack[:, first.shape[1] :]
+
+
+def tail_kernel(rows, out):
+    out[...] = rows[pl.ds(rows.shape[0] - out.shape[0], out.shape[0]), :]
 
 
 def gather_kernel(tile, nodes, send, recv, *refs):
@@ -234,6 +255,16 @@
     return [bias_ref[line : line + 1, g * per : (g + 1) * per] for g in range(n_groups)]
 
 
+def far_weights(halved, k, w_in, parts, w_out):
+    lanes = halved
+    group = lax.axis_index("groups")
+    for ref, pair in zip(w_out, parts):
+        for who, part in zip((group, 1 - group), pair):
+            spot = pl.ds(pl.multiple_of(who * lanes, LANES), lanes)
+            ref[:, spot] = part[:, part.shape[1] - lanes :]
+    return [[[(w, 0, k)], [(ref, 0, ref.shape[1])]] for w, ref in zip(w_in, w_out)]
+
+
 def half_sums(out, half, nh, new_fine, recv_row):
     sum_rows(out, 0, [place_in_half((nh, recv_row[...] - half * nh))], [new_fine[...]])
 
@@ -242,16 +273,18 @@
     half_sums(out, core_index(), nh, new_fine, recv_row)
 
 
-def fine_kernel(tile, sizes, spots, layer, *refs):
+def fine_kernel(tile, sizes, spots, layer, halved, *refs):
     count, hr, cp, parts, cores = sizes
     it = iter(refs)
     fine, sent, received, send, recv_row, gain_ref = (next(it) for _ in range(6))
     prev, nxt = ((next(it), next(it)) for _ in range(2))
-    groups = take_groups(it, spots, cores)
+    groups = take_groups(it, spots, 2 if halved else cores)
+    far_in = [next(it) for _ in range(2 if halved else 0)]
+    parts = [(next(it), next(it)) for _ in far_in]
     bias_in = None if layer == 0 else next(it)
     new_fine = next(it)
     bias_out = next(it) if layer == 0 else None
-    agg_other, halo_tab = it
+    agg_other, halo_tab, *far_out = it
 
     core = core_index()
     width = gain_ref.shape[-1]
@@ -268,6 +301,8 @@
                 rows = pack[0:16, at : at + hidden].astype(jnp.float32)
                 bias_out[:, spot : spot + hidden] = rows[:8]
                 spot += hidden
+    if halved:
+        groups.append(far_weights(halved, 3 * width, far_in, parts, far_out))
     biases = bias_rows_of(bias_out if layer == 0 else bias_in, layer, len(groups))
     gain = gain_ref[layer : layer + 1, :].astype(jnp.float32)
 
@@ -309,23 +344,28 @@
     out[...] = total.astype(out.dtype)
 
 
-def coarse_kernel(tile, sizes, spots, layer, *refs):
+def coarse_kernel(tile, sizes, spots, layer, halved, *refs):
     count, hr, cp, parts, cores = sizes
     it = iter(refs)
     new_fine, recv_row, coarse_own, gain_ref, bias_ref = (next(it) for _ in range(5))
     given = next(it)
     arrived = [(next(it), next(it)) for _ in range(parts - 1)]
-    groups = take_groups(it, spots, cores)
-    state, *aggs, coarse_tab = it
+    groups = take_groups(it, spots, 2 if halved else cores)
+    far_in = [next(it) for _ in range(2 if halved else 0)]
+    halves = [(next(it), next(it)) for _ in far_in]
+    state, *aggs = (next(it) for _ in range(3))
+    coarse_tab, *far_out = it
 
     core, me = core_index(), lax.axis_index("mesh")
     width = gain_ref.shape[-1]
     hh, ch, nh = hr // 2, cp // 2, count // 2
+    if halved:
+        groups.append(far_weights(halved, 3 * width, far_in, halves, far_out))
 
     coarse_tab[pl.ds(pl.multiple_of(me * cp, cp), cp), :] = coarse_own[...]
     for i, pair in enumerate(arrived):
         owner = lax.rem(me + parts - 1 - i, parts)
-        skip = hh if i in (0, parts - 2) or parts == RELAYED else 0
+        skip = hh if i in (0, parts - 2) else 0
         for who, ref in zip((core, 1 - core), pair):
             spot = pl.multiple_of(owner * cp + who * ch, ch)
             coarse_tab[pl.ds(spot, ch), :] = ref[pl.ds(skip, ch), 0:width]
@@ -335,8 +375,7 @@
         unit = (lane == lax.broadcasted_iota(jnp.int32, (per, width), 0)).astype(jnp.bfloat16)
         blocks = [(given, 0)]
         for i, (ref, _) in enumerate(arrived):
-            near = i in (0, parts - 2) or parts == RELAYED
-            blocks.append((ref, ch + (hh if near else 0)))
+            blocks.append((ref, ch + (hh if i in (0, parts - 2) else 0)))
         for i, (ref, skip) in enumerate(blocks):
             rows = pl.ds(i * per, per)
             state[rows, :width] = ref[pl.ds(skip, per), :]
@@ -384,7 +423,7 @@
         group = lax.axis_index("groups")
         for ref, (mine, other) in zip(far, parts):
             ref[:, pl.ds(pl.multiple_of(group * cut, LANES), cut)] = mine[:, :cut]
-            ref[:, pl.ds(pl.multiple_of((1 - group) * cut, LANES), cut)] = other[...]
+            ref[:, pl.ds(pl.multiple_of((1 - group) * cut, LANES), cut)] = other[:, :cut]
         groups.append([[[(ref, at, to) for _, at, to in pieces] for pieces in spots] for ref in far])
     nh = out.shape[0]
     agg = []
@@ -478,37 +517,51 @@
     lanes = kn + width
     cut = lanes // 2 if two and lax.axis_size("groups") == 2 else 0
     plans = [
-        [(0, 0, 0), (1, 0, k)],
         [(2, 0, 0), (3, 0, kn)],
         [(2, 1, 0), (3, 1, kn)],
-        [(1, 1, cut)],
+        [(1, 1, 0)],
         [(0, 1, 0)],
-    ] + ([[]] if cut else [])
-    halves = {3: 1, 5: 2}
+    ] + ([[], []] if cut else [])
+    halves = {4: ((0, 0), (2, cut)), 5: ((1, 0),)} if cut else {}
+
+    def copying(kernel, args, scratch, shapes, n_copies, name):
+        return call(
+            kernel,
+            tuple(bf16(*shape) for shape in shapes),
+            args,
+            scratch=scratch
+            + [pltpu.VMEM(shape, jnp.bfloat16) for shape in shapes]
+            + [pltpu.SemaphoreType.DMA((n_copies,))],
+            memory=[pl.ANY] * len(args),
+            out_memory=pl.ANY,
+            limit=3 * VMEM_BYTES,
+            name=name,
+        )
+
     block = own_coarse + 16
     near, far = hr // 2 + cp // 2 + block, cp // 2 + block
-    widths = [k + width + LANES, lanes, lanes, cut + width, k] + ([cut] if cut else [])
-    shapes = [(w_hidden, n) for n in widths]
     direct = parts != RELAYED
-    shapes += [(near, width), (near, width)] + [(far, width)] * direct
-    shapes += [(cp, width), (block, width)]
+    shapes = [(w_hidden, k + width + LANES), (near, width), (near, width)]
+    shapes += [(far, width)] * direct + [(cp, width), (block, width)]
     small = [edge_b1, node_b1, nodes, halo_row, coarse_edges]
     small += [x.reshape(1, own_coarse) for x in (coarse_send, coarse_recv)]
-    n_copies = len(small) + sum(len(p) for p in plans) + len(shapes)
-    made = call(
-        functools.partial(prepare_kernel, plans, halves, cut, len(small)),
-        tuple(bf16(*shape) for shape in shapes),
-        [edge_w1, edge_w2, node_w1, node_w2, *small],
-        scratch=[pltpu.VMEM(x.shape, x.dtype) for x in small]
-        + [pltpu.VMEM(shape, jnp.bfloat16) for shape in shapes]
-        + [pltpu.SemaphoreType.DMA((n_copies,))],
-        memory=[pl.ANY] * (4 + len(small)),
-        out_memory=pl.ANY,
-        limit=3 * VMEM_BYTES,
-        name="weights_and_halo_rows",
-    )
-    first_pack, node0, node1, mixed, edge1, *node1_half = made[: len(widths)]
-    *rows_out, coarse_own, block = made[len(widths) :]
+    first_pack, *rows_out, coarse_own, block = copying(
+        functools.partial(first_kernel, 2 + len(small), len(shapes)),
+        [edge_w1, edge_w2, *small],
+        [pltpu.VMEM(x.shape, x.dtype) for x in small],
+        shapes,
+        len(small) + 2 + len(shapes),
+        "first_weights_and_rows",
+    )
+    widths = [lanes, lanes, width, k] + ([cut + width // 2, cut] if cut else [])
+    later = copying(
+        functools.partial(later_kernel, plans, halves),
+        [edge_w1, edge_w2, node_w1, node_w2],
+        [],
+        [(w_hidden, n) for n in widths],
+        sum(len(p) for p in plans) + len(widths),
+        "later_weights",
+    )
     node_spots = (((0, 0, kn),), ((0, kn, lanes),))
 
     send_col = fine_send.reshape(fine_count, 1)
@@ -534,7 +587,10 @@
         return [shift(to_next, 1), *between, shift(to_prev, parts - 1)]
 
     def far_rows(moved):
-        return [shift(moved[0], 1)] if parts == RELAYED else moved[1:-1]
+        if parts != RELAYED:
+            return moved[1:-1]
+        rows = moved[0].shape[0] - hr // 2
+        return [shift(call(tail_kernel, bf16(rows, width), [moved[0]], name="far_rows"), 1)]
 
     def gather(nodes, *carried):
         return call(
@@ -545,17 +601,18 @@
             name="gather_rows",
         )
 
-    def fine_update(s, fine, sent, received, halo, weights, spots):
+    def fine_update(s, fine, sent, received, halo, weights, spots, halved=0):
         outs = [bf16(fine_count, width)]
         if s == 0:
             outs.append(jax.ShapeDtypeStruct((8, hidden), jnp.float32))
         fine_rows = nh - cp // 2
         outs.append(bf16(fine_rows, width))
         return call(
-            functools.partial(fine_kernel, tile, sizes, spots, s),
+            functools.partial(fine_kernel, tile, sizes, spots, s, halved),
             tuple(outs),
             [fine, sent, received, send_col, recv_row, edge_gain] + halo + weights + ([bias_rows] if s else []),
-            scratch=[pltpu.VMEM((2 * hr, width), jnp.bfloat16)],
+            scratch=[pltpu.VMEM((2 * hr, width), jnp.bfloat16)]
+            + ([pltpu.VMEM((w_hidden, width), jnp.bfloat16)] * 2 if halved else []),
             flops=8 * fine_count * width * hidden,
             name="fine_edges",
         )
@@ -568,13 +625,14 @@
             name="own_sums",
         )
 
-    def coarse_update(s, new_fine, coarse_own, state, arrived, weights, spots):
+    def coarse_update(s, new_fine, coarse_own, state, arrived, weights, spots, halved=0):
         aggs = [bf16(cp // 2, width), jax.ShapeDtypeStruct((cp // 2, width), jnp.float32)]
         return call(
-            functools.partial(coarse_kernel, ctile, sizes, spots, s),
+            functools.partial(coarse_kernel, ctile, sizes, spots, s, halved),
             (bf16(coarse_count, width + LANES), *aggs),
             [new_fine, recv_row, coarse_own, edge_gain, bias_rows, state] + arrived + weights,
-            scratch=[pltpu.VMEM((parts * cp, width), jnp.bfloat16)],
+            scratch=[pltpu.VMEM((parts * cp, width), jnp.bfloat16)]
+            + ([pltpu.VMEM((w_hidden, width), jnp.bfloat16)] * 2 if halved else []),
             flops=COARSE_FLOPS[s],
             name="coarse_edges_and_sums",
         )
@@ -613,7 +671,10 @@
 
     far_first = spread(first_pack)
     moved = exchange(*rows_out)
-    send_col, recv_col, recv_row = after((send_col, recv_col, recv_row))
+    send_col, recv_col, recv_row, *later = after(
+        (send_col, recv_col, recv_row, *later, rows_out[0])
+    )[:-1]
+    node0, node1, edge1_w2, edge1, *sent_halves = later
     if two:
         near, sent, received = gather(nodes, swap(first_pack))
     else:
@@ -623,41 +684,9 @@
     swapped = {i: swap(moved[i]) for i in (0, -1)}
     weights = [first_pack, near, *both(far_first)] if two else shards(first_pack, far_first)
     spots = (((0, 0, k),), ((0, k, k + width),))
-    far = spread(mixed)
+    far = across(sent_halves[0]) if cut else spread(edge1_w2)
     fine_edges, bias_rows, other = fine_update(
         0, fine_edges, sent, received, halo_of(moved, swapped), weights, spots
-    )
-    other, far, *relayed = after((other, far, *relayed))
-    swapped = [swapped[0], *(swap(m) for m in relayed), swapped[-1]]
-    moved = [moved[0], *relayed, moved[-1]]
-    partial = core_sum(own_sums(fine_edges), other)
-    mixed = shards(mixed, far)
-    fine_part = chip_sums(partial)
-    state, other, own = coarse_update(
-        0, fine_edges, coarse_own, block, pairs(moved, swapped), weights, spots
-    )
-    if cut:
-        others = other_group(call(part_kernel, bf16(w_hidden, cut), [far], name="part"))
-        own, others = after((own, others))
-        weights = both(node0) + pairs(mixed[2:], both(others))
-    else:
-        weights = shards(node0, spread(node0))
-    sums = [fine_part, chip_sums(core_sum(own, other))]
-    sums[1][-1], edge1 = after((sums[1][-1], edge1))
-    far = spread(edge1)
-    halves = node_update(0, nodes, sums, weights, node_spots, cut)
-
-    *rows_out, coarse_own, nodes = node_rows_out(*halves)
-    moved = exchange(*rows_out)
-    sent, received = gather(nodes)
-    *moved, far, sent = after((*moved, far, sent))
-    weights = pairs(shards(edge1, far), mixed)
-    spots = (((0, 0, k),), ((1, cut, cut + width),))
-    relayed = far_rows(moved)
-    swapped = {i: swap(moved[i]) for i in (0, -1)}
-    far = across(node1_half[0]) if cut else spread(node1)
-    fine_edges, other = fine_update(
-        1, fine_edges, sent, received, halo_of(moved, swapped), weights, spots
     )
     other, far, *relayed = after((other, far, *relayed))
     swapped = [swapped[0], *(swap(m) for m in relayed), swapped[-1]]
@@ -665,7 +694,52 @@
     partial = core_sum(own_sums(fine_edges), other)
     fine_part = chip_sums(partial)
     state, other, own = coarse_update(
-        1, fine_edges, coarse_own, state, pairs(moved, swapped), weights, spots
+        0, fine_edges, coarse_own, block, pairs(moved, swapped), weights, spots
+    )
+    if cut:
+        node_part, edge_part = call(
+            parts_kernel, (bf16(w_hidden, cut), bf16(w_hidden, width // 2)), [far], name="parts"
+        )
+        others = other_group(node_part)
+        own, others = after((own, others))
+    sums = [fine_part, chip_sums(core_sum(own, other))]
+    if cut:
+        weights = both(node0) + pairs(both(far), both(others))
+    else:
+        weights = shards(node0, spread(node0))
+    sums[1][-1], edge1 = after((sums[1][-1], edge1))
+    mixed = far
+    far = spread(edge1)
+    halves = node_update(0, nodes, sums, weights, node_spots, cut)
+
+    *rows_out, coarse_own, nodes = node_rows_out(*halves)
+    moved = exchange(*rows_out)
+    sent, received = gather(nodes)
+    if cut:
+        edge_part = other_group(edge_part)
+        *moved, far, sent, edge_part = after((*moved, far, sent, edge_part))
+    else:
+        *moved, far, sent = after((*moved, far, sent))
+    halved = width // 2 if cut else 0
+    if cut:
+        w2_parts = pairs(both(mixed), both(edge_part))
+        weights = pairs(both(edge1), both(edge1_w2)) + both(far) + w2_parts
+    else:
+        weights = pairs(shards(edge1, far), shards(edge1_w2, mixed))
+    spots = (((0, 0, k),), ((1, 0, width),))
+    relayed = far_rows(moved)
+    swapped = {i: swap(moved[i]) for i in (0, -1)}
+    far = across(sent_halves[1]) if cut else spread(node1)
+    fine_edges, other = fine_update(
+        1, fine_edges, sent, received, halo_of(moved, swapped), weights, spots, halved
+    )
+    other, far, *relayed = after((other, far, *relayed))
+    swapped = [swapped[0], *(swap(m) for m in relayed), swapped[-1]]
+    moved = [moved[0], *relayed, moved[-1]]
+    partial = core_sum(own_sums(fine_edges), other)
+    fine_part = chip_sums(partial)
+    state, other, own = coarse_update(
+        1, fine_edges, coarse_own, state, pairs(moved, swapped), weights, spots, halved
     )
     if cut:
         others = other_group(far)

time: 93.9 us -> 92.6 us (0.986)
  waiting for transfers between devices: 28.5 us -> 23.9 us
  Pallas kernels: 37.8 us -> 39.5 us
  starting transfers between devices: 26.3 us -> 27.6 us
    pallas_call x18 -> x21, Pallas kernels: 37.8 us -> 39.5 us  [call(): pl.pallas_call(kernel, out_shape=out_shape, in_specs=in_specs, out_specs=...]
    ppermute x6, waiting for transfers between devices: 6.75 us -> 5.07 us  [shift(): lax.ppermute(x, 'mesh', [(i, (i + by) % parts) for i in range(parts)])]
    ppermute x8, waiting for transfers between devices: 10.4 us -> 8.81 us  [across(): return lax.ppermute(x, 'feat', [(i, i ^ 2) for i in range(cores)])]
    ppermute x2 -> x3, starting transfers between devices: 3.11 us -> 4.06 us  [other_group(): return lax.ppermute(x, 'groups', [(0, 1), (1, 0)])]
    ppermute x23 -> x24, waiting for transfers between devices: 9.87 us -> 9.49 us  [swap(): return lax.ppermute(x, 'feat', [(i, i ^ 1) for i in range(cores)])]
    ppermute x23 -> x24, starting transfers between devices: 4.43 us -> 4.47 us  [swap(): return lax.ppermute(x, 'feat', [(i, i ^ 1) for i in range(cores)])]
  transfers between devices with their start and end apart: 39 -> 41, of which waited for: 20 -> 16; matrix products, arithmetic and copies ran while one was open for 1% -> 1% of each run, Pallas kernels for 31% -> 34%
where the time goes in v6:
time: 92.6 us; the launch traced here: 92.3 us
  Pallas kernels  39.5 us (43%)
  starting transfers between devices  27.6 us (30%)
  waiting for transfers between devices  23.9 us (26%)
    pallas_call x21, Pallas kernels, call(): pl.pallas_call(kernel, out_shape=out_shape, in_specs=in_specs, out_specs=...  39.5 us
    ppermute x6, starting transfers between devices, shift(): lax.ppermute(x, 'mesh', [(i, (i + by) % parts) for i in range(parts)])  9.99 us
    ppermute x24, waiting for transfers between devices, swap(): return lax.ppermute(x, 'feat', [(i, i ^ 1) for i in range(cores)])  9.49 us
    ppermute x8, starting transfers between devices, across(): return lax.ppermute(x, 'feat', [(i, i ^ 2) for i in range(cores)])  9.12 us
    ppermute x8, waiting for transfers between devices, across(): return lax.ppermute(x, 'feat', [(i, i ^ 2) for i in range(cores)])  8.81 us
    ppermute x6, waiting for transfers between devices, shift(): lax.ppermute(x, 'mesh', [(i, (i + by) % parts) for i in range(parts)])  5.07 us
    ppermute x24, starting transfers between devices, swap(): return lax.ppermute(x, 'feat', [(i, i ^ 1) for i in range(cores)])  4.47 us
    ppermute x3, starting transfers between devices, other_group(): return lax.ppermute(x, 'groups', [(0, 1), (1, 0)])  4.06 us
  transfers between devices with their start and end apart: 41, of which 16 were waited for; matrix products, arithmetic and copies ran while one was open for 1% of the time, Pallas kernels for 34%

profile of v6, /device:TPU:0, one launch (start us, length us, event | category | flops | bytes accessed | tf_op | source)
XLA Modules:
  0.0 92.3 jit_solution(5610574156095617853)
XLA Ops:
  0.0 3.2 %first_weights_and_rows.1 = (bf16[128,2176]{1,0:T(8,128)(2,1)}, bf16[240,512]{1,0:T(8,128)(2,1)}, bf16[240,512]{1,0:T(8,128)(2,1)}, bf16[128,512]{1,0:T(8,128)(2,1)}, bf16[112,512]{1,0:T(8,128)(2,1)}) custom-call(bf16[2,128,1536]{2,1,0:T(8,128)(2,1)} %refs_0_.5, bf16[2,128,512]{2,1,0:T(8,128)(2,1)} %refs_1_.3, bf16[2,128]{1,0:T(2,128)(2,1)} %refs_2_.4, ...), custom_call_target="tpu_custom_call" | custom-call | tf_op jit(solution)/shard_map/first_weights_and_rows/pallas_call | solution.py:76
  3.7 2.5 %collective-permute-start.2 = (bf16[128,2176]{1,0:T(8,128)(2,1)}, bf16[128,2176]{1,0:T(8,128)(2,1)S(1)}, u32[]{:S(2)}, u32[]{:S(2)}) collective-permute-start(bf16[128,2176]{1,0:T(8,128)(2,1)} %get-tuple-element.69.refs_10_.refs_12_), channel_id=1, source_target_pairs={{0,2},{1,3},{2,0},{3,1},{4,6},{5,7},{6,4},{7,5},{8,10},{9,11},{10,... | collective-permute-start | bytes 1671176 | tf_op jit(solution)/shard_map/ppermute | solution.py:491
  6.3 3.6 %collective-permute-start.1 = (bf16[240,512]{1,0:T(8,128)(2,1)}, bf16[240,512]{1,0:T(8,128)(2,1)}, u32[]{:S(2)}, u32[]{:S(2)}) collective-permute-start(bf16[240,512]{1,0:T(8,128)(2,1)} %get-tuple-element.68), channel_id=1, source_target_pairs={{0,12},{4,0},{8,4},{12,8},{1,13},{5,1},{9,5},{13,9},{2,14},{6,2},{... | collective-permute-start | bytes 737288 | tf_op jit(solution)/shard_map/ppermute | solution.py:494
  9.9 2.4 %later_weights.1 = (bf16[128,1536]{1,0:T(8,128)(2,1)}, bf16[128,1536]{1,0:T(8,128)(2,1)}, bf16[128,512]{1,0:T(8,128)(2,1)}, bf16[128,1536]{1,0:T(8,128)(2,1)}, b...) custom-call(bf16[2,128,1536]{2,1,0:T(8,128)(2,1)} %refs_0_.5, bf16[2,128,512]{2,1,0:T(8,128)(2,1)} %refs_1_.3, ...), custom_call_target="tpu_custom_call" | custom-call | tf_op jit(solution)/shard_map/later_weights/pallas_call | solution.py:76
  13.0 4.7 %gather_rows.2 = (bf16[128,2176]{1,0:T(8,128)(2,1)S(1)}, bf16[1536,512]{1,0:T(8,128)(2,1)S(1)}, bf16[1536,512]{1,0:T(8,128)(2,1)S(1)}) custom-call(bf16[1024,512]{1,0:T(8,128)(2,1)S(1)} %copy-done, s32[1536,1]{1,0:T(8,128)S(1)} %copy.17.send.refs_3_, s32[1536,1]{1,0:T(8,128)S(1)} %copy.18.recv, bf16[128,2176]{1,0:T(8,128)(2,1)} %collective-permute-done.3.refs_0_), custom_call_target="tpu_custom_call" | custom-call | flops 3221225472 | tf_op jit(solution)/shard_map/gather_rows/pallas_call | solution.py:76
  17.7 4.1 %collective-permute-done.refs_6_.rows = bf16[240,512]{1,0:T(8,128)(2,1)S(1)} collective-permute-done((bf16[240,512]{1,0:T(8,128)(2,1)}, bf16[240,512]{1,0:T(8,128)(2,1)S(1)}, u32[]{:S(2)}, u32[]{:S(2)}) %collective-permute-start) | collective-permute-done | bytes 245792 | tf_op jit(solution)/shard_map/ppermute | solution.py:494
  22.9 1.9 %collective-permute-start.8 = (bf16[176,512]{1,0:T(8,128)(2,1)S(1)}, bf16[176,512]{1,0:T(8,128)(2,1)S(1)}, u32[]{:S(2)}, u32[]{:S(2)}) collective-permute-start(bf16[176,512]{1,0:T(8,128)(2,1)S(1)} %far_rows.2), channel_id=1, source_target_pairs={{0,4},{4,8},{8,12},{12,0},{1,5},{5,9},{9,13},{13,1},{2,6},{6,10},{... | collective-permute-start | bytes 540680 | tf_op jit(solution)/shard_map/ppermute | solution.py:494
  24.8 6.2 %fine_edges.2 = (bf16[1536,512]{1,0:T(8,128)(2,1)S(1)}, f32[8,512]{1,0:T(8,128)S(1)}, bf16[448,512]{1,0:T(8,128)(2,1)S(1)}) custom-call(bf16[1536,512]{1,0:T(8,128)(2,1)S(1)} %copy-done.11, bf16[1536,512]{1,0:T(8,128)(2,1)S(1)} %get-tuple-element.79.refs_1_, bf16[1536,512]{1,0:T(8,128)(2,1)S(1)} %get-tuple-element.80.refs_2_, ...), custom_call_target="tpu_custom_call" | custom-call | flops 3221225472 | tf_op jit(solution)/shard_map/fine_edges/pallas_call | solution.py:76
  33.5 1.6 %collective-permute-start.10 = (bf16[448,512]{1,0:T(8,128)(2,1)S(1)}, bf16[448,512]{1,0:T(8,128)(2,1)S(1)}, u32[]{:S(2)}, u32[]{:S(2)}) collective-permute-start(bf16[448,512]{1,0:T(8,128)(2,1)S(1)} %core_sum.4.refs_3_), channel_id=1, source_target_pairs={{0,2},{1,3},{2,0},{3,1},{4,6},{5,7},{6,4},{7,5},{8,10},{9,11},{10,... | collective-permute-start | bytes 1376264 | tf_op jit(solution)/shard_map/ppermute | solution.py:491
  35.1 1.6 %collective-permute-start.12 = (bf16[128,768]{1,0:T(8,128)(2,1)S(1)}, bf16[128,768]{1,0:T(8,128)(2,1)S(1)}, u32[]{:S(2)}, u32[]{:S(2)}) collective-permute-start(bf16[128,768]{1,0:T(8,128)(2,1)S(1)} %get-tuple-element.96), channel_id=1, source_target_pairs={{0,16},{16,0},{1,17},{17,1},{2,18},{18,2},{3,19},{19,3},{4,20},{20... | collective-permute-start | bytes 589832 | tf_op jit(solution)/shard_map/ppermute | solution.py:670
  37.2 1.5 %collective-permute-done.11.refs_9_ = bf16[176,512]{1,0:T(8,128)(2,1)S(1)} collective-permute-done((bf16[176,512]{1,0:T(8,128)(2,1)S(1)}, bf16[176,512]{1,0:T(8,128)(2,1)S(1)}, u32[]{:S(2)}, u32[]{:S(2)}) %collective-permute-start.11) | collective-permute-done | bytes 180256 | tf_op jit(solution)/shard_map/ppermute | solution.py:488
  38.7 3.8 %coarse_edges_and_sums.2 = (bf16[384,640]{1,0:T(8,128)(2,1)S(1)}, bf16[64,512]{1,0:T(8,128)(2,1)S(1)}, f32[64,512]{1,0:T(8,128)S(1)}) custom-call(bf16[1536,512]{1,0:T(8,128)(2,1)S(1)} %get-tuple-element.87.new_fine.refs_0_, s32[1,1536]{1,0:T(1,128)S(1)} %reshape.23.refs_4_.recv_row.refs_1_, bf16[128,512]{1,0:T(8,128)(2,1)S(1)} %copy-done.6, ...), custom_call_target="tpu_custom_call" | custom-call | tf_op jit(solution)/shard_map/coarse_edges_and_sums/pallas_call | solution.py:76
  43.1 1.0 %collective-permute-done.13.arrived = bf16[64,512]{1,0:T(8,128)(2,1)S(1)} collective-permute-done((bf16[64,512]{1,0:T(8,128)(2,1)S(1)}, bf16[64,512]{1,0:T(8,128)(2,1)S(1)}, u32[]{:S(2)}, u32[]{:S(2)}) %collective-permute-start.13) | collective-permute-done | bytes 65568 | tf_op jit(solution)/shard_map/ppermute | solution.py:488
  44.8 3.7 %collective-permute-done.14.refs_6_ = bf16[64,512]{1,0:T(8,128)(2,1)S(1)} collective-permute-done((bf16[64,512]{1,0:T(8,128)(2,1)S(1)}, bf16[64,512]{1,0:T(8,128)(2,1)S(1)}, u32[]{:S(2)}, u32[]{:S(2)}) %collective-permute-start.14) | collective-permute-done | bytes 65568 | tf_op jit(solution)/shard_map/ppermute | solution.py:491
  48.5 1.7 %node_update.2.refs_0_ = bf16[512,512]{1,0:T(8,128)(2,1)S(1)} custom-call(bf16[1024,512]{1,0:T(8,128)(2,1)S(1)} %copy-done, f32[8,512]{1,0:T(8,128)S(1)} %get-tuple-element.86.refs_4_.refs_1_.refs_20_, bf16[2,512]{1,0:T(2,128)(2,1)S(1)} %copy-done.9, bf16[448,512]{1,0:T(8,128)(2,1)S(1)} %core_sum.4.refs_3_, ...), custom_call_target="tpu_custom_call" | custom-call | tf_op jit(solution)/shard_map/node_update/pallas_call | solution.py:76
  50.9 1.5 %collective-permute-start.22 = (bf16[128,256]{1,0:T(8,128)(2,1)S(1)}, bf16[128,256]{1,0:T(8,128)(2,1)S(1)}, u32[]{:S(2)}, u32[]{:S(2)}) collective-permute-start(bf16[128,256]{1,0:T(8,128)(2,1)S(1)} %get-tuple-element.108), channel_id=1, source_target_pairs={{0,16},{16,0},{1,17},{17,1},{2,18},{18,2},{3,19},{19,3},{4,20},{20... | collective-permute-start | bytes 196616 | tf_op jit(solution)/shard_map/ppermute | solution.py:670
  53.5 3.5 %collective-permute-start.20 = (bf16[128,512]{1,0:T(8,128)(2,1)S(1)}, bf16[128,512]{1,0:T(8,128)(2,1)S(1)}, u32[]{:S(2)}, u32[]{:S(2)}) collective-permute-start(bf16[128,512]{1,0:T(8,128)(2,1)S(1)} %get-tuple-element.105), channel_id=1, source_target_pairs={{0,12},{4,0},{8,4},{12,8},{1,13},{5,1},{9,5},{13,9},{2,14},{6,2},{... | collective-permute-start | bytes 393224 | tf_op jit(solution)/shard_map/ppermute | solution.py:494
  57.1 3.5 %gather_rows.3 = (bf16[1536,512]{1,0:T(8,128)(2,1)S(1)}, bf16[1536,512]{1,0:T(8,128)(2,1)S(1)}) custom-call(bf16[1024,512]{1,0:T(8,128)(2,1)S(1)} %get-tuple-element.103.nodes.refs_0_, s32[1536,1]{1,0:T(8,128)S(1)} %copy.17.send.refs_3_, s32[1536,1]{1,0:T(8,128)S(1)} %copy.18.recv), custom_call_target="tpu_custom_call" | custom-call | flops 3221225472 | tf_op jit(solution)/shard_map/gather_rows/pallas_call | solution.py:76
  60.6 1.2 %collective-permute-done.21.refs_14_.refs_16_ = bf16[128,1536]{1,0:T(8,128)(2,1)S(1)} collective-permute-done((bf16[128,1536]{1,0:T(8,128)(2,1)S(1)}, bf16[128,1536]{1,0:T(8,128)(2,1)S(1)}, u32[]{:S(2)}, u32[]{:S(2)}) %collective-permute-start.21) | collective-permute-done | bytes 393248 | tf_op jit(solution)/shard_map/ppermute | solution.py:491
  64.3 1.1 %collective-permute-start.29 = (bf16[128,768]{1,0:T(8,128)(2,1)S(1)}, bf16[128,768]{1,0:T(8,128)(2,1)S(1)}, u32[]{:S(2)}, u32[]{:S(2)}) collective-permute-start(bf16[128,768]{1,0:T(8,128)(2,1)S(1)} %copy-done.15), channel_id=1, source_target_pairs={{0,2},{1,3},{2,0},{3,1},{4,6},{5,7},{6,4},{7,5},{8,10},{9,11},{10,... | collective-permute-start | bytes 589832 | tf_op jit(solution)/shard_map/ppermute | solution.py:491
  66.1 5.3 %fine_edges.3 = (bf16[1536,512]{1,0:T(8,128)(2,1)S(1)}, bf16[448,512]{1,0:T(8,128)(2,1)S(1)}) custom-call(bf16[1536,512]{1,0:T(8,128)(2,1)S(1)} %get-tuple-element.87.new_fine.refs_0_, bf16[1536,512]{1,0:T(8,128)(2,1)S(1)} %get-tuple-element.109.refs_1_, bf16[1536,512]{1,0:T(8,128)(2,1)S(1)} %get-tuple-element.110.refs_2_, s32[1536,1]{1,0:T(8,128)S(1)} %copy.17.send.refs_3_, ...), custom_call_target="tpu_custom_call" | custom-call | flops 3221225472 | tf_op jit(solution)/shard_map/fine_edges/pallas_call | solution.py:76
  72.4 0.9 %collective-permute-done.31.arrived = bf16[448,512]{1,0:T(8,128)(2,1)S(1)} collective-permute-done((bf16[448,512]{1,0:T(8,128)(2,1)S(1)}, bf16[448,512]{1,0:T(8,128)(2,1)S(1)}, u32[]{:S(2)}, u32[]{:S(2)}) %collective-permute-start.31) | collective-permute-done | bytes 458784 | tf_op jit(solution)/shard_map/ppermute | solution.py:488
  73.5 1.1 %collective-permute-start.32 = (bf16[448,512]{1,0:T(8,128)(2,1)S(1)}, bf16[448,512]{1,0:T(8,128)(2,1)S(1)}, u32[]{:S(2)}, u32[]{:S(2)}) collective-permute-start(bf16[448,512]{1,0:T(8,128)(2,1)S(1)} %core_sum.6.refs_3_), channel_id=1, source_target_pairs={{0,2},{1,3},{2,0},{3,1},{4,6},{5,7},{6,4},{7,5},{8,10},{9,11},{10,... | collective-permute-start | bytes 1376264 | tf_op jit(solution)/shard_map/ppermute | solution.py:491
  74.6 0.9 %collective-permute-start.34 = (bf16[128,768]{1,0:T(8,128)(2,1)S(1)}, bf16[128,768]{1,0:T(8,128)(2,1)S(1)}, u32[]{:S(2)}, u32[]{:S(2)}) collective-permute-start(bf16[128,768]{1,0:T(8,128)(2,1)S(1)} %collective-permute-done.29.refs_9_), channel_id=1, source_target_pairs={{0,16},{16,0},{1,17},{17,1},{2,18},{18,2},{3,19},{19,3},{4,20},{20... | collective-permute-start | bytes 589832 | tf_op jit(solution)/shard_map/ppermute | solution.py:670
  76.1 1.3 %collective-permute-done.33.refs_9_ = bf16[64,512]{1,0:T(8,128)(2,1)S(1)} collective-permute-done((bf16[64,512]{1,0:T(8,128)(2,1)S(1)}, bf16[64,512]{1,0:T(8,128)(2,1)S(1)}, u32[]{:S(2)}, u32[]{:S(2)}) %collective-permute-start.33) | collective-permute-done | bytes 65568 | tf_op jit(solution)/shard_map/ppermute | solution.py:488
  77.4 3.3 %coarse_edges_and_sums.3 = (bf16[384,640]{1,0:T(8,128)(2,1)}, bf16[64,512]{1,0:T(8,128)(2,1)S(1)}, f32[64,512]{1,0:T(8,128)S(1)}) custom-call(bf16[1536,512]{1,0:T(8,128)(2,1)S(1)} %get-tuple-element.116.new_fine.refs_0_, s32[1,1536]{1,0:T(1,128)S(1)} %reshape.23.refs_4_.recv_row.refs_1_, bf16[128,512]{1,0:T(8,128)(2,1)S(1)} %get-tuple-element.120.refs_2_, ...), custom_call_target="tpu_custom_call" | custom-call | tf_op jit(solution)/shard_map/coarse_edges_and_sums/pallas_call | solution.py:76
  81.8 1.0 %collective-permute-done.35.arrived = bf16[64,512]{1,0:T(8,128)(2,1)S(1)} collective-permute-done((bf16[64,512]{1,0:T(8,128)(2,1)S(1)}, bf16[64,512]{1,0:T(8,128)(2,1)S(1)}, u32[]{:S(2)}, u32[]{:S(2)}) %collective-permute-start.35) | collective-permute-done | bytes 65568 | tf_op jit(solution)/shard_map/ppermute | solution.py:488
  82.8 1.1 %collective-permute-start.36 = (bf16[64,512]{1,0:T(8,128)(2,1)S(1)}, bf16[64,512]{1,0:T(8,128)(2,1)S(1)}, u32[]{:S(2)}, u32[]{:S(2)}) collective-permute-start(bf16[64,512]{1,0:T(8,128)(2,1)S(1)} %core_sum.7.refs_5_), channel_id=1, source_target_pairs={{0,2},{1,3},{2,0},{3,1},{4,6},{5,7},{6,4},{7,5},{8,10},{9,11},{10,... | collective-permute-start | bytes 196616 | tf_op jit(solution)/shard_map/ppermute | solution.py:491
  83.9 3.6 %collective-permute-done.36.refs_6_ = bf16[64,512]{1,0:T(8,128)(2,1)S(1)} collective-permute-done((bf16[64,512]{1,0:T(8,128)(2,1)S(1)}, bf16[64,512]{1,0:T(8,128)(2,1)S(1)}, u32[]{:S(2)}, u32[]{:S(2)}) %collective-permute-start.36) | collective-permute-done | bytes 65568 | tf_op jit(solution)/shard_map/ppermute | solution.py:491
  87.5 1.7 %node_update.3.own = bf16[512,512]{1,0:T(8,128)(2,1)S(1)} custom-call(bf16[1024,512]{1,0:T(8,128)(2,1)S(1)} %get-tuple-element.103.nodes.refs_0_, f32[8,512]{1,0:T(8,128)S(1)} %get-tuple-element.86.refs_4_.refs_1_.refs_20_, bf16[2,512]{1,0:T(2,128)(2,1)S(1)} %copy-done.9, bf16[448,512]{1,0:T(8,128)(2,1)S(1)} %core_sum.6.refs_3_, ...), custom_call_target="tpu_custom_call" | custom-call | tf_op jit(solution)/shard_map/node_update/pallas_call | solution.py:76
  89.3 1.9 %collective-permute-done.40.other = bf16[512,512]{1,0:T(8,128)(2,1)S(1)} collective-permute-done((bf16[512,512]{1,0:T(8,128)(2,1)S(1)}, bf16[512,512]{1,0:T(8,128)(2,1)S(1)}, u32[]{:S(2)}, u32[]{:S(2)}) %collective-permute-start.40) | collective-permute-done | bytes 524320 | tf_op jit(solution)/shard_map/ppermute | solution.py:488
  91.2 1.0 %nodes_out.1 = bf16[1024,512]{1,0:T(8,128)(2,1)} custom-call(bf16[512,512]{1,0:T(8,128)(2,1)S(1)} %node_update.3.own, bf16[512,512]{1,0:T(8,128)(2,1)S(1)} %collective-permute-done.40.other), custom_call_target="tpu_custom_call" | custom-call | tf_op jit(solution)/shard_map/nodes_out/pallas_call | solution.py:76
  (108 shorter events, 14.2 us)
Async XLA Ops:
  3.2 9.8 %collective-permute-start.3 = (bf16[128,2176]{1,0:T(8,128)(2,1)}, bf16[128,2176]{1,0:T(8,128)(2,1)}, u32[]{:S(2)}, u32[]{:S(2)}) collective-permute-start(bf16[128,2176]{1,0:T(8,128)(2,1)} %get-tuple-element.69.refs_10_.refs_12_), channel_id=1, source_target_pairs={{0,1},{1,0},{2,3},{3,2},{4,5},{5,4},{6,7},{7,6},{8,9},{9,8},{10,11... | collective-permute-start | bytes 1671176 | tf_op jit(solution)/shard_map/ppermute | solution.py:488
  3.7 18.1 %collective-permute-start.2 = (bf16[128,2176]{1,0:T(8,128)(2,1)}, bf16[128,2176]{1,0:T(8,128)(2,1)S(1)}, u32[]{:S(2)}, u32[]{:S(2)}) collective-permute-start(bf16[128,2176]{1,0:T(8,128)(2,1)} %get-tuple-element.69.refs_10_.refs_12_), channel_id=1, source_target_pairs={{0,2},{1,3},{2,0},{3,1},{4,6},{5,7},{6,4},{7,5},{8,10},{9,11},{10,... | collective-permute-start | bytes 1671176 | tf_op jit(solution)/shard_map/ppermute | solution.py:491
  6.3 11.4 %collective-permute-start.1 = (bf16[240,512]{1,0:T(8,128)(2,1)}, bf16[240,512]{1,0:T(8,128)(2,1)}, u32[]{:S(2)}, u32[]{:S(2)}) collective-permute-start(bf16[240,512]{1,0:T(8,128)(2,1)} %get-tuple-element.68), channel_id=1, source_target_pairs={{0,12},{4,0},{8,4},{12,8},{1,13},{5,1},{9,5},{13,9},{2,14},{6,2},{... | collective-permute-start | bytes 737288 | tf_op jit(solution)/shard_map/ppermute | solution.py:494
  9.9 11.9 %collective-permute-start = (bf16[240,512]{1,0:T(8,128)(2,1)}, bf16[240,512]{1,0:T(8,128)(2,1)S(1)}, u32[]{:S(2)}, u32[]{:S(2)}) collective-permute-start(bf16[240,512]{1,0:T(8,128)(2,1)} %get-tuple-element.67), channel_id=1, source_target_pairs={{0,4},{4,8},{8,12},{12,0},{1,5},{5,9},{9,13},{13,1},{2,6},{6,10},{... | collective-permute-start | bytes 737288 | tf_op jit(solution)/shard_map/ppermute | solution.py:494
  21.8 2.9 %collective-permute-start.6 = (bf16[128,2176]{1,0:T(8,128)(2,1)S(1)}, bf16[128,2176]{1,0:T(8,128)(2,1)S(1)}, u32[]{:S(2)}, u32[]{:S(2)}) collective-permute-start(bf16[128,2176]{1,0:T(8,128)(2,1)S(1)} %collective-permute-done.2.refs_12_.refs_14_), channel_id=1, source_target_pairs={{0,1},{1,0},{2,3},{3,2},{4,5},{5,4},{6,7},{7,6},{8,9},{9,8},{10,11... | collective-permute-start | bytes 1671176 | tf_op jit(solution)/shard_map/ppermute | solution.py:488
  21.8 2.9 %collective-permute-start.4 = (bf16[240,512]{1,0:T(8,128)(2,1)S(1)}, bf16[240,512]{1,0:T(8,128)(2,1)S(1)}, u32[]{:S(2)}, u32[]{:S(2)}) collective-permute-start(bf16[240,512]{1,0:T(8,128)(2,1)S(1)} %collective-permute-done.refs_6_.rows), channel_id=1, source_target_pairs={{0,1},{1,0},{2,3},{3,2},{4,5},{5,4},{6,7},{7,6},{8,9},{9,8},{10,11... | collective-permute-start | bytes 737288 | tf_op jit(solution)/shard_map/ppermute | solution.py:488
  22.3 2.4 %collective-permute-start.5 = (bf16[240,512]{1,0:T(8,128)(2,1)}, bf16[240,512]{1,0:T(8,128)(2,1)S(1)}, u32[]{:S(2)}, u32[]{:S(2)}) collective-permute-start(bf16[240,512]{1,0:T(8,128)(2,1)} %collective-permute-done.1.refs_8_.refs_10_), channel_id=1, source_target_pairs={{0,1},{1,0},{2,3},{3,2},{4,5},{5,4},{6,7},{7,6},{8,9},{9,8},{10,11... | collective-permute-start | bytes 737288 | tf_op jit(solution)/shard_map/ppermute | solution.py:488
  22.3 8.7 %collective-permute-start.7 = (bf16[128,1024]{1,0:T(8,128)(2,1)S(1)}, bf16[128,1024]{1,0:T(8,128)(2,1)S(1)}, u32[]{:S(2)}, u32[]{:S(2)}) collective-permute-start(bf16[128,1024]{1,0:T(8,128)(2,1)S(1)} %copy-done.14), channel_id=1, source_target_pairs={{0,2},{1,3},{2,0},{3,1},{4,6},{5,7},{6,4},{7,5},{8,10},{9,11},{10,... | collective-permute-start | bytes 786440 | tf_op jit(solution)/shard_map/ppermute | solution.py:491
  22.9 8.7 %collective-permute-start.8 = (bf16[176,512]{1,0:T(8,128)(2,1)S(1)}, bf16[176,512]{1,0:T(8,128)(2,1)S(1)}, u32[]{:S(2)}, u32[]{:S(2)}) collective-permute-start(bf16[176,512]{1,0:T(8,128)(2,1)S(1)} %far_rows.2), channel_id=1, source_target_pairs={{0,4},{4,8},{8,12},{12,0},{1,5},{5,9},{9,13},{13,1},{2,6},{6,10},{... | collective-permute-start | bytes 540680 | tf_op jit(solution)/shard_map/ppermute | solution.py:494
  33.5 15.0 %collective-permute-start.10 = (bf16[448,512]{1,0:T(8,128)(2,1)S(1)}, bf16[448,512]{1,0:T(8,128)(2,1)S(1)}, u32[]{:S(2)}, u32[]{:S(2)}) collective-permute-start(bf16[448,512]{1,0:T(8,128)(2,1)S(1)} %core_sum.4.refs_3_), channel_id=1, source_target_pairs={{0,2},{1,3},{2,0},{3,1},{4,6},{5,7},{6,4},{7,5},{8,10},{9,11},{10,... | collective-permute-start | bytes 1376264 | tf_op jit(solution)/shard_map/ppermute | solution.py:491
  35.1 7.4 %collective-permute-start.12 = (bf16[128,768]{1,0:T(8,128)(2,1)S(1)}, bf16[128,768]{1,0:T(8,128)(2,1)S(1)}, u32[]{:S(2)}, u32[]{:S(2)}) collective-permute-start(bf16[128,768]{1,0:T(8,128)(2,1)S(1)} %get-tuple-element.96), channel_id=1, source_target_pairs={{0,16},{16,0},{1,17},{17,1},{2,18},{18,2},{3,19},{19,3},{4,20},{20... | collective-permute-start | bytes 589832 | tf_op jit(solution)/shard_map/ppermute | solution.py:670
  36.7 11.8 %collective-permute-start.15 = (bf16[128,1536]{1,0:T(8,128)(2,1)S(1)}, bf16[128,1536]{1,0:T(8,128)(2,1)S(1)}, u32[]{:S(2)}, u32[]{:S(2)}) collective-permute-start(bf16[128,1536]{1,0:T(8,128)(2,1)S(1)} %copy-done.4), channel_id=1, source_target_pairs={{0,1},{1,0},{2,3},{3,2},{4,5},{5,4},{6,7},{7,6},{8,9},{9,8},{10,11... | collective-permute-start | bytes 1179656 | tf_op jit(solution)/shard_map/ppermute | solution.py:488
  37.2 11.3 %collective-permute-start.16 = (bf16[128,1024]{1,0:T(8,128)(2,1)S(1)}, bf16[128,1024]{1,0:T(8,128)(2,1)S(1)}, u32[]{:S(2)}, u32[]{:S(2)}) collective-permute-start(bf16[128,1024]{1,0:T(8,128)(2,1)S(1)} %collective-permute-done.7.pack.refs_9_.refs_16_.refs_18_), channel_id=1, source_target_pairs={{0,1},{1,0},{2,3},{3,2},{4,5},{5,4},{6,7},{7,6},{8,9},{9,8},{10,11... | collective-permute-start | bytes 786440 | tf_op jit(solution)/shard_map/ppermute | solution.py:488
  42.5 6.0 %collective-permute-start.17 = (bf16[128,768]{1,0:T(8,128)(2,1)S(1)}, bf16[128,768]{1,0:T(8,128)(2,1)S(1)}, u32[]{:S(2)}, u32[]{:S(2)}) collective-permute-start(bf16[128,768]{1,0:T(8,128)(2,1)S(1)} %collective-permute-done.12.refs_10_), channel_id=1, source_target_pairs={{0,1},{1,0},{2,3},{3,2},{4,5},{5,4},{6,7},{7,6},{8,9},{9,8},{10,11... | collective-permute-start | bytes 589832 | tf_op jit(solution)/shard_map/ppermute | solution.py:488
  44.1 4.3 %collective-permute-start.14 = (bf16[64,512]{1,0:T(8,128)(2,1)S(1)}, bf16[64,512]{1,0:T(8,128)(2,1)S(1)}, u32[]{:S(2)}, u32[]{:S(2)}) collective-permute-start(bf16[64,512]{1,0:T(8,128)(2,1)S(1)} %core_sum.5.refs_5_), channel_id=1, source_target_pairs={{0,2},{1,3},{2,0},{3,1},{4,6},{5,7},{6,4},{7,5},{8,10},{9,11},{10,... | collective-permute-start | bytes 196616 | tf_op jit(solution)/shard_map/ppermute | solution.py:491
  50.2 2.2 %collective-permute-start.18 = (bf16[512,512]{1,0:T(8,128)(2,1)S(1)}, bf16[512,512]{1,0:T(8,128)(2,1)S(1)}, u32[]{:S(2)}, u32[]{:S(2)}) collective-permute-start(bf16[512,512]{1,0:T(8,128)(2,1)S(1)} %node_update.2.refs_0_), channel_id=1, source_target_pairs={{0,1},{1,0},{2,3},{3,2},{4,5},{5,4},{6,7},{7,6},{8,9},{9,8},{10,11... | collective-permute-start | bytes 1572872 | tf_op jit(solution)/shard_map/ppermute | solution.py:488
  50.3 11.5 %collective-permute-start.21 = (bf16[128,1536]{1,0:T(8,128)(2,1)S(1)}, bf16[128,1536]{1,0:T(8,128)(2,1)S(1)}, u32[]{:S(2)}, u32[]{:S(2)}) collective-permute-start(bf16[128,1536]{1,0:T(8,128)(2,1)S(1)} %copy-done.3), channel_id=1, source_target_pairs={{0,2},{1,3},{2,0},{3,1},{4,6},{5,7},{6,4},{7,5},{8,10},{9,11},{10,... | collective-permute-start | bytes 1179656 | tf_op jit(solution)/shard_map/ppermute | solution.py:491
  50.9 9.7 %collective-permute-start.22 = (bf16[128,256]{1,0:T(8,128)(2,1)S(1)}, bf16[128,256]{1,0:T(8,128)(2,1)S(1)}, u32[]{:S(2)}, u32[]{:S(2)}) collective-permute-start(bf16[128,256]{1,0:T(8,128)(2,1)S(1)} %get-tuple-element.108), channel_id=1, source_target_pairs={{0,16},{16,0},{1,17},{17,1},{2,18},{18,2},{3,19},{19,3},{4,20},{20... | collective-permute-start | bytes 196616 | tf_op jit(solution)/shard_map/ppermute | solution.py:670
  52.4 11.9 %collective-permute-start.25 = (bf16[128,1536]{1,0:T(8,128)(2,1)S(1)}, bf16[128,1536]{1,0:T(8,128)(2,1)S(1)}, u32[]{:S(2)}, u32[]{:S(2)}) collective-permute-start(bf16[128,1536]{1,0:T(8,128)(2,1)S(1)} %copy-done.3), channel_id=1, source_target_pairs={{0,1},{1,0},{2,3},{3,2},{4,5},{5,4},{6,7},{7,6},{8,9},{9,8},{10,11... | collective-permute-start | bytes 1179656 | tf_op jit(solution)/shard_map/ppermute | solution.py:488
  53.2 8.6 %collective-permute-start.19 = (bf16[128,512]{1,0:T(8,128)(2,1)S(1)}, bf16[128,512]{1,0:T(8,128)(2,1)S(1)}, u32[]{:S(2)}, u32[]{:S(2)}) collective-permute-start(bf16[128,512]{1,0:T(8,128)(2,1)S(1)} %get-tuple-element.104), channel_id=1, source_target_pairs={{0,4},{4,8},{8,12},{12,0},{1,5},{5,9},{9,13},{13,1},{2,6},{6,10},{... | collective-permute-start | bytes 393224 | tf_op jit(solution)/shard_map/ppermute | solution.py:494
  53.5 8.7 %collective-permute-start.20 = (bf16[128,512]{1,0:T(8,128)(2,1)S(1)}, bf16[128,512]{1,0:T(8,128)(2,1)S(1)}, u32[]{:S(2)}, u32[]{:S(2)}) collective-permute-start(bf16[128,512]{1,0:T(8,128)(2,1)S(1)} %get-tuple-element.105), channel_id=1, source_target_pairs={{0,12},{4,0},{8,4},{12,8},{1,13},{5,1},{9,5},{13,9},{2,14},{6,2},{... | collective-permute-start | bytes 393224 | tf_op jit(solution)/shard_map/ppermute | solution.py:494
  62.2 3.9 %collective-permute-start.27 = (bf16[128,1536]{1,0:T(8,128)(2,1)S(1)}, bf16[128,1536]{1,0:T(8,128)(2,1)S(1)}, u32[]{:S(2)}, u32[]{:S(2)}) collective-permute-start(bf16[128,1536]{1,0:T(8,128)(2,1)S(1)} %collective-permute-done.21.refs_14_.refs_16_), channel_id=1, source_target_pairs={{0,1},{1,0},{2,3},{3,2},{4,5},{5,4},{6,7},{7,6},{8,9},{9,8},{10,11... | collective-permute-start | bytes 1179656 | tf_op jit(solution)/shard_map/ppermute | solution.py:488
  62.8 3.3 %collective-permute-start.23 = (bf16[128,512]{1,0:T(8,128)(2,1)S(1)}, bf16[128,512]{1,0:T(8,128)(2,1)S(1)}, u32[]{:S(2)}, u32[]{:S(2)}) collective-permute-start(bf16[128,512]{1,0:T(8,128)(2,1)S(1)} %collective-permute-done.19.refs_6_.rows), channel_id=1, source_target_pairs={{0,1},{1,0},{2,3},{3,2},{4,5},{5,4},{6,7},{7,6},{8,9},{9,8},{10,11... | collective-permute-start | bytes 393224 | tf_op jit(solution)/shard_map/ppermute | solution.py:488
  62.8 3.3 %collective-permute-start.24 = (bf16[128,512]{1,0:T(8,128)(2,1)S(1)}, bf16[128,512]{1,0:T(8,128)(2,1)S(1)}, u32[]{:S(2)}, u32[]{:S(2)}) collective-permute-start(bf16[128,512]{1,0:T(8,128)(2,1)S(1)} %collective-permute-done.20.refs_8_.refs_10_), channel_id=1, source_target_pairs={{0,1},{1,0},{2,3},{3,2},{4,5},{5,4},{6,7},{7,6},{8,9},{9,8},{10,11... | collective-permute-start | bytes 393224 | tf_op jit(solution)/shard_map/ppermute | solution.py:488
  64.3 7.2 %collective-permute-start.29 = (bf16[128,768]{1,0:T(8,128)(2,1)S(1)}, bf16[128,768]{1,0:T(8,128)(2,1)S(1)}, u32[]{:S(2)}, u32[]{:S(2)}) collective-permute-start(bf16[128,768]{1,0:T(8,128)(2,1)S(1)} %copy-done.15), channel_id=1, source_target_pairs={{0,2},{1,3},{2,0},{3,1},{4,6},{5,7},{6,4},{7,5},{8,10},{9,11},{10,... | collective-permute-start | bytes 589832 | tf_op jit(solution)/shard_map/ppermute | solution.py:491
  65.4 6.1 %collective-permute-start.30 = (bf16[64,512]{1,0:T(8,128)(2,1)S(1)}, bf16[64,512]{1,0:T(8,128)(2,1)S(1)}, u32[]{:S(2)}, u32[]{:S(2)}) collective-permute-start(bf16[64,512]{1,0:T(8,128)(2,1)S(1)} %far_rows.3), channel_id=1, source_target_pairs={{0,4},{4,8},{8,12},{12,0},{1,5},{5,9},{9,13},{13,1},{2,6},{6,10},{... | collective-permute-start | bytes 196616 | tf_op jit(solution)/shard_map/ppermute | solution.py:494
  73.5 14.0 %collective-permute-start.32 = (bf16[448,512]{1,0:T(8,128)(2,1)S(1)}, bf16[448,512]{1,0:T(8,128)(2,1)S(1)}, u32[]{:S(2)}, u32[]{:S(2)}) collective-permute-start(bf16[448,512]{1,0:T(8,128)(2,1)S(1)} %core_sum.6.refs_3_), channel_id=1, source_target_pairs={{0,2},{1,3},{2,0},{3,1},{4,6},{5,7},{6,4},{7,5},{8,10},{9,11},{10,... | collective-permute-start | bytes 1376264 | tf_op jit(solution)/shard_map/ppermute | solution.py:491
  74.6 6.7 %collective-permute-start.34 = (bf16[128,768]{1,0:T(8,128)(2,1)S(1)}, bf16[128,768]{1,0:T(8,128)(2,1)S(1)}, u32[]{:S(2)}, u32[]{:S(2)}) collective-permute-start(bf16[128,768]{1,0:T(8,128)(2,1)S(1)} %collective-permute-done.29.refs_9_), channel_id=1, source_target_pairs={{0,16},{16,0},{1,17},{17,1},{2,18},{18,2},{3,19},{19,3},{4,20},{20... | collective-permute-start | bytes 589832 | tf_op jit(solution)/shard_map/ppermute | solution.py:670
  75.5 8.3 %collective-permute-start.37 = (bf16[128,1536]{1,0:T(8,128)(2,1)S(1)}, bf16[128,1536]{1,0:T(8,128)(2,1)S(1)}, u32[]{:S(2)}, u32[]{:S(2)}) collective-permute-start(bf16[128,1536]{1,0:T(8,128)(2,1)S(1)} %copy-done.2), channel_id=1, source_target_pairs={{0,1},{1,0},{2,3},{3,2},{4,5},{5,4},{6,7},{7,6},{8,9},{9,8},{10,11... | collective-permute-start | bytes 1179656 | tf_op jit(solution)/shard_map/ppermute | solution.py:488
  76.0 7.8 %collective-permute-start.38 = (bf16[128,768]{1,0:T(8,128)(2,1)S(1)}, bf16[128,768]{1,0:T(8,128)(2,1)S(1)}, u32[]{:S(2)}, u32[]{:S(2)}) collective-permute-start(bf16[128,768]{1,0:T(8,128)(2,1)S(1)} %collective-permute-done.29.refs_9_), channel_id=1, source_target_pairs={{0,1},{1,0},{2,3},{3,2},{4,5},{5,4},{6,7},{7,6},{8,9},{9,8},{10,11... | collective-permute-start | bytes 589832 | tf_op jit(solution)/shard_map/ppermute | solution.py:488
  81.3 6.3 %collective-permute-start.39 = (bf16[128,768]{1,0:T(8,128)(2,1)S(1)}, bf16[128,768]{1,0:T(8,128)(2,1)S(1)}, u32[]{:S(2)}, u32[]{:S(2)}) collective-permute-start(bf16[128,768]{1,0:T(8,128)(2,1)S(1)} %collective-permute-done.34.refs_10_), channel_id=1, source_target_pairs={{0,1},{1,0},{2,3},{3,2},{4,5},{5,4},{6,7},{7,6},{8,9},{9,8},{10,11... | collective-permute-start | bytes 589832 | tf_op jit(solution)/shard_map/ppermute | solution.py:488
  82.8 4.7 %collective-permute-start.36 = (bf16[64,512]{1,0:T(8,128)(2,1)S(1)}, bf16[64,512]{1,0:T(8,128)(2,1)S(1)}, u32[]{:S(2)}, u32[]{:S(2)}) collective-permute-start(bf16[64,512]{1,0:T(8,128)(2,1)S(1)} %core_sum.7.refs_5_), channel_id=1, source_target_pairs={{0,2},{1,3},{2,0},{3,1},{4,6},{5,7},{6,4},{7,5},{8,10},{9,11},{10,... | collective-permute-start | bytes 196616 | tf_op jit(solution)/shard_map/ppermute | solution.py:491
  (25 other events, 140.3 us)

commit v7 on v6

--- a/solution.py
+++ b/solution.py
@@ -30,7 +30,8 @@
 
 
 def silu(x):
-    return x * (0.5 * jnp.tanh(0.5 * x) + 0.5)
+    half = 0.5 * x
+    return half * jnp.tanh(half) + half
 
 
 def layer_norm(values, gain):

time: 92.6 us -> 92.6 us (level)
  transfers between devices with their start and end apart: 41 -> 41, of which waited for: 16 -> 16; matrix products, arithmetic and copies ran while one was open for 1% -> 1% of each run, Pallas kernels for 34% -> 35%
where the time goes in v7:
time: 92.6 us; the launch traced here: 92.4 us
  Pallas kernels  39.7 us (43%)
  starting transfers between devices  27.7 us (30%)
  waiting for transfers between devices  23.8 us (26%)
    pallas_call x21, Pallas kernels, call(): pl.pallas_call(kernel, out_shape=out_shape, in_specs=in_specs, out_specs=...  39.7 us
    ppermute x6, starting transfers between devices, shift(): lax.ppermute(x, 'mesh', [(i, (i + by) % parts) for i in range(parts)])  10 us
    ppermute x24, waiting for transfers between devices, swap(): return lax.ppermute(x, 'feat', [(i, i ^ 1) for i in range(cores)])  9.48 us
    ppermute x8, starting transfers between devices, across(): return lax.ppermute(x, 'feat', [(i, i ^ 2) for i in range(cores)])  9.13 us
    ppermute x8, waiting for transfers between devices, across(): return lax.ppermute(x, 'feat', [(i, i ^ 2) for i in range(cores)])  8.74 us
    ppermute x6, waiting for transfers between devices, shift(): lax.ppermute(x, 'mesh', [(i, (i + by) % parts) for i in range(parts)])  5.02 us
    ppermute x24, starting transfers between devices, swap(): return lax.ppermute(x, 'feat', [(i, i ^ 1) for i in range(cores)])  4.47 us
    ppermute x3, starting transfers between devices, other_group(): return lax.ppermute(x, 'groups', [(0, 1), (1, 0)])  4.05 us
  transfers between devices with their start and end apart: 41, of which 16 were waited for; matrix products, arithmetic and copies ran while one was open for 1% of the time, Pallas kernels for 35%

profile of v7, /device:TPU:0, one launch (start us, length us, event | category | flops | bytes accessed | tf_op | source)
XLA Modules:
  0.0 92.4 jit_solution(11085792450255130839)
XLA Ops:
  0.0 3.2 %first_weights_and_rows.1 = (bf16[128,2176]{1,0:T(8,128)(2,1)}, bf16[240,512]{1,0:T(8,128)(2,1)}, bf16[240,512]{1,0:T(8,128)(2,1)}, bf16[128,512]{1,0:T(8,128)(2,1)}, bf16[112,512]{1,0:T(8,128)(2,1)}) custom-call(bf16[2,128,1536]{2,1,0:T(8,128)(2,1)} %refs_0_.5, bf16[2,128,512]{2,1,0:T(8,128)(2,1)} %refs_1_.3, bf16[2,128]{1,0:T(2,128)(2,1)} %refs_2_.4, ...), custom_call_target="tpu_custom_call" | custom-call | tf_op jit(solution)/shard_map/first_weights_and_rows/pallas_call | solution.py:77
  3.7 2.5 %collective-permute-start.2 = (bf16[128,2176]{1,0:T(8,128)(2,1)}, bf16[128,2176]{1,0:T(8,128)(2,1)S(1)}, u32[]{:S(2)}, u32[]{:S(2)}) collective-permute-start(bf16[128,2176]{1,0:T(8,128)(2,1)} %get-tuple-element.69.refs_10_.refs_12_), channel_id=1, source_target_pairs={{0,2},{1,3},{2,0},{3,1},{4,6},{5,7},{6,4},{7,5},{8,10},{9,11},{10,... | collective-permute-start | bytes 1671176 | tf_op jit(solution)/shard_map/ppermute | solution.py:492
  6.3 3.6 %collective-permute-start.1 = (bf16[240,512]{1,0:T(8,128)(2,1)}, bf16[240,512]{1,0:T(8,128)(2,1)}, u32[]{:S(2)}, u32[]{:S(2)}) collective-permute-start(bf16[240,512]{1,0:T(8,128)(2,1)} %get-tuple-element.68), channel_id=1, source_target_pairs={{0,12},{4,0},{8,4},{12,8},{1,13},{5,1},{9,5},{13,9},{2,14},{6,2},{... | collective-permute-start | bytes 737288 | tf_op jit(solution)/shard_map/ppermute | solution.py:495
  9.9 2.4 %later_weights.1 = (bf16[128,1536]{1,0:T(8,128)(2,1)}, bf16[128,1536]{1,0:T(8,128)(2,1)}, bf16[128,512]{1,0:T(8,128)(2,1)}, bf16[128,1536]{1,0:T(8,128)(2,1)}, b...) custom-call(bf16[2,128,1536]{2,1,0:T(8,128)(2,1)} %refs_0_.5, bf16[2,128,512]{2,1,0:T(8,128)(2,1)} %refs_1_.3, ...), custom_call_target="tpu_custom_call" | custom-call | tf_op jit(solution)/shard_map/later_weights/pallas_call | solution.py:77
  13.0 4.7 %gather_rows.2 = (bf16[128,2176]{1,0:T(8,128)(2,1)S(1)}, bf16[1536,512]{1,0:T(8,128)(2,1)S(1)}, bf16[1536,512]{1,0:T(8,128)(2,1)S(1)}) custom-call(bf16[1024,512]{1,0:T(8,128)(2,1)S(1)} %copy-done, s32[1536,1]{1,0:T(8,128)S(1)} %copy.17.send.refs_3_, s32[1536,1]{1,0:T(8,128)S(1)} %copy.18.recv, bf16[128,2176]{1,0:T(8,128)(2,1)} %collective-permute-done.3.refs_0_), custom_call_target="tpu_custom_call" | custom-call | flops 3221225472 | tf_op jit(solution)/shard_map/gather_rows/pallas_call | solution.py:77
  17.7 4.1 %collective-permute-done.refs_6_.rows = bf16[240,512]{1,0:T(8,128)(2,1)S(1)} collective-permute-done((bf16[240,512]{1,0:T(8,128)(2,1)}, bf16[240,512]{1,0:T(8,128)(2,1)S(1)}, u32[]{:S(2)}, u32[]{:S(2)}) %collective-permute-start) | collective-permute-done | bytes 245792 | tf_op jit(solution)/shard_map/ppermute | solution.py:495
  22.9 1.9 %collective-permute-start.8 = (bf16[176,512]{1,0:T(8,128)(2,1)S(1)}, bf16[176,512]{1,0:T(8,128)(2,1)S(1)}, u32[]{:S(2)}, u32[]{:S(2)}) collective-permute-start(bf16[176,512]{1,0:T(8,128)(2,1)S(1)} %far_rows.2), channel_id=1, source_target_pairs={{0,4},{4,8},{8,12},{12,0},{1,5},{5,9},{9,13},{13,1},{2,6},{6,10},{... | collective-permute-start | bytes 540680 | tf_op jit(solution)/shard_map/ppermute | solution.py:495
  24.8 6.3 %fine_edges.2 = (bf16[1536,512]{1,0:T(8,128)(2,1)S(1)}, f32[8,512]{1,0:T(8,128)S(1)}, bf16[448,512]{1,0:T(8,128)(2,1)S(1)}) custom-call(bf16[1536,512]{1,0:T(8,128)(2,1)S(1)} %copy-done.11, bf16[1536,512]{1,0:T(8,128)(2,1)S(1)} %get-tuple-element.79.refs_1_, bf16[1536,512]{1,0:T(8,128)(2,1)S(1)} %get-tuple-element.80.refs_2_, ...), custom_call_target="tpu_custom_call" | custom-call | flops 3221225472 | tf_op jit(solution)/shard_map/fine_edges/pallas_call | solution.py:77
  33.5 1.6 %collective-permute-start.10 = (bf16[448,512]{1,0:T(8,128)(2,1)S(1)}, bf16[448,512]{1,0:T(8,128)(2,1)S(1)}, u32[]{:S(2)}, u32[]{:S(2)}) collective-permute-start(bf16[448,512]{1,0:T(8,128)(2,1)S(1)} %core_sum.4.refs_3_), channel_id=1, source_target_pairs={{0,2},{1,3},{2,0},{3,1},{4,6},{5,7},{6,4},{7,5},{8,10},{9,11},{10,... | collective-permute-start | bytes 1376264 | tf_op jit(solution)/shard_map/ppermute | solution.py:492
  35.1 1.6 %collective-permute-start.12 = (bf16[128,768]{1,0:T(8,128)(2,1)S(1)}, bf16[128,768]{1,0:T(8,128)(2,1)S(1)}, u32[]{:S(2)}, u32[]{:S(2)}) collective-permute-start(bf16[128,768]{1,0:T(8,128)(2,1)S(1)} %get-tuple-element.96), channel_id=1, source_target_pairs={{0,16},{16,0},{1,17},{17,1},{2,18},{18,2},{3,19},{19,3},{4,20},{20... | collective-permute-start | bytes 589832 | tf_op jit(solution)/shard_map/ppermute | solution.py:671
  37.2 1.5 %collective-permute-done.11.refs_9_ = bf16[176,512]{1,0:T(8,128)(2,1)S(1)} collective-permute-done((bf16[176,512]{1,0:T(8,128)(2,1)S(1)}, bf16[176,512]{1,0:T(8,128)(2,1)S(1)}, u32[]{:S(2)}, u32[]{:S(2)}) %collective-permute-start.11) | collective-permute-done | bytes 180256 | tf_op jit(solution)/shard_map/ppermute | solution.py:489
  38.7 3.9 %coarse_edges_and_sums.2 = (bf16[384,640]{1,0:T(8,128)(2,1)S(1)}, bf16[64,512]{1,0:T(8,128)(2,1)S(1)}, f32[64,512]{1,0:T(8,128)S(1)}) custom-call(bf16[1536,512]{1,0:T(8,128)(2,1)S(1)} %get-tuple-element.87.new_fine.refs_0_, s32[1,1536]{1,0:T(1,128)S(1)} %reshape.23.refs_4_.recv_row.refs_1_, bf16[128,512]{1,0:T(8,128)(2,1)S(1)} %copy-done.6, ...), custom_call_target="tpu_custom_call" | custom-call | tf_op jit(solution)/shard_map/coarse_edges_and_sums/pallas_call | solution.py:77
  43.1 1.0 %collective-permute-done.13.arrived = bf16[64,512]{1,0:T(8,128)(2,1)S(1)} collective-permute-done((bf16[64,512]{1,0:T(8,128)(2,1)S(1)}, bf16[64,512]{1,0:T(8,128)(2,1)S(1)}, u32[]{:S(2)}, u32[]{:S(2)}) %collective-permute-start.13) | collective-permute-done | bytes 65568 | tf_op jit(solution)/shard_map/ppermute | solution.py:489
  44.8 3.7 %collective-permute-done.14.refs_6_ = bf16[64,512]{1,0:T(8,128)(2,1)S(1)} collective-permute-done((bf16[64,512]{1,0:T(8,128)(2,1)S(1)}, bf16[64,512]{1,0:T(8,128)(2,1)S(1)}, u32[]{:S(2)}, u32[]{:S(2)}) %collective-permute-start.14) | collective-permute-done | bytes 65568 | tf_op jit(solution)/shard_map/ppermute | solution.py:492
  48.5 1.7 %node_update.2.refs_0_ = bf16[512,512]{1,0:T(8,128)(2,1)S(1)} custom-call(bf16[1024,512]{1,0:T(8,128)(2,1)S(1)} %copy-done, f32[8,512]{1,0:T(8,128)S(1)} %get-tuple-element.86.refs_4_.refs_1_.refs_20_, bf16[2,512]{1,0:T(2,128)(2,1)S(1)} %copy-done.9, bf16[448,512]{1,0:T(8,128)(2,1)S(1)} %core_sum.4.refs_3_, ...), custom_call_target="tpu_custom_call" | custom-call | tf_op jit(solution)/shard_map/node_update/pallas_call | solution.py:77
  50.9 1.5 %collective-permute-start.22 = (bf16[128,256]{1,0:T(8,128)(2,1)S(1)}, bf16[128,256]{1,0:T(8,128)(2,1)S(1)}, u32[]{:S(2)}, u32[]{:S(2)}) collective-permute-start(bf16[128,256]{1,0:T(8,128)(2,1)S(1)} %get-tuple-element.108), channel_id=1, source_target_pairs={{0,16},{16,0},{1,17},{17,1},{2,18},{18,2},{3,19},{19,3},{4,20},{20... | collective-permute-start | bytes 196616 | tf_op jit(solution)/shard_map/ppermute | solution.py:671
  53.6 3.5 %collective-permute-start.20 = (bf16[128,512]{1,0:T(8,128)(2,1)S(1)}, bf16[128,512]{1,0:T(8,128)(2,1)S(1)}, u32[]{:S(2)}, u32[]{:S(2)}) collective-permute-start(bf16[128,512]{1,0:T(8,128)(2,1)S(1)} %get-tuple-element.105), channel_id=1, source_target_pairs={{0,12},{4,0},{8,4},{12,8},{1,13},{5,1},{9,5},{13,9},{2,14},{6,2},{... | collective-permute-start | bytes 393224 | tf_op jit(solution)/shard_map/ppermute | solution.py:495
  57.1 3.5 %gather_rows.3 = (bf16[1536,512]{1,0:T(8,128)(2,1)S(1)}, bf16[1536,512]{1,0:T(8,128)(2,1)S(1)}) custom-call(bf16[1024,512]{1,0:T(8,128)(2,1)S(1)} %get-tuple-element.103.nodes.refs_0_, s32[1536,1]{1,0:T(8,128)S(1)} %copy.17.send.refs_3_, s32[1536,1]{1,0:T(8,128)S(1)} %copy.18.recv), custom_call_target="tpu_custom_call" | custom-call | flops 3221225472 | tf_op jit(solution)/shard_map/gather_rows/pallas_call | solution.py:77
  60.6 1.3 %collective-permute-done.21.refs_14_.refs_16_ = bf16[128,1536]{1,0:T(8,128)(2,1)S(1)} collective-permute-done((bf16[128,1536]{1,0:T(8,128)(2,1)S(1)}, bf16[128,1536]{1,0:T(8,128)(2,1)S(1)}, u32[]{:S(2)}, u32[]{:S(2)}) %collective-permute-start.21) | collective-permute-done | bytes 393248 | tf_op jit(solution)/shard_map/ppermute | solution.py:492
  64.3 1.1 %collective-permute-start.29 = (bf16[128,768]{1,0:T(8,128)(2,1)S(1)}, bf16[128,768]{1,0:T(8,128)(2,1)S(1)}, u32[]{:S(2)}, u32[]{:S(2)}) collective-permute-start(bf16[128,768]{1,0:T(8,128)(2,1)S(1)} %copy-done.15), channel_id=1, source_target_pairs={{0,2},{1,3},{2,0},{3,1},{4,6},{5,7},{6,4},{7,5},{8,10},{9,11},{10,... | collective-permute-start | bytes 589832 | tf_op jit(solution)/shard_map/ppermute | solution.py:492
  66.2 5.3 %fine_edges.3 = (bf16[1536,512]{1,0:T(8,128)(2,1)S(1)}, bf16[448,512]{1,0:T(8,128)(2,1)S(1)}) custom-call(bf16[1536,512]{1,0:T(8,128)(2,1)S(1)} %get-tuple-element.87.new_fine.refs_0_, bf16[1536,512]{1,0:T(8,128)(2,1)S(1)} %get-tuple-element.109.refs_1_, bf16[1536,512]{1,0:T(8,128)(2,1)S(1)} %get-tuple-element.110.refs_2_, s32[1536,1]{1,0:T(8,128)S(1)} %copy.17.send.refs_3_, ...), custom_call_target="tpu_custom_call" | custom-call | flops 3221225472 | tf_op jit(solution)/shard_map/fine_edges/pallas_call | solution.py:77
  72.5 0.9 %collective-permute-done.31.arrived = bf16[448,512]{1,0:T(8,128)(2,1)S(1)} collective-permute-done((bf16[448,512]{1,0:T(8,128)(2,1)S(1)}, bf16[448,512]{1,0:T(8,128)(2,1)S(1)}, u32[]{:S(2)}, u32[]{:S(2)}) %collective-permute-start.31) | collective-permute-done | bytes 458784 | tf_op jit(solution)/shard_map/ppermute | solution.py:489
  73.5 1.1 %collective-permute-start.32 = (bf16[448,512]{1,0:T(8,128)(2,1)S(1)}, bf16[448,512]{1,0:T(8,128)(2,1)S(1)}, u32[]{:S(2)}, u32[]{:S(2)}) collective-permute-start(bf16[448,512]{1,0:T(8,128)(2,1)S(1)} %core_sum.6.refs_3_), channel_id=1, source_target_pairs={{0,2},{1,3},{2,0},{3,1},{4,6},{5,7},{6,4},{7,5},{8,10},{9,11},{10,... | collective-permute-start | bytes 1376264 | tf_op jit(solution)/shard_map/ppermute | solution.py:492
  74.6 1.0 %collective-permute-start.34 = (bf16[128,768]{1,0:T(8,128)(2,1)S(1)}, bf16[128,768]{1,0:T(8,128)(2,1)S(1)}, u32[]{:S(2)}, u32[]{:S(2)}) collective-permute-start(bf16[128,768]{1,0:T(8,128)(2,1)S(1)} %collective-permute-done.29.refs_9_), channel_id=1, source_target_pairs={{0,16},{16,0},{1,17},{17,1},{2,18},{18,2},{3,19},{19,3},{4,20},{20... | collective-permute-start | bytes 589832 | tf_op jit(solution)/shard_map/ppermute | solution.py:671
  76.1 1.3 %collective-permute-done.33.refs_9_ = bf16[64,512]{1,0:T(8,128)(2,1)S(1)} collective-permute-done((bf16[64,512]{1,0:T(8,128)(2,1)S(1)}, bf16[64,512]{1,0:T(8,128)(2,1)S(1)}, u32[]{:S(2)}, u32[]{:S(2)}) %collective-permute-start.33) | collective-permute-done | bytes 65568 | tf_op jit(solution)/shard_map/ppermute | solution.py:489
  77.4 3.4 %coarse_edges_and_sums.3 = (bf16[384,640]{1,0:T(8,128)(2,1)}, bf16[64,512]{1,0:T(8,128)(2,1)S(1)}, f32[64,512]{1,0:T(8,128)S(1)}) custom-call(bf16[1536,512]{1,0:T(8,128)(2,1)S(1)} %get-tuple-element.116.new_fine.refs_0_, s32[1,1536]{1,0:T(1,128)S(1)} %reshape.23.refs_4_.recv_row.refs_1_, bf16[128,512]{1,0:T(8,128)(2,1)S(1)} %get-tuple-element.120.refs_2_, ...), custom_call_target="tpu_custom_call" | custom-call | tf_op jit(solution)/shard_map/coarse_edges_and_sums/pallas_call | solution.py:77
  81.8 1.0 %collective-permute-done.35.arrived = bf16[64,512]{1,0:T(8,128)(2,1)S(1)} collective-permute-done((bf16[64,512]{1,0:T(8,128)(2,1)S(1)}, bf16[64,512]{1,0:T(8,128)(2,1)S(1)}, u32[]{:S(2)}, u32[]{:S(2)}) %collective-permute-start.35) | collective-permute-done | bytes 65568 | tf_op jit(solution)/shard_map/ppermute | solution.py:489
  82.8 1.0 %collective-permute-start.36 = (bf16[64,512]{1,0:T(8,128)(2,1)S(1)}, bf16[64,512]{1,0:T(8,128)(2,1)S(1)}, u32[]{:S(2)}, u32[]{:S(2)}) collective-permute-start(bf16[64,512]{1,0:T(8,128)(2,1)S(1)} %core_sum.7.refs_5_), channel_id=1, source_target_pairs={{0,2},{1,3},{2,0},{3,1},{4,6},{5,7},{6,4},{7,5},{8,10},{9,11},{10,... | collective-permute-start | bytes 196616 | tf_op jit(solution)/shard_map/ppermute | solution.py:492
  83.9 3.6 %collective-permute-done.36.refs_6_ = bf16[64,512]{1,0:T(8,128)(2,1)S(1)} collective-permute-done((bf16[64,512]{1,0:T(8,128)(2,1)S(1)}, bf16[64,512]{1,0:T(8,128)(2,1)S(1)}, u32[]{:S(2)}, u32[]{:S(2)}) %collective-permute-start.36) | collective-permute-done | bytes 65568 | tf_op jit(solution)/shard_map/ppermute | solution.py:492
  87.5 1.7 %node_update.3.own = bf16[512,512]{1,0:T(8,128)(2,1)S(1)} custom-call(bf16[1024,512]{1,0:T(8,128)(2,1)S(1)} %get-tuple-element.103.nodes.refs_0_, f32[8,512]{1,0:T(8,128)S(1)} %get-tuple-element.86.refs_4_.refs_1_.refs_20_, bf16[2,512]{1,0:T(2,128)(2,1)S(1)} %copy-done.9, bf16[448,512]{1,0:T(8,128)(2,1)S(1)} %core_sum.6.refs_3_, ...), custom_call_target="tpu_custom_call" | custom-call | tf_op jit(solution)/shard_map/node_update/pallas_call | solution.py:77
  89.3 1.9 %collective-permute-done.40.other = bf16[512,512]{1,0:T(8,128)(2,1)S(1)} collective-permute-done((bf16[512,512]{1,0:T(8,128)(2,1)S(1)}, bf16[512,512]{1,0:T(8,128)(2,1)S(1)}, u32[]{:S(2)}, u32[]{:S(2)}) %collective-permute-start.40) | collective-permute-done | bytes 524320 | tf_op jit(solution)/shard_map/ppermute | solution.py:489
  91.2 1.0 %nodes_out.1 = bf16[1024,512]{1,0:T(8,128)(2,1)} custom-call(bf16[512,512]{1,0:T(8,128)(2,1)S(1)} %node_update.3.own, bf16[512,512]{1,0:T(8,128)(2,1)S(1)} %collective-permute-done.40.other), custom_call_target="tpu_custom_call" | custom-call | tf_op jit(solution)/shard_map/nodes_out/pallas_call | solution.py:77
  (108 shorter events, 14.1 us)
Async XLA Ops:
  3.2 9.8 %collective-permute-start.3 = (bf16[128,2176]{1,0:T(8,128)(2,1)}, bf16[128,2176]{1,0:T(8,128)(2,1)}, u32[]{:S(2)}, u32[]{:S(2)}) collective-permute-start(bf16[128,2176]{1,0:T(8,128)(2,1)} %get-tuple-element.69.refs_10_.refs_12_), channel_id=1, source_target_pairs={{0,1},{1,0},{2,3},{3,2},{4,5},{5,4},{6,7},{7,6},{8,9},{9,8},{10,11... | collective-permute-start | bytes 1671176 | tf_op jit(solution)/shard_map/ppermute | solution.py:489
  3.7 18.1 %collective-permute-start.2 = (bf16[128,2176]{1,0:T(8,128)(2,1)}, bf16[128,2176]{1,0:T(8,128)(2,1)S(1)}, u32[]{:S(2)}, u32[]{:S(2)}) collective-permute-start(bf16[128,2176]{1,0:T(8,128)(2,1)} %get-tuple-element.69.refs_10_.refs_12_), channel_id=1, source_target_pairs={{0,2},{1,3},{2,0},{3,1},{4,6},{5,7},{6,4},{7,5},{8,10},{9,11},{10,... | collective-permute-start | bytes 1671176 | tf_op jit(solution)/shard_map/ppermute | solution.py:492
  6.3 11.4 %collective-permute-start.1 = (bf16[240,512]{1,0:T(8,128)(2,1)}, bf16[240,512]{1,0:T(8,128)(2,1)}, u32[]{:S(2)}, u32[]{:S(2)}) collective-permute-start(bf16[240,512]{1,0:T(8,128)(2,1)} %get-tuple-element.68), channel_id=1, source_target_pairs={{0,12},{4,0},{8,4},{12,8},{1,13},{5,1},{9,5},{13,9},{2,14},{6,2},{... | collective-permute-start | bytes 737288 | tf_op jit(solution)/shard_map/ppermute | solution.py:495
  9.9 11.9 %collective-permute-start = (bf16[240,512]{1,0:T(8,128)(2,1)}, bf16[240,512]{1,0:T(8,128)(2,1)S(1)}, u32[]{:S(2)}, u32[]{:S(2)}) collective-permute-start(bf16[240,512]{1,0:T(8,128)(2,1)} %get-tuple-element.67), channel_id=1, source_target_pairs={{0,4},{4,8},{8,12},{12,0},{1,5},{5,9},{9,13},{13,1},{2,6},{6,10},{... | collective-permute-start | bytes 737288 | tf_op jit(solution)/shard_map/ppermute | solution.py:495
  21.8 2.9 %collective-permute-start.6 = (bf16[128,2176]{1,0:T(8,128)(2,1)S(1)}, bf16[128,2176]{1,0:T(8,128)(2,1)S(1)}, u32[]{:S(2)}, u32[]{:S(2)}) collective-permute-start(bf16[128,2176]{1,0:T(8,128)(2,1)S(1)} %collective-permute-done.2.refs_12_.refs_14_), channel_id=1, source_target_pairs={{0,1},{1,0},{2,3},{3,2},{4,5},{5,4},{6,7},{7,6},{8,9},{9,8},{10,11... | collective-permute-start | bytes 1671176 | tf_op jit(solution)/shard_map/ppermute | solution.py:489
  21.8 2.9 %collective-permute-start.4 = (bf16[240,512]{1,0:T(8,128)(2,1)S(1)}, bf16[240,512]{1,0:T(8,128)(2,1)S(1)}, u32[]{:S(2)}, u32[]{:S(2)}) collective-permute-start(bf16[240,512]{1,0:T(8,128)(2,1)S(1)} %collective-permute-done.refs_6_.rows), channel_id=1, source_target_pairs={{0,1},{1,0},{2,3},{3,2},{4,5},{5,4},{6,7},{7,6},{8,9},{9,8},{10,11... | collective-permute-start | bytes 737288 | tf_op jit(solution)/shard_map/ppermute | solution.py:489
  22.3 2.4 %collective-permute-start.5 = (bf16[240,512]{1,0:T(8,128)(2,1)}, bf16[240,512]{1,0:T(8,128)(2,1)S(1)}, u32[]{:S(2)}, u32[]{:S(2)}) collective-permute-start(bf16[240,512]{1,0:T(8,128)(2,1)} %collective-permute-done.1.refs_8_.refs_10_), channel_id=1, source_target_pairs={{0,1},{1,0},{2,3},{3,2},{4,5},{5,4},{6,7},{7,6},{8,9},{9,8},{10,11... | collective-permute-start | bytes 737288 | tf_op jit(solution)/shard_map/ppermute | solution.py:489
  22.3 8.7 %collective-permute-start.7 = (bf16[128,1024]{1,0:T(8,128)(2,1)S(1)}, bf16[128,1024]{1,0:T(8,128)(2,1)S(1)}, u32[]{:S(2)}, u32[]{:S(2)}) collective-permute-start(bf16[128,1024]{1,0:T(8,128)(2,1)S(1)} %copy-done.14), channel_id=1, source_target_pairs={{0,2},{1,3},{2,0},{3,1},{4,6},{5,7},{6,4},{7,5},{8,10},{9,11},{10,... | collective-permute-start | bytes 786440 | tf_op jit(solution)/shard_map/ppermute | solution.py:492
  22.9 8.7 %collective-permute-start.8 = (bf16[176,512]{1,0:T(8,128)(2,1)S(1)}, bf16[176,512]{1,0:T(8,128)(2,1)S(1)}, u32[]{:S(2)}, u32[]{:S(2)}) collective-permute-start(bf16[176,512]{1,0:T(8,128)(2,1)S(1)} %far_rows.2), channel_id=1, source_target_pairs={{0,4},{4,8},{8,12},{12,0},{1,5},{5,9},{9,13},{13,1},{2,6},{6,10},{... | collective-permute-start | bytes 540680 | tf_op jit(solution)/shard_map/ppermute | solution.py:495
  33.5 15.0 %collective-permute-start.10 = (bf16[448,512]{1,0:T(8,128)(2,1)S(1)}, bf16[448,512]{1,0:T(8,128)(2,1)S(1)}, u32[]{:S(2)}, u32[]{:S(2)}) collective-permute-start(bf16[448,512]{1,0:T(8,128)(2,1)S(1)} %core_sum.4.refs_3_), channel_id=1, source_target_pairs={{0,2},{1,3},{2,0},{3,1},{4,6},{5,7},{6,4},{7,5},{8,10},{9,11},{10,... | collective-permute-start | bytes 1376264 | tf_op jit(solution)/shard_map/ppermute | solution.py:492
  35.1 7.4 %collective-permute-start.12 = (bf16[128,768]{1,0:T(8,128)(2,1)S(1)}, bf16[128,768]{1,0:T(8,128)(2,1)S(1)}, u32[]{:S(2)}, u32[]{:S(2)}) collective-permute-start(bf16[128,768]{1,0:T(8,128)(2,1)S(1)} %get-tuple-element.96), channel_id=1, source_target_pairs={{0,16},{16,0},{1,17},{17,1},{2,18},{18,2},{3,19},{19,3},{4,20},{20... | collective-permute-start | bytes 589832 | tf_op jit(solution)/shard_map/ppermute | solution.py:671
  36.7 11.8 %collective-permute-start.15 = (bf16[128,1536]{1,0:T(8,128)(2,1)S(1)}, bf16[128,1536]{1,0:T(8,128)(2,1)S(1)}, u32[]{:S(2)}, u32[]{:S(2)}) collective-permute-start(bf16[128,1536]{1,0:T(8,128)(2,1)S(1)} %copy-done.4), channel_id=1, source_target_pairs={{0,1},{1,0},{2,3},{3,2},{4,5},{5,4},{6,7},{7,6},{8,9},{9,8},{10,11... | collective-permute-start | bytes 1179656 | tf_op jit(solution)/shard_map/ppermute | solution.py:489
  37.2 11.3 %collective-permute-start.16 = (bf16[128,1024]{1,0:T(8,128)(2,1)S(1)}, bf16[128,1024]{1,0:T(8,128)(2,1)S(1)}, u32[]{:S(2)}, u32[]{:S(2)}) collective-permute-start(bf16[128,1024]{1,0:T(8,128)(2,1)S(1)} %collective-permute-done.7.pack.refs_9_.refs_16_.refs_18_), channel_id=1, source_target_pairs={{0,1},{1,0},{2,3},{3,2},{4,5},{5,4},{6,7},{7,6},{8,9},{9,8},{10,11... | collective-permute-start | bytes 786440 | tf_op jit(solution)/shard_map/ppermute | solution.py:489
  42.5 6.0 %collective-permute-start.17 = (bf16[128,768]{1,0:T(8,128)(2,1)S(1)}, bf16[128,768]{1,0:T(8,128)(2,1)S(1)}, u32[]{:S(2)}, u32[]{:S(2)}) collective-permute-start(bf16[128,768]{1,0:T(8,128)(2,1)S(1)} %collective-permute-done.12.refs_10_), channel_id=1, source_target_pairs={{0,1},{1,0},{2,3},{3,2},{4,5},{5,4},{6,7},{7,6},{8,9},{9,8},{10,11... | collective-permute-start | bytes 589832 | tf_op jit(solution)/shard_map/ppermute | solution.py:489
  44.2 4.3 %collective-permute-start.14 = (bf16[64,512]{1,0:T(8,128)(2,1)S(1)}, bf16[64,512]{1,0:T(8,128)(2,1)S(1)}, u32[]{:S(2)}, u32[]{:S(2)}) collective-permute-start(bf16[64,512]{1,0:T(8,128)(2,1)S(1)} %core_sum.5.refs_5_), channel_id=1, source_target_pairs={{0,2},{1,3},{2,0},{3,1},{4,6},{5,7},{6,4},{7,5},{8,10},{9,11},{10,... | collective-permute-start | bytes 196616 | tf_op jit(solution)/shard_map/ppermute | solution.py:492
  50.2 2.2 %collective-permute-start.18 = (bf16[512,512]{1,0:T(8,128)(2,1)S(1)}, bf16[512,512]{1,0:T(8,128)(2,1)S(1)}, u32[]{:S(2)}, u32[]{:S(2)}) collective-permute-start(bf16[512,512]{1,0:T(8,128)(2,1)S(1)} %node_update.2.refs_0_), channel_id=1, source_target_pairs={{0,1},{1,0},{2,3},{3,2},{4,5},{5,4},{6,7},{7,6},{8,9},{9,8},{10,11... | collective-permute-start | bytes 1572872 | tf_op jit(solution)/shard_map/ppermute | solution.py:489
  50.3 11.5 %collective-permute-start.21 = (bf16[128,1536]{1,0:T(8,128)(2,1)S(1)}, bf16[128,1536]{1,0:T(8,128)(2,1)S(1)}, u32[]{:S(2)}, u32[]{:S(2)}) collective-permute-start(bf16[128,1536]{1,0:T(8,128)(2,1)S(1)} %copy-done.3), channel_id=1, source_target_pairs={{0,2},{1,3},{2,0},{3,1},{4,6},{5,7},{6,4},{7,5},{8,10},{9,11},{10,... | collective-permute-start | bytes 1179656 | tf_op jit(solution)/shard_map/ppermute | solution.py:492
  50.9 9.7 %collective-permute-start.22 = (bf16[128,256]{1,0:T(8,128)(2,1)S(1)}, bf16[128,256]{1,0:T(8,128)(2,1)S(1)}, u32[]{:S(2)}, u32[]{:S(2)}) collective-permute-start(bf16[128,256]{1,0:T(8,128)(2,1)S(1)} %get-tuple-element.108), channel_id=1, source_target_pairs={{0,16},{16,0},{1,17},{17,1},{2,18},{18,2},{3,19},{19,3},{4,20},{20... | collective-permute-start | bytes 196616 | tf_op jit(solution)/shard_map/ppermute | solution.py:671
  52.4 11.9 %collective-permute-start.25 = (bf16[128,1536]{1,0:T(8,128)(2,1)S(1)}, bf16[128,1536]{1,0:T(8,128)(2,1)S(1)}, u32[]{:S(2)}, u32[]{:S(2)}) collective-permute-start(bf16[128,1536]{1,0:T(8,128)(2,1)S(1)} %copy-done.3), channel_id=1, source_target_pairs={{0,1},{1,0},{2,3},{3,2},{4,5},{5,4},{6,7},{7,6},{8,9},{9,8},{10,11... | collective-permute-start | bytes 1179656 | tf_op jit(solution)/shard_map/ppermute | solution.py:489
  53.2 8.6 %collective-permute-start.19 = (bf16[128,512]{1,0:T(8,128)(2,1)S(1)}, bf16[128,512]{1,0:T(8,128)(2,1)S(1)}, u32[]{:S(2)}, u32[]{:S(2)}) collective-permute-start(bf16[128,512]{1,0:T(8,128)(2,1)S(1)} %get-tuple-element.104), channel_id=1, source_target_pairs={{0,4},{4,8},{8,12},{12,0},{1,5},{5,9},{9,13},{13,1},{2,6},{6,10},{... | collective-permute-start | bytes 393224 | tf_op jit(solution)/shard_map/ppermute | solution.py:495
  53.6 8.7 %collective-permute-start.20 = (bf16[128,512]{1,0:T(8,128)(2,1)S(1)}, bf16[128,512]{1,0:T(8,128)(2,1)S(1)}, u32[]{:S(2)}, u32[]{:S(2)}) collective-permute-start(bf16[128,512]{1,0:T(8,128)(2,1)S(1)} %get-tuple-element.105), channel_id=1, source_target_pairs={{0,12},{4,0},{8,4},{12,8},{1,13},{5,1},{9,5},{13,9},{2,14},{6,2},{... | collective-permute-start | bytes 393224 | tf_op jit(solution)/shard_map/ppermute | solution.py:495
  62.3 3.9 %collective-permute-start.27 = (bf16[128,1536]{1,0:T(8,128)(2,1)S(1)}, bf16[128,1536]{1,0:T(8,128)(2,1)S(1)}, u32[]{:S(2)}, u32[]{:S(2)}) collective-permute-start(bf16[128,1536]{1,0:T(8,128)(2,1)S(1)} %collective-permute-done.21.refs_14_.refs_16_), channel_id=1, source_target_pairs={{0,1},{1,0},{2,3},{3,2},{4,5},{5,4},{6,7},{7,6},{8,9},{9,8},{10,11... | collective-permute-start | bytes 1179656 | tf_op jit(solution)/shard_map/ppermute | solution.py:489
  62.8 3.4 %collective-permute-start.23 = (bf16[128,512]{1,0:T(8,128)(2,1)S(1)}, bf16[128,512]{1,0:T(8,128)(2,1)S(1)}, u32[]{:S(2)}, u32[]{:S(2)}) collective-permute-start(bf16[128,512]{1,0:T(8,128)(2,1)S(1)} %collective-permute-done.19.refs_6_.rows), channel_id=1, source_target_pairs={{0,1},{1,0},{2,3},{3,2},{4,5},{5,4},{6,7},{7,6},{8,9},{9,8},{10,11... | collective-permute-start | bytes 393224 | tf_op jit(solution)/shard_map/ppermute | solution.py:489
  62.8 3.4 %collective-permute-start.24 = (bf16[128,512]{1,0:T(8,128)(2,1)S(1)}, bf16[128,512]{1,0:T(8,128)(2,1)S(1)}, u32[]{:S(2)}, u32[]{:S(2)}) collective-permute-start(bf16[128,512]{1,0:T(8,128)(2,1)S(1)} %collective-permute-done.20.refs_8_.refs_10_), channel_id=1, source_target_pairs={{0,1},{1,0},{2,3},{3,2},{4,5},{5,4},{6,7},{7,6},{8,9},{9,8},{10,11... | collective-permute-start | bytes 393224 | tf_op jit(solution)/shard_map/ppermute | solution.py:489
  64.3 7.2 %collective-permute-start.29 = (bf16[128,768]{1,0:T(8,128)(2,1)S(1)}, bf16[128,768]{1,0:T(8,128)(2,1)S(1)}, u32[]{:S(2)}, u32[]{:S(2)}) collective-permute-start(bf16[128,768]{1,0:T(8,128)(2,1)S(1)} %copy-done.15), channel_id=1, source_target_pairs={{0,2},{1,3},{2,0},{3,1},{4,6},{5,7},{6,4},{7,5},{8,10},{9,11},{10,... | collective-permute-start | bytes 589832 | tf_op jit(solution)/shard_map/ppermute | solution.py:492
  65.5 6.1 %collective-permute-start.30 = (bf16[64,512]{1,0:T(8,128)(2,1)S(1)}, bf16[64,512]{1,0:T(8,128)(2,1)S(1)}, u32[]{:S(2)}, u32[]{:S(2)}) collective-permute-start(bf16[64,512]{1,0:T(8,128)(2,1)S(1)} %far_rows.3), channel_id=1, source_target_pairs={{0,4},{4,8},{8,12},{12,0},{1,5},{5,9},{9,13},{13,1},{2,6},{6,10},{... | collective-permute-start | bytes 196616 | tf_op jit(solution)/shard_map/ppermute | solution.py:495
  73.5 14.0 %collective-permute-start.32 = (bf16[448,512]{1,0:T(8,128)(2,1)S(1)}, bf16[448,512]{1,0:T(8,128)(2,1)S(1)}, u32[]{:S(2)}, u32[]{:S(2)}) collective-permute-start(bf16[448,512]{1,0:T(8,128)(2,1)S(1)} %core_sum.6.refs_3_), channel_id=1, source_target_pairs={{0,2},{1,3},{2,0},{3,1},{4,6},{5,7},{6,4},{7,5},{8,10},{9,11},{10,... | collective-permute-start | bytes 1376264 | tf_op jit(solution)/shard_map/ppermute | solution.py:492
  74.6 6.7 %collective-permute-start.34 = (bf16[128,768]{1,0:T(8,128)(2,1)S(1)}, bf16[128,768]{1,0:T(8,128)(2,1)S(1)}, u32[]{:S(2)}, u32[]{:S(2)}) collective-permute-start(bf16[128,768]{1,0:T(8,128)(2,1)S(1)} %collective-permute-done.29.refs_9_), channel_id=1, source_target_pairs={{0,16},{16,0},{1,17},{17,1},{2,18},{18,2},{3,19},{19,3},{4,20},{20... | collective-permute-start | bytes 589832 | tf_op jit(solution)/shard_map/ppermute | solution.py:671
  75.6 8.3 %collective-permute-start.37 = (bf16[128,1536]{1,0:T(8,128)(2,1)S(1)}, bf16[128,1536]{1,0:T(8,128)(2,1)S(1)}, u32[]{:S(2)}, u32[]{:S(2)}) collective-permute-start(bf16[128,1536]{1,0:T(8,128)(2,1)S(1)} %copy-done.2), channel_id=1, source_target_pairs={{0,1},{1,0},{2,3},{3,2},{4,5},{5,4},{6,7},{7,6},{8,9},{9,8},{10,11... | collective-permute-start | bytes 1179656 | tf_op jit(solution)/shard_map/ppermute | solution.py:489
  76.1 7.8 %collective-permute-start.38 = (bf16[128,768]{1,0:T(8,128)(2,1)S(1)}, bf16[128,768]{1,0:T(8,128)(2,1)S(1)}, u32[]{:S(2)}, u32[]{:S(2)}) collective-permute-start(bf16[128,768]{1,0:T(8,128)(2,1)S(1)} %collective-permute-done.29.refs_9_), channel_id=1, source_target_pairs={{0,1},{1,0},{2,3},{3,2},{4,5},{5,4},{6,7},{7,6},{8,9},{9,8},{10,11... | collective-permute-start | bytes 589832 | tf_op jit(solution)/shard_map/ppermute | solution.py:489
  81.3 6.3 %collective-permute-start.39 = (bf16[128,768]{1,0:T(8,128)(2,1)S(1)}, bf16[128,768]{1,0:T(8,128)(2,1)S(1)}, u32[]{:S(2)}, u32[]{:S(2)}) collective-permute-start(bf16[128,768]{1,0:T(8,128)(2,1)S(1)} %collective-permute-done.34.refs_10_), channel_id=1, source_target_pairs={{0,1},{1,0},{2,3},{3,2},{4,5},{5,4},{6,7},{7,6},{8,9},{9,8},{10,11... | collective-permute-start | bytes 589832 | tf_op jit(solution)/shard_map/ppermute | solution.py:489
  82.8 4.7 %collective-permute-start.36 = (bf16[64,512]{1,0:T(8,128)(2,1)S(1)}, bf16[64,512]{1,0:T(8,128)(2,1)S(1)}, u32[]{:S(2)}, u32[]{:S(2)}) collective-permute-start(bf16[64,512]{1,0:T(8,128)(2,1)S(1)} %core_sum.7.refs_5_), channel_id=1, source_target_pairs={{0,2},{1,3},{2,0},{3,1},{4,6},{5,7},{6,4},{7,5},{8,10},{9,11},{10,... | collective-permute-start | bytes 196616 | tf_op jit(solution)/shard_map/ppermute | solution.py:492
  (25 other events, 140.4 us)
